TPU v7x, 32 devices: a whole 2x2x4 slice. The times are simulated.
32 devices in a mesh: members: 2 (over y), loop: 8 (over z, x), lat: 2 (over core).
Axes of the slice: x: 2, y: 2, z: 4, core: 2. Of those that a mesh axis runs over, the one named last changes fastest.
Arguments:
- state: float32 [4, 50, 64, 256], P('members', None, 'loop', 'lat'), parts along dimension 0, may hold values from -6 to 6
- observed: float32 [4, 50, 64, 256], P('members', None, 'loop', 'lat'), parts along dimension 0, may hold values from -4.5 to 6
- weight: float32 [50, 64, 256], P(None, 'loop', 'lat'), may hold values from 0.2 to 2
- control: float32 [4, 64, 256], P('members', 'loop', 'lat'), parts along dimension 0, may hold values from -6 to 6
- depth_index: int32 [64, 256], P('loop', 'lat'), may hold values from 0 to 50
- diffusivity: float32 [64, 256], P('loop', 'lat'), may hold values from 0.02 to 0.22
- damping: float32 [64, 256], P('loop', 'lat'), may hold values from 0.25 to 2
- history_step: float32 [16, 2, 64, 256], P('members', None, 'loop', 'lat'), parts along dimension 0, may hold values from -0.5 to 0.5
- history_change: float32 [16, 2, 64, 256], P('members', None, 'loop', 'lat'), parts along dimension 0, may hold values from -2.5 to 2.5, as said below
Outputs:
- state_next: float32 [4, 50, 64, 256], P('members', None, 'loop', 'lat'), parts along dimension 0
- gradient: float32 [4, 64, 256], P('members', 'loop', 'lat'), parts along dimension 0
- direction: float32 [4, 64, 256], P('members', 'loop', 'lat'), parts along dimension 0
There are 2 independent parts, one for each index of `members`. A program takes and returns all parts, laid end to end along the dimension named above; an argument that names none is the same for every part. Nothing has to cross between parts.
Inputs may be any that keep to these rules, and one draw needn't show every extreme that they name: `history_change`: each entry of a stored change has the sign of the matching entry of its step, so that every pair's inner product is positive.
All inputs are finite; a program needn't handle non-finite values.
Results may differ from a plain program's by a relative error of at most 0.0003.
Values sent between devices are 32-bit elements; how exact they have to be, the bound alone decides.
No kernel may reach another device: no remote copies, remote signals or barrier semaphores. Data moves between devices by JAX's collectives and lax.ppermute only.
A program may use at most 64 MiB of HBM per device.

v0:
```python
import jax
import jax.numpy as jnp
from jax import lax
from jax.sharding import PartitionSpec as P

ITERS = 3
SUB = 3


SURFACE_GAIN = 5.0
NEIGHBOURS = ((0, 1), (2, 1), (1, 0), (1, 2))


def extended(block, sides, width):
    for axis, dim in sides:
        count = lax.axis_size(axis)
        forward = [(i, i + 1) for i in range(count - 1)]
        forward.append((count - 1, 0))
        backward = [(target, source) for source, target in forward]
        low = lax.ppermute(
            lax.slice_in_dim(block, block.shape[dim] - width, None, axis=dim), axis, forward
        )
        high = lax.ppermute(lax.slice_in_dim(block, 0, width, axis=dim), axis, backward)
        block = jnp.concatenate([low, block, high], axis=dim)
    return block


def interior(array, width):
    rows = array.shape[-2]
    cols = array.shape[-1]
    return array[..., width : rows - width, width : cols - width]


def smooth(field, depths, spread, levels):
    rows = field.shape[-2] - 2
    cols = field.shape[-1] - 2
    centre = field[..., 1 : rows + 1, 1 : cols + 1]
    depth_here = depths[1 : rows + 1, 1 : cols + 1]
    spread_here = spread[1 : rows + 1, 1 : cols + 1]
    total = centre
    for row_at, col_at in NEIGHBOURS:
        beside = field[..., row_at : row_at + rows, col_at : col_at + cols]
        depth_there = depths[row_at : row_at + rows, col_at : col_at + cols]
        spread_there = spread[row_at : row_at + rows, col_at : col_at + cols]
        open_face = (levels < jnp.minimum(depth_here, depth_there)).astype(jnp.float32)
        total = total + 0.5 * (spread_here + spread_there) * open_face * (beside - centre)
    return total


def couplings_of(depths, spread):
    rows = depths.shape[0] - 2
    cols = depths.shape[1] - 2
    wet_here = (depths[1 : rows + 1, 1 : cols + 1] > 0.5).astype(jnp.float32)
    spread_here = spread[1 : rows + 1, 1 : cols + 1]
    result = []
    for row_at, col_at in NEIGHBOURS:
        wet_there = (depths[row_at : row_at + rows, col_at : col_at + cols] > 0.5).astype(
            jnp.float32
        )
        spread_there = spread[row_at : row_at + rows, col_at : col_at + cols]
        result.append(SURFACE_GAIN * 0.5 * (spread_here + spread_there) * wet_here * wet_there)
    return result


def surface_apply(field, couplings, damping):
    padded = extended(field, (("loop", 0), ("lat", 1)), 1)
    rows = field.shape[0]
    cols = field.shape[1]
    total = damping * field
    for (row_at, col_at), coupling in zip(NEIGHBOURS, couplings):
        total = total + coupling * (field - padded[row_at : row_at + rows, col_at : col_at + cols])
    return total


def solver_total(value):
    return lax.psum(value, ("loop", "lat"))


def conjugate(rhs, couplings, damping):
    solution = jnp.zeros_like(rhs)
    residual = rhs
    search = rhs
    norm_now = solver_total(jnp.sum(residual * residual))
    for sweep in range(ITERS):
        image = surface_apply(search, couplings, damping)
        alpha = norm_now / solver_total(jnp.sum(search * image))
        solution = solution + alpha * search
        residual = residual - alpha * image
        norm_next = solver_total(jnp.sum(residual * residual))
        search = residual + norm_next / norm_now * search
        norm_now = norm_next
    return solution


def pair_total(value):
    return lax.psum(value, ("loop", "lat"))


def on_device(
    state,
    observed,
    weight,
    control,
    depth_index,
    diffusivity,
    damping,
    history_step,
    history_change,
):
    width = SUB
    levels_count = state.shape[1]
    count = history_step.shape[0]
    levels = jnp.arange(levels_count, dtype=jnp.float32)[:, None, None]
    depth = depth_index.astype(jnp.float32)
    columns = jnp.stack([diffusivity, depth])
    padded_columns = extended(columns, (("loop", 1), ("lat", 2)), width)
    lat_here = lax.axis_index("lat")
    lat_count = lax.axis_size("lat")
    col_ids = jnp.arange(padded_columns.shape[2])
    outside = (lat_here == 0) & (col_ids < width) | (lat_here == lat_count - 1) & (
        col_ids >= depth.shape[1] + width
    )
    depth_ext = jnp.where(outside[None, :], 0.0, padded_columns[1])
    spread_ext = padded_columns[0]
    column_mask = (levels < depth).astype(jnp.float32)
    sea_top = (depth > 0.5).astype(jnp.float32)
    couplings = couplings_of(interior(depth_ext, width - 1), interior(spread_ext, width - 1))
    scale = levels_count ** (-0.5)

    def mixing(field):
        depth_near = interior(depth_ext, width - 1)
        spread_near = interior(spread_ext, width - 1)
        for sweep in range(width):
            padded = extended(field, (("loop", 2), ("lat", 3)), 1)
            field = smooth(padded, depth_near, spread_near, levels)
        return field

    lifted = state.at[:, 0].add(sea_top * control)
    mixed = mixing(lifted)
    buoyancy = scale * jnp.sum(column_mask * (mixed[0] - mixed[1]), axis=0)
    elevation = conjugate(buoyancy, couplings, damping)
    lowered = column_mask * elevation
    state_next = jnp.stack([mixed[0] - lowered, mixed[1] + lowered])
    misfit = weight * (state_next - observed)
    pressure = jnp.sum(column_mask * (misfit[1] - misfit[0]), axis=0)
    response = conjugate(pressure, couplings, damping)
    raised = scale * column_mask * response
    carried = jnp.stack([misfit[0] + raised, misfit[1] - raised])
    returned = mixing(carried)
    gradient = sea_top * returned[:, 0]
    pair_inner, change_inner = lax.psum(
        (
            jnp.sum(history_step * history_change, axis=(1, 2, 3)),
            jnp.sum(history_change[count - 1] * history_change[count - 1]),
        ),
        ("loop", "lat"),
    )
    gamma = pair_inner[count - 1] / change_inner
    factors = [None] * count
    carry = gradient
    for index in range(count - 1, -1, -1):
        factors[index] = pair_total(jnp.sum(history_step[index] * carry)) / pair_inner[index]
        carry = carry - factors[index] * history_change[index]
    result = gamma * carry
    for index in range(count):
        beta = pair_total(jnp.sum(history_change[index] * result)) / pair_inner[index]
        result = result + (factors[index] - beta) * history_step[index]
    return (state_next, gradient, -result)


def solution(mesh):
    return jax.shard_map(
        on_device,
        mesh=mesh,
        in_specs=(
            P("members", None, "loop", "lat"),
            P("members", None, "loop", "lat"),
            P(None, "loop", "lat"),
            P("members", "loop", "lat"),
            P("loop", "lat"),
            P("loop", "lat"),
            P("loop", "lat"),
            P("members", None, "loop", "lat"),
            P("members", None, "loop", "lat"),
        ),
        out_specs=(
            P("members", None, "loop", "lat"),
            P("members", "loop", "lat"),
            P("members", "loop", "lat"),
        ),
        check_vma=False,
    )
```

profile of v0, /device:TPU:0, one launch (start us, length us, event | category | flops | bytes accessed | tf_op | source)
XLA Modules:
  0.0 969.9 jit_solution(5247787938064262507)
XLA Ops:
  55.7 30.4 %all-reduce.3 = (f32[]{:T(128)}, f32[]{:T(128)}) all-reduce(f32[]{:T(128)} %get-tuple-element.29, f32[]{:T(128)} %get-tuple-element.28), channel_id=1, replica_groups=mesh['members'=2,'loop'=8,'lat'=2] {'loop','lat'}, use_global_device_ids=true, to_apply=%region_2.3 | all-reduce | flops 2 | bytes 16 | tf_op jit(solution)/shard_map/psum | solution.py:76
  88.1 30.1 %psum.212 = f32[]{:T(128)} all-reduce(f32[]{:T(128)} %get-tuple-element.61), channel_id=1, replica_groups=mesh['members'=2,'loop'=8,'lat'=2] {'loop','lat'}, use_global_device_ids=true, to_apply=%region_6.7 | all-reduce | flops 1 | bytes 8 | tf_op jit(solution)/shard_map/psum | solution.py:76
  128.0 30.4 %psum.213 = f32[]{:T(128)} all-reduce(f32[]{:T(128)} %get-tuple-element.59), channel_id=1, replica_groups=mesh['members'=2,'loop'=8,'lat'=2] {'loop','lat'}, use_global_device_ids=true, to_apply=%region_8.9 | all-reduce | flops 1 | bytes 8 | tf_op jit(solution)/shard_map/psum | solution.py:76
  160.4 30.3 %psum.214 = f32[]{:T(128)} all-reduce(f32[]{:T(128)} %multiply_reduce_fusion.6), channel_id=1, replica_groups=mesh['members'=2,'loop'=8,'lat'=2] {'loop','lat'}, use_global_device_ids=true, to_apply=%region_10.11 | all-reduce | flops 1 | bytes 8 | tf_op jit(solution)/shard_map/psum | solution.py:76
  200.5 30.4 %psum.215 = f32[]{:T(128)} all-reduce(f32[]{:T(128)} %fusion.168), channel_id=1, replica_groups=mesh['members'=2,'loop'=8,'lat'=2] {'loop','lat'}, use_global_device_ids=true, to_apply=%region_12.13 | all-reduce | flops 1 | bytes 8 | tf_op jit(solution)/shard_map/psum | solution.py:76
  242.7 30.4 %all-reduce.2 = (f32[]{:T(128)}, f32[]{:T(128)}) all-reduce(f32[]{:T(128)} %get-tuple-element.27, f32[]{:T(128)} %get-tuple-element.26), channel_id=1, replica_groups=mesh['members'=2,'loop'=8,'lat'=2] {'loop','lat'}, use_global_device_ids=true, to_apply=%region_15.16 | all-reduce | flops 2 | bytes 16 | tf_op jit(solution)/shard_map/psum | solution.py:76
  275.1 30.1 %psum.218 = f32[]{:T(128)} all-reduce(f32[]{:T(128)} %get-tuple-element.56), channel_id=1, replica_groups=mesh['members'=2,'loop'=8,'lat'=2] {'loop','lat'}, use_global_device_ids=true, to_apply=%region_19.20 | all-reduce | flops 1 | bytes 8 | tf_op jit(solution)/shard_map/psum | solution.py:76
  315.0 30.4 %psum.219 = f32[]{:T(128)} all-reduce(f32[]{:T(128)} %get-tuple-element.54), channel_id=1, replica_groups=mesh['members'=2,'loop'=8,'lat'=2] {'loop','lat'}, use_global_device_ids=true, to_apply=%region_21.22 | all-reduce | flops 1 | bytes 8 | tf_op jit(solution)/shard_map/psum | solution.py:76
  347.4 30.1 %psum.220 = f32[]{:T(128)} all-reduce(f32[]{:T(128)} %multiply_reduce_fusion.1), channel_id=1, replica_groups=mesh['members'=2,'loop'=8,'lat'=2] {'loop','lat'}, use_global_device_ids=true, to_apply=%region_23.24 | all-reduce | flops 1 | bytes 8 | tf_op jit(solution)/shard_map/psum | solution.py:76
  387.3 30.4 %psum.221 = f32[]{:T(128)} all-reduce(f32[]{:T(128)} %fusion.130), channel_id=1, replica_groups=mesh['members'=2,'loop'=8,'lat'=2] {'loop','lat'}, use_global_device_ids=true, to_apply=%region_25.26 | all-reduce | flops 1 | bytes 8 | tf_op jit(solution)/shard_map/psum | solution.py:76
  454.2 30.5 %all-reduce.1 = (f32[]{:T(128)}, f32[8]{0:T(128)S(1)}) all-reduce(f32[]{:T(128)} %get-tuple-element.52, f32[8]{0:T(128)S(1)} %multiply_reduce_fusion), channel_id=1, replica_groups=mesh['members'=2,'loop'=8,'lat'=2] {'loop','lat'}, use_global_device_ids=true, to_apply=%region_31.32 | all-reduce | flops 9 | bytes 72 | tf_op jit(solution)/shard_map/psum | solution.py:96
  487.3 30.2 %psum.225 = f32[]{:T(128)} all-reduce(f32[]{:T(128)} %get-tuple-element.25), channel_id=1, replica_groups=mesh['members'=2,'loop'=8,'lat'=2] {'loop','lat'}, use_global_device_ids=true, to_apply=%region_33.34 | all-reduce | flops 1 | bytes 8 | tf_op jit(solution)/shard_map/psum | solution.py:96
  519.4 30.2 %psum.226 = f32[]{:T(128)} all-reduce(f32[]{:T(128)} %get-tuple-element.50), channel_id=1, replica_groups=mesh['members'=2,'loop'=8,'lat'=2] {'loop','lat'}, use_global_device_ids=true, to_apply=%region_35.36 | all-reduce | flops 1 | bytes 8 | tf_op jit(solution)/shard_map/psum | solution.py:96
  583.4 30.2 %psum.228 = f32[]{:T(128)} all-reduce(f32[]{:T(128)} %get-tuple-element.48), channel_id=1, replica_groups=mesh['members'=2,'loop'=8,'lat'=2] {'loop','lat'}, use_global_device_ids=true, to_apply=%region_39.40 | all-reduce | flops 1 | bytes 8 | tf_op jit(solution)/shard_map/psum | solution.py:96
  647.5 30.2 %psum.230 = f32[]{:T(128)} all-reduce(f32[]{:T(128)} %get-tuple-element.46), channel_id=1, replica_groups=mesh['members'=2,'loop'=8,'lat'=2] {'loop','lat'}, use_global_device_ids=true, to_apply=%region_43.44 | all-reduce | flops 1 | bytes 8 | tf_op jit(solution)/shard_map/psum | solution.py:96
  679.5 30.1 %all-reduce = (f32[]{:T(128)}, f32[]{:T(128)}) all-reduce(f32[]{:T(128)} %fusion.93, f32[]{:T(128)} %get-tuple-element.24), channel_id=1, replica_groups=mesh['members'=2,'loop'=8,'lat'=2] {'loop','lat'}, use_global_device_ids=true, to_apply=%region_45.46 | all-reduce | flops 2 | bytes 16 | tf_op jit(solution)/shard_map/psum | solution.py:96
  712.9 30.1 %psum.232 = f32[]{:T(128)} all-reduce(f32[]{:T(128)} %get-tuple-element.44), channel_id=1, replica_groups=mesh['members'=2,'loop'=8,'lat'=2] {'loop','lat'}, use_global_device_ids=true, to_apply=%region_47.48 | all-reduce | flops 1 | bytes 8 | tf_op jit(solution)/shard_map/psum | solution.py:96
  745.0 30.1 %psum.233 = f32[]{:T(128)} all-reduce(f32[]{:T(128)} %fusion.96), channel_id=1, replica_groups=mesh['members'=2,'loop'=8,'lat'=2] {'loop','lat'}, use_global_device_ids=true, to_apply=%region_49.50 | all-reduce | flops 1 | bytes 8 | tf_op jit(solution)/shard_map/psum | solution.py:96
  777.0 30.1 %psum.234 = f32[]{:T(128)} all-reduce(f32[]{:T(128)} %get-tuple-element.42), channel_id=1, replica_groups=mesh['members'=2,'loop'=8,'lat'=2] {'loop','lat'}, use_global_device_ids=true, to_apply=%region_51.52 | all-reduce | flops 1 | bytes 8 | tf_op jit(solution)/shard_map/psum | solution.py:96
  809.0 30.1 %psum.235 = f32[]{:T(128)} all-reduce(f32[]{:T(128)} %fusion.104), channel_id=1, replica_groups=mesh['members'=2,'loop'=8,'lat'=2] {'loop','lat'}, use_global_device_ids=true, to_apply=%region_53.54 | all-reduce | flops 1 | bytes 8 | tf_op jit(solution)/shard_map/psum | solution.py:96
  841.0 30.1 %psum.236 = f32[]{:T(128)} all-reduce(f32[]{:T(128)} %get-tuple-element.40), channel_id=1, replica_groups=mesh['members'=2,'loop'=8,'lat'=2] {'loop','lat'}, use_global_device_ids=true, to_apply=%region_55.56 | all-reduce | flops 1 | bytes 8 | tf_op jit(solution)/shard_map/psum | solution.py:96
  873.1 30.1 %psum.237 = f32[]{:T(128)} all-reduce(f32[]{:T(128)} %fusion.112), channel_id=1, replica_groups=mesh['members'=2,'loop'=8,'lat'=2] {'loop','lat'}, use_global_device_ids=true, to_apply=%region_57.58 | all-reduce | flops 1 | bytes 8 | tf_op jit(solution)/shard_map/psum | solution.py:96
  905.1 30.1 %psum.238 = f32[]{:T(128)} all-reduce(f32[]{:T(128)} %get-tuple-element.38), channel_id=1, replica_groups=mesh['members'=2,'loop'=8,'lat'=2] {'loop','lat'}, use_global_device_ids=true, to_apply=%region_59.60 | all-reduce | flops 1 | bytes 8 | tf_op jit(solution)/shard_map/psum | solution.py:96
  937.8 30.1 %psum.239 = f32[]{:T(128)} all-reduce(f32[]{:T(128)} %fusion.124), channel_id=1, replica_groups=mesh['members'=2,'loop'=8,'lat'=2] {'loop','lat'}, use_global_device_ids=true, to_apply=%region_61.62 | all-reduce | flops 1 | bytes 8 | tf_op jit(solution)/shard_map/psum | solution.py:96
  (261 shorter events, 207.4 us)
Async XLA Ops:
  1.3 12.0 %collective-permute-start.1 = (f32[2,3,128]{2,1,0:T(4,128)S(1)}, f32[2,3,128]{2,1,0:T(4,128)S(1)}, u32[]{:S(2)}, u32[]{:S(2)}) collective-permute-start(f32[2,3,128]{2,1,0:T(4,128)S(1)} %get-tuple-element.119), channel_id=1, source_target_pairs={{2,0},{4,2},{6,4},{8,6},{10,8},{12,10},{14,12},{0,14},{3,1},{5,3},... | collective-permute-start | bytes 9224 | tf_op jit(solution)/shard_map/ppermute | solution.py:23
  7.4 6.3 collective-permute-start
  8.5 6.9 collective-permute-start.5
  13.3 6.8 collective-permute-start.4
  24.5 4.2 collective-permute-start.9
  24.6 6.9 collective-permute-start.8
  35.9 4.2 collective-permute-start.13
  35.9 6.9 collective-permute-start.12
  47.2 3.6 collective-permute-start.17
  47.3 6.3 collective-permute-start.16
  119.5 3.6 collective-permute-start.21
  119.6 6.3 collective-permute-start.20
  192.0 3.6 collective-permute-start.25
  192.1 6.3 collective-permute-start.24
  234.3 6.3 collective-permute-start.28
  306.5 3.6 collective-permute-start.33
  306.6 6.3 collective-permute-start.32
  378.9 6.3 collective-permute-start.36
  419.2 4.2 collective-permute-start.41
  419.3 6.9 collective-permute-start.40
  431.3 4.2 collective-permute-start.45
  431.4 6.9 collective-permute-start.44
  442.6 4.2 collective-permute-start.49
  442.7 7.1 collective-permute-start.48
  (42 other events, 611.5 us)
where the time goes:
time: 971 us; the launch traced here: 970 us
  blocking collectives  786 us (81%)
  waiting for transfers between devices  62.1 us (6%)
  starting transfers between devices  40.6 us (4%)
  between operations  37.1 us (4%)
  other arithmetic  23.4 us (2%)
  local copies, waits for them, and re-layouts  21.1 us (2%)
    psum x16, blocking collectives, pair_total(): return lax.psum(value, ('loop', 'lat'))  482 us
    psum x10, blocking collectives, solver_total(): return lax.psum(value, ('loop', 'lat'))  303 us
    ppermute x26, waiting for transfers between devices, extended(): lax.ppermute(lax.slice_in_dim(block, block.shape[dim] - width, None, axis...  36.8 us
    ppermute x26, starting transfers between devices, extended(): lax.ppermute(lax.slice_in_dim(block, block.shape[dim] - width, None, axis...  28.8 us
    ppermute x26, waiting for transfers between devices, extended(): lax.ppermute(lax.slice_in_dim(block, 0, width, axis=dim), axis, backward)  25.2 us
  transfers between devices with their start and end apart: 52, of which 43 were waited for; matrix products, arithmetic and copies ran while one was open for 1% of the time, Pallas kernels for 0%

commit v1 on v0

v1 whole, which is shorter than its diff:
```python
import functools

import jax
import jax.numpy as jnp
from jax import lax
from jax.experimental import pallas as pl
from jax.experimental.pallas import tpu as pltpu
from jax.sharding import PartitionSpec as P

ITERS = 3
SUB = 3
SURFACE_GAIN = 5.0
SLOT = 8
GRID = ("loop", "lat")
VMEM = pl.BlockSpec(memory_space=pltpu.VMEM)
F32 = jnp.float32


def round_up(value, to):
    return (value + to - 1) // to * to


def call(kernel, out_shapes, scratch=(), vmem=32 * 1024 * 1024, name=None):
    return pl.pallas_call(
        kernel,
        out_shape=[jax.ShapeDtypeStruct(shape, F32) for shape in out_shapes],
        out_specs=[VMEM] * len(out_shapes),
        scratch_shapes=list(scratch),
        compiler_params=pltpu.CompilerParams(vmem_limit_bytes=vmem),
        name=name,
    )


def iota(shape, dim):
    return lax.broadcasted_iota(jnp.int32, shape, dim)


def pack_kernel(
    levels, padded, state_ref, control_ref, depth_ref, spread_ref, damping_ref, weight_ref,
    rows_ref, up_ref, down_ref, still_ref,
):
    rows, cols = depth_ref.shape
    depth = depth_ref[...].astype(F32)
    spread = spread_ref[...]
    first = iota((levels, cols), 0) == 0
    rest = jnp.zeros((padded - levels, cols), F32)
    for row in range(rows):
        for tracer in range(2):
            lift = jnp.where(depth[row : row + 1] > 0.5, control_ref[tracer, row : row + 1, :], 0.0)
            value = state_ref[tracer, pl.ds(row, levels, stride=rows), :]
            rows_ref[row, pl.ds(tracer * padded, levels), :] = value + jnp.where(first, lift, 0.0)
            rows_ref[row, pl.ds(tracer * padded + levels, padded - levels), :] = rest
        rows_ref[row, pl.ds(levels, 1), :] = spread[row : row + 1]
        rows_ref[row, pl.ds(levels + 1, 1), :] = depth[row : row + 1]
        if row < SUB:
            down_ref[row] = rows_ref[row]
        if row >= rows - SUB:
            up_ref[row - rows + SUB] = rows_ref[row]
    total = jnp.zeros((rows, cols), F32)
    for level in range(levels):
        total = total + jnp.where(level < depth, weight_ref[pl.ds(level * rows, rows), :], 0.0)
    still_ref[0] = 2.0 * total
    still_ref[1] = weight_ref[pl.ds(0, rows), :]
    still_ref[2] = spread
    still_ref[3] = depth
    still_ref[4] = damping_ref[...]


def edge_of(rows_of, indices, cols, lat):
    lane = iota((1, cols), 1)
    slot = lane // SLOT
    place = lane % SLOT - SUB * lat
    mine = (place >= 0) & (place < SUB)
    total = None
    for index in indices:
        moved = pltpu.roll(rows_of(index), SLOT * index + SUB, 1)
        piece = jnp.where(mine & (slot == index), moved, 0.0)
        total = piece if total is None else total + piece
    return total


def pairs_kernel(rows_ref, step_ref, change_ref, edge_ref, gram_ref):
    rows, _, cols = rows_ref.shape
    lat = lax.axis_index("lat")
    edge_ref[...] = edge_of(lambda i: rows_ref[i - SUB], range(SUB, rows + SUB), cols, lat)
    count = step_ref.shape[0]
    lane = iota((1, cols), 1)
    total = jnp.zeros((1, cols), F32)
    at = 2 * count
    for left_ref in (step_ref, change_ref):
        for i in range(count):
            for j in range(i, count):
                value = jnp.sum(left_ref[i] * change_ref[j], axis=(0, 1), keepdims=True)
                total = total + jnp.where(lane == at, value, 0.0)
                at += 1
    gram_ref[...] = total


def border_kernel(edge_ref, low_ref, high_ref, rows_ref, out_ref):
    cols = edge_ref.shape[-1]
    rows = rows_ref.shape[0]
    lat = lax.axis_index("lat")
    total = edge_ref[...] + edge_of(lambda i: low_ref[i], range(SUB), cols, lat)
    out_ref[...] = total + edge_of(
        lambda i: high_ref[i - rows - SUB], range(rows + SUB, rows + 2 * SUB), cols, lat
    )


def mix_kernel(
    levels, padded, scale, copies,
    rows_ref, low_ref, high_ref, edge_ref, other_ref, weight_ref, observed_ref,
    mixed_ref, fields_ref, work_ref, row_face_ref, col_face_ref, part_ref,
):
    rows, planes, cols = rows_ref.shape
    lat = lax.axis_index("lat")
    lane = iota((1, cols), 1)
    level = iota((padded, cols), 0).astype(F32)
    count = rows + 2 * SUB
    work_ref[pl.ds(0, SUB)] = low_ref[...]
    work_ref[pl.ds(SUB, rows)] = rows_ref[...]
    work_ref[pl.ds(SUB + rows, SUB)] = high_ref[...]

    def left(value, by=1):
        return pltpu.roll(value, cols - by, 1)

    def right(value, by=1):
        return pltpu.roll(value, by, 1)

    def face(depth_here, depth_there, spread_here, spread_there):
        opened = level < jnp.minimum(depth_here, depth_there)
        return jnp.where(opened, 0.5 * (spread_here + spread_there), 0.0)

    spreads = [work_ref[i, pl.ds(levels, 1), :] for i in range(count)]
    depths = [work_ref[i, pl.ds(levels + 1, 1), :] for i in range(count)]
    for i in range(count - 1):
        row_face_ref[i] = face(depths[i], depths[i + 1], spreads[i], spreads[i + 1])
    for i in range(1, count - 1):
        there = jnp.where(lane < cols - 1, left(depths[i]), 0.0)
        col_face_ref[i] = face(depths[i], there, spreads[i], left(spreads[i]))

    strip = edge_ref[...] + other_ref[...]
    spread = strip[levels : levels + 1]
    depth = strip[levels + 1 : levels + 2]
    within = lane % SLOT < 2 * SUB - 1
    strip_col = face(depth, jnp.where(within, left(depth), 0.0), spread, left(spread))
    strip_row = face(depth, left(depth, SLOT), spread, left(spread, SLOT))

    first = lat == 0
    target = jnp.where(first, cols - 1, 0)
    at_border = lane == target
    for tracer in range(2):
        part = strip[tracer * padded : (tracer + 1) * padded]
        here = pl.ds(tracer * padded, padded)
        for sweep in range(1, SUB + 1):
            over_col = strip_col * (left(part) - part)
            inward = jnp.where(first, over_col, -right(over_col))
            last = None
            for i in range(sweep, count - sweep):
                centre = work_ref[i, here, :]
                if last is None:
                    last = row_face_ref[i - 1] * (centre - work_ref[i - 1, here, :])
                over_row = row_face_ref[i] * (work_ref[i + 1, here, :] - centre)
                across = col_face_ref[i] * (left(centre) - centre)
                border = right(inward, (cols - 1 - (SUB - 1) - SLOT * i) % cols)
                value = centre + (over_row - last) + (across - right(across))
                value = value + jnp.where(at_border, border, 0.0)
                last = over_row
                if sweep < SUB:
                    work_ref[i, here, :] = value
                else:
                    work_ref[i, here, :] = value
            if sweep < SUB:
                over_row = strip_row * (left(part, SLOT) - part)
                part = part + (over_col - right(over_col)) + (over_row - right(over_row, SLOT))

    for row in range(rows):
        i = row + SUB
        at = pl.ds(row, levels, stride=rows)
        mixed = [work_ref[i, pl.ds(tracer * padded, levels), :] for tracer in range(2)]
        wet = level[:levels] < depths[i]
        weight = weight_ref[at, :]
        misfit = []
        for tracer in range(2):
            mixed_ref[tracer, at, :] = mixed[tracer]
            misfit.append(weight * (mixed[tracer] - observed_ref[tracer, at, :]))
        here = pl.ds(row, 1)
        part_ref[0, here, :] = scale * jnp.sum(
            jnp.where(wet, mixed[0] - mixed[1], 0.0), axis=0, keepdims=True
        )
        part_ref[1, here, :] = jnp.sum(
            jnp.where(wet, misfit[1] - misfit[0], 0.0), axis=0, keepdims=True
        )
        part_ref[2, here, :] = misfit[0][0:1]
        part_ref[3, here, :] = misfit[1][0:1]
    for copy in range(copies):
        fields_ref[copy] = part_ref[...]


def solve_kernel(
    levels, scale,
    fields_ref, still_ref, mixed_ref, step_ref, change_ref, gram_ref,
    state_ref, gradient_ref, inner_ref, own_ref,
):
    blocks, _, rows, cols = fields_ref.shape
    lats = 2
    loops = blocks // lats
    height = loops * rows
    width = lats * cols
    mine_loop = lax.axis_index("loop")
    mine_lat = lax.axis_index("lat")

    def whole(ref, field):
        return jnp.concatenate(
            [
                jnp.concatenate([ref[lats * i + j, field] for j in range(lats)], axis=1)
                for i in range(loops)
            ],
            axis=0,
        )

    def below(value):
        return pltpu.roll(value, height - 1, 0)

    def above(value):
        return pltpu.roll(value, 1, 0)

    def left(value):
        return pltpu.roll(value, width - 1, 1)

    def right(value):
        return pltpu.roll(value, 1, 1)

    def total(value):
        return jnp.sum(value, axis=(0, 1), keepdims=True)

    buoyancy, pressure_base, base_0, base_1 = (whole(fields_ref, f) for f in range(4))
    response_weight, weight, spread, depth, damping = (whole(still_ref, f) for f in range(5))
    wet = jnp.where(depth > 0.5, 1.0, 0.0)
    inside = iota((height, width), 1) < width - 1
    row_face = 0.5 * (spread + below(spread)) * wet * below(wet)
    col_face = jnp.where(inside, 0.5 * (spread + left(spread)) * wet * left(wet), 0.0)

    def outflow(value):
        over_row = row_face * (value - below(value))
        over_col = col_face * (value - left(value))
        return (over_row - above(over_row)) + (over_col - right(over_col))

    def conjugate(rhs):
        residual = rhs
        search = rhs
        solution = None
        norm_now = total(rhs * rhs)
        for sweep in range(ITERS):
            image = damping * search + SURFACE_GAIN * outflow(search)
            alpha = norm_now / total(search * image)
            solution = alpha * search if solution is None else solution + alpha * search
            if sweep < ITERS - 1:
                residual = residual - alpha * image
                norm_next = total(residual * residual)
                search = residual + (norm_next / norm_now) * search
                norm_now = norm_next
        return solution

    elevation = conjugate(buoyancy)
    response = conjugate(pressure_base + response_weight * elevation)
    lowered = weight * wet * elevation
    raised = scale * wet * response

    def own(value, slot):
        for i in range(loops):
            for j in range(lats):
                own_ref[slot, lats * i + j] = value[
                    i * rows : (i + 1) * rows, j * cols : (j + 1) * cols
                ]
        return own_ref[slot, lats * mine_loop + mine_lat]

    depth_here = still_ref[lats * mine_loop + mine_lat, 3]
    elevation_here = own(elevation, 0)
    for level in range(levels):
        at = pl.ds(level * rows, rows)
        change = jnp.where(level < depth_here, elevation_here, 0.0)
        state_ref[0, at, :] = mixed_ref[0, at, :] - change
        state_ref[1, at, :] = mixed_ref[1, at, :] + change

    for tracer, carried in enumerate((base_0 - lowered + raised, base_1 + lowered - raised)):
        for sweep in range(SUB):
            carried = carried - outflow(carried)
        gradient_ref[tracer] = own(wet * carried, 1 + tracer)

    gradient = [gradient_ref[tracer] for tracer in range(2)]
    lane = iota((1, cols), 1)
    inner = gram_ref[...]
    count = step_ref.shape[0]
    for index, ref in enumerate((step_ref, change_ref)):
        for i in range(count):
            value = ref[i, pl.ds(0, rows), :] * gradient[0] + ref[i, pl.ds(rows, rows), :] * gradient[1]
            inner = inner + jnp.where(lane == index * count + i, total(value), 0.0)
    inner_ref[...] = jnp.broadcast_to(inner[None], inner_ref.shape)


def direction_kernel(inner_ref, gradient_ref, step_ref, change_ref, out_ref):
    count = step_ref.shape[0]
    rows = gradient_ref.shape[1]
    inner = jnp.sum(inner_ref[...], axis=0)

    def scalar(at):
        return inner[:, at : at + 1]

    step_grad = [scalar(i) for i in range(count)]
    change_grad = [scalar(count + i) for i in range(count)]
    at = 2 * count
    step_change = {}
    change_change = {}
    for table in (step_change, change_change):
        for i in range(count):
            for j in range(i, count):
                table[i, j] = table[j, i] = scalar(at)
                at += 1
    gamma = step_change[count - 1, count - 1] / change_change[count - 1, count - 1]
    factors = [None] * count
    for i in range(count - 1, -1, -1):
        factors[i] = step_grad[i] / step_change[i, i]
        for j in range(count):
            if j < i:
                step_grad[j] = step_grad[j] - factors[i] * step_change[j, i]
            change_grad[j] = change_grad[j] - factors[i] * change_change[j, i]
    change_grad = [gamma * value for value in change_grad]
    weights = []
    for i in range(count):
        weights.append(factors[i] - change_grad[i] / step_change[i, i])
        for j in range(i + 1, count):
            change_grad[j] = change_grad[j] + weights[i] * step_change[i, j]
    for tracer in range(2):
        at = pl.ds(tracer * rows, rows)
        value = gradient_ref[tracer]
        for i in range(count - 1, -1, -1):
            value = value - factors[i] * change_ref[i, at, :]
        value = gamma * value
        for i in range(count):
            value = value + weights[i] * step_ref[i, at, :]
        out_ref[tracer] = -value


def on_device(
    state, observed, weight, control, depth_index, diffusivity, damping, history_step, history_change
):
    _, levels, rows, cols = state.shape
    count = history_step.shape[0]
    padded = round_up(levels + 2, 8)
    planes = 2 * padded
    loops = lax.axis_size("loop")
    lats = lax.axis_size("lat")
    blocks = loops * lats
    scale = levels ** (-0.5)
    flat = (2, levels * rows, cols)
    state = state.reshape(flat)
    observed = observed.reshape(flat)
    weight = weight.reshape(flat[1:])
    step = history_step.reshape(count, 2 * rows, cols)
    change = history_change.reshape(count, 2 * rows, cols)

    packed, up, down, still = call(
        functools.partial(pack_kernel, levels, padded),
        [(rows, planes, cols), (SUB, planes, cols), (SUB, planes, cols), (5, rows, cols)],
        name="pack",
    )(state, control, depth_index, diffusivity, damping, weight)
    forward = [(i, (i + 1) % loops) for i in range(loops)]
    backward = [(target, source) for source, target in forward]
    low = lax.ppermute(up, "loop", forward)
    high = lax.ppermute(down, "loop", backward)
    still_all = lax.all_gather(still, GRID)
    edge, gram = call(pairs_kernel, [(planes, cols), (1, cols)], name="pairs")(packed, step, change)
    (edge,) = call(border_kernel, [(planes, cols)], name="border")(edge, low, high, packed)
    other = lax.ppermute(edge, "lat", [(0, 1), (1, 0)])
    mixed, fields = call(
        functools.partial(mix_kernel, levels, padded, scale, blocks),
        [flat, (blocks, 4, rows, cols)],
        scratch=[
            pltpu.VMEM((rows + 2 * SUB, planes, cols), F32),
            pltpu.VMEM((rows + 2 * SUB, padded, cols), F32),
            pltpu.VMEM((rows + 2 * SUB, padded, cols), F32),
            pltpu.VMEM((4, rows, cols), F32),
        ],
        name="mix",
    )(packed, low, high, edge, other, weight, observed)
    fields_all = lax.all_to_all(fields, GRID, 0, 0)
    state_next, gradient, inner = call(
        functools.partial(solve_kernel, levels, scale),
        [flat, (2, rows, cols), (blocks, 1, cols)],
        scratch=[pltpu.VMEM((3, blocks, rows, cols), F32)],
        vmem=56 * 1024 * 1024,
        name="solve",
    )(fields_all, still_all, mixed, step, change, gram)
    inner_all = lax.all_to_all(inner, GRID, 0, 0)
    (direction,) = call(direction_kernel, [(2, rows, cols)], name="direction")(
        inner_all, gradient, step, change
    )
    return (state_next.reshape(2, levels, rows, cols), gradient, direction)


def solution(mesh):
    return jax.shard_map(
        on_device,
        mesh=mesh,
        in_specs=(
            P("members", None, "loop", "lat"),
            P("members", None, "loop", "lat"),
            P(None, "loop", "lat"),
            P("members", "loop", "lat"),
            P("loop", "lat"),
            P("loop", "lat"),
            P("loop", "lat"),
            P("members", None, "loop", "lat"),
            P("members", None, "loop", "lat"),
        ),
        out_specs=(
            P("members", None, "loop", "lat"),
            P("members", "loop", "lat"),
            P("members", "loop", "lat"),
        ),
        check_vma=False,
    )
```

time: 971 us -> 73.6 us (0.08)
  blocking collectives: 786 us -> 34 us
  waiting for transfers between devices: 62.1 us -> 6.84 us
  between operations: 37.1 us -> 0.7 us
  starting transfers between devices: 40.6 us -> 10.9 us
  other arithmetic: 23.4 us -> 0 us
  local copies, waits for them, and re-layouts: 21.1 us -> 6.62 us
  Pallas kernels: 0 us -> 14.1 us
    psum x26 -> x0, blocking collectives: 786 us -> none  [the longest x16 482 us: pair_total(): return lax.psum(value, ('loop', 'lat'))]
    ppermute x52 -> x3, waiting for transfers between devices: 62.1 us -> 6.83 us  [the longest x1 3.6 us: on_device(): low = lax.ppermute(up, 'loop', forward)]
    ppermute x52 -> x3, starting transfers between devices: 40.6 us -> 6.16 us  [the longest x1 3.1 us: on_device(): high = lax.ppermute(down, 'loop', backward)]
    all_gather x0 -> x1, blocking collectives: none -> 24.1 us  [on_device(): still_all = lax.all_gather(still, GRID)]
    reduce_sum x29 -> x0, other arithmetic: 16.5 us -> none  [the longest x8 4.83 us: on_device(): jnp.sum(history_change[index] * result)]
    pallas_call x0 -> x6, Pallas kernels: none -> 14.1 us  [the longest x1 6.19 us: on_device(): call(functools.partial(mix_kernel, levels, padded, scale, blocks), [flat,...]
    all_to_all x0 -> x1, blocking collectives: none -> 9.88 us  [on_device(): inner_all = lax.all_to_all(inner, GRID, 0, 0)]
  transfers between devices with their start and end apart: 52 -> 4, of which waited for: 43 -> 3; matrix products, arithmetic and copies ran while one was open for 1% -> 0% of each run, Pallas kernels for 0% -> 0%
where the time goes in v1:
time: 73.6 us; the launch traced here: 73.1 us
  blocking collectives  34 us (46%)
  Pallas kernels  14.1 us (19%)
  starting transfers between devices  10.9 us (15%)
  waiting for transfers between devices  6.84 us (9%)
  local copies, waits for them, and re-layouts  6.62 us (9%)
    all_gather x1, blocking collectives, on_device(): still_all = lax.all_gather(still, GRID)  24.1 us
    all_to_all x1, blocking collectives, on_device(): inner_all = lax.all_to_all(inner, GRID, 0, 0)  9.88 us
    unnamed x32, local copies, waits for them, and re-layouts  6.62 us
    pallas_call x1, Pallas kernels, on_device(): call(functools.partial(mix_kernel, levels, padded, scale, blocks), [flat,...  6.19 us
    pallas_call x1, Pallas kernels, on_device(): call(functools.partial(solve_kernel, levels, scale), [flat, (2, rows, col...  4.81 us
    all_to_all x1, starting transfers between devices, on_device(): fields_all = lax.all_to_all(fields, GRID, 0, 0)  4.7 us
    ppermute x1, waiting for transfers between devices, on_device(): low = lax.ppermute(up, 'loop', forward)  3.6 us
    ppermute x1, starting transfers between devices, on_device(): high = lax.ppermute(down, 'loop', backward)  3.1 us
  transfers between devices with their start and end apart: 4, of which 3 were waited for; matrix products, arithmetic and copies ran while one was open for 0% of the time, Pallas kernels for 0%

profile of v1, /device:TPU:0, one launch (start us, length us, event | category | flops | bytes accessed | tf_op | source)
XLA Modules:
  0.0 73.1 jit_solution(499201563186999748)
XLA Ops:
  0.6 0.9 %copy-done = f32[50,8,128]{2,1,0:T(8,128)S(1)} copy-done((f32[50,8,128]{2,1,0:T(8,128)S(1)}, f32[50,8,128]{2,1,0:T(8,128)}, u32[]{:S(2)}) %copy-start) | copy-done | bytes 204824
  1.6 1.0 %copy-done.6 = f32[2,50,8,128]{3,2,1,0:T(8,128)S(1)} copy-done((f32[2,50,8,128]{3,2,1,0:T(8,128)S(1)}, f32[2,50,8,128]{3,2,1,0:T(8,128)}, u32[]{:S(2)}) %copy-start.6) | copy-done | bytes 409624
  2.6 0.7 copy-done.9
  3.3 0.7 copy-done.11
  4.0 0.7 copy-done.12
  4.6 0.7 copy-done.13
  5.3 0.2 pack.1
  5.5 3.0 %collective-permute-start = (f32[3,112,128]{2,1,0:T(8,128)S(1)}, f32[3,112,128]{2,1,0:T(8,128)S(1)}, u32[]{:S(2)}, u32[]{:S(2)}) collective-permute-start(f32[3,112,128]{2,1,0:T(8,128)S(1)} %get-tuple-element.15), channel_id=1, source_target_pairs={{0,2},{2,4},{4,6},{6,8},{8,10},{10,12},{12,14},{14,0},{1,3},{3,5},... | collective-permute-start | bytes 516104 | tf_op jit(solution)/shard_map/ppermute | solution.py:369
  8.5 3.1 %collective-permute-start.1 = (f32[3,112,128]{2,1,0:T(8,128)S(1)}, f32[3,112,128]{2,1,0:T(8,128)S(1)}, u32[]{:S(2)}, u32[]{:S(2)}) collective-permute-start(f32[3,112,128]{2,1,0:T(8,128)S(1)} %get-tuple-element.16), channel_id=1, source_target_pairs={{2,0},{4,2},{6,4},{8,6},{10,8},{12,10},{14,12},{0,14},{3,1},{5,3},... | collective-permute-start | bytes 516104 | tf_op jit(solution)/shard_map/ppermute | solution.py:370
  11.6 0.3 pairs.1
  11.9 0.5 copy-done.14
  12.4 3.6 %collective-permute-done.low_ref = f32[3,112,128]{2,1,0:T(8,128)S(1)} collective-permute-done((f32[3,112,128]{2,1,0:T(8,128)S(1)}, f32[3,112,128]{2,1,0:T(8,128)S(1)}, u32[]{:S(2)}, u32[]{:S(2)}) %collective-permute-start) | collective-permute-done | bytes 172064 | tf_op jit(solution)/shard_map/ppermute | solution.py:369
  16.0 2.0 %collective-permute-done.1.high_ref = f32[3,112,128]{2,1,0:T(8,128)S(1)} collective-permute-done((f32[3,112,128]{2,1,0:T(8,128)S(1)}, f32[3,112,128]{2,1,0:T(8,128)S(1)}, u32[]{:S(2)}, u32[]{:S(2)}) %collective-permute-start.1) | collective-permute-done | bytes 172064 | tf_op jit(solution)/shard_map/ppermute | solution.py:370
  18.0 0.2 border.1.edge_ref
  18.2 0.1 collective-permute-start.2
  18.2 1.2 %collective-permute-done.2.other_ref = f32[112,128]{1,0:T(8,128)S(1)} collective-permute-done((f32[112,128]{1,0:T(8,128)S(1)}, f32[112,128]{1,0:T(8,128)S(1)}, u32[]{:S(2)}, u32[]{:S(2)}) %collective-permute-start.2) | collective-permute-done | bytes 57376 | tf_op jit(solution)/shard_map/ppermute | solution.py:374
  19.5 6.2 %mix.1 = (f32[2,400,128]{2,1,0:T(8,128)S(1)}, f32[16,4,8,128]{3,2,1,0:T(8,128)}) custom-call(f32[8,112,128]{2,1,0:T(8,128)S(1)} %get-tuple-element.14.rows_ref, f32[3,112,128]{2,1,0:T(8,128)S(1)} %collective-permute-done.low_ref, f32[3,112,128]{2,1,0:T(8,128)S(1)} %collective-permute-done.1.high_ref, f32[112,128]{1,0:T(8,128)S(1)} %border.1.edge_ref, ...), custom_call_target="tpu_custom_call" | custom-call | tf_op jit(solution)/shard_map/mix/pallas_call | solution.py:375
  25.7 0.7 %copy-done.8 = f32[2,400,128]{2,1,0:T(8,128)} copy-done((f32[2,400,128]{2,1,0:T(8,128)}, f32[2,400,128]{2,1,0:T(8,128)S(1)}, u32[]{:S(2)}) %copy-start.8) | copy-done | bytes 409624
  26.4 4.7 %all-to-all-start = ((f32[16,4,8,128]{3,2,1,0:T(8,128)}), f32[16,4,8,128]{3,2,1,0:T(8,128)S(1)}, u32[]{:S(2)}, u32[]{:S(2)}) async-start(f32[16,4,8,128]{3,2,1,0:T(8,128)} %get-tuple-element.18), calls=%async_computation | async-start | bytes 524288 | tf_op jit(solution)/shard_map/all_to_all | solution.py:386
  31.1 24.1 %all-gather = f32[80,8,128]{2,1,0:T(8,128)} all-gather(f32[5,8,128]{2,1,0:T(8,128)S(1)} %get-tuple-element.19), channel_id=2, replica_groups=mesh['members'=2,'loop'=8,'lat'=2] {'loop','lat'}, dimensions={0}, use_global_device_ids=true | all-gather | bytes 348160 | tf_op jit(solution)/shard_map/all_gather | solution.py:371
  55.2 0.7 copy-done.15
  55.9 4.8 %solve.1 = (f32[2,400,128]{2,1,0:T(8,128)}, f32[2,8,128]{2,1,0:T(8,128)}, f32[16,1,128]{2,1,0:T(1,128)}) custom-call(f32[16,4,8,128]{3,2,1,0:T(8,128)} %copy-done.15, f32[16,5,8,128]{3,2,1,0:T(8,128)} %bitcast.17, f32[2,400,128]{2,1,0:T(8,128)} %copy-done.8, f32[8,16,128]{2,1,0:T(8,128)} %bitcast.9, f32[8,16,128]{2,1,0:T(8,128)} %bitcast.12, f32[1,128]{1,0:T(1,128)} %copy-done.14), custom_call_target="tpu_custom_call" | custom-call | tf_op jit(solution)/shard_map/solve/pallas_call | solution.py:387
  60.7 9.9 %all_to_all.10.inner_ref = f32[16,1,128]{2,1,0:T(1,128)S(1)} all-to-all(f32[16,1,128]{2,1,0:T(1,128)} %get-tuple-element.24), channel_id=1, replica_groups=mesh['members'=2,'loop'=8,'lat'=2] {'loop','lat'}, dimensions={0} | all-to-all | bytes 16384 | tf_op jit(solution)/shard_map/all_to_all | solution.py:394
  70.6 2.5 %direction.1 = f32[2,8,128]{2,1,0:T(8,128)} custom-call(f32[16,1,128]{2,1,0:T(1,128)S(1)} %all_to_all.10.inner_ref, f32[2,8,128]{2,1,0:T(8,128)S(1)} %copy-done.10, f32[8,16,128]{2,1,0:T(8,128)S(1)} %bitcast.11, f32[8,16,128]{2,1,0:T(8,128)S(1)} %bitcast.14), custom_call_target="tpu_custom_call" | custom-call | tf_op jit(solution)/shard_map/direction/pallas_call | solution.py:395
  (24 shorter events, 0.0 us)
Async XLA Ops:
  0.6 0.9 %copy-start = (f32[50,8,128]{2,1,0:T(8,128)S(1)}, f32[50,8,128]{2,1,0:T(8,128)}, u32[]{:S(2)}) copy-start(f32[50,8,128]{2,1,0:T(8,128)} %param.11) | copy-start | bytes 614404
  1.6 1.0 %copy-start.6 = (f32[2,50,8,128]{3,2,1,0:T(8,128)S(1)}, f32[2,50,8,128]{3,2,1,0:T(8,128)}, u32[]{:S(2)}) copy-start(f32[2,50,8,128]{3,2,1,0:T(8,128)} %param.9) | copy-start | bytes 1228804
  2.6 0.7 copy-start.9
  3.3 0.7 copy-start.11
  4.0 0.7 copy-start.12
  4.6 0.7 copy-start.13
  5.3 6.3 %copy-start.2 = (f32[8,2,8,128]{3,2,1,0:T(8,128)S(1)}, f32[8,2,8,128]{3,2,1,0:T(8,128)}, u32[]{:S(2)}) copy-start(f32[8,2,8,128]{3,2,1,0:T(8,128)} %param.16) | copy-start | bytes 196612
  5.3 6.3 %copy-start.4 = (f32[8,2,8,128]{3,2,1,0:T(8,128)S(1)}, f32[8,2,8,128]{3,2,1,0:T(8,128)}, u32[]{:S(2)}) copy-start(f32[8,2,8,128]{3,2,1,0:T(8,128)} %param.17) | copy-start | bytes 196612
  5.5 10.5 %collective-permute-start = (f32[3,112,128]{2,1,0:T(8,128)S(1)}, f32[3,112,128]{2,1,0:T(8,128)S(1)}, u32[]{:S(2)}, u32[]{:S(2)}) collective-permute-start(f32[3,112,128]{2,1,0:T(8,128)S(1)} %get-tuple-element.15), channel_id=1, source_target_pairs={{0,2},{2,4},{4,6},{6,8},{8,10},{10,12},{12,14},{14,0},{1,3},{3,5},... | collective-permute-start | bytes 516104 | tf_op jit(solution)/shard_map/ppermute | solution.py:369
  8.5 9.5 %collective-permute-start.1 = (f32[3,112,128]{2,1,0:T(8,128)S(1)}, f32[3,112,128]{2,1,0:T(8,128)S(1)}, u32[]{:S(2)}, u32[]{:S(2)}) collective-permute-start(f32[3,112,128]{2,1,0:T(8,128)S(1)} %get-tuple-element.16), channel_id=1, source_target_pairs={{2,0},{4,2},{6,4},{8,6},{10,8},{12,10},{14,12},{0,14},{3,1},{5,3},... | collective-permute-start | bytes 516104 | tf_op jit(solution)/shard_map/ppermute | solution.py:370
  11.9 0.5 copy-start.14
  18.0 1.5 %copy-start.1 = (f32[50,8,128]{2,1,0:T(8,128)S(1)}, f32[50,8,128]{2,1,0:T(8,128)}, u32[]{:S(2)}) copy-start(f32[50,8,128]{2,1,0:T(8,128)} %param.11) | copy-start | bytes 614404
  18.0 1.5 %copy-start.7 = (f32[2,50,8,128]{3,2,1,0:T(8,128)S(1)}, f32[2,50,8,128]{3,2,1,0:T(8,128)}, u32[]{:S(2)}) copy-start(f32[2,50,8,128]{3,2,1,0:T(8,128)} %param.10) | copy-start | bytes 1228804
  18.2 1.3 %collective-permute-start.2 = (f32[112,128]{1,0:T(8,128)S(1)}, f32[112,128]{1,0:T(8,128)S(1)}, u32[]{:S(2)}, u32[]{:S(2)}) collective-permute-start(f32[112,128]{1,0:T(8,128)S(1)} %border.1.edge_ref), channel_id=1, source_target_pairs={{0,1},{1,0},{2,3},{3,2},{4,5},{5,4},{6,7},{7,6},{8,9},{9,8},{10,11... | collective-permute-start | bytes 172040 | tf_op jit(solution)/shard_map/ppermute | solution.py:374
  25.7 0.7 %copy-start.8 = (f32[2,400,128]{2,1,0:T(8,128)}, f32[2,400,128]{2,1,0:T(8,128)S(1)}, u32[]{:S(2)}) copy-start(f32[2,400,128]{2,1,0:T(8,128)S(1)} %get-tuple-element.20.mixed_ref) | copy-start | bytes 1228804
  26.4 28.8 %all-to-all-start = ((f32[16,4,8,128]{3,2,1,0:T(8,128)}), f32[16,4,8,128]{3,2,1,0:T(8,128)S(1)}, u32[]{:S(2)}, u32[]{:S(2)}) async-start(f32[16,4,8,128]{3,2,1,0:T(8,128)} %get-tuple-element.18), calls=%async_computation | async-start | bytes 524288 | tf_op jit(solution)/shard_map/all_to_all | solution.py:386
  55.2 0.7 copy-start.15
  55.9 14.7 %copy-start.3 = (f32[8,2,8,128]{3,2,1,0:T(8,128)S(1)}, f32[8,2,8,128]{3,2,1,0:T(8,128)}, u32[]{:S(2)}) copy-start(f32[8,2,8,128]{3,2,1,0:T(8,128)} %param.16) | copy-start | bytes 196612
  55.9 14.7 %copy-start.5 = (f32[8,2,8,128]{3,2,1,0:T(8,128)S(1)}, f32[8,2,8,128]{3,2,1,0:T(8,128)}, u32[]{:S(2)}) copy-start(f32[8,2,8,128]{3,2,1,0:T(8,128)} %param.17) | copy-start | bytes 196612
  60.7 9.9 %copy-start.10 = (f32[2,8,128]{2,1,0:T(8,128)S(1)}, f32[2,8,128]{2,1,0:T(8,128)}, u32[]{:S(2)}) copy-start(f32[2,8,128]{2,1,0:T(8,128)} %get-tuple-element.12.gradient_ref) | copy-start | bytes 24580

commit v2 on v1

v2 whole, which is shorter than its diff:
```python
import functools

import jax
import jax.numpy as jnp
from jax import lax
from jax.experimental import pallas as pl
from jax.experimental.pallas import tpu as pltpu
from jax.sharding import PartitionSpec as P

ITERS = 3
SUB = 3
SURFACE_GAIN = 5.0
SLOT = 8
GRID = ("loop", "lat")
VMEM = pl.BlockSpec(memory_space=pltpu.VMEM)
F32 = jnp.float32
VMEM_BYTES = 16 * 1024 * 1024


def round_up(value, to):
    return (value + to - 1) // to * to


def call(kernel, out_shapes, scratch=(), vmem=VMEM_BYTES, name=None):
    return pl.pallas_call(
        kernel,
        out_shape=[jax.ShapeDtypeStruct(shape, F32) for shape in out_shapes],
        out_specs=[VMEM] * len(out_shapes),
        scratch_shapes=list(scratch),
        compiler_params=pltpu.CompilerParams(vmem_limit_bytes=vmem),
        name=name,
    )


def iota(shape, dim):
    return lax.broadcasted_iota(jnp.int32, shape, dim)


def pack_kernel(
    levels, padded, state_hbm, control_hbm, depth_hbm, spread_hbm,
    rows_ref, up_ref, down_ref, state_ref, control_ref, depth_ref, spread_ref, sems,
):
    copies = [
        pltpu.make_async_copy(source, target, sems.at[at])
        for at, (source, target) in enumerate(
            (
                (state_hbm, state_ref),
                (control_hbm, control_ref),
                (depth_hbm, depth_ref),
                (spread_hbm, spread_ref),
            )
        )
    ]
    for copy in copies:
        copy.start()
    for copy in copies:
        copy.wait()
    rows, cols = depth_ref.shape
    depth = depth_ref[...].astype(F32)
    spread = spread_ref[...]
    first = iota((levels, cols), 0) == 0
    rest = jnp.zeros((padded - levels, cols), F32)
    for row in range(rows):
        targets = [rows_ref.at[row]]
        if row < SUB:
            targets.append(down_ref.at[row])
        if row >= rows - SUB:
            targets.append(up_ref.at[row - rows + SUB])
        for tracer in range(2):
            lift = jnp.where(depth[row : row + 1] > 0.5, control_ref[tracer, row : row + 1, :], 0.0)
            value = state_ref[tracer, pl.ds(row, levels, stride=rows), :]
            value = value + jnp.where(first, lift, 0.0)
            for target in targets:
                target[pl.ds(tracer * padded, levels), :] = value
                target[pl.ds(tracer * padded + levels, padded - levels), :] = rest
        for target in targets:
            target[pl.ds(levels, 1), :] = spread[row : row + 1]
            target[pl.ds(levels + 1, 1), :] = depth[row : row + 1]


def edge_of(rows_of, indices, cols, lat):
    lane = iota((1, cols), 1)
    slot = lane // SLOT
    place = lane % SLOT - SUB * lat
    mine = (place >= 0) & (place < SUB)
    total = None
    for index in indices:
        moved = pltpu.roll(rows_of(index), SLOT * index + SUB, 1)
        piece = jnp.where(mine & (slot == index), moved, 0.0)
        total = piece if total is None else total + piece
    return total


def pairs_kernel(
    rows_ref, step_ref, change_ref, depth_ref, spread_ref, damping_ref, weight_ref,
    edge_ref, gram_ref, still_ref,
):
    rows, _, cols = rows_ref.shape
    lat = lax.axis_index("lat")
    edge_ref[...] = edge_of(lambda i: rows_ref[i - SUB], range(SUB, rows + SUB), cols, lat)
    count = step_ref.shape[0]
    lane = iota((1, cols), 1)
    total = jnp.zeros((1, cols), F32)
    at = 2 * count
    for left_ref in (step_ref, change_ref):
        for i in range(count):
            for j in range(i, count):
                value = jnp.sum(left_ref[i] * change_ref[j], axis=(0, 1), keepdims=True)
                total = total + jnp.where(lane == at, value, 0.0)
                at += 1
    gram_ref[...] = total
    depth = depth_ref[...]
    total = jnp.zeros((rows, cols), F32)
    for level in range(weight_ref.shape[0] // rows):
        total = total + jnp.where(level < depth, weight_ref[pl.ds(level * rows, rows), :], 0.0)
    still_ref[0] = 2.0 * total
    still_ref[1] = weight_ref[pl.ds(0, rows), :]
    still_ref[2] = jnp.where(depth > 0, spread_ref[...], 0.0)
    still_ref[3] = damping_ref[...]


def border_kernel(edge_ref, low_ref, high_ref, rows_ref, out_ref):
    cols = edge_ref.shape[-1]
    rows = rows_ref.shape[0]
    lat = lax.axis_index("lat")
    total = edge_ref[...] + edge_of(lambda i: low_ref[i], range(SUB), cols, lat)
    out_ref[...] = total + edge_of(
        lambda i: high_ref[i - rows - SUB], range(rows + SUB, rows + 2 * SUB), cols, lat
    )


def mix_kernel(
    levels, padded, scale, copies,
    rows_ref, low_ref, high_ref, edge_ref, other_ref, weight_ref, observed_ref, still_ref,
    mixed_ref, fields_ref, face_ref, part_ref,
):
    rows, _, cols = rows_ref.shape
    lat = lax.axis_index("lat")
    lane = iota((1, cols), 1)
    place = lane % SLOT
    tall = 8
    count = rows + 2 * SUB

    def left(value, by=1):
        return pltpu.roll(value, cols - by, 1)

    def right(value, by=1):
        return pltpu.roll(value, by, 1)

    def source(i):
        if i < SUB:
            return low_ref, i
        if i < SUB + rows:
            return rows_ref, i - SUB
        return high_ref, i - SUB - rows

    def load(i, start, size):
        ref, at = source(i)
        return ref[at, pl.ds(start, size), :]

    spreads = [load(i, levels, 1) for i in range(count)]
    depths = [load(i, levels + 1, 1) for i in range(count)]
    wide = (tall, cols)
    row_at = lambda i: i
    col_at = lambda i: count + i
    for i in range(count - 1):
        face_ref[0, row_at(i)] = jnp.broadcast_to(jnp.minimum(depths[i], depths[i + 1]), wide)
        face_ref[1, row_at(i)] = jnp.broadcast_to(0.5 * (spreads[i] + spreads[i + 1]), wide)
    for i in range(1, count - 1):
        there = jnp.where(lane < cols - 1, left(depths[i]), 0.0)
        face_ref[0, col_at(i)] = jnp.broadcast_to(jnp.minimum(depths[i], there), wide)
        face_ref[1, col_at(i)] = jnp.broadcast_to(0.5 * (spreads[i] + left(spreads[i])), wide)

    spread = edge_ref[pl.ds(levels, 1), :] + other_ref[pl.ds(levels, 1), :]
    depth = edge_ref[pl.ds(levels + 1, 1), :] + other_ref[pl.ds(levels + 1, 1), :]
    within = place < 2 * SUB - 1
    strip_col_depth = jnp.minimum(depth, jnp.where(within, left(depth), 0.0))
    strip_col_spread = 0.5 * (spread + left(spread))
    strip_row_depth = jnp.minimum(depth, left(depth, SLOT))
    strip_row_spread = 0.5 * (spread + left(spread, SLOT))
    out_of_low = place == jnp.where(lat == 0, SUB - 1, SLOT)
    out_of_high = place == jnp.where(lat == 0, SLOT, SUB)
    start = jnp.where(lat == 0, cols - SUB, 0)
    at_border = (lane >= start) & (lane < start + SUB)

    buoyancy = [None] * rows
    pressure = [None] * rows
    for start in range(0, levels, tall):
        size = min(tall, levels - start)
        level = iota(wide, 0).astype(F32) + float(start)

        def face(at):
            return jnp.where(level < face_ref[0, at], face_ref[1, at], 0.0)

        row_face = [face(row_at(i)) for i in range(count - 1)]
        col_face = [None] + [face(col_at(i)) for i in range(1, count - 1)]
        strip_col = jnp.where(level < strip_col_depth, strip_col_spread, 0.0)
        strip_row = jnp.where(level < strip_row_depth, strip_row_spread, 0.0)
        strip_own = jnp.where(place == SUB - 1, 0.0, strip_col)

        def stripped(value, over_col):
            over_row = strip_row * (left(value, SLOT) - value)
            return value + (over_col - right(over_col)) + (over_row - right(over_row, SLOT))

        mixed = []
        for tracer in range(2):
            here = tracer * padded + start
            value = [load(i, here, tall) for i in range(count)]
            part = edge_ref[pl.ds(here, tall), :] + other_ref[pl.ds(here, tall), :]
            extra = None
            for sweep in range(1, SUB + 1):
                over_col = strip_col * (left(part) - part)
                across = jnp.where(out_of_low, over_col, 0.0) - jnp.where(
                    out_of_high, right(over_col), 0.0
                )
                if extra is None:
                    extra = across
                else:
                    extra = stripped(extra, strip_own * (left(extra) - extra)) + across
                if sweep < SUB:
                    part = stripped(part, over_col)
                after = list(value)
                over_row = [None] * count
                for i in range(sweep - 1, count - sweep):
                    over_row[i] = row_face[i] * (value[i + 1] - value[i])
                for i in range(sweep, count - sweep):
                    flux = col_face[i] * (left(value[i]) - value[i])
                    after[i] = value[i] + (over_row[i] - over_row[i - 1]) + (flux - right(flux))
                value = after
            mixed.append(
                [
                    value[i] + jnp.where(at_border, left(extra, SLOT * i + SUB), 0.0)
                    for i in range(SUB, SUB + rows)
                ]
            )
        for row in range(rows):
            at = pl.ds(start * rows + row, size, stride=rows)
            wet = level[:size] < depths[row + SUB]
            weight = weight_ref[at, :]
            misfit = []
            ends = []
            for tracer in range(2):
                end = mixed[tracer][row][:size]
                ends.append(end)
                mixed_ref[tracer, at, :] = end
                misfit.append(weight * (end - observed_ref[tracer, at, :]))
            up = jnp.where(wet, ends[0] - ends[1], 0.0)
            down = jnp.where(wet, misfit[1] - misfit[0], 0.0)
            if size < tall:
                up = jnp.sum(up, axis=0, keepdims=True)
                down = jnp.sum(down, axis=0, keepdims=True)
                up = jnp.sum(buoyancy[row], axis=0, keepdims=True) + up
                down = jnp.sum(pressure[row], axis=0, keepdims=True) + down
                buoyancy[row], pressure[row] = up, down
            else:
                buoyancy[row] = up if start == 0 else buoyancy[row] + up
                pressure[row] = down if start == 0 else pressure[row] + down
            if start == 0:
                part_ref[2, pl.ds(row, 1), :] = misfit[0][0:1]
                part_ref[3, pl.ds(row, 1), :] = misfit[1][0:1]
    for row in range(rows):
        part_ref[0, pl.ds(row, 1), :] = scale * jnp.sum(buoyancy[row], axis=0, keepdims=True)
        part_ref[1, pl.ds(row, 1), :] = jnp.sum(pressure[row], axis=0, keepdims=True)
    for copy in range(copies):
        for field in range(4):
            fields_ref[copy, field] = part_ref[field]
            fields_ref[copy, 4 + field] = still_ref[field]


def solve_kernel(
    levels, scale, copies,
    mine_ref, other_ref, mixed_ref, depth_ref, step_ref, change_ref, gram_ref,
    state_ref, gradient_ref, inner_ref, kept_ref,
):
    loops, _, rows, cols = mine_ref.shape
    height = loops * rows
    width = 2 * cols
    loop = lax.axis_index("loop")
    closed = jnp.where(lax.axis_index("lat") == 0, width - 1, cols - 1)

    def whole(field):
        return jnp.concatenate(
            [
                jnp.concatenate([mine_ref[i, field], other_ref[i, field]], axis=1)
                for i in range(loops)
            ],
            axis=0,
        )

    def around(field):
        parts = []
        for shift in (loops - 1, 0, 1):
            at = lax.rem(loop + shift, loops)
            parts.append(jnp.concatenate([mine_ref[at, field], other_ref[at, field]], axis=1))
        return jnp.concatenate(parts, axis=0)

    def below(value):
        return pltpu.roll(value, value.shape[0] - 1, 0)

    def above(value):
        return pltpu.roll(value, 1, 0)

    def left(value):
        return pltpu.roll(value, width - 1, 1)

    def right(value):
        return pltpu.roll(value, 1, 1)

    def total(value):
        return jnp.sum(value, axis=(0, 1), keepdims=True)

    def faces(spread):
        wet = spread > 0.0
        inside = iota(spread.shape, 1) != closed
        row_face = jnp.where(wet & (below(spread) > 0.0), 0.5 * (spread + below(spread)), 0.0)
        col_face = jnp.where(
            inside & wet & (left(spread) > 0.0), 0.5 * (spread + left(spread)), 0.0
        )
        return row_face, col_face

    def outflow(value, row_face, col_face):
        over_row = row_face * (value - below(value))
        over_col = col_face * (value - left(value))
        return (over_row - above(over_row)) + (over_col - right(over_col))

    row_face, col_face = (SURFACE_GAIN * face for face in faces(whole(6)))
    damping = whole(7)

    def conjugate(rhs):
        residual = rhs
        search = rhs
        solution = None
        norm_now = total(rhs * rhs)
        for sweep in range(ITERS):
            image = damping * search + outflow(search, row_face, col_face)
            alpha = norm_now / total(search * image)
            solution = alpha * search if solution is None else solution + alpha * search
            if sweep < ITERS - 1:
                residual = residual - alpha * image
                norm_next = total(residual * residual)
                search = residual + (norm_next / norm_now) * search
                norm_now = norm_next
        return solution

    def keep(slot, value):
        for i in range(loops):
            kept_ref[slot, i] = value[i * rows : (i + 1) * rows]

    def kept_around(slot):
        return jnp.concatenate(
            [kept_ref[slot, lax.rem(loop + shift, loops)] for shift in (loops - 1, 0, 1)], axis=0
        )

    elevation = conjugate(whole(0))
    keep(0, elevation)
    response = conjugate(whole(1) + whole(4) * elevation)
    keep(1, response)

    elevation = kept_around(0)
    spread = around(6)
    sea = spread > 0.0
    lowered = jnp.where(sea, around(5) * elevation, 0.0)
    raised = jnp.where(sea, scale * kept_around(1), 0.0)
    near_row, near_col = faces(spread)
    gradient = []
    for tracer in range(2):
        carried = around(2 + tracer)
        carried = carried - lowered + raised if tracer == 0 else carried + lowered - raised
        for sweep in range(SUB):
            carried = carried - outflow(carried, near_row, near_col)
        value = jnp.where(sea, carried, 0.0)[rows : 2 * rows, :cols]
        gradient_ref[tracer] = value
        gradient.append(value)

    lane = iota((1, cols), 1)
    inner = gram_ref[...]
    count = step_ref.shape[0]
    for index, ref in enumerate((step_ref, change_ref)):
        for i in range(count):
            value = ref[i, pl.ds(0, rows), :] * gradient[0] + ref[i, pl.ds(rows, rows), :] * gradient[1]
            inner = inner + jnp.where(lane == index * count + i, total(value), 0.0)
    inner_ref[...] = jnp.broadcast_to(inner[None], inner_ref.shape)

    depth = depth_ref[...]
    here = elevation[rows : 2 * rows, :cols]
    for level in range(levels):
        at = pl.ds(level * rows, rows)
        change = jnp.where(level < depth, here, 0.0)
        state_ref[0, at, :] = mixed_ref[0, at, :] - change
        state_ref[1, at, :] = mixed_ref[1, at, :] + change


def direction_kernel(inner_ref, gradient_ref, step_ref, change_ref, out_ref):
    count = step_ref.shape[0]
    rows = gradient_ref.shape[1]
    inner = jnp.sum(inner_ref[...], axis=0)

    def scalar(at):
        return inner[:, at : at + 1]

    step_grad = [scalar(i) for i in range(count)]
    change_grad = [scalar(count + i) for i in range(count)]
    at = 2 * count
    step_change = {}
    change_change = {}
    for table in (step_change, change_change):
        for i in range(count):
            for j in range(i, count):
                table[i, j] = table[j, i] = scalar(at)
                at += 1
    gamma = step_change[count - 1, count - 1] / change_change[count - 1, count - 1]
    factors = [None] * count
    for i in range(count - 1, -1, -1):
        factors[i] = step_grad[i] / step_change[i, i]
        for j in range(count):
            if j < i:
                step_grad[j] = step_grad[j] - factors[i] * step_change[j, i]
            change_grad[j] = change_grad[j] - factors[i] * change_change[j, i]
    change_grad = [gamma * value for value in change_grad]
    weights = []
    for i in range(count):
        weights.append(factors[i] - change_grad[i] / step_change[i, i])
        for j in range(i + 1, count):
            change_grad[j] = change_grad[j] + weights[i] * step_change[i, j]
    for tracer in range(2):
        at = pl.ds(tracer * rows, rows)
        value = gradient_ref[tracer]
        for i in range(count - 1, -1, -1):
            value = value - factors[i] * change_ref[i, at, :]
        value = gamma * value
        for i in range(count):
            value = value + weights[i] * step_ref[i, at, :]
        out_ref[tracer] = -value


def on_device(
    state, observed, weight, control, depth_index, diffusivity, damping, history_step, history_change
):
    _, levels, rows, cols = state.shape
    count = history_step.shape[0]
    padded = round_up(levels + 2, 8)
    planes = 2 * padded
    loops = lax.axis_size("loop")
    lats = lax.axis_size("lat")
    blocks = loops * lats
    scale = levels ** (-0.5)
    flat = (2, levels * rows, cols)
    state = state.reshape(flat)
    observed = observed.reshape(flat)
    weight = weight.reshape(flat[1:])
    step = history_step.reshape(count, 2 * rows, cols)
    change = history_change.reshape(count, 2 * rows, cols)

    packed, up, down = pl.pallas_call(
        functools.partial(pack_kernel, levels, padded),
        out_shape=[
            jax.ShapeDtypeStruct(shape, F32)
            for shape in ((rows, planes, cols), (SUB, planes, cols), (SUB, planes, cols))
        ],
        in_specs=[pl.BlockSpec(memory_space=pltpu.HBM)] * 4,
        out_specs=[VMEM] * 3,
        scratch_shapes=[
            pltpu.VMEM(flat, F32),
            pltpu.VMEM((2, rows, cols), F32),
            pltpu.VMEM((rows, cols), jnp.int32),
            pltpu.VMEM((rows, cols), F32),
            pltpu.SemaphoreType.DMA((4,)),
        ],
        compiler_params=pltpu.CompilerParams(vmem_limit_bytes=VMEM_BYTES),
        name="pack",
    )(state, control, depth_index, diffusivity)
    forward = [(i, (i + 1) % loops) for i in range(loops)]
    backward = [(target, source) for source, target in forward]
    swap = [(0, 1), (1, 0)]
    low = lax.ppermute(up, "loop", forward)
    high = lax.ppermute(down, "loop", backward)
    edge, gram, still = call(
        pairs_kernel, [(planes, cols), (1, cols), (4, rows, cols)], name="pairs"
    )(packed, step, change, depth_index, diffusivity, damping, weight)
    (edge,) = call(border_kernel, [(planes, cols)], name="border")(edge, low, high, packed)
    other = lax.ppermute(edge, "lat", swap)
    mixed, fields = call(
        functools.partial(mix_kernel, levels, padded, scale, loops),
        [flat, (loops, 8, rows, cols)],
        scratch=[
            pltpu.VMEM((2, 2 * (rows + 2 * SUB), 8, cols), F32),
            pltpu.VMEM((4, rows, cols), F32),
        ],
        name="mix",
    )(packed, low, high, edge, other, weight, observed, still)
    mine = lax.all_to_all(fields, "loop", 0, 0)
    theirs = lax.ppermute(mine, "lat", swap)
    state_next, gradient, inner = call(
        functools.partial(solve_kernel, levels, scale, blocks),
        [flat, (2, rows, cols), (blocks, 1, cols)],
        scratch=[pltpu.VMEM((2, loops, rows, 2 * cols), F32)],
        vmem=VMEM_BYTES if loops <= 16 else 2 * VMEM_BYTES,
        name="solve",
    )(mine, theirs, mixed, depth_index, step, change, gram)
    inner_all = lax.all_to_all(inner, GRID, 0, 0)
    (direction,) = call(direction_kernel, [(2, rows, cols)], name="direction")(
        inner_all, gradient, step, change
    )
    return (state_next.reshape(2, levels, rows, cols), gradient, direction)


def solution(mesh):
    return jax.shard_map(
        on_device,
        mesh=mesh,
        in_specs=(
            P("members", None, "loop", "lat"),
            P("members", None, "loop", "lat"),
            P(None, "loop", "lat"),
            P("members", "loop", "lat"),
            P("loop", "lat"),
            P("loop", "lat"),
            P("loop", "lat"),
            P("members", None, "loop", "lat"),
            P("members", None, "loop", "lat"),
        ),
        out_specs=(
            P("members", None, "loop", "lat"),
            P("members", "loop", "lat"),
            P("members", "loop", "lat"),
        ),
        check_vma=False,
    )
```

time: 73.6 us -> 55.5 us (0.75)
  blocking collectives: 34 us -> 23.7 us
  starting transfers between devices: 10.9 us -> 6.18 us
  local copies, waits for them, and re-layouts: 6.62 us -> 3.09 us
  waiting for transfers between devices: 6.84 us -> 8.82 us
  Pallas kernels: 14.1 us -> 12.6 us
    all_gather x1 -> x0, blocking collectives: 24.1 us -> none  [on_device(): still_all = lax.all_gather(still, GRID)]
    all_to_all x0 -> x1, blocking collectives: none -> 13.6 us  [on_device(): mine = lax.all_to_all(fields, 'loop', 0, 0)]
    all_to_all x1 -> x0, starting transfers between devices: 4.7 us -> none  [on_device(): fields_all = lax.all_to_all(fields, GRID, 0, 0)]
    unnamed x32 -> x22, local copies, waits for them, and re-layouts: 6.62 us -> 3.09 us
    ppermute x1 -> x2, waiting for transfers between devices: 1.23 us -> 2.76 us  [the longest x1 1.53 us: on_device(): theirs = lax.ppermute(mine, 'lat', swap)]
    pallas_call x4, Pallas kernels: 11.5 us -> 10 us  [the longest x1 5.83 us: on_device(): call(functools.partial(mix_kernel, levels, padded, scale, loops), [flat,...]
  transfers between devices with their start and end apart: 4 -> 4, of which waited for: 3 -> 4; matrix products, arithmetic and copies ran while one was open for 0% -> 0% of each run, Pallas kernels for 0% -> 1%
where the time goes in v2:
time: 55.5 us; the launch traced here: 55.1 us
  blocking collectives  23.7 us (43%)
  Pallas kernels  12.6 us (23%)
  waiting for transfers between devices  8.82 us (16%)
  starting transfers between devices  6.18 us (11%)
  local copies, waits for them, and re-layouts  3.09 us (6%)
  between operations  0.69 us (1%)
    all_to_all x1, blocking collectives, on_device(): mine = lax.all_to_all(fields, 'loop', 0, 0)  13.6 us
    all_to_all x1, blocking collectives, on_device(): inner_all = lax.all_to_all(inner, GRID, 0, 0)  10 us
    pallas_call x1, Pallas kernels, on_device(): call(functools.partial(mix_kernel, levels, padded, scale, loops), [flat,...  5.83 us
    ppermute x1, waiting for transfers between devices, on_device(): low = lax.ppermute(up, 'loop', forward)  4.05 us
    pallas_call x1, Pallas kernels, on_device(): call(functools.partial(solve_kernel, levels, scale, blocks), [flat, (2, r...  3.48 us
    ppermute x1, starting transfers between devices, on_device(): high = lax.ppermute(down, 'loop', backward)  3.11 us
    unnamed x22, local copies, waits for them, and re-layouts  3.09 us
    ppermute x1, starting transfers between devices, on_device(): low = lax.ppermute(up, 'loop', forward)  2.99 us
  transfers between devices with their start and end apart: 4, of which 4 were waited for; matrix products, arithmetic and copies ran while one was open for 0% of the time, Pallas kernels for 1%

profile of v2, /device:TPU:0, one launch (start us, length us, event | category | flops | bytes accessed | tf_op | source)
XLA Modules:
  0.0 55.1 jit_solution(17463979974238714646)
XLA Ops:
  0.6 0.0 copy-start.4
  0.6 1.0 %copy-done.4 = f32[2,50,8,128]{3,2,1,0:T(8,128)S(1)} copy-done((f32[2,50,8,128]{3,2,1,0:T(8,128)S(1)}, f32[2,50,8,128]{3,2,1,0:T(8,128)}, u32[]{:S(2)}) %copy-start.4) | copy-done | bytes 409624
  1.6 0.7 %copy-done.5 = s32[8,128]{1,0:T(8,128)S(1)} copy-done((s32[8,128]{1,0:T(8,128)S(1)}, s32[8,128]{1,0:T(8,128)}, u32[]{:S(2)}) %copy-start.5) | copy-done | bytes 4120
  2.3 0.7 %copy-done.7 = f32[8,128]{1,0:T(8,128)S(1)} copy-done((f32[8,128]{1,0:T(8,128)S(1)}, f32[8,128]{1,0:T(8,128)}, u32[]{:S(2)}) %copy-start.7) | copy-done | bytes 4120
  3.0 0.7 %copy-done.9 = f32[2,8,128]{2,1,0:T(8,128)S(1)} copy-done((f32[2,8,128]{2,1,0:T(8,128)S(1)}, f32[2,8,128]{2,1,0:T(8,128)}, u32[]{:S(2)}) %copy-start.9) | copy-done | bytes 8216
  3.7 0.4 pack.1
  4.1 3.0 %collective-permute-start = (f32[3,112,128]{2,1,0:T(8,128)S(1)}, f32[3,112,128]{2,1,0:T(8,128)S(1)}, u32[]{:S(2)}, u32[]{:S(2)}) collective-permute-start(f32[3,112,128]{2,1,0:T(8,128)S(1)} %get-tuple-element.15), channel_id=1, source_target_pairs={{0,2},{2,4},{4,6},{6,8},{8,10},{10,12},{12,14},{14,0},{1,3},{3,5},... | collective-permute-start | bytes 516104 | tf_op jit(solution)/shard_map/ppermute | solution.py:475
  7.1 3.1 %collective-permute-start.1 = (f32[3,112,128]{2,1,0:T(8,128)S(1)}, f32[3,112,128]{2,1,0:T(8,128)S(1)}, u32[]{:S(2)}, u32[]{:S(2)}) collective-permute-start(f32[3,112,128]{2,1,0:T(8,128)S(1)} %get-tuple-element.16), channel_id=1, source_target_pairs={{2,0},{4,2},{6,4},{8,6},{10,8},{12,10},{14,12},{0,14},{3,1},{5,3},... | collective-permute-start | bytes 516104 | tf_op jit(solution)/shard_map/ppermute | solution.py:476
  10.2 0.0 copy-done
  10.2 0.3 pairs.1
  10.5 4.1 %collective-permute-done.low_ref = f32[3,112,128]{2,1,0:T(8,128)S(1)} collective-permute-done((f32[3,112,128]{2,1,0:T(8,128)S(1)}, f32[3,112,128]{2,1,0:T(8,128)S(1)}, u32[]{:S(2)}, u32[]{:S(2)}) %collective-permute-start) | collective-permute-done | bytes 172064 | tf_op jit(solution)/shard_map/ppermute | solution.py:475
  14.6 2.0 %collective-permute-done.1.high_ref = f32[3,112,128]{2,1,0:T(8,128)S(1)} collective-permute-done((f32[3,112,128]{2,1,0:T(8,128)S(1)}, f32[3,112,128]{2,1,0:T(8,128)S(1)}, u32[]{:S(2)}, u32[]{:S(2)}) %collective-permute-start.1) | collective-permute-done | bytes 172064 | tf_op jit(solution)/shard_map/ppermute | solution.py:476
  16.6 0.2 border.1.edge_ref
  16.8 0.1 collective-permute-start.2
  16.8 1.2 %collective-permute-done.2.other_ref = f32[112,128]{1,0:T(8,128)S(1)} collective-permute-done((f32[112,128]{1,0:T(8,128)S(1)}, f32[112,128]{1,0:T(8,128)S(1)}, u32[]{:S(2)}, u32[]{:S(2)}) %collective-permute-start.2) | collective-permute-done | bytes 57376 | tf_op jit(solution)/shard_map/ppermute | solution.py:481
  18.1 5.8 %mix.1 = (f32[2,400,128]{2,1,0:T(8,128)S(1)}, f32[8,8,8,128]{3,2,1,0:T(8,128)S(1)}) custom-call(f32[8,112,128]{2,1,0:T(8,128)S(1)} %get-tuple-element.14.rows_ref, f32[3,112,128]{2,1,0:T(8,128)S(1)} %collective-permute-done.low_ref, f32[3,112,128]{2,1,0:T(8,128)S(1)} %collective-permute-done.1.high_ref, f32[112,128]{1,0:T(8,128)S(1)} %border.1.edge_ref, ...), custom_call_target="tpu_custom_call" | custom-call | tf_op jit(solution)/shard_map/mix/pallas_call | solution.py:482
  23.9 0.0 copy-start.6
  23.9 13.6 %all_to_all.10.mine_ref = f32[8,8,8,128]{3,2,1,0:T(8,128)S(1)} all-to-all(f32[8,8,8,128]{3,2,1,0:T(8,128)S(1)} %get-tuple-element.19), channel_id=1, replica_groups=mesh['members'=2,'loop'=8,'lat'=2] {'loop'}, dimensions={0} | all-to-all | bytes 524288 | tf_op jit(solution)/shard_map/all_to_all | solution.py:491
  37.6 0.0 collective-permute-start.3
  37.6 1.5 %collective-permute-done.3.other_ref = f32[8,8,8,128]{3,2,1,0:T(8,128)S(1)} collective-permute-done((f32[8,8,8,128]{3,2,1,0:T(8,128)S(1)}, f32[8,8,8,128]{3,2,1,0:T(8,128)S(1)}, u32[]{:S(2)}, u32[]{:S(2)}) %collective-permute-start.3) | collective-permute-done | bytes 262176 | tf_op jit(solution)/shard_map/ppermute | solution.py:492
  39.1 3.5 %solve.1 = (f32[2,400,128]{2,1,0:T(8,128)}, f32[2,8,128]{2,1,0:T(8,128)}, f32[16,1,128]{2,1,0:T(1,128)S(1)}) custom-call(f32[8,8,8,128]{3,2,1,0:T(8,128)S(1)} %all_to_all.10.mine_ref, f32[8,8,8,128]{3,2,1,0:T(8,128)S(1)} %collective-permute-done.3.other_ref, f32[2,400,128]{2,1,0:T(8,128)S(1)} %get-tuple-element.20.mixed_ref, s32[8,128]{1,0:T(8,128)S(1)} %copy-done.6, ...), custom_call_target="tpu_custom_call" | custom-call | tf_op jit(solution)/shard_map/solve/pallas_call | solution.py:493
  42.6 10.0 %all_to_all.11.inner_ref = f32[16,1,128]{2,1,0:T(1,128)S(1)} all-to-all(f32[16,1,128]{2,1,0:T(1,128)S(1)} %get-tuple-element.24), channel_id=1, replica_groups=mesh['members'=2,'loop'=8,'lat'=2] {'loop','lat'}, dimensions={0} | all-to-all | bytes 16384 | tf_op jit(solution)/shard_map/all_to_all | solution.py:500
  52.6 0.0 copy-done.8
  52.6 2.5 %direction.1 = f32[2,8,128]{2,1,0:T(8,128)} custom-call(f32[16,1,128]{2,1,0:T(1,128)S(1)} %all_to_all.11.inner_ref, f32[2,8,128]{2,1,0:T(8,128)S(1)} %copy-done.8, f32[8,16,128]{2,1,0:T(8,128)S(1)} %bitcast.10, f32[8,16,128]{2,1,0:T(8,128)S(1)} %bitcast.13), custom_call_target="tpu_custom_call" | custom-call | tf_op jit(solution)/shard_map/direction/pallas_call | solution.py:501
  (14 shorter events, 0.0 us)
Async XLA Ops:
  0.6 1.0 %copy-start.4 = (f32[2,50,8,128]{3,2,1,0:T(8,128)S(1)}, f32[2,50,8,128]{3,2,1,0:T(8,128)}, u32[]{:S(2)}) copy-start(f32[2,50,8,128]{3,2,1,0:T(8,128)} %param.9) | copy-start | bytes 1228804
  1.6 0.7 %copy-start.5 = (s32[8,128]{1,0:T(8,128)S(1)}, s32[8,128]{1,0:T(8,128)}, u32[]{:S(2)}) copy-start(s32[8,128]{1,0:T(8,128)} %depth_ref.3) | copy-start | bytes 12292
  2.3 0.7 %copy-start.7 = (f32[8,128]{1,0:T(8,128)S(1)}, f32[8,128]{1,0:T(8,128)}, u32[]{:S(2)}) copy-start(f32[8,128]{1,0:T(8,128)} %spread_ref.1) | copy-start | bytes 12292
  3.0 0.7 %copy-start.9 = (f32[2,8,128]{2,1,0:T(8,128)S(1)}, f32[2,8,128]{2,1,0:T(8,128)}, u32[]{:S(2)}) copy-start(f32[2,8,128]{2,1,0:T(8,128)} %control_hbm.1) | copy-start | bytes 24580
  3.7 6.5 %copy-start = (f32[50,8,128]{2,1,0:T(8,128)S(1)}, f32[50,8,128]{2,1,0:T(8,128)}, u32[]{:S(2)}) copy-start(f32[50,8,128]{2,1,0:T(8,128)} %param.11) | copy-start | bytes 614404
  3.7 6.5 %copy-start.1 = (f32[8,2,8,128]{3,2,1,0:T(8,128)S(1)}, f32[8,2,8,128]{3,2,1,0:T(8,128)}, u32[]{:S(2)}) copy-start(f32[8,2,8,128]{3,2,1,0:T(8,128)} %param.16) | copy-start | bytes 196612
  3.7 6.5 %copy-start.2 = (f32[8,2,8,128]{3,2,1,0:T(8,128)S(1)}, f32[8,2,8,128]{3,2,1,0:T(8,128)}, u32[]{:S(2)}) copy-start(f32[8,2,8,128]{3,2,1,0:T(8,128)} %param.17) | copy-start | bytes 196612
  4.1 10.5 %collective-permute-start = (f32[3,112,128]{2,1,0:T(8,128)S(1)}, f32[3,112,128]{2,1,0:T(8,128)S(1)}, u32[]{:S(2)}, u32[]{:S(2)}) collective-permute-start(f32[3,112,128]{2,1,0:T(8,128)S(1)} %get-tuple-element.15), channel_id=1, source_target_pairs={{0,2},{2,4},{4,6},{6,8},{8,10},{10,12},{12,14},{14,0},{1,3},{3,5},... | collective-permute-start | bytes 516104 | tf_op jit(solution)/shard_map/ppermute | solution.py:475
  7.1 3.1 %copy-start.10 = (f32[8,128]{1,0:T(8,128)S(1)}, f32[8,128]{1,0:T(8,128)}, u32[]{:S(2)}) copy-start(f32[8,128]{1,0:T(8,128)} %damping_ref.1) | copy-start | bytes 12292
  7.1 9.5 %collective-permute-start.1 = (f32[3,112,128]{2,1,0:T(8,128)S(1)}, f32[3,112,128]{2,1,0:T(8,128)S(1)}, u32[]{:S(2)}, u32[]{:S(2)}) collective-permute-start(f32[3,112,128]{2,1,0:T(8,128)S(1)} %get-tuple-element.16), channel_id=1, source_target_pairs={{2,0},{4,2},{6,4},{8,6},{10,8},{12,10},{14,12},{0,14},{3,1},{5,3},... | collective-permute-start | bytes 516104 | tf_op jit(solution)/shard_map/ppermute | solution.py:476
  16.6 1.5 %copy-start.3 = (f32[2,50,8,128]{3,2,1,0:T(8,128)S(1)}, f32[2,50,8,128]{3,2,1,0:T(8,128)}, u32[]{:S(2)}) copy-start(f32[2,50,8,128]{3,2,1,0:T(8,128)} %param.10) | copy-start | bytes 1228804
  16.8 1.3 %collective-permute-start.2 = (f32[112,128]{1,0:T(8,128)S(1)}, f32[112,128]{1,0:T(8,128)S(1)}, u32[]{:S(2)}, u32[]{:S(2)}) collective-permute-start(f32[112,128]{1,0:T(8,128)S(1)} %border.1.edge_ref), channel_id=1, source_target_pairs={{0,1},{1,0},{2,3},{3,2},{4,5},{5,4},{6,7},{7,6},{8,9},{9,8},{10,11... | collective-permute-start | bytes 172040 | tf_op jit(solution)/shard_map/ppermute | solution.py:481
  23.9 15.2 %copy-start.6 = (s32[8,128]{1,0:T(8,128)S(1)}, s32[8,128]{1,0:T(8,128)}, u32[]{:S(2)}) copy-start(s32[8,128]{1,0:T(8,128)} %depth_ref.3) | copy-start | bytes 12292
  37.6 1.5 %collective-permute-start.3 = (f32[8,8,8,128]{3,2,1,0:T(8,128)S(1)}, f32[8,8,8,128]{3,2,1,0:T(8,128)S(1)}, u32[]{:S(2)}, u32[]{:S(2)}) collective-permute-start(f32[8,8,8,128]{3,2,1,0:T(8,128)S(1)} %all_to_all.10.mine_ref), channel_id=1, source_target_pairs={{0,1},{1,0},{2,3},{3,2},{4,5},{5,4},{6,7},{7,6},{8,9},{9,8},{10,11... | collective-permute-start | bytes 786440 | tf_op jit(solution)/shard_map/ppermute | solution.py:492
  42.6 10.0 %copy-start.8 = (f32[2,8,128]{2,1,0:T(8,128)S(1)}, f32[2,8,128]{2,1,0:T(8,128)}, u32[]{:S(2)}) copy-start(f32[2,8,128]{2,1,0:T(8,128)} %get-tuple-element.12.gradient_ref) | copy-start | bytes 24580

commit v3 on v2

--- a/solution.py
+++ b/solution.py
@@ -132,135 +132,127 @@
 def mix_kernel(
     levels, padded, scale, copies,
     rows_ref, low_ref, high_ref, edge_ref, other_ref, weight_ref, observed_ref, still_ref,
-    mixed_ref, fields_ref, face_ref, part_ref,
+    mixed_ref, fields_ref, face_ref, here_ref, there_ref, part_ref,
 ):
-    rows, _, cols = rows_ref.shape
+    rows, planes, cols = rows_ref.shape
     lat = lax.axis_index("lat")
     lane = iota((1, cols), 1)
     place = lane % SLOT
-    tall = 8
     count = rows + 2 * SUB
+    level = iota((padded, cols), 0).astype(F32)
 
     def left(value, by=1):
-        return pltpu.roll(value, cols - by, 1)
+        return pltpu.roll(value, (cols - by) % cols, 1)
 
     def right(value, by=1):
         return pltpu.roll(value, by, 1)
 
     def source(i):
         if i < SUB:
-            return low_ref, i
+            return low_ref.at[i]
         if i < SUB + rows:
-            return rows_ref, i - SUB
-        return high_ref, i - SUB - rows
-
-    def load(i, start, size):
-        ref, at = source(i)
-        return ref[at, pl.ds(start, size), :]
-
-    spreads = [load(i, levels, 1) for i in range(count)]
-    depths = [load(i, levels + 1, 1) for i in range(count)]
-    wide = (tall, cols)
-    row_at = lambda i: i
-    col_at = lambda i: count + i
-    for i in range(count - 1):
-        face_ref[0, row_at(i)] = jnp.broadcast_to(jnp.minimum(depths[i], depths[i + 1]), wide)
-        face_ref[1, row_at(i)] = jnp.broadcast_to(0.5 * (spreads[i] + spreads[i + 1]), wide)
-    for i in range(1, count - 1):
-        there = jnp.where(lane < cols - 1, left(depths[i]), 0.0)
-        face_ref[0, col_at(i)] = jnp.broadcast_to(jnp.minimum(depths[i], there), wide)
-        face_ref[1, col_at(i)] = jnp.broadcast_to(0.5 * (spreads[i] + left(spreads[i])), wide)
+            return rows_ref.at[i - SUB]
+        return high_ref.at[i - SUB - rows]
+
+    def face(depth_here, depth_there, spread_here, spread_there):
+        opened = level < jnp.minimum(depth_here, depth_there)
+        return jnp.where(opened, 0.5 * (spread_here + spread_there), 0.0)
 
     spread = edge_ref[pl.ds(levels, 1), :] + other_ref[pl.ds(levels, 1), :]
     depth = edge_ref[pl.ds(levels + 1, 1), :] + other_ref[pl.ds(levels + 1, 1), :]
     within = place < 2 * SUB - 1
-    strip_col_depth = jnp.minimum(depth, jnp.where(within, left(depth), 0.0))
-    strip_col_spread = 0.5 * (spread + left(spread))
-    strip_row_depth = jnp.minimum(depth, left(depth, SLOT))
-    strip_row_spread = 0.5 * (spread + left(spread, SLOT))
+    col_depth = jnp.minimum(depth, jnp.where(within, left(depth), 0.0))
+    col_spread = 0.5 * (spread + left(spread))
+    row_depth = jnp.minimum(depth, left(depth, SLOT))
+    row_spread = 0.5 * (spread + left(spread, SLOT))
+
+    def strip_face(limit, value):
+        return jnp.where(level < limit, value, 0.0)
+
+    to_left = strip_face(right(col_depth), right(col_spread))
+    to_right = strip_face(col_depth, col_spread)
+    to_above = strip_face(right(row_depth, SLOT), right(row_spread, SLOT))
+    to_below = strip_face(row_depth, row_spread)
     out_of_low = place == jnp.where(lat == 0, SUB - 1, SLOT)
     out_of_high = place == jnp.where(lat == 0, SLOT, SUB)
+    over_low = jnp.where(out_of_low, to_right, 0.0)
+    over_high = jnp.where(out_of_high, to_left, 0.0)
+    own_right = jnp.where(place == SUB - 1, 0.0, to_right)
+    own_left = jnp.where(place == SUB, 0.0, to_left)
     start = jnp.where(lat == 0, cols - SUB, 0)
     at_border = (lane >= start) & (lane < start + SUB)
 
-    buoyancy = [None] * rows
-    pressure = [None] * rows
-    for start in range(0, levels, tall):
-        size = min(tall, levels - start)
-        level = iota(wide, 0).astype(F32) + float(start)
-
-        def face(at):
-            return jnp.where(level < face_ref[0, at], face_ref[1, at], 0.0)
-
-        row_face = [face(row_at(i)) for i in range(count - 1)]
-        col_face = [None] + [face(col_at(i)) for i in range(1, count - 1)]
-        strip_col = jnp.where(level < strip_col_depth, strip_col_spread, 0.0)
-        strip_row = jnp.where(level < strip_row_depth, strip_row_spread, 0.0)
-        strip_own = jnp.where(place == SUB - 1, 0.0, strip_col)
-
-        def stripped(value, over_col):
-            over_row = strip_row * (left(value, SLOT) - value)
-            return value + (over_col - right(over_col)) + (over_row - right(over_row, SLOT))
-
+    def spread_out(value, east, west):
+        before, after = right(value), left(value)
+        above, below = right(value, SLOT), left(value, SLOT)
+        total = value + east * (after - value) + west * (before - value)
+        return total + to_below * (below - value) + to_above * (above - value)
+
+    parts = []
+    extras = [None, None]
+    for tracer in range(2):
+        at = pl.ds(tracer * padded, padded)
+        parts.append(edge_ref[at, :] + other_ref[at, :])
+
+    spreads = [source(i)[pl.ds(levels, 1), :] for i in range(count)]
+    depths = [source(i)[pl.ds(levels + 1, 1), :] for i in range(count)]
+    for i in range(count - 1):
+        face_ref[0, i] = face(depths[i], depths[i + 1], spreads[i], spreads[i + 1])
+    for i in range(1, count - 1):
+        there = jnp.where(lane < cols - 1, left(depths[i]), 0.0)
+        face_ref[1, i] = face(depths[i], there, spreads[i], left(spreads[i]))
+        there = jnp.where(lane > 0, right(depths[i]), 0.0)
+        face_ref[2, i] = face(depths[i], there, spreads[i], right(spreads[i]))
+
+    for sweep in range(1, SUB + 1):
+        for tracer in range(2):
+            part = parts[tracer]
+            across = over_low * (left(part) - part) + over_high * (right(part) - part)
+            extra = extras[tracer]
+            if extra is not None:
+                across = across + spread_out(extra, own_right, own_left)
+            extras[tracer] = across
+            if sweep < SUB:
+                parts[tracer] = spread_out(part, to_right, to_left)
+        target = here_ref if sweep % 2 else there_ref
+        for i in range(sweep, count - sweep):
+            def field(at):
+                if sweep == 1:
+                    return source(at)
+                return (there_ref if sweep % 2 else here_ref).at[at]
+
+            for tracer in range(2):
+                at = pl.ds(tracer * padded, padded)
+                centre = field(i)[at, :]
+                total = centre + face_ref[0, i] * (field(i + 1)[at, :] - centre)
+                total = total + face_ref[0, i - 1] * (field(i - 1)[at, :] - centre)
+                total = total + face_ref[1, i] * (left(centre) - centre)
+                total = total + face_ref[2, i] * (right(centre) - centre)
+                target[i, at, :] = total
+
+    target = here_ref if SUB % 2 else there_ref
+    for row in range(rows):
+        i = row + SUB
+        at = pl.ds(row, levels, stride=rows)
         mixed = []
         for tracer in range(2):
-            here = tracer * padded + start
-            value = [load(i, here, tall) for i in range(count)]
-            part = edge_ref[pl.ds(here, tall), :] + other_ref[pl.ds(here, tall), :]
-            extra = None
-            for sweep in range(1, SUB + 1):
-                over_col = strip_col * (left(part) - part)
-                across = jnp.where(out_of_low, over_col, 0.0) - jnp.where(
-                    out_of_high, right(over_col), 0.0
-                )
-                if extra is None:
-                    extra = across
-                else:
-                    extra = stripped(extra, strip_own * (left(extra) - extra)) + across
-                if sweep < SUB:
-                    part = stripped(part, over_col)
-                after = list(value)
-                over_row = [None] * count
-                for i in range(sweep - 1, count - sweep):
-                    over_row[i] = row_face[i] * (value[i + 1] - value[i])
-                for i in range(sweep, count - sweep):
-                    flux = col_face[i] * (left(value[i]) - value[i])
-                    after[i] = value[i] + (over_row[i] - over_row[i - 1]) + (flux - right(flux))
-                value = after
-            mixed.append(
-                [
-                    value[i] + jnp.where(at_border, left(extra, SLOT * i + SUB), 0.0)
-                    for i in range(SUB, SUB + rows)
-                ]
-            )
-        for row in range(rows):
-            at = pl.ds(start * rows + row, size, stride=rows)
-            wet = level[:size] < depths[row + SUB]
-            weight = weight_ref[at, :]
-            misfit = []
-            ends = []
-            for tracer in range(2):
-                end = mixed[tracer][row][:size]
-                ends.append(end)
-                mixed_ref[tracer, at, :] = end
-                misfit.append(weight * (end - observed_ref[tracer, at, :]))
-            up = jnp.where(wet, ends[0] - ends[1], 0.0)
-            down = jnp.where(wet, misfit[1] - misfit[0], 0.0)
-            if size < tall:
-                up = jnp.sum(up, axis=0, keepdims=True)
-                down = jnp.sum(down, axis=0, keepdims=True)
-                up = jnp.sum(buoyancy[row], axis=0, keepdims=True) + up
-                down = jnp.sum(pressure[row], axis=0, keepdims=True) + down
-                buoyancy[row], pressure[row] = up, down
-            else:
-                buoyancy[row] = up if start == 0 else buoyancy[row] + up
-                pressure[row] = down if start == 0 else pressure[row] + down
-            if start == 0:
-                part_ref[2, pl.ds(row, 1), :] = misfit[0][0:1]
-                part_ref[3, pl.ds(row, 1), :] = misfit[1][0:1]
-    for row in range(rows):
-        part_ref[0, pl.ds(row, 1), :] = scale * jnp.sum(buoyancy[row], axis=0, keepdims=True)
-        part_ref[1, pl.ds(row, 1), :] = jnp.sum(pressure[row], axis=0, keepdims=True)
+            border = jnp.where(at_border, left(extras[tracer], SLOT * i + SUB), 0.0)
+            mixed.append((target[i, pl.ds(tracer * padded, padded), :] + border)[:levels])
+        wet = level[:levels] < depths[i]
+        weight = weight_ref[at, :]
+        misfit = []
+        for tracer in range(2):
+            mixed_ref[tracer, at, :] = mixed[tracer]
+            misfit.append(weight * (mixed[tracer] - observed_ref[tracer, at, :]))
+        here = pl.ds(row, 1)
+        part_ref[0, here, :] = scale * jnp.sum(
+            jnp.where(wet, mixed[0] - mixed[1], 0.0), axis=0, keepdims=True
+        )
+        part_ref[1, here, :] = jnp.sum(
+            jnp.where(wet, misfit[1] - misfit[0], 0.0), axis=0, keepdims=True
+        )
+        part_ref[2, here, :] = misfit[0][0:1]
+        part_ref[3, here, :] = misfit[1][0:1]
     for copy in range(copies):
         for field in range(4):
             fields_ref[copy, field] = part_ref[field]
@@ -316,14 +308,13 @@
         col_face = jnp.where(
             inside & wet & (left(spread) > 0.0), 0.5 * (spread + left(spread)), 0.0
         )
-        return row_face, col_face
-
-    def outflow(value, row_face, col_face):
-        over_row = row_face * (value - below(value))
-        over_col = col_face * (value - left(value))
-        return (over_row - above(over_row)) + (over_col - right(over_col))
-
-    row_face, col_face = (SURFACE_GAIN * face for face in faces(whole(6)))
+        return row_face, above(row_face), col_face, right(col_face)
+
+    def outflow(value, to_below, to_above, to_right, to_left):
+        total = to_right * (value - left(value)) + to_left * (value - right(value))
+        return total + to_below * (value - below(value)) + to_above * (value - above(value))
+
+    gained = [SURFACE_GAIN * face for face in faces(whole(6))]
     damping = whole(7)
 
     def conjugate(rhs):
@@ -332,7 +323,7 @@
         solution = None
         norm_now = total(rhs * rhs)
         for sweep in range(ITERS):
-            image = damping * search + outflow(search, row_face, col_face)
+            image = damping * search + outflow(search, *gained)
             alpha = norm_now / total(search * image)
             solution = alpha * search if solution is None else solution + alpha * search
             if sweep < ITERS - 1:
@@ -361,16 +352,13 @@
     sea = spread > 0.0
     lowered = jnp.where(sea, around(5) * elevation, 0.0)
     raised = jnp.where(sea, scale * kept_around(1), 0.0)
-    near_row, near_col = faces(spread)
-    gradient = []
+    near = faces(spread)
+    carried = [around(2) - lowered + raised, around(3) + lowered - raised]
+    for sweep in range(SUB):
+        carried = [value - outflow(value, *near) for value in carried]
+    gradient = [jnp.where(sea, value, 0.0)[rows : 2 * rows, :cols] for value in carried]
     for tracer in range(2):
-        carried = around(2 + tracer)
-        carried = carried - lowered + raised if tracer == 0 else carried + lowered - raised
-        for sweep in range(SUB):
-            carried = carried - outflow(carried, near_row, near_col)
-        value = jnp.where(sea, carried, 0.0)[rows : 2 * rows, :cols]
-        gradient_ref[tracer] = value
-        gradient.append(value)
+        gradient_ref[tracer] = gradient[tracer]
 
     lane = iota((1, cols), 1)
     inner = gram_ref[...]
@@ -468,7 +456,7 @@
         ],
         compiler_params=pltpu.CompilerParams(vmem_limit_bytes=VMEM_BYTES),
         name="pack",
-    )(state, control, depth_index, diffusivity)
+    )(*(pltpu.with_memory_space_constraint(x, pltpu.HBM) for x in (state, control, depth_index, diffusivity)))
     forward = [(i, (i + 1) % loops) for i in range(loops)]
     backward = [(target, source) for source, target in forward]
     swap = [(0, 1), (1, 0)]
@@ -483,7 +471,9 @@
         functools.partial(mix_kernel, levels, padded, scale, loops),
         [flat, (loops, 8, rows, cols)],
         scratch=[
-            pltpu.VMEM((2, 2 * (rows + 2 * SUB), 8, cols), F32),
+            pltpu.VMEM((3, rows + 2 * SUB, padded, cols), F32),
+            pltpu.VMEM((rows + 2 * SUB, planes, cols), F32),
+            pltpu.VMEM((rows + 2 * SUB, planes, cols), F32),
             pltpu.VMEM((4, rows, cols), F32),
         ],
         name="mix",

time: 55.5 us -> 48.7 us (0.88)
  Pallas kernels: 12.6 us -> 9.1 us
  local copies, waits for them, and re-layouts: 3.09 us -> 0.03 us
    pallas_call x1, Pallas kernels: 5.83 us -> 1.86 us  [on_device(): call(functools.partial(mix_kernel, levels, padded, scale, loops), [flat,...]
    unnamed x22 -> x16, local copies, waits for them, and re-layouts: 3.09 us -> 0.03 us
    pallas_call x1, Pallas kernels: 0.37 us -> 1.2 us  [on_device(): pl.pallas_call(functools.partial(pack_kernel, levels, padded), out_shape=...]
where the time goes in v3:
time: 48.7 us; the launch traced here: 48.5 us
  blocking collectives  23.7 us (49%)
  Pallas kernels  9.1 us (19%)
  waiting for transfers between devices  8.79 us (18%)
  starting transfers between devices  6.19 us (13%)
  between operations  0.72 us (1%)
    all_to_all x1, blocking collectives, on_device(): mine = lax.all_to_all(fields, 'loop', 0, 0)  13.6 us
    all_to_all x1, blocking collectives, on_device(): inner_all = lax.all_to_all(inner, GRID, 0, 0)  10 us
    ppermute x1, waiting for transfers between devices, on_device(): low = lax.ppermute(up, 'loop', forward)  4.02 us
    ppermute x1, starting transfers between devices, on_device(): high = lax.ppermute(down, 'loop', backward)  3.12 us
    pallas_call x1, Pallas kernels, on_device(): call(functools.partial(solve_kernel, levels, scale, blocks), [flat, (2, r...  3.08 us
    ppermute x1, starting transfers between devices, on_device(): low = lax.ppermute(up, 'loop', forward)  2.99 us
    pallas_call x1, Pallas kernels, on_device(): call(direction_kernel, [(2, rows, cols)], name='direction')  2.47 us
    ppermute x1, waiting for transfers between devices, on_device(): high = lax.ppermute(down, 'loop', backward)  2.01 us
  transfers between devices with their start and end apart: 4, of which 4 were waited for; matrix products, arithmetic and copies ran while one was open for 0% of the time, Pallas kernels for 1%

profile of v3, /device:TPU:0, one launch (start us, length us, event | category | flops | bytes accessed | tf_op | source)
XLA Modules:
  0.0 48.5 jit_solution(13196174530843287618)
XLA Ops:
  0.6 0.0 copy-start
  0.6 0.0 copy-start.1
  0.7 0.0 copy-start.2
  0.7 0.0 copy-start.7
  0.7 1.2 %pack.1 = (f32[8,112,128]{2,1,0:T(8,128)S(1)}, f32[3,112,128]{2,1,0:T(8,128)S(1)}, f32[3,112,128]{2,1,0:T(8,128)S(1)}) custom-call(f32[2,400,128]{2,1,0:T(8,128)} %bitcast.15, f32[2,8,128]{2,1,0:T(8,128)} %control_hbm.1, s32[8,128]{1,0:T(8,128)} %depth_ref.3, f32[8,128]{1,0:T(8,128)} %spread_ref.1), custom_call_target="tpu_custom_call" | custom-call | tf_op jit(solution)/shard_map/pack/pallas_call | solution.py:442
  1.9 3.0 %collective-permute-start = (f32[3,112,128]{2,1,0:T(8,128)S(1)}, f32[3,112,128]{2,1,0:T(8,128)S(1)}, u32[]{:S(2)}, u32[]{:S(2)}) collective-permute-start(f32[3,112,128]{2,1,0:T(8,128)S(1)} %get-tuple-element.15), channel_id=1, source_target_pairs={{0,2},{2,4},{4,6},{6,8},{8,10},{10,12},{12,14},{14,0},{1,3},{3,5},... | collective-permute-start | bytes 516104 | tf_op jit(solution)/shard_map/ppermute | solution.py:463
  4.9 3.1 %collective-permute-start.1 = (f32[3,112,128]{2,1,0:T(8,128)S(1)}, f32[3,112,128]{2,1,0:T(8,128)S(1)}, u32[]{:S(2)}, u32[]{:S(2)}) collective-permute-start(f32[3,112,128]{2,1,0:T(8,128)S(1)} %get-tuple-element.16), channel_id=1, source_target_pairs={{2,0},{4,2},{6,4},{8,6},{10,8},{12,10},{14,12},{0,14},{3,1},{5,3},... | collective-permute-start | bytes 516104 | tf_op jit(solution)/shard_map/ppermute | solution.py:464
  8.0 0.0 copy-done
  8.0 0.0 copy-done.1
  8.0 0.0 copy-done.2
  8.0 0.3 pairs.1
  8.4 4.0 %collective-permute-done.low_ref = f32[3,112,128]{2,1,0:T(8,128)S(1)} collective-permute-done((f32[3,112,128]{2,1,0:T(8,128)S(1)}, f32[3,112,128]{2,1,0:T(8,128)S(1)}, u32[]{:S(2)}, u32[]{:S(2)}) %collective-permute-start) | collective-permute-done | bytes 172064 | tf_op jit(solution)/shard_map/ppermute | solution.py:463
  12.4 2.0 %collective-permute-done.1.high_ref = f32[3,112,128]{2,1,0:T(8,128)S(1)} collective-permute-done((f32[3,112,128]{2,1,0:T(8,128)S(1)}, f32[3,112,128]{2,1,0:T(8,128)S(1)}, u32[]{:S(2)}, u32[]{:S(2)}) %collective-permute-start.1) | collective-permute-done | bytes 172064 | tf_op jit(solution)/shard_map/ppermute | solution.py:464
  14.4 0.2 border.1.edge_ref
  14.6 0.1 collective-permute-start.2
  14.6 1.2 %collective-permute-done.2.other_ref = f32[112,128]{1,0:T(8,128)S(1)} collective-permute-done((f32[112,128]{1,0:T(8,128)S(1)}, f32[112,128]{1,0:T(8,128)S(1)}, u32[]{:S(2)}, u32[]{:S(2)}) %collective-permute-start.2) | collective-permute-done | bytes 57376 | tf_op jit(solution)/shard_map/ppermute | solution.py:469
  15.9 1.9 %mix.1 = (f32[2,400,128]{2,1,0:T(8,128)S(1)}, f32[8,8,8,128]{3,2,1,0:T(8,128)S(1)}) custom-call(f32[8,112,128]{2,1,0:T(8,128)S(1)} %get-tuple-element.14.rows_ref, f32[3,112,128]{2,1,0:T(8,128)S(1)} %collective-permute-done.low_ref, f32[3,112,128]{2,1,0:T(8,128)S(1)} %collective-permute-done.1.high_ref, f32[112,128]{1,0:T(8,128)S(1)} %border.1.edge_ref, ...), custom_call_target="tpu_custom_call" | custom-call | tf_op jit(solution)/shard_map/mix/pallas_call | solution.py:470
  17.7 13.6 %all_to_all.10.mine_ref = f32[8,8,8,128]{3,2,1,0:T(8,128)S(1)} all-to-all(f32[8,8,8,128]{3,2,1,0:T(8,128)S(1)} %get-tuple-element.19), channel_id=1, replica_groups=mesh['members'=2,'loop'=8,'lat'=2] {'loop'}, dimensions={0} | all-to-all | bytes 524288 | tf_op jit(solution)/shard_map/all_to_all | solution.py:481
  31.4 0.0 collective-permute-start.3
  31.4 1.5 %collective-permute-done.3.other_ref = f32[8,8,8,128]{3,2,1,0:T(8,128)S(1)} collective-permute-done((f32[8,8,8,128]{3,2,1,0:T(8,128)S(1)}, f32[8,8,8,128]{3,2,1,0:T(8,128)S(1)}, u32[]{:S(2)}, u32[]{:S(2)}) %collective-permute-start.3) | collective-permute-done | bytes 262176 | tf_op jit(solution)/shard_map/ppermute | solution.py:482
  32.9 3.1 %solve.1 = (f32[2,400,128]{2,1,0:T(8,128)}, f32[2,8,128]{2,1,0:T(8,128)}, f32[16,1,128]{2,1,0:T(1,128)S(1)}) custom-call(f32[8,8,8,128]{3,2,1,0:T(8,128)S(1)} %all_to_all.10.mine_ref, f32[8,8,8,128]{3,2,1,0:T(8,128)S(1)} %collective-permute-done.3.other_ref, f32[2,400,128]{2,1,0:T(8,128)S(1)} %get-tuple-element.20.mixed_ref, s32[8,128]{1,0:T(8,128)S(1)} %copy-done.4, ...), custom_call_target="tpu_custom_call" | custom-call | tf_op jit(solution)/shard_map/solve/pallas_call | solution.py:483
  36.0 10.0 %all_to_all.11.inner_ref = f32[16,1,128]{2,1,0:T(1,128)S(1)} all-to-all(f32[16,1,128]{2,1,0:T(1,128)S(1)} %get-tuple-element.24), channel_id=1, replica_groups=mesh['members'=2,'loop'=8,'lat'=2] {'loop','lat'}, dimensions={0} | all-to-all | bytes 16384 | tf_op jit(solution)/shard_map/all_to_all | solution.py:490
  46.0 0.0 copy-done.6
  46.0 2.5 %direction.1 = f32[2,8,128]{2,1,0:T(8,128)} custom-call(f32[16,1,128]{2,1,0:T(1,128)S(1)} %all_to_all.11.inner_ref, f32[2,8,128]{2,1,0:T(8,128)S(1)} %copy-done.6, f32[8,16,128]{2,1,0:T(8,128)S(1)} %bitcast.10, f32[8,16,128]{2,1,0:T(8,128)S(1)} %bitcast.13), custom_call_target="tpu_custom_call" | custom-call | tf_op jit(solution)/shard_map/direction/pallas_call | solution.py:491
  (8 shorter events, 0.0 us)
Async XLA Ops:
  0.6 7.4 %copy-start = (f32[50,8,128]{2,1,0:T(8,128)S(1)}, f32[50,8,128]{2,1,0:T(8,128)}, u32[]{:S(2)}) copy-start(f32[50,8,128]{2,1,0:T(8,128)} %param.11) | copy-start | bytes 614404
  0.6 7.4 %copy-start.1 = (f32[8,2,8,128]{3,2,1,0:T(8,128)S(1)}, f32[8,2,8,128]{3,2,1,0:T(8,128)}, u32[]{:S(2)}) copy-start(f32[8,2,8,128]{3,2,1,0:T(8,128)} %param.16) | copy-start | bytes 196612
  0.7 7.4 %copy-start.2 = (f32[8,2,8,128]{3,2,1,0:T(8,128)S(1)}, f32[8,2,8,128]{3,2,1,0:T(8,128)}, u32[]{:S(2)}) copy-start(f32[8,2,8,128]{3,2,1,0:T(8,128)} %param.17) | copy-start | bytes 196612
  0.7 7.4 %copy-start.7 = (f32[8,128]{1,0:T(8,128)S(1)}, f32[8,128]{1,0:T(8,128)}, u32[]{:S(2)}) copy-start(f32[8,128]{1,0:T(8,128)} %damping_ref.1) | copy-start | bytes 12292
  1.9 10.5 %collective-permute-start = (f32[3,112,128]{2,1,0:T(8,128)S(1)}, f32[3,112,128]{2,1,0:T(8,128)S(1)}, u32[]{:S(2)}, u32[]{:S(2)}) collective-permute-start(f32[3,112,128]{2,1,0:T(8,128)S(1)} %get-tuple-element.15), channel_id=1, source_target_pairs={{0,2},{2,4},{4,6},{6,8},{8,10},{10,12},{12,14},{14,0},{1,3},{3,5},... | collective-permute-start | bytes 516104 | tf_op jit(solution)/shard_map/ppermute | solution.py:463
  4.9 3.1 %copy-start.5 = (f32[8,128]{1,0:T(8,128)S(1)}, f32[8,128]{1,0:T(8,128)}, u32[]{:S(2)}) copy-start(f32[8,128]{1,0:T(8,128)} %spread_ref.1) | copy-start | bytes 12292
  4.9 3.2 %copy-start.4 = (s32[8,128]{1,0:T(8,128)S(1)}, s32[8,128]{1,0:T(8,128)}, u32[]{:S(2)}) copy-start(s32[8,128]{1,0:T(8,128)} %depth_ref.3) | copy-start | bytes 12292
  4.9 9.5 %collective-permute-start.1 = (f32[3,112,128]{2,1,0:T(8,128)S(1)}, f32[3,112,128]{2,1,0:T(8,128)S(1)}, u32[]{:S(2)}, u32[]{:S(2)}) collective-permute-start(f32[3,112,128]{2,1,0:T(8,128)S(1)} %get-tuple-element.16), channel_id=1, source_target_pairs={{2,0},{4,2},{6,4},{8,6},{10,8},{12,10},{14,12},{0,14},{3,1},{5,3},... | collective-permute-start | bytes 516104 | tf_op jit(solution)/shard_map/ppermute | solution.py:464
  14.4 1.5 %copy-start.3 = (f32[2,50,8,128]{3,2,1,0:T(8,128)S(1)}, f32[2,50,8,128]{3,2,1,0:T(8,128)}, u32[]{:S(2)}) copy-start(f32[2,50,8,128]{3,2,1,0:T(8,128)} %param.10) | copy-start | bytes 1228804
  14.6 1.3 %collective-permute-start.2 = (f32[112,128]{1,0:T(8,128)S(1)}, f32[112,128]{1,0:T(8,128)S(1)}, u32[]{:S(2)}, u32[]{:S(2)}) collective-permute-start(f32[112,128]{1,0:T(8,128)S(1)} %border.1.edge_ref), channel_id=1, source_target_pairs={{0,1},{1,0},{2,3},{3,2},{4,5},{5,4},{6,7},{7,6},{8,9},{9,8},{10,11... | collective-permute-start | bytes 172040 | tf_op jit(solution)/shard_map/ppermute | solution.py:469
  31.4 1.5 %collective-permute-start.3 = (f32[8,8,8,128]{3,2,1,0:T(8,128)S(1)}, f32[8,8,8,128]{3,2,1,0:T(8,128)S(1)}, u32[]{:S(2)}, u32[]{:S(2)}) collective-permute-start(f32[8,8,8,128]{3,2,1,0:T(8,128)S(1)} %all_to_all.10.mine_ref), channel_id=1, source_target_pairs={{0,1},{1,0},{2,3},{3,2},{4,5},{5,4},{6,7},{7,6},{8,9},{9,8},{10,11... | collective-permute-start | bytes 786440 | tf_op jit(solution)/shard_map/ppermute | solution.py:482
  36.0 10.0 %copy-start.6 = (f32[2,8,128]{2,1,0:T(8,128)S(1)}, f32[2,8,128]{2,1,0:T(8,128)}, u32[]{:S(2)}) copy-start(f32[2,8,128]{2,1,0:T(8,128)} %get-tuple-element.12.gradient_ref) | copy-start | bytes 24580

commit v4 on v3

--- a/solution.py
+++ b/solution.py
@@ -11,6 +11,10 @@
 SUB = 3
 SURFACE_GAIN = 5.0
 SLOT = 8
+REACH = SUB + 2 * (ITERS - 1)
+SHIFT = 5.0
+SPAN = 5.0
+FUNCTIONALS = 1 + ITERS + ITERS + ITERS * ITERS
 GRID = ("loop", "lat")
 VMEM = pl.BlockSpec(memory_space=pltpu.VMEM)
 F32 = jnp.float32
@@ -37,45 +41,79 @@
 
 
 def pack_kernel(
-    levels, padded, state_hbm, control_hbm, depth_hbm, spread_hbm,
-    rows_ref, up_ref, down_ref, state_ref, control_ref, depth_ref, spread_ref, sems,
+    levels, padded, *refs
 ):
+    sources, (rows_ref, hist_ref, up_ref, down_ref), targets, sems = (
+        refs[:8], refs[8:12], refs[12:20], refs[20]
+    )
     copies = [
         pltpu.make_async_copy(source, target, sems.at[at])
-        for at, (source, target) in enumerate(
-            (
-                (state_hbm, state_ref),
-                (control_hbm, control_ref),
-                (depth_hbm, depth_ref),
-                (spread_hbm, spread_ref),
-            )
-        )
+        for at, (source, target) in enumerate(zip(sources, targets))
     ]
     for copy in copies:
         copy.start()
     for copy in copies:
         copy.wait()
+    state_ref, control_ref, depth_ref, spread_ref, damping_ref, weight_ref, step_ref, change_ref = targets
     rows, cols = depth_ref.shape
+    planes = 2 * padded
+    count = step_ref.shape[0] // (2 * rows)
+    pairs = 2 * count
+    near = planes + 2 * pairs
+    far = SUB * near
     depth = depth_ref[...].astype(F32)
     spread = spread_ref[...]
+    wet = depth > 0.5
+    total = jnp.zeros((rows, cols), F32)
+    for level in range(levels):
+        total = total + jnp.where(level < depth, weight_ref[pl.ds(level * rows, rows), :], 0.0)
+    fixed = (
+        spread,
+        depth,
+        damping_ref[...],
+        2.0 * total,
+        weight_ref[pl.ds(0, rows), :],
+        jnp.where(wet, spread, 0.0),
+    )
     first = iota((levels, cols), 0) == 0
     rest = jnp.zeros((padded - levels, cols), F32)
+    for ref in (up_ref, down_ref):
+        ref[pl.ds(ref.shape[0] - 8, 8), :] = jnp.zeros((8, cols), F32)
     for row in range(rows):
-        targets = [rows_ref.at[row]]
+        targets = [(rows_ref.at[row], 0, hist_ref.at[row], 0)]
         if row < SUB:
-            targets.append(down_ref.at[row])
+            targets.append((down_ref, row * near, down_ref, row * near + planes))
         if row >= rows - SUB:
-            targets.append(up_ref.at[row - rows + SUB])
+            at = (row - rows + SUB) * near
+            targets.append((up_ref, at, up_ref, at + planes))
+        here = slice(row, row + 1)
         for tracer in range(2):
-            lift = jnp.where(depth[row : row + 1] > 0.5, control_ref[tracer, row : row + 1, :], 0.0)
+            lift = jnp.where(wet[here], control_ref[tracer, here, :], 0.0)
             value = state_ref[tracer, pl.ds(row, levels, stride=rows), :]
             value = value + jnp.where(first, lift, 0.0)
-            for target in targets:
-                target[pl.ds(tracer * padded, levels), :] = value
-                target[pl.ds(tracer * padded + levels, padded - levels), :] = rest
-        for target in targets:
-            target[pl.ds(levels, 1), :] = spread[row : row + 1]
-            target[pl.ds(levels + 1, 1), :] = depth[row : row + 1]
+            for target, at, _, _ in targets:
+                at = at + tracer * padded
+                target[pl.ds(at, levels), :] = value
+                target[pl.ds(at + levels, padded - levels), :] = rest
+        for at, field in enumerate(fixed):
+            for target, start, _, _ in targets:
+                target[pl.ds(start + levels + at, 1), :] = field[here]
+        distant = []
+        if SUB <= row < REACH:
+            distant.append((down_ref, row - SUB))
+        if rows - REACH <= row < rows - SUB:
+            distant.append((up_ref, row - rows + REACH))
+        for which, ref in enumerate((step_ref, change_ref)):
+            both = [ref[pl.ds(tracer * rows + row, count, stride=2 * rows), :] for tracer in range(2)]
+            apart = jnp.where(wet[here], both[0] - both[1], 0.0)
+            joint = jnp.where(wet[here], both[0] + both[1], 0.0)
+            for _, _, target, at in targets:
+                target[pl.ds(at + which * count, count), :] = apart
+                target[pl.ds(at + pairs + which * count, count), :] = joint
+            for target, at in distant:
+                target[pl.ds(far + at * pairs + which * count, count), :] = apart
+        for target, at in distant:
+            target[pl.ds(far + (REACH - SUB) * pairs + at, 1), :] = fixed[5][here]
 
 
 def edge_of(rows_of, indices, cols, lat):
@@ -91,50 +129,176 @@
     return total
 
 
-def pairs_kernel(
-    rows_ref, step_ref, change_ref, depth_ref, spread_ref, damping_ref, weight_ref,
-    edge_ref, gram_ref, still_ref,
-):
+def pairs_kernel(rows_ref, step_ref, change_ref, edge_ref, gram_ref):
     rows, _, cols = rows_ref.shape
     lat = lax.axis_index("lat")
     edge_ref[...] = edge_of(lambda i: rows_ref[i - SUB], range(SUB, rows + SUB), cols, lat)
     count = step_ref.shape[0]
     lane = iota((1, cols), 1)
-    total = jnp.zeros((1, cols), F32)
-    at = 2 * count
+    total = [jnp.zeros((1, cols), F32) for _ in range(count)]
+    at = FUNCTIONALS
     for left_ref in (step_ref, change_ref):
         for i in range(count):
             for j in range(i, count):
                 value = jnp.sum(left_ref[i] * change_ref[j], axis=(0, 1), keepdims=True)
-                total = total + jnp.where(lane == at, value, 0.0)
-                at += 1
-    gram_ref[...] = total
-    depth = depth_ref[...]
-    total = jnp.zeros((rows, cols), F32)
-    for level in range(weight_ref.shape[0] // rows):
-        total = total + jnp.where(level < depth, weight_ref[pl.ds(level * rows, rows), :], 0.0)
-    still_ref[0] = 2.0 * total
-    still_ref[1] = weight_ref[pl.ds(0, rows), :]
-    still_ref[2] = jnp.where(depth > 0, spread_ref[...], 0.0)
-    still_ref[3] = damping_ref[...]
-
-
-def border_kernel(edge_ref, low_ref, high_ref, rows_ref, out_ref):
-    cols = edge_ref.shape[-1]
-    rows = rows_ref.shape[0]
+                total[i] = total[i] + jnp.where(lane == at + j, value, 0.0)
+                if i != j:
+                    total[j] = total[j] + jnp.where(lane == at + i, value, 0.0)
+        at += count
+    for i in range(count):
+        gram_ref[pl.ds(i, 1), :] = total[i]
+
+
+def border_layout(planes, rows, pairs):
+    tall = rows + 2 * REACH
+    short = rows + 2 * SUB
+    apart = planes
+    joint = apart + tall * pairs
+    fields = [joint + short * pairs]
+    for size in (tall, short, short, short):
+        fields.append(fields[-1] + round_up(size, 8))
+    return apart, joint, fields
+
+
+def border_kernel(levels, edge_ref, low_ref, high_ref, rows_ref, hist_ref, out_ref):
+    rows, planes, cols = rows_ref.shape
+    pairs = hist_ref.shape[1] // 2
+    near = planes + 2 * pairs
+    far = SUB * near
     lat = lax.axis_index("lat")
-    total = edge_ref[...] + edge_of(lambda i: low_ref[i], range(SUB), cols, lat)
-    out_ref[...] = total + edge_of(
-        lambda i: high_ref[i - rows - SUB], range(rows + SUB, rows + 2 * SUB), cols, lat
-    )
+    total = edge_ref[...] + edge_of(
+        lambda i: low_ref[pl.ds(i * near, planes), :], range(SUB), cols, lat
+    )
+    out_ref[pl.ds(0, planes), :] = total + edge_of(
+        lambda i: high_ref[pl.ds((i - rows - SUB) * near, planes), :],
+        range(rows + SUB, rows + 2 * SUB),
+        cols,
+        lat,
+    )
+    apart, joint, fields = border_layout(planes, rows, pairs)
+    for start, stop in zip(fields, fields[1:]):
+        out_ref[pl.ds(stop - 8, 8), :] = jnp.zeros((8, cols), F32)
+    ahead = REACH - SUB
+    for i in range(rows + 2 * REACH):
+        at = i - REACH
+        distant = None
+        if at < -SUB:
+            distant = (low_ref, i)
+        elif at < 0:
+            state, here, start = low_ref, low_ref, (at + SUB) * near
+        elif at < rows:
+            state, here, start = rows_ref.at[at], hist_ref.at[at], 0
+        elif at < rows + SUB:
+            state, here, start = high_ref, high_ref, (at - rows) * near
+        else:
+            distant = (high_ref, at - rows - SUB)
+        target = pl.ds(apart + i * pairs, pairs)
+        if distant is not None:
+            ref, at = distant
+            out_ref[target, :] = ref[pl.ds(far + at * pairs, pairs), :]
+            out_ref[pl.ds(fields[0] + i, 1), :] = ref[pl.ds(far + ahead * pairs + at, 1), :]
+            continue
+        offset = 0 if 0 <= at < rows else start + planes
+        out_ref[target, :] = here[pl.ds(offset, pairs), :]
+        out_ref[pl.ds(joint + (i - ahead) * pairs, pairs), :] = here[pl.ds(offset + pairs, pairs), :]
+        for field, plane, index in ((0, 5, i), (1, 2, i - ahead), (2, 3, i - ahead), (3, 4, i - ahead)):
+            out_ref[pl.ds(fields[field] + index, 1), :] = state[pl.ds(start + levels + plane, 1), :]
+
+
+def faces_between(here, there, opened=True):
+    return jnp.where((here > 0.0) & (there > 0.0) & opened, 0.5 * (here + there), 0.0)
+
+
+def basis_kernel(planes, rows, pairs, mine_ref, other_ref, out_ref, *work):
+    cols = mine_ref.shape[1]
+    width = 2 * cols
+    apart, joint, fields = border_layout(planes, rows, pairs)
+    tall = rows + 2 * REACH
+    ahead = REACH - SUB
+    opened = iota((1, width), 1) != jnp.where(lax.axis_index("lat") == 0, width - 1, cols - 1)
+
+    def wide(at, size):
+        return jnp.concatenate([mine_ref[pl.ds(at, size), :], other_ref[pl.ds(at, size), :]], axis=1)
+
+    def left(value):
+        return pltpu.roll(value, width - 1, 1)
+
+    def right(value):
+        return pltpu.roll(value, 1, 1)
+
+    spread = [wide(fields[0] + i, 1) for i in range(tall)]
+    to_right = [faces_between(value, left(value), opened) for value in spread]
+    to_left = [right(value) for value in to_right]
+    to_below = [faces_between(spread[i], spread[i + 1]) for i in range(tall - 1)]
+    inner = range(ahead, tall - ahead)
+    damping = {i: (wide(fields[1] + i - ahead, 1) - SHIFT) * (1.0 / SPAN) for i in inner}
+    response_weight = {i: wide(fields[2] + i - ahead, 1) for i in inner}
+    weight = {i: wide(fields[3] + i - ahead, 1) for i in inner}
+    gain = SURFACE_GAIN / SPAN
+
+    def outflow(get, i):
+        value = get(i)
+        total = to_right[i] * (value - left(value)) + to_left[i] * (value - right(value))
+        total = total + to_below[i] * (value - get(i + 1))
+        return value, total + to_below[i - 1] * (value - get(i - 1))
+
+    def mixed(get, ref, reach):
+        for i in range(REACH - reach, REACH + rows + reach):
+            value, out = outflow(get, i)
+            ref[i] = value - out
+        return lambda i: ref[i]
+
+    def applied(get, ref, reach):
+        for i in range(REACH - reach, REACH + rows + reach):
+            value, out = outflow(get, i)
+            ref[i] = damping[i] * value + gain * out
+        return lambda i: ref[i]
+
+    def keep(slot, get):
+        for i in range(rows):
+            out_ref[slot, i] = get(i + REACH)[:, :cols]
+
+    def start_apart(i):
+        return wide(apart + i * pairs, pairs)
+
+    def start_joint(i):
+        return wide(joint + (i - ahead) * pairs, pairs)
+
+    both = (start_apart, start_joint)
+    for sweep in range(SUB):
+        both = (
+            mixed(both[0], work[sweep], REACH - 1 - sweep),
+            mixed(both[1], work[SUB + sweep], SUB - 1 - sweep),
+        )
+    keep(0, both[1])
+    reach = REACH - SUB
+    powers = [both[0]]
+    for power in range(1, ITERS):
+        powers.append(applied(powers[-1], work[2 * SUB + power - 1], reach - power))
+    for power in range(ITERS):
+        keep(1 + power, powers[power])
+    reach = ITERS - 1
+    slot = 1 + ITERS
+    at = 2 * SUB + ITERS - 1
+    chains = []
+    for factor, power in [(weight, 0)] + [(response_weight, power) for power in range(ITERS)]:
+        get = powers[power]
+        chains.append(lambda i, factor=factor, get=get: factor[i] * get(i))
+    for power in range(1, ITERS):
+        for index in range(len(chains)):
+            chains[index] = applied(chains[index], work[at], reach - power)
+            at += 1
+            keep(slot + index * (ITERS - 1) + power - 1, chains[index])
 
 
 def mix_kernel(
     levels, padded, scale, copies,
-    rows_ref, low_ref, high_ref, edge_ref, other_ref, weight_ref, observed_ref, still_ref,
+    rows_ref, low_ref, high_ref, edge_ref, other_ref, weight_ref, observed_ref, basis_ref, gram_ref,
     mixed_ref, fields_ref, face_ref, here_ref, there_ref, part_ref,
 ):
     rows, planes, cols = rows_ref.shape
+    pairs = basis_ref.shape[2]
+    near = planes + 2 * pairs
     lat = lax.axis_index("lat")
     lane = iota((1, cols), 1)
     place = lane % SLOT
@@ -149,10 +313,10 @@
 
     def source(i):
         if i < SUB:
-            return low_ref.at[i]
+            return low_ref.at[pl.ds(i * near, planes)]
         if i < SUB + rows:
             return rows_ref.at[i - SUB]
-        return high_ref.at[i - SUB - rows]
+        return high_ref.at[pl.ds((i - SUB - rows) * near, planes)]
 
     def face(depth_here, depth_there, spread_here, spread_there):
         opened = level < jnp.minimum(depth_here, depth_there)
@@ -253,16 +417,47 @@
         )
         part_ref[2, here, :] = misfit[0][0:1]
         part_ref[3, here, :] = misfit[1][0:1]
+    for field, plane in enumerate((3, 4, 5, 2)):
+        for row in range(rows):
+            part_ref[4 + field, pl.ds(row, 1), :] = rows_ref[row, pl.ds(levels + plane, 1), :]
+
+    sums = [None] * FUNCTIONALS
+
+    def add(at, slot, row, factor):
+        value = basis_ref[slot, row] * factor
+        sums[at] = value if sums[at] is None else sums[at] + value
+
+    chain = 1 + ITERS
+    for row in range(rows):
+        here = pl.ds(row, 1)
+        get = lambda field: part_ref[field, here, :]
+        surface, base = get(0), get(1)
+        add(0, 0, row, 0.5 * (get(2) + get(3)))
+        add(0, 1, row, 0.5 * (get(2) - get(3)))
+        add(1, 1, row, get(5) * surface)
+        for power in range(1, ITERS):
+            add(1 + power, chain + power - 1, row, surface)
+        for j in range(ITERS):
+            add(1 + ITERS + j, 1 + j, row, base)
+            at = 1 + 2 * ITERS + j * ITERS
+            add(at, 1 + j, row, get(4) * surface)
+            for power in range(1, ITERS):
+                add(at + power, chain + (1 + j) * (ITERS - 1) + power - 1, row, surface)
+    half = pairs // 2
+    total = gram_ref[...]
+    for at in range(FUNCTIONALS):
+        value = jnp.sum(sums[at], axis=1, keepdims=True)
+        total = total + jnp.where(lane == at, value[:half], 0.0)
+        total = total + jnp.where(lane == cols // 2 + at, value[half:], 0.0)
+    part_ref[8] = total
     for copy in range(copies):
-        for field in range(4):
-            fields_ref[copy, field] = part_ref[field]
-            fields_ref[copy, 4 + field] = still_ref[field]
+        fields_ref[copy] = part_ref[...]
 
 
 def solve_kernel(
-    levels, scale, copies,
-    mine_ref, other_ref, mixed_ref, depth_ref, step_ref, change_ref, gram_ref,
-    state_ref, gradient_ref, inner_ref, kept_ref,
+    levels, scale,
+    mine_ref, other_ref, mixed_ref, depth_ref, step_ref, change_ref,
+    state_ref, gradient_ref, direction_ref, kept_ref,
 ):
     loops, _, rows, cols = mine_ref.shape
     height = loops * rows
@@ -302,12 +497,8 @@
         return jnp.sum(value, axis=(0, 1), keepdims=True)
 
     def faces(spread):
-        wet = spread > 0.0
-        inside = iota(spread.shape, 1) != closed
-        row_face = jnp.where(wet & (below(spread) > 0.0), 0.5 * (spread + below(spread)), 0.0)
-        col_face = jnp.where(
-            inside & wet & (left(spread) > 0.0), 0.5 * (spread + left(spread)), 0.0
-        )
+        row_face = faces_between(spread, below(spread))
+        col_face = faces_between(spread, left(spread), iota(spread.shape, 1) != closed)
         return row_face, above(row_face), col_face, right(col_face)
 
     def outflow(value, to_below, to_above, to_right, to_left):
@@ -320,18 +511,36 @@
     def conjugate(rhs):
         residual = rhs
         search = rhs
-        solution = None
+        solution = jnp.zeros_like(rhs)
         norm_now = total(rhs * rhs)
+        one = jnp.ones((1, 1), F32)
+        residual_of = [one]
+        search_of = [one]
+        solution_of = []
         for sweep in range(ITERS):
             image = damping * search + outflow(search, *gained)
             alpha = norm_now / total(search * image)
-            solution = alpha * search if solution is None else solution + alpha * search
+            solution = solution + alpha * search
+            solution_of = add_up(solution_of, alpha, search_of)
             if sweep < ITERS - 1:
                 residual = residual - alpha * image
                 norm_next = total(residual * residual)
-                search = residual + (norm_next / norm_now) * search
+                beta = norm_next / norm_now
+                search = residual + beta * search
                 norm_now = norm_next
-        return solution
+                image_of = [SHIFT * value for value in search_of]
+                image_of = add_up(image_of, SPAN, [None] + search_of)
+                residual_of = add_up(residual_of, -alpha, image_of)
+                search_of = add_up(residual_of, beta, search_of)
+        return solution, solution_of
+
+    def add_up(terms, factor, others):
+        result = list(terms) + [None] * (len(others) - len(terms))
+        for at, value in enumerate(others):
+            if value is not None:
+                value = factor * value
+                result[at] = value if result[at] is None else result[at] + value
+        return result
 
     def keep(slot, value):
         for i in range(loops):
@@ -342,9 +551,9 @@
             [kept_ref[slot, lax.rem(loop + shift, loops)] for shift in (loops - 1, 0, 1)], axis=0
         )
 
-    elevation = conjugate(whole(0))
+    elevation, elevation_of = conjugate(whole(0))
     keep(0, elevation)
-    response = conjugate(whole(1) + whole(4) * elevation)
+    response, response_of = conjugate(whole(1) + whole(4) * elevation)
     keep(1, response)
 
     elevation = kept_around(0)
@@ -360,14 +569,56 @@
     for tracer in range(2):
         gradient_ref[tracer] = gradient[tracer]
 
+    count = step_ref.shape[0]
+    inner = mine_ref[0, 8]
+    for i in range(loops):
+        if i:
+            inner = inner + mine_ref[i, 8]
+        inner = inner + other_ref[i, 8]
     lane = iota((1, cols), 1)
-    inner = gram_ref[...]
-    count = step_ref.shape[0]
-    for index, ref in enumerate((step_ref, change_ref)):
+    place = lane % (cols // 2)
+    factor = jnp.where(place == 0, 1.0, 0.0)
+    for j in range(ITERS):
+        factor = jnp.where(place == 1 + j, -elevation_of[j], factor)
+        part = scale * response_of[j]
+        factor = jnp.where(place == 1 + ITERS + j, part, factor)
+        for k in range(ITERS):
+            at = 1 + 2 * ITERS + j * ITERS + k
+            factor = jnp.where(place == at, part * elevation_of[k], factor)
+    products = inner * factor
+    step_grad = jnp.sum(jnp.where(lane < cols // 2, products, 0.0), axis=1, keepdims=True)
+    change_grad = jnp.sum(jnp.where(lane >= cols // 2, products, 0.0), axis=1, keepdims=True)
+
+    def column(at):
+        return inner[:, at : at + 1]
+
+    step_change = [column(FUNCTIONALS + i) for i in range(count)]
+    change_change = [column(FUNCTIONALS + count + i) for i in range(count)]
+    pick = lambda value, i: value[i : i + 1]
+    last = count - 1
+    gamma = pick(step_change[last], last) / pick(change_change[last], last)
+    rho = [1.0 / pick(step_change[i], i) for i in range(count)]
+    factors = [None] * count
+    for i in range(count - 1, -1, -1):
+        factors[i] = rho[i] * pick(step_grad, i)
+        step_grad = step_grad - factors[i] * step_change[i]
+        change_grad = change_grad - factors[i] * change_change[i]
+    change_grad = gamma * change_grad
+    weights = []
+    for i in range(count):
+        weights.append(factors[i] - rho[i] * pick(change_grad, i))
+        change_grad = change_grad + weights[i] * step_change[i]
+    factors = [jnp.broadcast_to(value, (rows, cols)) for value in factors]
+    weights = [jnp.broadcast_to(value, (rows, cols)) for value in weights]
+    for tracer in range(2):
+        at = pl.ds(tracer * rows, rows)
+        value = gradient[tracer]
+        for i in range(count - 1, -1, -1):
+            value = value - factors[i] * change_ref[i, at, :]
+        value = gamma * value
         for i in range(count):
-            value = ref[i, pl.ds(0, rows), :] * gradient[0] + ref[i, pl.ds(rows, rows), :] * gradient[1]
-            inner = inner + jnp.where(lane == index * count + i, total(value), 0.0)
-    inner_ref[...] = jnp.broadcast_to(inner[None], inner_ref.shape)
+            value = value + weights[i] * step_ref[i, at, :]
+        direction_ref[tracer] = -value
 
     depth = depth_ref[...]
     here = elevation[rows : 2 * rows, :cols]
@@ -376,49 +627,6 @@
         change = jnp.where(level < depth, here, 0.0)
         state_ref[0, at, :] = mixed_ref[0, at, :] - change
         state_ref[1, at, :] = mixed_ref[1, at, :] + change
-
-
-def direction_kernel(inner_ref, gradient_ref, step_ref, change_ref, out_ref):
-    count = step_ref.shape[0]
-    rows = gradient_ref.shape[1]
-    inner = jnp.sum(inner_ref[...], axis=0)
-
-    def scalar(at):
-        return inner[:, at : at + 1]
-
-    step_grad = [scalar(i) for i in range(count)]
-    change_grad = [scalar(count + i) for i in range(count)]
-    at = 2 * count
-    step_change = {}
-    change_change = {}
-    for table in (step_change, change_change):
-        for i in range(count):
-            for j in range(i, count):
-                table[i, j] = table[j, i] = scalar(at)
-                at += 1
-    gamma = step_change[count - 1, count - 1] / change_change[count - 1, count - 1]
-    factors = [None] * count
-    for i in range(count - 1, -1, -1):
-        factors[i] = step_grad[i] / step_change[i, i]
-        for j in range(count):
-            if j < i:
-                step_grad[j] = step_grad[j] - factors[i] * step_change[j, i]
-            change_grad[j] = change_grad[j] - factors[i] * change_change[j, i]
-    change_grad = [gamma * value for value in change_grad]
-    weights = []
-    for i in range(count):
-        weights.append(factors[i] - change_grad[i] / step_change[i, i])
-        for j in range(i + 1, count):
-            change_grad[j] = change_grad[j] + weights[i] * step_change[i, j]
-    for tracer in range(2):
-        at = pl.ds(tracer * rows, rows)
-        value = gradient_ref[tracer]
-        for i in range(count - 1, -1, -1):
-            value = value - factors[i] * change_ref[i, at, :]
-        value = gamma * value
-        for i in range(count):
-            value = value + weights[i] * step_ref[i, at, :]
-        out_ref[tracer] = -value
 
 
 def on_device(
@@ -439,58 +647,66 @@
     step = history_step.reshape(count, 2 * rows, cols)
     change = history_change.reshape(count, 2 * rows, cols)
 
-    packed, up, down = pl.pallas_call(
+    pairs = 2 * count
+    near = planes + 2 * pairs
+    ahead = REACH - SUB
+    sent = SUB * near + ahead * pairs + round_up(ahead, 8)
+    inputs = (
+        state, control, depth_index, diffusivity, damping, weight,
+        history_step.reshape(-1, cols), history_change.reshape(-1, cols),
+    )
+    shapes = ((rows, planes, cols), (rows, 2 * pairs, cols), (sent, cols), (sent, cols))
+    packed, hist, up, down = pl.pallas_call(
         functools.partial(pack_kernel, levels, padded),
-        out_shape=[
-            jax.ShapeDtypeStruct(shape, F32)
-            for shape in ((rows, planes, cols), (SUB, planes, cols), (SUB, planes, cols))
-        ],
-        in_specs=[pl.BlockSpec(memory_space=pltpu.HBM)] * 4,
-        out_specs=[VMEM] * 3,
-        scratch_shapes=[
-            pltpu.VMEM(flat, F32),
-            pltpu.VMEM((2, rows, cols), F32),
-            pltpu.VMEM((rows, cols), jnp.int32),
-            pltpu.VMEM((rows, cols), F32),
-            pltpu.SemaphoreType.DMA((4,)),
-        ],
+        out_shape=[jax.ShapeDtypeStruct(shape, F32) for shape in shapes],
+        in_specs=[pl.BlockSpec(memory_space=pltpu.HBM)] * len(inputs),
+        out_specs=[VMEM] * len(shapes),
+        scratch_shapes=[pltpu.VMEM(x.shape, x.dtype) for x in inputs]
+        + [pltpu.SemaphoreType.DMA((len(inputs),))],
         compiler_params=pltpu.CompilerParams(vmem_limit_bytes=VMEM_BYTES),
         name="pack",
-    )(*(pltpu.with_memory_space_constraint(x, pltpu.HBM) for x in (state, control, depth_index, diffusivity)))
+    )(*(pltpu.with_memory_space_constraint(x, pltpu.HBM) for x in inputs))
     forward = [(i, (i + 1) % loops) for i in range(loops)]
     backward = [(target, source) for source, target in forward]
     swap = [(0, 1), (1, 0)]
     low = lax.ppermute(up, "loop", forward)
     high = lax.ppermute(down, "loop", backward)
-    edge, gram, still = call(
-        pairs_kernel, [(planes, cols), (1, cols), (4, rows, cols)], name="pairs"
-    )(packed, step, change, depth_index, diffusivity, damping, weight)
-    (edge,) = call(border_kernel, [(planes, cols)], name="border")(edge, low, high, packed)
+    edge, gram = call(pairs_kernel, [(planes, cols), (rows, cols)], name="pairs")(
+        packed, step, change
+    )
+    border = border_layout(planes, rows, pairs)[2][-1]
+    (edge,) = call(functools.partial(border_kernel, levels), [(border, cols)], name="border")(
+        edge, low, high, packed, hist
+    )
     other = lax.ppermute(edge, "lat", swap)
+    chains = 1 + ITERS
+    buffers = 2 * SUB + ITERS - 1 + chains * (ITERS - 1)
+    (basis,) = call(
+        functools.partial(basis_kernel, planes, rows, pairs),
+        [(1 + ITERS + chains * (ITERS - 1), rows, pairs, cols)],
+        scratch=[pltpu.VMEM((rows + 2 * REACH, pairs, 2 * cols), F32)] * buffers,
+        name="basis",
+    )(edge, other)
     mixed, fields = call(
         functools.partial(mix_kernel, levels, padded, scale, loops),
-        [flat, (loops, 8, rows, cols)],
+        [flat, (loops, 9, rows, cols)],
         scratch=[
             pltpu.VMEM((3, rows + 2 * SUB, padded, cols), F32),
             pltpu.VMEM((rows + 2 * SUB, planes, cols), F32),
             pltpu.VMEM((rows + 2 * SUB, planes, cols), F32),
-            pltpu.VMEM((4, rows, cols), F32),
+            pltpu.VMEM((9, rows, cols), F32),
         ],
         name="mix",
-    )(packed, low, high, edge, other, weight, observed, still)
+    )(packed, low, high, edge, other, weight, observed, basis, gram)
     mine = lax.all_to_all(fields, "loop", 0, 0)
     theirs = lax.ppermute(mine, "lat", swap)
-    state_next, gradient, inner = call(
-        functools.partial(solve_kernel, levels, scale, blocks),
-        [flat, (2, rows, cols), (blocks, 1, cols)],
+    state_next, gradient, direction = call(
+        functools.partial(solve_kernel, levels, scale),
+        [flat, (2, rows, cols), (2, rows, cols)],
         scratch=[pltpu.VMEM((2, loops, rows, 2 * cols), F32)],
         vmem=VMEM_BYTES if loops <= 16 else 2 * VMEM_BYTES,
         name="solve",
-    )(mine, theirs, mixed, depth_index, step, change, gram)
-    inner_all = lax.all_to_all(inner, GRID, 0, 0)
-    (direction,) = call(direction_kernel, [(2, rows, cols)], name="direction")(
-        inner_all, gradient, step, change
-    )
+    )(mine, theirs, mixed, depth_index, step, change)
     return (state_next.reshape(2, levels, rows, cols), gradient, direction)
 
 

time: 48.7 us -> 45.9 us (0.943)
  blocking collectives: 23.7 us -> 15 us
  waiting for transfers between devices: 8.79 us -> 13 us
  Pallas kernels: 9.1 us -> 10.7 us
    all_to_all x1 -> x0, blocking collectives: 10 us -> none  [on_device(): inner_all = lax.all_to_all(inner, GRID, 0, 0)]
    ppermute x1, waiting for transfers between devices: 4.02 us -> 7.54 us  [on_device(): low = lax.ppermute(up, 'loop', forward)]
    all_to_all x1, blocking collectives: 13.6 us -> 15 us  [on_device(): mine = lax.all_to_all(fields, 'loop', 0, 0)]
    pallas_call x4, Pallas kernels: 6.04 us -> 7.26 us  [the longest x1 4.89 us: on_device(): call(functools.partial(solve_kernel, levels, scale), [flat, (2, rows, col...]
where the time goes in v4:
time: 45.9 us; the launch traced here: 45.7 us
  blocking collectives  15 us (33%)
  waiting for transfers between devices  13 us (28%)
  Pallas kernels  10.7 us (23%)
  starting transfers between devices  6.17 us (13%)
  between operations  0.73 us (2%)
    all_to_all x1, blocking collectives, on_device(): mine = lax.all_to_all(fields, 'loop', 0, 0)  15 us
    ppermute x1, waiting for transfers between devices, on_device(): low = lax.ppermute(up, 'loop', forward)  7.54 us
    pallas_call x1, Pallas kernels, on_device(): call(functools.partial(solve_kernel, levels, scale), [flat, (2, rows, col...  4.89 us
    ppermute x1, starting transfers between devices, on_device(): high = lax.ppermute(down, 'loop', backward)  3.1 us
    ppermute x1, starting transfers between devices, on_device(): low = lax.ppermute(up, 'loop', forward)  2.99 us
    ppermute x1, waiting for transfers between devices, on_device(): high = lax.ppermute(down, 'loop', backward)  2.2 us
    pallas_call x1, Pallas kernels, on_device(): call(functools.partial(mix_kernel, levels, padded, scale, loops), [flat,...  2.02 us
    pallas_call x1, Pallas kernels, on_device(): call(functools.partial(basis_kernel, planes, rows, pairs), [(1 + ITERS +...  1.86 us
  transfers between devices with their start and end apart: 4, of which 4 were waited for; matrix products, arithmetic and copies ran while one was open for 0% of the time, Pallas kernels for 1%

profile of v4, /device:TPU:0, one launch (start us, length us, event | category | flops | bytes accessed | tf_op | source)
XLA Modules:
  0.0 45.7 jit_solution(3482897509347636780)
XLA Ops:
  0.6 0.0 copy-start.1
  0.6 0.0 copy-start.2
  0.7 1.4 %pack.1 = (f32[8,112,128]{2,1,0:T(8,128)S(1)}, f32[8,32,128]{2,1,0:T(8,128)S(1)}, f32[504,128]{1,0:T(8,128)S(1)}, f32[504,128]{1,0:T(8,128)S(1)}) custom-call(f32[2,400,128]{2,1,0:T(8,128)} %bitcast.17, f32[2,8,128]{2,1,0:T(8,128)} %refs_1_.1, s32[8,128]{1,0:T(8,128)} %depth_ref.1, f32[8,128]{1,0:T(8,128)} %refs_3_.1, f32[8,128]{1,0:T(8,128)} %refs_4_.1, ...), custom_call_target="tpu_custom_call" | custom-call | tf_op jit(solution)/shard_map/pack/pallas_call | solution.py:659
  2.1 3.0 %collective-permute-start = (f32[504,128]{1,0:T(8,128)S(1)}, f32[504,128]{1,0:T(8,128)S(1)}, u32[]{:S(2)}, u32[]{:S(2)}) collective-permute-start(f32[504,128]{1,0:T(8,128)S(1)} %get-tuple-element.15), channel_id=1, source_target_pairs={{0,2},{2,4},{4,6},{6,8},{8,10},{10,12},{12,14},{14,0},{1,3},{3,5},... | collective-permute-start | bytes 774152 | tf_op jit(solution)/shard_map/ppermute | solution.py:672
  5.1 3.1 %collective-permute-start.1 = (f32[504,128]{1,0:T(8,128)S(1)}, f32[504,128]{1,0:T(8,128)S(1)}, u32[]{:S(2)}, u32[]{:S(2)}) collective-permute-start(f32[504,128]{1,0:T(8,128)S(1)} %get-tuple-element.16), channel_id=1, source_target_pairs={{2,0},{4,2},{6,4},{8,6},{10,8},{12,10},{14,12},{0,14},{3,1},{5,3},... | collective-permute-start | bytes 774152 | tf_op jit(solution)/shard_map/ppermute | solution.py:673
  8.2 0.0 copy-done.1
  8.2 0.0 copy-done.2
  8.2 0.4 pairs.1
  8.5 7.5 %collective-permute-done.low_ref = f32[504,128]{1,0:T(8,128)S(1)} collective-permute-done((f32[504,128]{1,0:T(8,128)S(1)}, f32[504,128]{1,0:T(8,128)S(1)}, u32[]{:S(2)}, u32[]{:S(2)}) %collective-permute-start) | collective-permute-done | bytes 258080 | tf_op jit(solution)/shard_map/ppermute | solution.py:672
  16.1 2.2 %collective-permute-done.1.high_ref = f32[504,128]{1,0:T(8,128)S(1)} collective-permute-done((f32[504,128]{1,0:T(8,128)S(1)}, f32[504,128]{1,0:T(8,128)S(1)}, u32[]{:S(2)}, u32[]{:S(2)}) %collective-permute-start.1) | collective-permute-done | bytes 258080 | tf_op jit(solution)/shard_map/ppermute | solution.py:673
  18.3 0.2 border.1.mine_ref.edge_ref
  18.4 0.0 copy-start
  18.5 0.0 copy-start.3
  18.5 0.1 collective-permute-start.2
  18.5 1.7 %collective-permute-done.2.other_ref = f32[760,128]{1,0:T(8,128)S(1)} collective-permute-done((f32[760,128]{1,0:T(8,128)S(1)}, f32[760,128]{1,0:T(8,128)S(1)}, u32[]{:S(2)}, u32[]{:S(2)}) %collective-permute-start.2) | collective-permute-done | bytes 389152 | tf_op jit(solution)/shard_map/ppermute | solution.py:681
  20.3 1.9 %basis.1.basis_ref = f32[12,8,16,128]{3,2,1,0:T(8,128)S(1)} custom-call(f32[760,128]{1,0:T(8,128)S(1)} %border.1.mine_ref.edge_ref, f32[760,128]{1,0:T(8,128)S(1)} %collective-permute-done.2.other_ref), custom_call_target="tpu_custom_call" | custom-call | tf_op jit(solution)/shard_map/basis/pallas_call | solution.py:684
  22.1 0.0 copy-done
  22.1 0.0 copy-done.3
  22.1 2.0 %mix.1 = (f32[2,400,128]{2,1,0:T(8,128)S(1)}, f32[8,9,8,128]{3,2,1,0:T(8,128)S(1)}) custom-call(f32[8,112,128]{2,1,0:T(8,128)S(1)} %get-tuple-element.14.rows_ref, f32[504,128]{1,0:T(8,128)S(1)} %collective-permute-done.low_ref, f32[504,128]{1,0:T(8,128)S(1)} %collective-permute-done.1.high_ref, f32[760,128]{1,0:T(8,128)S(1)} %border.1.mine_ref.edge_ref, ...), custom_call_target="tpu_custom_call" | custom-call | tf_op jit(solution)/shard_map/mix/pallas_call | solution.py:690
  24.2 0.0 copy-start.4
  24.2 15.0 %all_to_all.5.mine_ref = f32[8,9,8,128]{3,2,1,0:T(8,128)S(1)} all-to-all(f32[8,9,8,128]{3,2,1,0:T(8,128)S(1)} %get-tuple-element.20), channel_id=1, replica_groups=mesh['members'=2,'loop'=8,'lat'=2] {'loop'}, dimensions={0} | all-to-all | bytes 589824 | tf_op jit(solution)/shard_map/all_to_all | solution.py:701
  39.2 0.0 collective-permute-start.3
  39.2 1.6 %collective-permute-done.3.other_ref = f32[8,9,8,128]{3,2,1,0:T(8,128)S(1)} collective-permute-done((f32[8,9,8,128]{3,2,1,0:T(8,128)S(1)}, f32[8,9,8,128]{3,2,1,0:T(8,128)S(1)}, u32[]{:S(2)}, u32[]{:S(2)}) %collective-permute-start.3) | collective-permute-done | bytes 294944 | tf_op jit(solution)/shard_map/ppermute | solution.py:702
  40.8 4.9 %solve.1 = (f32[2,400,128]{2,1,0:T(8,128)}, f32[2,8,128]{2,1,0:T(8,128)}, f32[2,8,128]{2,1,0:T(8,128)}) custom-call(f32[8,9,8,128]{3,2,1,0:T(8,128)S(1)} %all_to_all.5.mine_ref, f32[8,9,8,128]{3,2,1,0:T(8,128)S(1)} %collective-permute-done.3.other_ref, f32[2,400,128]{2,1,0:T(8,128)S(1)} %get-tuple-element.21.mixed_ref, s32[8,128]{1,0:T(8,128)S(1)} %copy-done.4, ...), custom_call_target="tpu_custom_call" | custom-call | tf_op jit(solution)/shard_map/solve/pallas_call | solution.py:703
  (1 shorter events, 0.0 us)
Async XLA Ops:
  0.6 7.6 %copy-start.1 = (f32[8,2,8,128]{3,2,1,0:T(8,128)S(1)}, f32[8,2,8,128]{3,2,1,0:T(8,128)}, u32[]{:S(2)}) copy-start(f32[8,2,8,128]{3,2,1,0:T(8,128)} %param.16) | copy-start | bytes 196612
  0.6 7.5 %copy-start.2 = (f32[8,2,8,128]{3,2,1,0:T(8,128)S(1)}, f32[8,2,8,128]{3,2,1,0:T(8,128)}, u32[]{:S(2)}) copy-start(f32[8,2,8,128]{3,2,1,0:T(8,128)} %param.17) | copy-start | bytes 196612
  2.1 14.0 %collective-permute-start = (f32[504,128]{1,0:T(8,128)S(1)}, f32[504,128]{1,0:T(8,128)S(1)}, u32[]{:S(2)}, u32[]{:S(2)}) collective-permute-start(f32[504,128]{1,0:T(8,128)S(1)} %get-tuple-element.15), channel_id=1, source_target_pairs={{0,2},{2,4},{4,6},{6,8},{8,10},{10,12},{12,14},{14,0},{1,3},{3,5},... | collective-permute-start | bytes 774152 | tf_op jit(solution)/shard_map/ppermute | solution.py:672
  5.1 13.2 %collective-permute-start.1 = (f32[504,128]{1,0:T(8,128)S(1)}, f32[504,128]{1,0:T(8,128)S(1)}, u32[]{:S(2)}, u32[]{:S(2)}) collective-permute-start(f32[504,128]{1,0:T(8,128)S(1)} %get-tuple-element.16), channel_id=1, source_target_pairs={{2,0},{4,2},{6,4},{8,6},{10,8},{12,10},{14,12},{0,14},{3,1},{5,3},... | collective-permute-start | bytes 774152 | tf_op jit(solution)/shard_map/ppermute | solution.py:673
  18.4 3.7 %copy-start = (f32[50,8,128]{2,1,0:T(8,128)S(1)}, f32[50,8,128]{2,1,0:T(8,128)}, u32[]{:S(2)}) copy-start(f32[50,8,128]{2,1,0:T(8,128)} %param.11) | copy-start | bytes 614404
  18.5 3.7 %copy-start.3 = (f32[2,50,8,128]{3,2,1,0:T(8,128)S(1)}, f32[2,50,8,128]{3,2,1,0:T(8,128)}, u32[]{:S(2)}) copy-start(f32[2,50,8,128]{3,2,1,0:T(8,128)} %param.10) | copy-start | bytes 1228804
  18.5 1.8 %collective-permute-start.2 = (f32[760,128]{1,0:T(8,128)S(1)}, f32[760,128]{1,0:T(8,128)S(1)}, u32[]{:S(2)}, u32[]{:S(2)}) collective-permute-start(f32[760,128]{1,0:T(8,128)S(1)} %border.1.mine_ref.edge_ref), channel_id=1, source_target_pairs={{0,1},{1,0},{2,3},{3,2},{4,5},{5,4},{6,7},{7,6},{8,9},{9,8},{10,11... | collective-permute-start | bytes 1167368 | tf_op jit(solution)/shard_map/ppermute | solution.py:681
  24.2 16.6 %copy-start.4 = (s32[8,128]{1,0:T(8,128)S(1)}, s32[8,128]{1,0:T(8,128)}, u32[]{:S(2)}) copy-start(s32[8,128]{1,0:T(8,128)} %depth_ref.1) | copy-start | bytes 12292
  39.2 1.6 %collective-permute-start.3 = (f32[8,9,8,128]{3,2,1,0:T(8,128)S(1)}, f32[8,9,8,128]{3,2,1,0:T(8,128)S(1)}, u32[]{:S(2)}, u32[]{:S(2)}) collective-permute-start(f32[8,9,8,128]{3,2,1,0:T(8,128)S(1)} %all_to_all.5.mine_ref), channel_id=1, source_target_pairs={{0,1},{1,0},{2,3},{3,2},{4,5},{5,4},{6,7},{7,6},{8,9},{9,8},{10,11... | collective-permute-start | bytes 884744 | tf_op jit(solution)/shard_map/ppermute | solution.py:702

commit v5 on v4

v5 whole, which is shorter than its diff:
```python
import functools

import jax
import jax.numpy as jnp
from jax import lax
from jax.experimental import pallas as pl
from jax.experimental.pallas import tpu as pltpu
from jax.sharding import PartitionSpec as P

ITERS = 3
SUB = 3
SURFACE_GAIN = 5.0
SLOT = 8
REACH = SUB + 2 * (ITERS - 1)
SHIFT = 5.0
SPAN = 5.0
FUNCTIONALS = 1 + ITERS + ITERS + ITERS * ITERS
GRID = ("loop", "lat")
VMEM = pl.BlockSpec(memory_space=pltpu.VMEM)
F32 = jnp.float32
VMEM_BYTES = 16 * 1024 * 1024


def round_up(value, to):
    return (value + to - 1) // to * to


def call(kernel, out_shapes, scratch=(), vmem=VMEM_BYTES, name=None):
    return pl.pallas_call(
        kernel,
        out_shape=[jax.ShapeDtypeStruct(shape, F32) for shape in out_shapes],
        out_specs=[VMEM] * len(out_shapes),
        scratch_shapes=list(scratch),
        compiler_params=pltpu.CompilerParams(vmem_limit_bytes=vmem),
        name=name,
    )


def iota(shape, dim):
    return lax.broadcasted_iota(jnp.int32, shape, dim)


def state_rows(levels):
    return round_up(2 * levels + 2, 8), levels + 2


def pack_kernel(levels, padded, *refs):
    sources, outs, targets, sems = refs[:6], refs[6:10], refs[10:16], refs[16]
    rows_ref, hist_ref, up_ref, down_ref = outs
    copies = [
        pltpu.make_async_copy(source, target, sems.at[at])
        for at, (source, target) in enumerate(zip(sources, targets))
    ]
    for copy in copies:
        copy.start()
    for copy in copies:
        copy.wait()
    state_ref, control_ref, depth_ref, spread_ref, step_ref, change_ref = targets
    rows, cols = depth_ref.shape
    count = step_ref.shape[0] // (2 * rows)
    pairs = 2 * count
    near, second = state_rows(levels)
    hist = SUB * near
    up_hist_ref = up_ref.at[pl.ds(hist, up_ref.shape[0] - hist)]
    down_hist_ref = down_ref.at[pl.ds(hist, down_ref.shape[0] - hist)]
    far = SUB * 2 * pairs
    depth = depth_ref[...].astype(F32)
    spread = spread_ref[...]
    wet = depth > 0.5
    for row in range(rows):
        here = slice(row, row + 1)
        distant = []
        targets = [(hist_ref.at[row], 0)]
        if row < SUB:
            targets.append((down_hist_ref, row * 2 * pairs))
        elif row < REACH:
            distant.append((down_hist_ref, far + (row - SUB) * pairs))
        if row >= rows - SUB:
            targets.append((up_hist_ref, (row - rows + SUB) * 2 * pairs))
        elif row >= rows - REACH:
            distant.append((up_hist_ref, far + (row - rows + REACH) * pairs))
        for which, ref in enumerate((step_ref, change_ref)):
            both = [ref[pl.ds(tracer * rows + row, count, stride=2 * rows), :] for tracer in range(2)]
            apart = jnp.where(wet[here], both[0] - both[1], 0.0)
            joint = jnp.where(wet[here], both[0] + both[1], 0.0)
            for target, at in targets:
                target[pl.ds(at + which * count, count), :] = apart
                target[pl.ds(at + pairs + which * count, count), :] = joint
            for target, at in distant:
                target[pl.ds(at + which * count, count), :] = apart
    first = iota((levels, cols), 0) == 0
    rest = jnp.zeros((padded - levels, cols), F32)
    fill = jnp.zeros((near - 2 * levels - 2, cols), F32)
    for row in range(rows):
        here = slice(row, row + 1)
        targets = [(rows_ref.at[row], 0, padded)]
        if row < SUB:
            targets.append((down_ref, row * near, second))
        if row >= rows - SUB:
            targets.append((up_ref, (row - rows + SUB) * near, second))
        for tracer in range(2):
            lift = jnp.where(wet[here], control_ref[tracer, here, :], 0.0)
            value = state_ref[tracer, pl.ds(row, levels, stride=rows), :]
            value = value + jnp.where(first, lift, 0.0)
            for target, at, offset in targets:
                target[pl.ds(at + tracer * offset, levels), :] = value
            rows_ref[row, pl.ds(tracer * padded + levels, padded - levels), :] = rest
        for target, at, _ in targets:
            target[pl.ds(at + levels, 1), :] = spread[here]
            target[pl.ds(at + levels + 1, 1), :] = depth[here]
        for target, at, _ in targets[1:]:
            target[pl.ds(at + 2 * levels + 2, near - 2 * levels - 2), :] = fill


def edge_of(rows_of, indices, cols, lat):
    lane = iota((1, cols), 1)
    slot = lane // SLOT
    place = lane % SLOT - SUB * lat
    mine = (place >= 0) & (place < SUB)
    total = None
    for index in indices:
        moved = pltpu.roll(rows_of(index), SLOT * index + SUB, 1)
        piece = jnp.where(mine & (slot == index), moved, 0.0)
        total = piece if total is None else total + piece
    return total


def pairs_kernel(
    rows_ref, step_ref, change_ref, depth_ref, spread_ref, damping_ref, weight_ref,
    edge_ref, still_ref, gram_ref,
):
    rows, _, cols = rows_ref.shape
    lat = lax.axis_index("lat")
    count = step_ref.shape[0]
    lane = iota((1, cols), 1)
    gram = [jnp.zeros((1, cols), F32) for _ in range(count)]
    at = 0
    for left_ref in (step_ref, change_ref):
        for i in range(count):
            for j in range(i, count):
                value = jnp.sum(left_ref[i] * change_ref[j], axis=(0, 1), keepdims=True)
                gram[i] = gram[i] + jnp.where(lane == at + j, value, 0.0)
                if i != j:
                    gram[j] = gram[j] + jnp.where(lane == at + i, value, 0.0)
        at += count
    for i in range(count):
        gram_ref[pl.ds(i, 1), :] = gram[i]
    depth = depth_ref[...]
    total = jnp.zeros((rows, cols), F32)
    for level in range(weight_ref.shape[0] // rows):
        total = total + jnp.where(level < depth, weight_ref[pl.ds(level * rows, rows), :], 0.0)
    fields = (
        jnp.where(depth > 0, spread_ref[...], 0.0),
        damping_ref[...],
        2.0 * total,
        weight_ref[pl.ds(0, rows), :],
        gram_ref[...],
    )
    for copy in range(still_ref.shape[0]):
        for at, field in enumerate(fields):
            still_ref[copy, at] = field
    edge_ref[...] = edge_of(lambda i: rows_ref[i - SUB], range(SUB, rows + SUB), cols, lat)


def faces_between(here, there, opened=True):
    return jnp.where((here > 0.0) & (there > 0.0) & opened, 0.5 * (here + there), 0.0)


def closed_lane(cols):
    return jnp.where(lax.axis_index("lat") == 0, 2 * cols - 1, cols - 1)


def surface_faces(spread, closed):
    height, width = spread.shape
    below = faces_between(spread, pltpu.roll(spread, height - 1, 0))
    right = faces_between(
        spread, pltpu.roll(spread, width - 1, 1), iota(spread.shape, 1) != closed
    )
    return below, pltpu.roll(below, 1, 0), right, pltpu.roll(right, 1, 1)


def gathered(mine_ref, other_ref, field):
    return jnp.concatenate(
        [
            jnp.concatenate([mine_ref[i, field], other_ref[i, field]], axis=1)
            for i in range(mine_ref.shape[0])
        ],
        axis=0,
    )


def gathered_near(mine_ref, other_ref, field):
    loops = mine_ref.shape[0]
    parts = []
    for shift in (loops - 1, 0, 1):
        at = lax.rem(lax.axis_index("loop") + shift, loops)
        parts.append(jnp.concatenate([mine_ref[at, field], other_ref[at, field]], axis=1))
    return jnp.concatenate(parts, axis=0)


def plan_kernel(mine_ref, other_ref, faces_ref, near_ref, plan_ref):
    loops, _, rows, cols = mine_ref.shape
    closed = closed_lane(cols)
    for at, face in enumerate(surface_faces(gathered(mine_ref, other_ref, 0), closed)):
        faces_ref[at] = SURFACE_GAIN * face
    for field in (1, 2):
        faces_ref[3 + field] = gathered(mine_ref, other_ref, field)
    spread = gathered_near(mine_ref, other_ref, 0)
    for at, face in enumerate(surface_faces(spread, closed)):
        near_ref[at] = face
    near_ref[4] = jnp.where(spread > 0.0, gathered_near(mine_ref, other_ref, 3), 0.0)
    near_ref[5] = jnp.where(spread > 0.0, 1.0, 0.0)

    count = plan_ref.shape[0] // 2
    gram = mine_ref[0, 4] + other_ref[0, 4]
    for i in range(1, loops):
        gram = gram + (mine_ref[i, 4] + other_ref[i, 4])
    wide = (count, cols)
    step_change = [jnp.broadcast_to(gram[:, i : i + 1], wide) for i in range(count)]
    change_change = [
        jnp.broadcast_to(gram[:, count + i : count + i + 1], wide) for i in range(count)
    ]
    last = count - 1
    gamma = step_change[last][last:] / change_change[last][last:]
    rho = [1.0 / step_change[i][i : i + 1] for i in range(count)]
    row = iota(wide, 0)
    lane = iota(wide, 1)
    step_grad = jnp.where(lane == row, 1.0, 0.0)
    change_grad = jnp.where(lane == row + count, 1.0, 0.0)
    factors = [None] * count
    for i in range(count - 1, -1, -1):
        factors[i] = rho[i] * step_grad[i : i + 1]
        step_grad = step_grad - factors[i] * step_change[i]
        change_grad = change_grad - factors[i] * change_change[i]
    change_grad = gamma * change_grad
    for i in range(count):
        weight = factors[i] - rho[i] * change_grad[i : i + 1]
        change_grad = change_grad + weight * step_change[i]
        plan_ref[pl.ds(i, 1), :] = -weight
        plan_ref[pl.ds(count + i, 1), :] = gamma * factors[i]
    at = lane[:1] == 2 * count
    plan_ref[pl.ds(0, 1), :] = jnp.where(at, -gamma, plan_ref[pl.ds(0, 1), :])


def halo_kernel(levels, padded, rows, edge_ref, low_ref, high_ref, out_ref, halo_ref):
    planes, cols = out_ref.shape
    lat = lax.axis_index("lat")
    near, second = state_rows(levels)
    rest = jnp.zeros((padded - levels, cols), F32)
    for i in range(2 * SUB):
        ref = low_ref if i < SUB else high_ref
        at = i % SUB * near
        halo_ref[i, pl.ds(levels, padded - levels), :] = rest
        halo_ref[i, pl.ds(padded + levels, padded - levels), :] = rest
        halo_ref[i, pl.ds(0, levels + 2), :] = ref[pl.ds(at, levels + 2), :]
        halo_ref[i, pl.ds(padded, levels), :] = ref[pl.ds(at + second, levels), :]
    total = edge_ref[...] + edge_of(lambda i: halo_ref[i], range(SUB), cols, lat)
    out_ref[...] = total + edge_of(
        lambda i: halo_ref[i - rows], range(rows + SUB, rows + 2 * SUB), cols, lat
    )


def border_kernel(start, low_ref, high_ref, hist_ref, out_ref):
    low_ref = low_ref.at[pl.ds(start, low_ref.shape[0] - start)]
    high_ref = high_ref.at[pl.ds(start, high_ref.shape[0] - start)]
    rows = hist_ref.shape[0]
    pairs = hist_ref.shape[1] // 2
    far = SUB * 2 * pairs
    ahead = REACH - SUB
    joint = (rows + 2 * REACH) * pairs
    for i in range(rows + 2 * REACH):
        at = i - REACH
        target = pl.ds(i * pairs, pairs)
        if at < -SUB:
            out_ref[target, :] = low_ref[pl.ds(far + i * pairs, pairs), :]
            continue
        if at >= rows + SUB:
            out_ref[target, :] = high_ref[pl.ds(far + (at - rows - SUB) * pairs, pairs), :]
            continue
        if at < 0:
            ref, start = low_ref, (at + SUB) * 2 * pairs
        elif at < rows:
            ref, start = hist_ref.at[at], 0
        else:
            ref, start = high_ref, (at - rows) * 2 * pairs
        out_ref[target, :] = ref[pl.ds(start, pairs), :]
        out_ref[pl.ds(joint + (i - ahead) * pairs, pairs), :] = ref[pl.ds(start + pairs, pairs), :]


def basis_kernel(rows, pairs, mine_ref, other_ref, still_ref, still_other_ref, out_ref, *work):
    cols = mine_ref.shape[1]
    width = 2 * cols
    loops = still_ref.shape[0]
    tall = rows + 2 * REACH
    ahead = REACH - SUB
    joint = tall * pairs
    opened = iota((1, width), 1) != closed_lane(cols)

    def wide(at, size):
        return jnp.concatenate([mine_ref[pl.ds(at, size), :], other_ref[pl.ds(at, size), :]], axis=1)

    near = [lax.rem(lax.axis_index("loop") + shift, loops) for shift in (loops - 1, 0, 1)]

    def still(field, i):
        block, row = divmod(i - REACH + rows, rows)
        return jnp.concatenate(
            [
                ref[near[block], field, pl.ds(row, 1), :]
                for ref in (still_ref, still_other_ref)
            ],
            axis=1,
        )

    def left(value):
        return pltpu.roll(value, width - 1, 1)

    def right(value):
        return pltpu.roll(value, 1, 1)

    spread = [still(0, i) for i in range(tall)]
    to_right = [faces_between(value, left(value), opened) for value in spread]
    to_left = [right(value) for value in to_right]
    to_below = [faces_between(spread[i], spread[i + 1]) for i in range(tall - 1)]
    inner = range(ahead, tall - ahead)
    damping = {i: (still(1, i) - SHIFT) * (1.0 / SPAN) for i in inner}
    response_weight = {i: still(2, i) for i in inner}
    weight = {i: still(3, i) for i in inner}
    gain = SURFACE_GAIN / SPAN

    def outflow(get, i):
        value = get(i)
        total = to_right[i] * (value - left(value)) + to_left[i] * (value - right(value))
        total = total + to_below[i] * (value - get(i + 1))
        return value, total + to_below[i - 1] * (value - get(i - 1))

    def mixed(get, ref, reach):
        for i in range(REACH - reach, REACH + rows + reach):
            value, out = outflow(get, i)
            ref[i] = value - out
        return lambda i: ref[i]

    def applied(get, ref, reach):
        for i in range(REACH - reach, REACH + rows + reach):
            value, out = outflow(get, i)
            ref[i] = damping[i] * value + gain * out
        return lambda i: ref[i]

    def keep(slot, get):
        for i in range(rows):
            out_ref[slot, i] = get(i + REACH)[:, :cols]

    def start_apart(i):
        return wide(i * pairs, pairs)

    def start_joint(i):
        return wide(joint + (i - ahead) * pairs, pairs)

    both = (start_apart, start_joint)
    for sweep in range(SUB):
        both = (
            mixed(both[0], work[sweep], REACH - 1 - sweep),
            mixed(both[1], work[SUB + sweep], SUB - 1 - sweep),
        )
    keep(0, both[1])
    reach = REACH - SUB
    powers = [both[0]]
    for power in range(1, ITERS):
        powers.append(applied(powers[-1], work[2 * SUB + power - 1], reach - power))
    for power in range(ITERS):
        keep(1 + power, powers[power])
    reach = ITERS - 1
    slot = 1 + ITERS
    at = 2 * SUB + ITERS - 1
    chains = []
    for factor, power in [(weight, 0)] + [(response_weight, power) for power in range(ITERS)]:
        get = powers[power]
        chains.append(lambda i, factor=factor, get=get: factor[i] * get(i))
    for power in range(1, ITERS):
        for index in range(len(chains)):
            chains[index] = applied(chains[index], work[at], reach - power)
            at += 1
            keep(slot + index * (ITERS - 1) + power - 1, chains[index])


def mix_kernel(
    levels, padded, scale, copies,
    rows_ref, halo_ref, edge_ref, other_ref, weight_ref, observed_ref, basis_ref, still_ref,
    mixed_ref, fields_ref, face_ref, here_ref, there_ref, part_ref,
):
    rows, planes, cols = rows_ref.shape
    pairs = basis_ref.shape[2]
    lat = lax.axis_index("lat")
    lane = iota((1, cols), 1)
    place = lane % SLOT
    count = rows + 2 * SUB
    level = iota((padded, cols), 0).astype(F32)

    def left(value, by=1):
        return pltpu.roll(value, (cols - by) % cols, 1)

    def right(value, by=1):
        return pltpu.roll(value, by, 1)

    def source(i):
        if i < SUB:
            return halo_ref.at[i]
        if i < SUB + rows:
            return rows_ref.at[i - SUB]
        return halo_ref.at[i - rows]

    def face(depth_here, depth_there, spread_here, spread_there):
        opened = level < jnp.minimum(depth_here, depth_there)
        return jnp.where(opened, 0.5 * (spread_here + spread_there), 0.0)

    spread = edge_ref[pl.ds(levels, 1), :] + other_ref[pl.ds(levels, 1), :]
    depth = edge_ref[pl.ds(levels + 1, 1), :] + other_ref[pl.ds(levels + 1, 1), :]
    within = place < 2 * SUB - 1
    col_depth = jnp.minimum(depth, jnp.where(within, left(depth), 0.0))
    col_spread = 0.5 * (spread + left(spread))
    row_depth = jnp.minimum(depth, left(depth, SLOT))
    row_spread = 0.5 * (spread + left(spread, SLOT))

    def strip_face(limit, value):
        return jnp.where(level < limit, value, 0.0)

    to_left = strip_face(right(col_depth), right(col_spread))
    to_right = strip_face(col_depth, col_spread)
    to_above = strip_face(right(row_depth, SLOT), right(row_spread, SLOT))
    to_below = strip_face(row_depth, row_spread)
    out_of_low = place == jnp.where(lat == 0, SUB - 1, SLOT)
    out_of_high = place == jnp.where(lat == 0, SLOT, SUB)
    over_low = jnp.where(out_of_low, to_right, 0.0)
    over_high = jnp.where(out_of_high, to_left, 0.0)
    own_right = jnp.where(place == SUB - 1, 0.0, to_right)
    own_left = jnp.where(place == SUB, 0.0, to_left)
    start = jnp.where(lat == 0, cols - SUB, 0)
    at_border = (lane >= start) & (lane < start + SUB)

    def spread_out(value, east, west):
        before, after = right(value), left(value)
        above, below = right(value, SLOT), left(value, SLOT)
        total = value + east * (after - value) + west * (before - value)
        return total + to_below * (below - value) + to_above * (above - value)

    parts = []
    extras = [None, None]
    for tracer in range(2):
        at = pl.ds(tracer * padded, padded)
        parts.append(edge_ref[at, :] + other_ref[at, :])

    spreads = [source(i)[pl.ds(levels, 1), :] for i in range(count)]
    depths = [source(i)[pl.ds(levels + 1, 1), :] for i in range(count)]
    for i in range(count - 1):
        face_ref[0, i] = face(depths[i], depths[i + 1], spreads[i], spreads[i + 1])
    for i in range(1, count - 1):
        there = jnp.where(lane < cols - 1, left(depths[i]), 0.0)
        face_ref[1, i] = face(depths[i], there, spreads[i], left(spreads[i]))
        there = jnp.where(lane > 0, right(depths[i]), 0.0)
        face_ref[2, i] = face(depths[i], there, spreads[i], right(spreads[i]))

    for sweep in range(1, SUB + 1):
        for tracer in range(2):
            part = parts[tracer]
            across = over_low * (left(part) - part) + over_high * (right(part) - part)
            extra = extras[tracer]
            if extra is not None:
                across = across + spread_out(extra, own_right, own_left)
            extras[tracer] = across
            if sweep < SUB:
                parts[tracer] = spread_out(part, to_right, to_left)
        target = here_ref if sweep % 2 else there_ref
        for i in range(sweep, count - sweep):
            def field(at):
                if sweep == 1:
                    return source(at)
                return (there_ref if sweep % 2 else here_ref).at[at]

            for tracer in range(2):
                at = pl.ds(tracer * padded, padded)
                centre = field(i)[at, :]
                total = centre + face_ref[0, i] * (field(i + 1)[at, :] - centre)
                total = total + face_ref[0, i - 1] * (field(i - 1)[at, :] - centre)
                total = total + face_ref[1, i] * (left(centre) - centre)
                total = total + face_ref[2, i] * (right(centre) - centre)
                target[i, at, :] = total

    target = here_ref if SUB % 2 else there_ref
    for row in range(rows):
        i = row + SUB
        at = pl.ds(row, levels, stride=rows)
        mixed = []
        for tracer in range(2):
            border = jnp.where(at_border, left(extras[tracer], SLOT * i + SUB), 0.0)
            mixed.append((target[i, pl.ds(tracer * padded, padded), :] + border)[:levels])
        wet = level[:levels] < depths[i]
        weight = weight_ref[at, :]
        misfit = []
        for tracer in range(2):
            mixed_ref[tracer, at, :] = mixed[tracer]
            misfit.append(weight * (mixed[tracer] - observed_ref[tracer, at, :]))
        here = pl.ds(row, 1)
        part_ref[0, here, :] = scale * jnp.sum(
            jnp.where(wet, mixed[0] - mixed[1], 0.0), axis=0, keepdims=True
        )
        part_ref[1, here, :] = jnp.sum(
            jnp.where(wet, misfit[1] - misfit[0], 0.0), axis=0, keepdims=True
        )
        part_ref[2, here, :] = misfit[0][0:1]
        part_ref[3, here, :] = misfit[1][0:1]
    sums = [None] * FUNCTIONALS

    def add(at, slot, row, factor):
        value = basis_ref[slot, row] * factor
        sums[at] = value if sums[at] is None else sums[at] + value

    chain = 1 + ITERS
    for row in range(rows):
        here = pl.ds(row, 1)
        get = lambda field: part_ref[field, here, :]
        still = lambda field: still_ref[0, field, here, :]
        surface, base = get(0), get(1)
        add(0, 0, row, 0.5 * (get(2) + get(3)))
        add(0, 1, row, 0.5 * (get(2) - get(3)))
        add(1, 1, row, still(3) * surface)
        for power in range(1, ITERS):
            add(1 + power, chain + power - 1, row, surface)
        for j in range(ITERS):
            add(1 + ITERS + j, 1 + j, row, base)
            at = 1 + 2 * ITERS + j * ITERS
            add(at, 1 + j, row, still(2) * surface)
            for power in range(1, ITERS):
                add(at + power, chain + (1 + j) * (ITERS - 1) + power - 1, row, surface)
    half = pairs // 2
    total = jnp.zeros((half, cols), F32)
    for at in range(FUNCTIONALS):
        value = jnp.sum(sums[at], axis=1, keepdims=True)
        total = total + jnp.where(lane == at, value[:half], 0.0)
        total = total + jnp.where(lane == cols // 2 + at, value[half:], 0.0)
    part_ref[4] = total
    for copy in range(copies):
        fields_ref[copy] = part_ref[...]


def solve_kernel(
    levels, scale,
    mine_ref, other_ref, faces_ref, near_ref, plan_ref, mixed_ref, depth_ref, step_ref, change_ref,
    state_ref, gradient_ref, direction_ref, kept_ref,
):
    loops, _, rows, cols = mine_ref.shape
    loop = lax.axis_index("loop")

    def total(value):
        return jnp.sum(value, axis=(0, 1), keepdims=True)

    def outflow(value, to_below, to_above, to_right, to_left):
        height, width = value.shape
        result = to_right * (value - pltpu.roll(value, width - 1, 1))
        result = result + to_left * (value - pltpu.roll(value, 1, 1))
        result = result + to_below * (value - pltpu.roll(value, height - 1, 0))
        return result + to_above * (value - pltpu.roll(value, 1, 0))

    count = step_ref.shape[0]
    inner = mine_ref[0, 4] + other_ref[0, 4]
    for i in range(1, loops):
        inner = inner + (mine_ref[i, 4] + other_ref[i, 4])
    plan = plan_ref[...]
    shifted = pltpu.roll(inner, cols // 2, 1)
    linear = None
    for i in range(2 * count):
        source = inner if i < count else shifted
        part = plan[:, i : i + 1] * source[i % count : i % count + 1]
        linear = part if linear is None else linear + part
    gamma = plan[:1, 2 * count : 2 * count + 1]

    gained = [faces_ref[i] for i in range(4)]
    damping = faces_ref[4]

    def conjugate(rhs):
        residual = rhs
        search = rhs
        solution = jnp.zeros_like(rhs)
        norm_now = total(rhs * rhs)
        one = jnp.ones((1, 1), F32)
        residual_of = [one]
        search_of = [one]
        solution_of = []
        for sweep in range(ITERS):
            image = damping * search + outflow(search, *gained)
            alpha = norm_now / total(search * image)
            solution = solution + alpha * search
            solution_of = add_up(solution_of, alpha, search_of)
            if sweep < ITERS - 1:
                residual = residual - alpha * image
                norm_next = total(residual * residual)
                beta = norm_next / norm_now
                search = residual + beta * search
                norm_now = norm_next
                image_of = [SHIFT * value for value in search_of]
                image_of = add_up(image_of, SPAN, [None] + search_of)
                residual_of = add_up(residual_of, -alpha, image_of)
                search_of = add_up(residual_of, beta, search_of)
        return solution, solution_of

    def add_up(terms, factor, others):
        result = list(terms) + [None] * (len(others) - len(terms))
        for at, value in enumerate(others):
            if value is not None:
                value = factor * value
                result[at] = value if result[at] is None else result[at] + value
        return result

    def keep(slot, value):
        for i in range(loops):
            kept_ref[slot, i] = value[i * rows : (i + 1) * rows]

    def kept_around(slot):
        return jnp.concatenate(
            [kept_ref[slot, lax.rem(loop + shift, loops)] for shift in (loops - 1, 0, 1)], axis=0
        )

    elevation, elevation_of = conjugate(gathered(mine_ref, other_ref, 0))
    keep(0, elevation)
    pressure = gathered(mine_ref, other_ref, 1) + faces_ref[5] * elevation
    response, response_of = conjugate(pressure)
    keep(1, response)

    lane = iota((1, cols), 1)
    factor = jnp.where(lane == 0, 1.0, 0.0)
    for j in range(ITERS):
        factor = jnp.where(lane == 1 + j, -elevation_of[j], factor)
        part = scale * response_of[j]
        factor = jnp.where(lane == 1 + ITERS + j, part, factor)
        for k in range(ITERS):
            at = 1 + 2 * ITERS + j * ITERS + k
            factor = jnp.where(lane == at, part * elevation_of[k], factor)
    weights = jnp.sum(linear * factor, axis=1, keepdims=True)
    weights = [
        jnp.broadcast_to(weights[i : i + 1], (rows, cols)) for i in range(2 * count)
    ]

    elevation = kept_around(0)
    lowered = near_ref[4] * elevation
    sea = near_ref[5]
    raised = (scale * sea) * kept_around(1)
    near = [near_ref[i] for i in range(4)]
    carried = [
        gathered_near(mine_ref, other_ref, 2) - lowered + raised,
        gathered_near(mine_ref, other_ref, 3) + lowered - raised,
    ]
    for sweep in range(SUB):
        carried = [value - outflow(value, *near) for value in carried]
    for tracer in range(2):
        at = pl.ds(tracer * rows, rows)
        gradient = jnp.where(sea > 0.0, carried[tracer], 0.0)[rows : 2 * rows, :cols]
        gradient_ref[tracer] = gradient
        value = gamma * gradient
        for i in range(count):
            value = value + weights[i] * step_ref[i, at, :]
            value = value + weights[count + i] * change_ref[i, at, :]
        direction_ref[tracer] = value

    depth = depth_ref[...]
    here = elevation[rows : 2 * rows, :cols]
    for level in range(levels):
        at = pl.ds(level * rows, rows)
        change = jnp.where(level < depth, here, 0.0)
        state_ref[0, at, :] = mixed_ref[0, at, :] - change
        state_ref[1, at, :] = mixed_ref[1, at, :] + change


def on_device(
    state, observed, weight, control, depth_index, diffusivity, damping, history_step, history_change
):
    _, levels, rows, cols = state.shape
    count = history_step.shape[0]
    padded = round_up(levels + 2, 8)
    planes = 2 * padded
    loops = lax.axis_size("loop")
    lats = lax.axis_size("lat")
    blocks = loops * lats
    scale = levels ** (-0.5)
    flat = (2, levels * rows, cols)
    state = state.reshape(flat)
    observed = observed.reshape(flat)
    weight = weight.reshape(flat[1:])
    step = history_step.reshape(count, 2 * rows, cols)
    change = history_change.reshape(count, 2 * rows, cols)

    pairs = 2 * count
    inputs = (
        state, control, depth_index, diffusivity,
        history_step.reshape(-1, cols), history_change.reshape(-1, cols),
    )
    states = SUB * state_rows(levels)[0]
    sent = (states + (SUB + REACH) * pairs, cols)
    shapes = ((rows, planes, cols), (rows, 2 * pairs, cols), sent, sent)
    packed, hist, up, down = pl.pallas_call(
        functools.partial(pack_kernel, levels, padded),
        out_shape=[jax.ShapeDtypeStruct(shape, F32) for shape in shapes],
        in_specs=[pl.BlockSpec(memory_space=pltpu.HBM)] * len(inputs),
        out_specs=[VMEM] * len(shapes),
        scratch_shapes=[pltpu.VMEM(x.shape, x.dtype) for x in inputs]
        + [pltpu.SemaphoreType.DMA((len(inputs),))],
        compiler_params=pltpu.CompilerParams(vmem_limit_bytes=VMEM_BYTES),
        name="pack",
    )(*(pltpu.with_memory_space_constraint(x, pltpu.HBM) for x in inputs))
    forward = [(i, (i + 1) % loops) for i in range(loops)]
    backward = [(target, source) for source, target in forward]
    swap = [(0, 1), (1, 0)]
    low = lax.ppermute(up, "loop", forward)
    high = lax.ppermute(down, "loop", backward)
    edge, still, _ = call(
        pairs_kernel, [(planes, cols), (loops, 5, rows, cols), (count, cols)], name="pairs"
    )(packed, step, change, depth_index, diffusivity, damping, weight)
    still_own = still
    still = lax.all_to_all(still, "loop", 0, 0)
    still_other = lax.ppermute(still, "lat", swap)
    height = loops * rows
    large = VMEM_BYTES if loops <= 16 else 2 * VMEM_BYTES
    faces, near, plan = call(
        plan_kernel,
        [(6, height, 2 * cols), (6, 3 * rows, 2 * cols), (pairs, cols)],
        vmem=large,
        name="plan",
    )(still, still_other)
    (border,) = call(
        functools.partial(border_kernel, states),
        [((rows + 2 * REACH + rows + 2 * SUB) * pairs, cols)],
        name="border",
    )(low, high, hist)
    border_other = lax.ppermute(border, "lat", swap)
    chains = 1 + ITERS
    buffers = 2 * SUB + ITERS - 1 + chains * (ITERS - 1)
    (basis,) = call(
        functools.partial(basis_kernel, rows, pairs),
        [(1 + ITERS + chains * (ITERS - 1), rows, pairs, cols)],
        scratch=[pltpu.VMEM((rows + 2 * REACH, pairs, 2 * cols), F32)] * buffers,
        name="basis",
    )(border, border_other, still, still_other)
    edge, halo = call(
        functools.partial(halo_kernel, levels, padded, rows),
        [(planes, cols), (2 * SUB, planes, cols)],
        name="halo",
    )(edge, low, high)
    other = lax.ppermute(edge, "lat", swap)
    mixed, fields = call(
        functools.partial(mix_kernel, levels, padded, scale, loops),
        [flat, (loops, 5, rows, cols)],
        scratch=[
            pltpu.VMEM((3, rows + 2 * SUB, padded, cols), F32),
            pltpu.VMEM((rows + 2 * SUB, planes, cols), F32),
            pltpu.VMEM((rows + 2 * SUB, planes, cols), F32),
            pltpu.VMEM((5, rows, cols), F32),
        ],
        name="mix",
    )(packed, halo, edge, other, weight, observed, basis, still_own)
    mine = lax.all_to_all(fields, "loop", 0, 0)
    theirs = lax.ppermute(mine, "lat", swap)
    state_next, gradient, direction = call(
        functools.partial(solve_kernel, levels, scale),
        [flat, (2, rows, cols), (2, rows, cols)],
        scratch=[pltpu.VMEM((2, loops, rows, 2 * cols), F32)],
        vmem=large,
        name="solve",
    )(mine, theirs, faces, near, plan, mixed, depth_index, step, change)
    return (state_next.reshape(2, levels, rows, cols), gradient, direction)


def solution(mesh):
    return jax.shard_map(
        on_device,
        mesh=mesh,
        in_specs=(
            P("members", None, "loop", "lat"),
            P("members", None, "loop", "lat"),
            P(None, "loop", "lat"),
            P("members", "loop", "lat"),
            P("loop", "lat"),
            P("loop", "lat"),
            P("loop", "lat"),
            P("members", None, "loop", "lat"),
            P("members", None, "loop", "lat"),
        ),
        out_specs=(
            P("members", None, "loop", "lat"),
            P("members", "loop", "lat"),
            P("members", "loop", "lat"),
        ),
        check_vma=False,
    )
```

time: 45.9 us -> 42.4 us (0.924)
  starting transfers between devices: 6.17 us -> 10.1 us
  waiting for transfers between devices: 13 us -> 9.19 us
  blocking collectives: 15 us -> 11.7 us
  Pallas kernels: 10.7 us -> 10.2 us
    ppermute x1, waiting for transfers between devices: 7.54 us -> 3.93 us  [on_device(): low = lax.ppermute(up, 'loop', forward)]
    all_to_all x0 -> x1, starting transfers between devices: none -> 3.38 us  [on_device(): still = lax.all_to_all(still, 'loop', 0, 0)]
    all_to_all x1, blocking collectives: 15 us -> 11.7 us  [on_device(): mine = lax.all_to_all(fields, 'loop', 0, 0)]
    pallas_call x1, Pallas kernels: 4.89 us -> 2.92 us  [on_device(): call(functools.partial(solve_kernel, levels, scale), [flat, (2, rows, col...]
    ppermute x1, waiting for transfers between devices: 1.7 us -> 0.01 us  [on_device(): other = lax.ppermute(edge, 'lat', swap)]
    all_to_all x0 -> x1, waiting for transfers between devices: none -> 1.08 us  [on_device(): still = lax.all_to_all(still, 'loop', 0, 0)]
    pallas_call x3 -> x5, Pallas kernels: 2.37 us -> 3.18 us  [the longest x1 1.81 us: on_device(): call(functools.partial(basis_kernel, rows, pairs), [(1 + ITERS + chains *...]
    pallas_call x1, Pallas kernels: 2.02 us -> 2.82 us  [on_device(): call(functools.partial(mix_kernel, levels, padded, scale, loops), [flat,...]
  transfers between devices with their start and end apart: 4 -> 7, of which waited for: 4 -> 5; matrix products, arithmetic and copies ran while one was open for 0% -> 0% of each run, Pallas kernels for 1% -> 8%
where the time goes in v5:
time: 42.4 us; the launch traced here: 42.1 us
  blocking collectives  11.7 us (28%)
  Pallas kernels  10.2 us (24%)
  starting transfers between devices  10.1 us (24%)
  waiting for transfers between devices  9.19 us (22%)
  between operations  0.77 us (2%)
    all_to_all x1, blocking collectives, on_device(): mine = lax.all_to_all(fields, 'loop', 0, 0)  11.7 us
    ppermute x1, waiting for transfers between devices, on_device(): low = lax.ppermute(up, 'loop', forward)  3.93 us
    all_to_all x1, starting transfers between devices, on_device(): still = lax.all_to_all(still, 'loop', 0, 0)  3.38 us
    ppermute x1, starting transfers between devices, on_device(): high = lax.ppermute(down, 'loop', backward)  3.12 us
    ppermute x1, starting transfers between devices, on_device(): low = lax.ppermute(up, 'loop', forward)  2.99 us
    pallas_call x1, Pallas kernels, on_device(): call(functools.partial(solve_kernel, levels, scale), [flat, (2, rows, col...  2.92 us
    pallas_call x1, Pallas kernels, on_device(): call(functools.partial(mix_kernel, levels, padded, scale, loops), [flat,...  2.82 us
    ppermute x1, waiting for transfers between devices, on_device(): high = lax.ppermute(down, 'loop', backward)  2.39 us
  transfers between devices with their start and end apart: 7, of which 5 were waited for; matrix products, arithmetic and copies ran while one was open for 0% of the time, Pallas kernels for 8%

profile of v5, /device:TPU:0, one launch (start us, length us, event | category | flops | bytes accessed | tf_op | source)
XLA Modules:
  0.0 42.1 jit_solution(1148892613994447189)
XLA Ops:
  0.6 0.0 copy-start
  0.7 1.3 %pack.1 = (f32[8,112,128]{2,1,0:T(8,128)S(1)}, f32[8,32,128]{2,1,0:T(8,128)S(1)}, f32[472,128]{1,0:T(8,128)S(1)}, f32[472,128]{1,0:T(8,128)S(1)}) custom-call(f32[2,400,128]{2,1,0:T(8,128)} %bitcast.17, f32[2,8,128]{2,1,0:T(8,128)} %refs_1_.1, s32[8,128]{1,0:T(8,128)} %depth_ref.3, f32[8,128]{1,0:T(8,128)} %spread_ref.1, f32[128,128]{1,0:T(8,128)} %bitcast.10, ...), custom_call_target="tpu_custom_call" | custom-call | tf_op jit(solution)/shard_map/pack/pallas_call | solution.py:697
  2.0 3.0 %collective-permute-start = (f32[472,128]{1,0:T(8,128)S(1)}, f32[472,128]{1,0:T(8,128)S(1)}, u32[]{:S(2)}, u32[]{:S(2)}) collective-permute-start(f32[472,128]{1,0:T(8,128)S(1)} %get-tuple-element.21), channel_id=1, source_target_pairs={{0,2},{2,4},{4,6},{6,8},{8,10},{10,12},{12,14},{14,0},{1,3},{3,5},... | collective-permute-start | bytes 725000 | tf_op jit(solution)/shard_map/ppermute | solution.py:710
  5.0 3.1 %collective-permute-start.1 = (f32[472,128]{1,0:T(8,128)S(1)}, f32[472,128]{1,0:T(8,128)S(1)}, u32[]{:S(2)}, u32[]{:S(2)}) collective-permute-start(f32[472,128]{1,0:T(8,128)S(1)} %get-tuple-element.22), channel_id=1, source_target_pairs={{2,0},{4,2},{6,4},{8,6},{10,8},{12,10},{14,12},{0,14},{3,1},{5,3},... | collective-permute-start | bytes 725000 | tf_op jit(solution)/shard_map/ppermute | solution.py:711
  8.1 1.0 %pairs.1 = (f32[112,128]{1,0:T(8,128)S(1)}, f32[8,5,8,128]{3,2,1,0:T(8,128)}, f32[8,128]{1,0:T(8,128)}) custom-call(f32[8,112,128]{2,1,0:T(8,128)S(1)} %get-tuple-element.19.rows_ref, f32[8,16,128]{2,1,0:T(8,128)S(1)} %bitcast.11, f32[8,16,128]{2,1,0:T(8,128)S(1)} %bitcast.14, s32[8,128]{1,0:T(8,128)S(1)} %copy-done.4, f32[8,128]{1,0:T(8,128)S(1)} %copy-done.5, ...), custom_call_target="tpu_custom_call" | custom-call | tf_op jit(solution)/shard_map/pairs/pallas_call | solution.py:712
  9.1 3.4 %all-to-all-start = ((f32[8,5,8,128]{3,2,1,0:T(8,128)}), f32[8,5,8,128]{3,2,1,0:T(8,128)S(1)}, u32[]{:S(2)}, u32[]{:S(2)}) async-start(f32[8,5,8,128]{3,2,1,0:T(8,128)} %get-tuple-element.26.still_ref), calls=%async_computation | async-start | bytes 327680 | tf_op jit(solution)/shard_map/all_to_all | solution.py:716
  12.5 3.9 %collective-permute-done.low_ref = f32[472,128]{1,0:T(8,128)S(1)} collective-permute-done((f32[472,128]{1,0:T(8,128)S(1)}, f32[472,128]{1,0:T(8,128)S(1)}, u32[]{:S(2)}, u32[]{:S(2)}) %collective-permute-start) | collective-permute-done | bytes 241696 | tf_op jit(solution)/shard_map/ppermute | solution.py:710
  16.4 2.4 %collective-permute-done.1.high_ref = f32[472,128]{1,0:T(8,128)S(1)} collective-permute-done((f32[472,128]{1,0:T(8,128)S(1)}, f32[472,128]{1,0:T(8,128)S(1)}, u32[]{:S(2)}, u32[]{:S(2)}) %collective-permute-start.1) | collective-permute-done | bytes 241696 | tf_op jit(solution)/shard_map/ppermute | solution.py:711
  18.8 0.1 collective-permute-start.3
  18.9 1.1 %all-to-all-done.still_ref.mine_ref = f32[8,5,8,128]{3,2,1,0:T(8,128)S(1)} async-done(((f32[8,5,8,128]{3,2,1,0:T(8,128)}), f32[8,5,8,128]{3,2,1,0:T(8,128)S(1)}, u32[]{:S(2)}, u32[]{:S(2)}) %all-to-all-start) | async-done | bytes 163872 | tf_op jit(solution)/shard_map/all_to_all | solution.py:716
  20.0 0.0 collective-permute-start.4
  20.0 0.2 halo.1
  20.2 0.0 copy-start.3
  20.2 0.6 %collective-permute-start.2 = (f32[112,128]{1,0:T(8,128)S(1)}, f32[112,128]{1,0:T(8,128)S(1)}, u32[]{:S(2)}, u32[]{:S(2)}) collective-permute-start(f32[112,128]{1,0:T(8,128)S(1)} %get-tuple-element.24.edge_ref), channel_id=1, source_target_pairs={{0,1},{1,0},{2,3},{3,2},{4,5},{5,4},{6,7},{7,6},{8,9},{9,8},{10,11... | collective-permute-start | bytes 172040 | tf_op jit(solution)/shard_map/ppermute | solution.py:745
  20.7 0.6 %collective-permute-done.4.still_other_ref.other_ref = f32[8,5,8,128]{3,2,1,0:T(8,128)S(1)} collective-permute-done((f32[8,5,8,128]{3,2,1,0:T(8,128)S(1)}, f32[8,5,8,128]{3,2,1,0:T(8,128)S(1)}, u32[]{:S(2)}, u32[]{:S(2)}) %collective-permute-start.4) | collective-permute-done | bytes 163872 | tf_op jit(solution)/shard_map/ppermute | solution.py:717
  21.4 0.0 collective-permute-done.3.other_ref
  21.4 1.8 %basis.1.basis_ref = f32[12,8,16,128]{3,2,1,0:T(8,128)S(1)} custom-call(f32[576,128]{1,0:T(8,128)S(1)} %border.1.mine_ref, f32[576,128]{1,0:T(8,128)S(1)} %collective-permute-done.3.other_ref, f32[8,5,8,128]{3,2,1,0:T(8,128)S(1)} %all-to-all-done.still_ref.mine_ref, f32[8,5,8,128]{3,2,1,0:T(8,128)S(1)} %collective-permute-done.4.still_other_ref.other_ref), custom_call_target="tpu_custom_call" | custom-call | tf_op jit(solution)/shard_map/basis/pallas_call | solution.py:734
  23.2 0.0 collective-permute-done.2.other_ref
  23.2 2.8 %mix.1 = (f32[2,400,128]{2,1,0:T(8,128)S(1)}, f32[8,5,8,128]{3,2,1,0:T(8,128)S(1)}) custom-call(f32[8,112,128]{2,1,0:T(8,128)S(1)} %get-tuple-element.19.rows_ref, f32[6,112,128]{2,1,0:T(8,128)S(1)} %get-tuple-element.23.halo_ref, f32[112,128]{1,0:T(8,128)S(1)} %get-tuple-element.24.edge_ref, f32[112,128]{1,0:T(8,128)S(1)} %collective-permute-done.2.other_ref, ...), custom_call_target="tpu_custom_call" | custom-call | tf_op jit(solution)/shard_map/mix/pallas_call | solution.py:746
  26.0 11.7 %all_to_all.10.mine_ref = f32[8,5,8,128]{3,2,1,0:T(8,128)S(1)} all-to-all(f32[8,5,8,128]{3,2,1,0:T(8,128)S(1)} %get-tuple-element.27), channel_id=1, replica_groups=mesh['members'=2,'loop'=8,'lat'=2] {'loop'}, dimensions={0} | all-to-all | bytes 327680 | tf_op jit(solution)/shard_map/all_to_all | solution.py:757
  37.8 0.0 collective-permute-start.5
  37.8 0.2 plan.1
  38.0 1.2 %collective-permute-done.5.other_ref = f32[8,5,8,128]{3,2,1,0:T(8,128)S(1)} collective-permute-done((f32[8,5,8,128]{3,2,1,0:T(8,128)S(1)}, f32[8,5,8,128]{3,2,1,0:T(8,128)S(1)}, u32[]{:S(2)}, u32[]{:S(2)}) %collective-permute-start.5) | collective-permute-done | bytes 163872 | tf_op jit(solution)/shard_map/ppermute | solution.py:758
  39.2 2.9 %solve.1 = (f32[2,400,128]{2,1,0:T(8,128)}, f32[2,8,128]{2,1,0:T(8,128)}, f32[2,8,128]{2,1,0:T(8,128)}) custom-call(f32[8,5,8,128]{3,2,1,0:T(8,128)S(1)} %all_to_all.10.mine_ref, f32[8,5,8,128]{3,2,1,0:T(8,128)S(1)} %collective-permute-done.5.other_ref, f32[6,64,256]{2,1,0:T(8,128)S(1)} %get-tuple-element.28.faces_ref, ...), custom_call_target="tpu_custom_call" | custom-call | tf_op jit(solution)/shard_map/solve/pallas_call | solution.py:759
  (13 shorter events, 0.0 us)
Async XLA Ops:
  0.6 7.5 %copy-start = (f32[50,8,128]{2,1,0:T(8,128)S(1)}, f32[50,8,128]{2,1,0:T(8,128)}, u32[]{:S(2)}) copy-start(f32[50,8,128]{2,1,0:T(8,128)} %param.11) | copy-start | bytes 614404
  0.6 7.5 %copy-start.1 = (f32[8,2,8,128]{3,2,1,0:T(8,128)S(1)}, f32[8,2,8,128]{3,2,1,0:T(8,128)}, u32[]{:S(2)}) copy-start(f32[8,2,8,128]{3,2,1,0:T(8,128)} %param.16) | copy-start | bytes 196612
  0.7 7.5 %copy-start.2 = (f32[8,2,8,128]{3,2,1,0:T(8,128)S(1)}, f32[8,2,8,128]{3,2,1,0:T(8,128)}, u32[]{:S(2)}) copy-start(f32[8,2,8,128]{3,2,1,0:T(8,128)} %param.17) | copy-start | bytes 196612
  0.7 7.5 %copy-start.6 = (f32[8,128]{1,0:T(8,128)S(1)}, f32[8,128]{1,0:T(8,128)}, u32[]{:S(2)}) copy-start(f32[8,128]{1,0:T(8,128)} %damping_ref.1) | copy-start | bytes 12292
  2.0 14.4 %collective-permute-start = (f32[472,128]{1,0:T(8,128)S(1)}, f32[472,128]{1,0:T(8,128)S(1)}, u32[]{:S(2)}, u32[]{:S(2)}) collective-permute-start(f32[472,128]{1,0:T(8,128)S(1)} %get-tuple-element.21), channel_id=1, source_target_pairs={{0,2},{2,4},{4,6},{6,8},{8,10},{10,12},{12,14},{14,0},{1,3},{3,5},... | collective-permute-start | bytes 725000 | tf_op jit(solution)/shard_map/ppermute | solution.py:710
  5.0 3.1 %copy-start.5 = (f32[8,128]{1,0:T(8,128)S(1)}, f32[8,128]{1,0:T(8,128)}, u32[]{:S(2)}) copy-start(f32[8,128]{1,0:T(8,128)} %spread_ref.1) | copy-start | bytes 12292
  5.0 3.2 %copy-start.4 = (s32[8,128]{1,0:T(8,128)S(1)}, s32[8,128]{1,0:T(8,128)}, u32[]{:S(2)}) copy-start(s32[8,128]{1,0:T(8,128)} %depth_ref.3) | copy-start | bytes 12292
  5.0 13.8 %collective-permute-start.1 = (f32[472,128]{1,0:T(8,128)S(1)}, f32[472,128]{1,0:T(8,128)S(1)}, u32[]{:S(2)}, u32[]{:S(2)}) collective-permute-start(f32[472,128]{1,0:T(8,128)S(1)} %get-tuple-element.22), channel_id=1, source_target_pairs={{2,0},{4,2},{6,4},{8,6},{10,8},{12,10},{14,12},{0,14},{3,1},{5,3},... | collective-permute-start | bytes 725000 | tf_op jit(solution)/shard_map/ppermute | solution.py:711
  9.1 10.9 %all-to-all-start = ((f32[8,5,8,128]{3,2,1,0:T(8,128)}), f32[8,5,8,128]{3,2,1,0:T(8,128)S(1)}, u32[]{:S(2)}, u32[]{:S(2)}) async-start(f32[8,5,8,128]{3,2,1,0:T(8,128)} %get-tuple-element.26.still_ref), calls=%async_computation | async-start | bytes 327680 | tf_op jit(solution)/shard_map/all_to_all | solution.py:716
  18.8 2.6 %collective-permute-start.3 = (f32[576,128]{1,0:T(8,128)S(1)}, f32[576,128]{1,0:T(8,128)S(1)}, u32[]{:S(2)}, u32[]{:S(2)}) collective-permute-start(f32[576,128]{1,0:T(8,128)S(1)} %border.1.mine_ref), channel_id=1, source_target_pairs={{0,1},{1,0},{2,3},{3,2},{4,5},{5,4},{6,7},{7,6},{8,9},{9,8},{10,11... | collective-permute-start | bytes 884744 | tf_op jit(solution)/shard_map/ppermute | solution.py:731
  20.0 1.4 %collective-permute-start.4 = (f32[8,5,8,128]{3,2,1,0:T(8,128)S(1)}, f32[8,5,8,128]{3,2,1,0:T(8,128)S(1)}, u32[]{:S(2)}, u32[]{:S(2)}) collective-permute-start(f32[8,5,8,128]{3,2,1,0:T(8,128)S(1)} %all-to-all-done.still_ref.mine_ref), channel_id=1, source_target_pairs={{0,1},{1,0},{2,3},{3,2},{4,5},{5,4},{6,7},{7,6},{8,9},{9,8},{10,11... | collective-permute-start | bytes 491528 | tf_op jit(solution)/shard_map/ppermute | solution.py:717
  20.2 3.1 %copy-start.3 = (f32[2,50,8,128]{3,2,1,0:T(8,128)S(1)}, f32[2,50,8,128]{3,2,1,0:T(8,128)}, u32[]{:S(2)}) copy-start(f32[2,50,8,128]{3,2,1,0:T(8,128)} %param.10) | copy-start | bytes 1228804
  20.2 3.0 %collective-permute-start.2 = (f32[112,128]{1,0:T(8,128)S(1)}, f32[112,128]{1,0:T(8,128)S(1)}, u32[]{:S(2)}, u32[]{:S(2)}) collective-permute-start(f32[112,128]{1,0:T(8,128)S(1)} %get-tuple-element.24.edge_ref), channel_id=1, source_target_pairs={{0,1},{1,0},{2,3},{3,2},{4,5},{5,4},{6,7},{7,6},{8,9},{9,8},{10,11... | collective-permute-start | bytes 172040 | tf_op jit(solution)/shard_map/ppermute | solution.py:745
  37.8 1.4 %collective-permute-start.5 = (f32[8,5,8,128]{3,2,1,0:T(8,128)S(1)}, f32[8,5,8,128]{3,2,1,0:T(8,128)S(1)}, u32[]{:S(2)}, u32[]{:S(2)}) collective-permute-start(f32[8,5,8,128]{3,2,1,0:T(8,128)S(1)} %all_to_all.10.mine_ref), channel_id=1, source_target_pairs={{0,1},{1,0},{2,3},{3,2},{4,5},{5,4},{6,7},{7,6},{8,9},{9,8},{10,11... | collective-permute-start | bytes 491528 | tf_op jit(solution)/shard_map/ppermute | solution.py:758

commit v6 on v5

--- a/solution.py
+++ b/solution.py
@@ -127,7 +127,7 @@
 
 def pairs_kernel(
     rows_ref, step_ref, change_ref, depth_ref, spread_ref, damping_ref, weight_ref,
-    edge_ref, still_ref, gram_ref,
+    edge_ref, still_ref, own_ref, gram_ref,
 ):
     rows, _, cols = rows_ref.shape
     lat = lax.axis_index("lat")
@@ -156,8 +156,9 @@
         weight_ref[pl.ds(0, rows), :],
         gram_ref[...],
     )
-    for copy in range(still_ref.shape[0]):
-        for at, field in enumerate(fields):
+    for at, field in enumerate(fields):
+        own_ref[at] = field
+        for copy in range(still_ref.shape[0]):
             still_ref[copy, at] = field
     edge_ref[...] = edge_of(lambda i: rows_ref[i - SUB], range(SUB, rows + SUB), cols, lat)
 
@@ -242,8 +243,12 @@
     plan_ref[pl.ds(0, 1), :] = jnp.where(at, -gamma, plan_ref[pl.ds(0, 1), :])
 
 
-def halo_kernel(levels, padded, rows, edge_ref, low_ref, high_ref, out_ref, halo_ref):
-    planes, cols = out_ref.shape
+def border_kernel(
+    levels, padded, edge_ref, low_ref, high_ref, hist_ref, out_ref, halo_ref
+):
+    planes, cols = edge_ref.shape
+    rows = hist_ref.shape[0]
+    pairs = hist_ref.shape[1] // 2
     lat = lax.axis_index("lat")
     near, second = state_rows(levels)
     rest = jnp.zeros((padded - levels, cols), F32)
@@ -255,22 +260,17 @@
         halo_ref[i, pl.ds(0, levels + 2), :] = ref[pl.ds(at, levels + 2), :]
         halo_ref[i, pl.ds(padded, levels), :] = ref[pl.ds(at + second, levels), :]
     total = edge_ref[...] + edge_of(lambda i: halo_ref[i], range(SUB), cols, lat)
-    out_ref[...] = total + edge_of(
+    out_ref[pl.ds(0, planes), :] = total + edge_of(
         lambda i: halo_ref[i - rows], range(rows + SUB, rows + 2 * SUB), cols, lat
     )
-
-
-def border_kernel(start, low_ref, high_ref, hist_ref, out_ref):
-    low_ref = low_ref.at[pl.ds(start, low_ref.shape[0] - start)]
-    high_ref = high_ref.at[pl.ds(start, high_ref.shape[0] - start)]
-    rows = hist_ref.shape[0]
-    pairs = hist_ref.shape[1] // 2
-    far = SUB * 2 * pairs
+    start = SUB * near
+    far = start + SUB * 2 * pairs
     ahead = REACH - SUB
-    joint = (rows + 2 * REACH) * pairs
+    apart = planes
+    joint = apart + (rows + 2 * REACH) * pairs
     for i in range(rows + 2 * REACH):
         at = i - REACH
-        target = pl.ds(i * pairs, pairs)
+        target = pl.ds(apart + i * pairs, pairs)
         if at < -SUB:
             out_ref[target, :] = low_ref[pl.ds(far + i * pairs, pairs), :]
             continue
@@ -278,22 +278,24 @@
             out_ref[target, :] = high_ref[pl.ds(far + (at - rows - SUB) * pairs, pairs), :]
             continue
         if at < 0:
-            ref, start = low_ref, (at + SUB) * 2 * pairs
+            ref, here = low_ref, start + (at + SUB) * 2 * pairs
         elif at < rows:
-            ref, start = hist_ref.at[at], 0
+            ref, here = hist_ref.at[at], 0
         else:
-            ref, start = high_ref, (at - rows) * 2 * pairs
-        out_ref[target, :] = ref[pl.ds(start, pairs), :]
-        out_ref[pl.ds(joint + (i - ahead) * pairs, pairs), :] = ref[pl.ds(start + pairs, pairs), :]
-
-
-def basis_kernel(rows, pairs, mine_ref, other_ref, still_ref, still_other_ref, out_ref, *work):
+            ref, here = high_ref, start + (at - rows) * 2 * pairs
+        out_ref[target, :] = ref[pl.ds(here, pairs), :]
+        target = pl.ds(joint + (i - ahead) * pairs, pairs)
+        out_ref[target, :] = ref[pl.ds(here + pairs, pairs), :]
+
+
+def basis_kernel(planes, rows, pairs, mine_ref, other_ref, still_ref, still_other_ref, out_ref, *work):
     cols = mine_ref.shape[1]
     width = 2 * cols
     loops = still_ref.shape[0]
     tall = rows + 2 * REACH
     ahead = REACH - SUB
-    joint = tall * pairs
+    apart = planes
+    joint = apart + tall * pairs
     opened = iota((1, width), 1) != closed_lane(cols)
 
     def wide(at, size):
@@ -350,7 +352,7 @@
             out_ref[slot, i] = get(i + REACH)[:, :cols]
 
     def start_apart(i):
-        return wide(i * pairs, pairs)
+        return wide(apart + i * pairs, pairs)
 
     def start_joint(i):
         return wide(joint + (i - ahead) * pairs, pairs)
@@ -383,23 +385,18 @@
 
 
 def mix_kernel(
-    levels, padded, scale, copies,
-    rows_ref, halo_ref, edge_ref, other_ref, weight_ref, observed_ref, basis_ref, still_ref,
-    mixed_ref, fields_ref, face_ref, here_ref, there_ref, part_ref,
+    levels, padded, rows_ref, halo_ref, out_ref, face_ref, here_ref, there_ref
 ):
-    rows, planes, cols = rows_ref.shape
-    pairs = basis_ref.shape[2]
-    lat = lax.axis_index("lat")
+    rows, _, cols = rows_ref.shape
     lane = iota((1, cols), 1)
-    place = lane % SLOT
     count = rows + 2 * SUB
     level = iota((padded, cols), 0).astype(F32)
 
-    def left(value, by=1):
-        return pltpu.roll(value, (cols - by) % cols, 1)
-
-    def right(value, by=1):
-        return pltpu.roll(value, by, 1)
+    def left(value):
+        return pltpu.roll(value, cols - 1, 1)
+
+    def right(value):
+        return pltpu.roll(value, 1, 1)
 
     def source(i):
         if i < SUB:
@@ -411,6 +408,53 @@
     def face(depth_here, depth_there, spread_here, spread_there):
         opened = level < jnp.minimum(depth_here, depth_there)
         return jnp.where(opened, 0.5 * (spread_here + spread_there), 0.0)
+
+    spreads = [source(i)[pl.ds(levels, 1), :] for i in range(count)]
+    depths = [source(i)[pl.ds(levels + 1, 1), :] for i in range(count)]
+    for i in range(count - 1):
+        face_ref[0, i] = face(depths[i], depths[i + 1], spreads[i], spreads[i + 1])
+    for i in range(1, count - 1):
+        there = jnp.where(lane < cols - 1, left(depths[i]), 0.0)
+        face_ref[1, i] = face(depths[i], there, spreads[i], left(spreads[i]))
+        there = jnp.where(lane > 0, right(depths[i]), 0.0)
+        face_ref[2, i] = face(depths[i], there, spreads[i], right(spreads[i]))
+
+    for sweep in range(1, SUB + 1):
+        target = here_ref if sweep % 2 else there_ref
+        for i in range(sweep, count - sweep):
+            def field(at):
+                if sweep == 1:
+                    return source(at)
+                return (there_ref if sweep % 2 else here_ref).at[at]
+
+            into = out_ref.at[i - SUB] if sweep == SUB else target.at[i]
+            for tracer in range(2):
+                at = pl.ds(tracer * padded, padded)
+                centre = field(i)[at, :]
+                total = centre + face_ref[0, i] * (field(i + 1)[at, :] - centre)
+                total = total + face_ref[0, i - 1] * (field(i - 1)[at, :] - centre)
+                total = total + face_ref[1, i] * (left(centre) - centre)
+                total = total + face_ref[2, i] * (right(centre) - centre)
+                into[at, :] = total
+
+
+def fields_kernel(
+    levels, padded, scale,
+    rows_ref, main_ref, edge_ref, other_ref, weight_ref, observed_ref, basis_ref, still_ref,
+    mixed_ref, fields_ref, part_ref,
+):
+    rows, _, cols = rows_ref.shape
+    pairs = basis_ref.shape[2]
+    lat = lax.axis_index("lat")
+    lane = iota((1, cols), 1)
+    place = lane % SLOT
+    level = iota((padded, cols), 0).astype(F32)
+
+    def left(value, by=1):
+        return pltpu.roll(value, (cols - by) % cols, 1)
+
+    def right(value, by=1):
+        return pltpu.roll(value, by, 1)
 
     spread = edge_ref[pl.ds(levels, 1), :] + other_ref[pl.ds(levels, 1), :]
     depth = edge_ref[pl.ds(levels + 1, 1), :] + other_ref[pl.ds(levels + 1, 1), :]
@@ -448,16 +492,6 @@
         at = pl.ds(tracer * padded, padded)
         parts.append(edge_ref[at, :] + other_ref[at, :])
 
-    spreads = [source(i)[pl.ds(levels, 1), :] for i in range(count)]
-    depths = [source(i)[pl.ds(levels + 1, 1), :] for i in range(count)]
-    for i in range(count - 1):
-        face_ref[0, i] = face(depths[i], depths[i + 1], spreads[i], spreads[i + 1])
-    for i in range(1, count - 1):
-        there = jnp.where(lane < cols - 1, left(depths[i]), 0.0)
-        face_ref[1, i] = face(depths[i], there, spreads[i], left(spreads[i]))
-        there = jnp.where(lane > 0, right(depths[i]), 0.0)
-        face_ref[2, i] = face(depths[i], there, spreads[i], right(spreads[i]))
-
     for sweep in range(1, SUB + 1):
         for tracer in range(2):
             part = parts[tracer]
@@ -468,31 +502,15 @@
             extras[tracer] = across
             if sweep < SUB:
                 parts[tracer] = spread_out(part, to_right, to_left)
-        target = here_ref if sweep % 2 else there_ref
-        for i in range(sweep, count - sweep):
-            def field(at):
-                if sweep == 1:
-                    return source(at)
-                return (there_ref if sweep % 2 else here_ref).at[at]
-
-            for tracer in range(2):
-                at = pl.ds(tracer * padded, padded)
-                centre = field(i)[at, :]
-                total = centre + face_ref[0, i] * (field(i + 1)[at, :] - centre)
-                total = total + face_ref[0, i - 1] * (field(i - 1)[at, :] - centre)
-                total = total + face_ref[1, i] * (left(centre) - centre)
-                total = total + face_ref[2, i] * (right(centre) - centre)
-                target[i, at, :] = total
-
-    target = here_ref if SUB % 2 else there_ref
+
     for row in range(rows):
         i = row + SUB
         at = pl.ds(row, levels, stride=rows)
         mixed = []
         for tracer in range(2):
             border = jnp.where(at_border, left(extras[tracer], SLOT * i + SUB), 0.0)
-            mixed.append((target[i, pl.ds(tracer * padded, padded), :] + border)[:levels])
-        wet = level[:levels] < depths[i]
+            mixed.append((main_ref[row, pl.ds(tracer * padded, padded), :] + border)[:levels])
+        wet = level[:levels] < rows_ref[row, pl.ds(levels + 1, 1), :]
         weight = weight_ref[at, :]
         misfit = []
         for tracer in range(2):
@@ -517,7 +535,7 @@
     for row in range(rows):
         here = pl.ds(row, 1)
         get = lambda field: part_ref[field, here, :]
-        still = lambda field: still_ref[0, field, here, :]
+        still = lambda field: still_ref[field, here, :]
         surface, base = get(0), get(1)
         add(0, 0, row, 0.5 * (get(2) + get(3)))
         add(0, 1, row, 0.5 * (get(2) - get(3)))
@@ -537,7 +555,7 @@
         total = total + jnp.where(lane == at, value[:half], 0.0)
         total = total + jnp.where(lane == cols // 2 + at, value[half:], 0.0)
     part_ref[4] = total
-    for copy in range(copies):
+    for copy in range(fields_ref.shape[0]):
         fields_ref[copy] = part_ref[...]
 
 
@@ -709,10 +727,11 @@
     swap = [(0, 1), (1, 0)]
     low = lax.ppermute(up, "loop", forward)
     high = lax.ppermute(down, "loop", backward)
-    edge, still, _ = call(
-        pairs_kernel, [(planes, cols), (loops, 5, rows, cols), (count, cols)], name="pairs"
+    edge, still, still_own, _ = call(
+        pairs_kernel,
+        [(planes, cols), (loops, 5, rows, cols), (5, rows, cols), (count, cols)],
+        name="pairs",
     )(packed, step, change, depth_index, diffusivity, damping, weight)
-    still_own = still
     still = lax.all_to_all(still, "loop", 0, 0)
     still_other = lax.ppermute(still, "lat", swap)
     height = loops * rows
@@ -723,37 +742,35 @@
         vmem=large,
         name="plan",
     )(still, still_other)
-    (border,) = call(
-        functools.partial(border_kernel, states),
-        [((rows + 2 * REACH + rows + 2 * SUB) * pairs, cols)],
+    swapped = planes + (rows + 2 * REACH + rows + 2 * SUB) * pairs
+    border, halo = call(
+        functools.partial(border_kernel, levels, padded),
+        [(swapped, cols), (2 * SUB, planes, cols)],
         name="border",
-    )(low, high, hist)
-    border_other = lax.ppermute(border, "lat", swap)
+    )(edge, low, high, hist)
+    other = lax.ppermute(border, "lat", swap)
+    tall = rows + 2 * SUB
+    (mixed,) = call(
+        functools.partial(mix_kernel, levels, padded),
+        [(rows, planes, cols)],
+        scratch=[pltpu.VMEM((3, tall, padded, cols), F32)]
+        + [pltpu.VMEM((tall, planes, cols), F32)] * 2,
+        name="mix",
+    )(packed, halo)
     chains = 1 + ITERS
     buffers = 2 * SUB + ITERS - 1 + chains * (ITERS - 1)
     (basis,) = call(
-        functools.partial(basis_kernel, rows, pairs),
+        functools.partial(basis_kernel, planes, rows, pairs),
         [(1 + ITERS + chains * (ITERS - 1), rows, pairs, cols)],
         scratch=[pltpu.VMEM((rows + 2 * REACH, pairs, 2 * cols), F32)] * buffers,
         name="basis",
-    )(border, border_other, still, still_other)
-    edge, halo = call(
-        functools.partial(halo_kernel, levels, padded, rows),
-        [(planes, cols), (2 * SUB, planes, cols)],
-        name="halo",
-    )(edge, low, high)
-    other = lax.ppermute(edge, "lat", swap)
+    )(border, other, still, still_other)
     mixed, fields = call(
-        functools.partial(mix_kernel, levels, padded, scale, loops),
+        functools.partial(fields_kernel, levels, padded, scale),
         [flat, (loops, 5, rows, cols)],
-        scratch=[
-            pltpu.VMEM((3, rows + 2 * SUB, padded, cols), F32),
-            pltpu.VMEM((rows + 2 * SUB, planes, cols), F32),
-            pltpu.VMEM((rows + 2 * SUB, planes, cols), F32),
-            pltpu.VMEM((5, rows, cols), F32),
-        ],
-        name="mix",
-    )(packed, halo, edge, other, weight, observed, basis, still_own)
+        scratch=[pltpu.VMEM((5, rows, cols), F32)],
+        name="fields",
+    )(packed, mixed, border, other, weight, observed, basis, still_own)
     mine = lax.all_to_all(fields, "loop", 0, 0)
     theirs = lax.ppermute(mine, "lat", swap)
     state_next, gradient, direction = call(

time: 42.4 us -> 40.7 us (0.960)
  Pallas kernels: 10.2 us -> 9.46 us
  waiting for transfers between devices: 9.19 us -> 8.62 us
  starting transfers between devices: 10.1 us -> 9.57 us
    pallas_call x5, Pallas kernels: 5.77 us -> 5.02 us  [the longest x1 1.85 us: on_device(): call(functools.partial(basis_kernel, planes, rows, pairs), [(1 + ITERS +...]
    ppermute x2 -> x1, starting transfers between devices: 0.64 us -> 0.07 us  [on_device(): other = lax.ppermute(border, 'lat', swap)]
    ppermute x1, waiting for transfers between devices: 0.64 us -> 0.21 us  [on_device(): still_other = lax.ppermute(still, 'lat', swap)]
  transfers between devices with their start and end apart: 7 -> 6, of which waited for: 5 -> 5; matrix products, arithmetic and copies ran while one was open for 0% -> 0% of each run, Pallas kernels for 8% -> 6%
where the time goes in v6:
time: 40.7 us; the launch traced here: 40.4 us
  blocking collectives  11.9 us (29%)
  starting transfers between devices  9.57 us (24%)
  Pallas kernels  9.46 us (23%)
  waiting for transfers between devices  8.62 us (21%)
  between operations  0.77 us (2%)
    all_to_all x1, blocking collectives, on_device(): mine = lax.all_to_all(fields, 'loop', 0, 0)  11.9 us
    ppermute x1, waiting for transfers between devices, on_device(): low = lax.ppermute(up, 'loop', forward)  3.93 us
    all_to_all x1, starting transfers between devices, on_device(): still = lax.all_to_all(still, 'loop', 0, 0)  3.38 us
    ppermute x1, starting transfers between devices, on_device(): high = lax.ppermute(down, 'loop', backward)  3.12 us
    ppermute x1, starting transfers between devices, on_device(): low = lax.ppermute(up, 'loop', forward)  2.99 us
    pallas_call x1, Pallas kernels, on_device(): call(functools.partial(solve_kernel, levels, scale), [flat, (2, rows, col...  2.91 us
    ppermute x1, waiting for transfers between devices, on_device(): high = lax.ppermute(down, 'loop', backward)  2.39 us
    pallas_call x1, Pallas kernels, on_device(): call(functools.partial(basis_kernel, planes, rows, pairs), [(1 + ITERS +...  1.85 us
  transfers between devices with their start and end apart: 6, of which 5 were waited for; matrix products, arithmetic and copies ran while one was open for 0% of the time, Pallas kernels for 6%

profile of v6, /device:TPU:0, one launch (start us, length us, event | category | flops | bytes accessed | tf_op | source)
XLA Modules:
  0.0 40.4 jit_solution(11768540969088350485)
XLA Ops:
  0.6 0.0 copy-start
  0.6 0.0 copy-start.1
  0.7 1.3 %pack.1 = (f32[8,112,128]{2,1,0:T(8,128)S(1)}, f32[8,32,128]{2,1,0:T(8,128)S(1)}, f32[472,128]{1,0:T(8,128)S(1)}, f32[472,128]{1,0:T(8,128)S(1)}) custom-call(f32[2,400,128]{2,1,0:T(8,128)} %bitcast.17, f32[2,8,128]{2,1,0:T(8,128)} %refs_1_.1, s32[8,128]{1,0:T(8,128)} %depth_ref.3, f32[8,128]{1,0:T(8,128)} %spread_ref.1, f32[128,128]{1,0:T(8,128)} %bitcast.10, ...), custom_call_target="tpu_custom_call" | custom-call | tf_op jit(solution)/shard_map/pack/pallas_call | solution.py:715
  2.0 3.0 %collective-permute-start = (f32[472,128]{1,0:T(8,128)S(1)}, f32[472,128]{1,0:T(8,128)S(1)}, u32[]{:S(2)}, u32[]{:S(2)}) collective-permute-start(f32[472,128]{1,0:T(8,128)S(1)} %get-tuple-element.22), channel_id=1, source_target_pairs={{0,2},{2,4},{4,6},{6,8},{8,10},{10,12},{12,14},{14,0},{1,3},{3,5},... | collective-permute-start | bytes 725000 | tf_op jit(solution)/shard_map/ppermute | solution.py:728
  5.0 3.1 %collective-permute-start.1 = (f32[472,128]{1,0:T(8,128)S(1)}, f32[472,128]{1,0:T(8,128)S(1)}, u32[]{:S(2)}, u32[]{:S(2)}) collective-permute-start(f32[472,128]{1,0:T(8,128)S(1)} %get-tuple-element.23), channel_id=1, source_target_pairs={{2,0},{4,2},{6,4},{8,6},{10,8},{12,10},{14,12},{0,14},{3,1},{5,3},... | collective-permute-start | bytes 725000 | tf_op jit(solution)/shard_map/ppermute | solution.py:729
  8.1 1.0 %pairs.1 = (f32[112,128]{1,0:T(8,128)S(1)}, f32[8,5,8,128]{3,2,1,0:T(8,128)}, f32[5,8,128]{2,1,0:T(8,128)S(1)}, f32[8,128]{1,0:T(8,128)}) custom-call(f32[8,112,128]{2,1,0:T(8,128)S(1)} %get-tuple-element.20.rows_ref, f32[8,16,128]{2,1,0:T(8,128)S(1)} %bitcast.11, f32[8,16,128]{2,1,0:T(8,128)S(1)} %bitcast.14, s32[8,128]{1,0:T(8,128)S(1)} %copy-done.4, ...), custom_call_target="tpu_custom_call" | custom-call | tf_op jit(solution)/shard_map/pairs/pallas_call | solution.py:730
  9.1 3.4 %all-to-all-start = ((f32[8,5,8,128]{3,2,1,0:T(8,128)}), f32[8,5,8,128]{3,2,1,0:T(8,128)S(1)}, u32[]{:S(2)}, u32[]{:S(2)}) async-start(f32[8,5,8,128]{3,2,1,0:T(8,128)} %get-tuple-element.27), calls=%async_computation | async-start | bytes 327680 | tf_op jit(solution)/shard_map/all_to_all | solution.py:735
  12.5 3.9 %collective-permute-done.low_ref = f32[472,128]{1,0:T(8,128)S(1)} collective-permute-done((f32[472,128]{1,0:T(8,128)S(1)}, f32[472,128]{1,0:T(8,128)S(1)}, u32[]{:S(2)}, u32[]{:S(2)}) %collective-permute-start) | collective-permute-done | bytes 241696 | tf_op jit(solution)/shard_map/ppermute | solution.py:728
  16.4 2.4 %collective-permute-done.1.high_ref = f32[472,128]{1,0:T(8,128)S(1)} collective-permute-done((f32[472,128]{1,0:T(8,128)S(1)}, f32[472,128]{1,0:T(8,128)S(1)}, u32[]{:S(2)}, u32[]{:S(2)}) %collective-permute-start.1) | collective-permute-done | bytes 241696 | tf_op jit(solution)/shard_map/ppermute | solution.py:729
  18.8 0.2 border.1
  19.0 0.1 collective-permute-start.2
  19.1 0.9 %all-to-all-done.still_ref.mine_ref = f32[8,5,8,128]{3,2,1,0:T(8,128)S(1)} async-done(((f32[8,5,8,128]{3,2,1,0:T(8,128)}), f32[8,5,8,128]{3,2,1,0:T(8,128)S(1)}, u32[]{:S(2)}, u32[]{:S(2)}) %all-to-all-start) | async-done | bytes 163872 | tf_op jit(solution)/shard_map/all_to_all | solution.py:735
  20.0 0.0 collective-permute-start.3
  20.0 1.2 %mix.1.main_ref = f32[8,112,128]{2,1,0:T(8,128)S(1)} custom-call(f32[8,112,128]{2,1,0:T(8,128)S(1)} %get-tuple-element.20.rows_ref, f32[6,112,128]{2,1,0:T(8,128)S(1)} %get-tuple-element.25.halo_ref), custom_call_target="tpu_custom_call" | custom-call | tf_op jit(solution)/shard_map/mix/pallas_call | solution.py:753
  21.2 0.0 copy-start.3
  21.2 0.2 collective-permute-done.3.still_other_ref.other_ref
  21.4 0.0 collective-permute-done.2.other_ref
  21.4 1.8 %basis.1.basis_ref = f32[12,8,16,128]{3,2,1,0:T(8,128)S(1)} custom-call(f32[688,128]{1,0:T(8,128)S(1)} %get-tuple-element.26.mine_ref.edge_ref, f32[688,128]{1,0:T(8,128)S(1)} %collective-permute-done.2.other_ref, f32[8,5,8,128]{3,2,1,0:T(8,128)S(1)} %all-to-all-done.still_ref.mine_ref, f32[8,5,8,128]{3,2,1,0:T(8,128)S(1)} %collective-permute-done.3.still_other_ref.other_ref), custom_call_target="tpu_custom_call" | custom-call | tf_op jit(solution)/shard_map/basis/pallas_call | solution.py:762
  23.2 0.9 %fields.1 = (f32[2,400,128]{2,1,0:T(8,128)S(1)}, f32[8,5,8,128]{3,2,1,0:T(8,128)S(1)}) custom-call(f32[8,112,128]{2,1,0:T(8,128)S(1)} %get-tuple-element.20.rows_ref, f32[8,112,128]{2,1,0:T(8,128)S(1)} %mix.1.main_ref, f32[688,128]{1,0:T(8,128)S(1)} %get-tuple-element.26.mine_ref.edge_ref, f32[688,128]{1,0:T(8,128)S(1)} %collective-permute-done.2.other_ref, ...), custom_call_target="tpu_custom_call" | custom-call | tf_op jit(solution)/shard_map/fields/pallas_call | solution.py:768
  24.1 11.9 %all_to_all.10.mine_ref = f32[8,5,8,128]{3,2,1,0:T(8,128)S(1)} all-to-all(f32[8,5,8,128]{3,2,1,0:T(8,128)S(1)} %get-tuple-element.29), channel_id=1, replica_groups=mesh['members'=2,'loop'=8,'lat'=2] {'loop'}, dimensions={0} | all-to-all | bytes 327680 | tf_op jit(solution)/shard_map/all_to_all | solution.py:774
  36.1 0.0 collective-permute-start.4
  36.1 0.2 plan.1
  36.3 1.2 %collective-permute-done.4.other_ref = f32[8,5,8,128]{3,2,1,0:T(8,128)S(1)} collective-permute-done((f32[8,5,8,128]{3,2,1,0:T(8,128)S(1)}, f32[8,5,8,128]{3,2,1,0:T(8,128)S(1)}, u32[]{:S(2)}, u32[]{:S(2)}) %collective-permute-start.4) | collective-permute-done | bytes 163872 | tf_op jit(solution)/shard_map/ppermute | solution.py:775
  37.5 2.9 %solve.1 = (f32[2,400,128]{2,1,0:T(8,128)}, f32[2,8,128]{2,1,0:T(8,128)}, f32[2,8,128]{2,1,0:T(8,128)}) custom-call(f32[8,5,8,128]{3,2,1,0:T(8,128)S(1)} %all_to_all.10.mine_ref, f32[8,5,8,128]{3,2,1,0:T(8,128)S(1)} %collective-permute-done.4.other_ref, f32[6,64,256]{2,1,0:T(8,128)S(1)} %get-tuple-element.30.faces_ref, ...), custom_call_target="tpu_custom_call" | custom-call | tf_op jit(solution)/shard_map/solve/pallas_call | solution.py:776
  (11 shorter events, 0.0 us)
Async XLA Ops:
  0.6 7.5 %copy-start = (f32[50,8,128]{2,1,0:T(8,128)S(1)}, f32[50,8,128]{2,1,0:T(8,128)}, u32[]{:S(2)}) copy-start(f32[50,8,128]{2,1,0:T(8,128)} %param.11) | copy-start | bytes 614404
  0.6 7.5 %copy-start.1 = (f32[8,2,8,128]{3,2,1,0:T(8,128)S(1)}, f32[8,2,8,128]{3,2,1,0:T(8,128)}, u32[]{:S(2)}) copy-start(f32[8,2,8,128]{3,2,1,0:T(8,128)} %param.16) | copy-start | bytes 196612
  0.7 7.5 %copy-start.2 = (f32[8,2,8,128]{3,2,1,0:T(8,128)S(1)}, f32[8,2,8,128]{3,2,1,0:T(8,128)}, u32[]{:S(2)}) copy-start(f32[8,2,8,128]{3,2,1,0:T(8,128)} %param.17) | copy-start | bytes 196612
  0.7 7.5 %copy-start.6 = (f32[8,128]{1,0:T(8,128)S(1)}, f32[8,128]{1,0:T(8,128)}, u32[]{:S(2)}) copy-start(f32[8,128]{1,0:T(8,128)} %damping_ref.1) | copy-start | bytes 12292
  2.0 14.4 %collective-permute-start = (f32[472,128]{1,0:T(8,128)S(1)}, f32[472,128]{1,0:T(8,128)S(1)}, u32[]{:S(2)}, u32[]{:S(2)}) collective-permute-start(f32[472,128]{1,0:T(8,128)S(1)} %get-tuple-element.22), channel_id=1, source_target_pairs={{0,2},{2,4},{4,6},{6,8},{8,10},{10,12},{12,14},{14,0},{1,3},{3,5},... | collective-permute-start | bytes 725000 | tf_op jit(solution)/shard_map/ppermute | solution.py:728
  5.0 3.1 %copy-start.5 = (f32[8,128]{1,0:T(8,128)S(1)}, f32[8,128]{1,0:T(8,128)}, u32[]{:S(2)}) copy-start(f32[8,128]{1,0:T(8,128)} %spread_ref.1) | copy-start | bytes 12292
  5.0 3.2 %copy-start.4 = (s32[8,128]{1,0:T(8,128)S(1)}, s32[8,128]{1,0:T(8,128)}, u32[]{:S(2)}) copy-start(s32[8,128]{1,0:T(8,128)} %depth_ref.3) | copy-start | bytes 12292
  5.0 13.8 %collective-permute-start.1 = (f32[472,128]{1,0:T(8,128)S(1)}, f32[472,128]{1,0:T(8,128)S(1)}, u32[]{:S(2)}, u32[]{:S(2)}) collective-permute-start(f32[472,128]{1,0:T(8,128)S(1)} %get-tuple-element.23), channel_id=1, source_target_pairs={{2,0},{4,2},{6,4},{8,6},{10,8},{12,10},{14,12},{0,14},{3,1},{5,3},... | collective-permute-start | bytes 725000 | tf_op jit(solution)/shard_map/ppermute | solution.py:729
  9.1 10.9 %all-to-all-start = ((f32[8,5,8,128]{3,2,1,0:T(8,128)}), f32[8,5,8,128]{3,2,1,0:T(8,128)S(1)}, u32[]{:S(2)}, u32[]{:S(2)}) async-start(f32[8,5,8,128]{3,2,1,0:T(8,128)} %get-tuple-element.27), calls=%async_computation | async-start | bytes 327680 | tf_op jit(solution)/shard_map/all_to_all | solution.py:735
  19.0 2.4 %collective-permute-start.2 = (f32[688,128]{1,0:T(8,128)S(1)}, f32[688,128]{1,0:T(8,128)S(1)}, u32[]{:S(2)}, u32[]{:S(2)}) collective-permute-start(f32[688,128]{1,0:T(8,128)S(1)} %get-tuple-element.26.mine_ref.edge_ref), channel_id=1, source_target_pairs={{0,1},{1,0},{2,3},{3,2},{4,5},{5,4},{6,7},{7,6},{8,9},{9,8},{10,11... | collective-permute-start | bytes 1056776 | tf_op jit(solution)/shard_map/ppermute | solution.py:751
  20.0 1.4 %collective-permute-start.3 = (f32[8,5,8,128]{3,2,1,0:T(8,128)S(1)}, f32[8,5,8,128]{3,2,1,0:T(8,128)S(1)}, u32[]{:S(2)}, u32[]{:S(2)}) collective-permute-start(f32[8,5,8,128]{3,2,1,0:T(8,128)S(1)} %all-to-all-done.still_ref.mine_ref), channel_id=1, source_target_pairs={{0,1},{1,0},{2,3},{3,2},{4,5},{5,4},{6,7},{7,6},{8,9},{9,8},{10,11... | collective-permute-start | bytes 491528 | tf_op jit(solution)/shard_map/ppermute | solution.py:736
  21.2 2.1 %copy-start.3 = (f32[2,50,8,128]{3,2,1,0:T(8,128)S(1)}, f32[2,50,8,128]{3,2,1,0:T(8,128)}, u32[]{:S(2)}) copy-start(f32[2,50,8,128]{3,2,1,0:T(8,128)} %param.10) | copy-start | bytes 1228804
  36.1 1.4 %collective-permute-start.4 = (f32[8,5,8,128]{3,2,1,0:T(8,128)S(1)}, f32[8,5,8,128]{3,2,1,0:T(8,128)S(1)}, u32[]{:S(2)}, u32[]{:S(2)}) collective-permute-start(f32[8,5,8,128]{3,2,1,0:T(8,128)S(1)} %all_to_all.10.mine_ref), channel_id=1, source_target_pairs={{0,1},{1,0},{2,3},{3,2},{4,5},{5,4},{6,7},{7,6},{8,9},{9,8},{10,11... | collective-permute-start | bytes 491528 | tf_op jit(solution)/shard_map/ppermute | solution.py:775

commit v7 on v6

--- a/solution.py
+++ b/solution.py
@@ -40,76 +40,100 @@
     return lax.broadcasted_iota(jnp.int32, shape, dim)
 
 
-def state_rows(levels):
-    return round_up(2 * levels + 2, 8), levels + 2
+def row_layout(levels, pairs):
+    second = levels + 2
+    surface = second + levels
+    return surface + 5, second, surface, pairs + 3
 
 
 def pack_kernel(levels, padded, *refs):
-    sources, outs, targets, sems = refs[:6], refs[6:10], refs[10:16], refs[16]
+    sources, outs, targets, sems = refs[:9], refs[9:13], refs[13:22], refs[22]
     rows_ref, hist_ref, up_ref, down_ref = outs
-    copies = [
-        pltpu.make_async_copy(source, target, sems.at[at])
-        for at, (source, target) in enumerate(zip(sources, targets))
-    ]
+    rows, cols = targets[2].shape
+    copies = []
+    for at, (source, target) in enumerate(zip(sources, targets)):
+        if at == 8:
+            source = source.at[:, pl.ds(0, rows), :]
+        copies.append(pltpu.make_async_copy(source, target, sems.at[at]))
     for copy in copies:
         copy.start()
-    for copy in copies:
+    for copy in copies[2:]:
         copy.wait()
-    state_ref, control_ref, depth_ref, spread_ref, step_ref, change_ref = targets
-    rows, cols = depth_ref.shape
+    (
+        state_ref, control_ref, depth_ref, spread_ref, step_ref, change_ref, damping_ref, weight_ref,
+        observed_ref,
+    ) = targets
     count = step_ref.shape[0] // (2 * rows)
     pairs = 2 * count
-    near, second = state_rows(levels)
+    near, second, surface, distant = row_layout(levels, pairs)
     hist = SUB * near
-    up_hist_ref = up_ref.at[pl.ds(hist, up_ref.shape[0] - hist)]
-    down_hist_ref = down_ref.at[pl.ds(hist, down_ref.shape[0] - hist)]
-    far = SUB * 2 * pairs
+    far = hist + SUB * pairs
     depth = depth_ref[...].astype(F32)
     spread = spread_ref[...]
     wet = depth > 0.5
+    total = jnp.zeros((rows, cols), F32)
+    for level in range(levels):
+        total = total + jnp.where(level < depth, weight_ref[pl.ds(level * rows, rows), :], 0.0)
+    fields = [
+        damping_ref[...],
+        2.0 * total,
+        weight_ref[pl.ds(0, rows), :],
+        observed_ref[0],
+        observed_ref[1],
+    ]
+    for ref in (up_ref, down_ref):
+        ref[pl.ds(ref.shape[0] - 8, 8), :] = jnp.zeros((8, cols), F32)
+
+    def near_of(row):
+        if row < SUB:
+            return [(down_ref, row)]
+        return [(up_ref, row - rows + SUB)] if row >= rows - SUB else []
+
+    def far_of(row):
+        result = []
+        if SUB <= row < REACH:
+            result.append((down_ref, far + (row - SUB) * distant))
+        if rows - REACH <= row < rows - SUB:
+            result.append((up_ref, far + (row - rows + REACH) * distant))
+        return result
+
     for row in range(rows):
         here = slice(row, row + 1)
-        distant = []
         targets = [(hist_ref.at[row], 0)]
-        if row < SUB:
-            targets.append((down_hist_ref, row * 2 * pairs))
-        elif row < REACH:
-            distant.append((down_hist_ref, far + (row - SUB) * pairs))
-        if row >= rows - SUB:
-            targets.append((up_hist_ref, (row - rows + SUB) * 2 * pairs))
-        elif row >= rows - REACH:
-            distant.append((up_hist_ref, far + (row - rows + REACH) * pairs))
+        targets += [(ref, hist + at * pairs) for ref, at in near_of(row)] + far_of(row)
         for which, ref in enumerate((step_ref, change_ref)):
             both = [ref[pl.ds(tracer * rows + row, count, stride=2 * rows), :] for tracer in range(2)]
             apart = jnp.where(wet[here], both[0] - both[1], 0.0)
-            joint = jnp.where(wet[here], both[0] + both[1], 0.0)
             for target, at in targets:
                 target[pl.ds(at + which * count, count), :] = apart
-                target[pl.ds(at + pairs + which * count, count), :] = joint
-            for target, at in distant:
-                target[pl.ds(at + which * count, count), :] = apart
+        for target, at in far_of(row):
+            target[pl.ds(at + pairs, 1), :] = jnp.where(wet[here], spread[here], 0.0)
+        for target, at in near_of(row):
+            for field in range(5):
+                target[pl.ds(at * near + surface + field, 1), :] = fields[field][here]
+    for copy in copies[:2]:
+        copy.wait()
     first = iota((levels, cols), 0) == 0
     rest = jnp.zeros((padded - levels, cols), F32)
-    fill = jnp.zeros((near - 2 * levels - 2, cols), F32)
     for row in range(rows):
         here = slice(row, row + 1)
         targets = [(rows_ref.at[row], 0, padded)]
-        if row < SUB:
-            targets.append((down_ref, row * near, second))
-        if row >= rows - SUB:
-            targets.append((up_ref, (row - rows + SUB) * near, second))
+        targets += [(ref, at * near, second) for ref, at in near_of(row)]
         for tracer in range(2):
             lift = jnp.where(wet[here], control_ref[tracer, here, :], 0.0)
             value = state_ref[tracer, pl.ds(row, levels, stride=rows), :]
             value = value + jnp.where(first, lift, 0.0)
             for target, at, offset in targets:
                 target[pl.ds(at + tracer * offset, levels), :] = value
+            for target, at in far_of(row):
+                target[pl.ds(at + pairs + 1 + tracer, 1), :] = value[0:1]
             rows_ref[row, pl.ds(tracer * padded + levels, padded - levels), :] = rest
         for target, at, _ in targets:
             target[pl.ds(at + levels, 1), :] = spread[here]
             target[pl.ds(at + levels + 1, 1), :] = depth[here]
-        for target, at, _ in targets[1:]:
-            target[pl.ds(at + 2 * levels + 2, near - 2 * levels - 2), :] = fill
+        for field in range(4):
+            rows_ref[row, pl.ds(levels + 2 + field, 1), :] = fields[field][here]
+        rows_ref[row, pl.ds(padded + levels, 1), :] = fields[4][here]
 
 
 def edge_of(rows_of, indices, cols, lat):
@@ -125,10 +149,7 @@
     return total
 
 
-def pairs_kernel(
-    rows_ref, step_ref, change_ref, depth_ref, spread_ref, damping_ref, weight_ref,
-    edge_ref, still_ref, own_ref, gram_ref,
-):
+def pairs_kernel(levels, rows_ref, step_ref, change_ref, edge_ref, still_ref, depth_ref, gram_ref):
     rows, _, cols = rows_ref.shape
     lat = lax.axis_index("lat")
     count = step_ref.shape[0]
@@ -144,22 +165,16 @@
                     gram[j] = gram[j] + jnp.where(lane == at + i, value, 0.0)
         at += count
     for i in range(count):
-        gram_ref[pl.ds(i, 1), :] = gram[i]
-    depth = depth_ref[...]
-    total = jnp.zeros((rows, cols), F32)
-    for level in range(weight_ref.shape[0] // rows):
-        total = total + jnp.where(level < depth, weight_ref[pl.ds(level * rows, rows), :], 0.0)
-    fields = (
-        jnp.where(depth > 0, spread_ref[...], 0.0),
-        damping_ref[...],
-        2.0 * total,
-        weight_ref[pl.ds(0, rows), :],
-        gram_ref[...],
-    )
-    for at, field in enumerate(fields):
-        own_ref[at] = field
-        for copy in range(still_ref.shape[0]):
-            still_ref[copy, at] = field
+        gram_ref[3, pl.ds(i, 1), :] = gram[i]
+    for row in range(rows):
+        plane = lambda at: rows_ref[row, pl.ds(levels + at, 1), :]
+        here = pl.ds(row, 1)
+        depth_ref[here, :] = plane(1)
+        gram_ref[0, here, :] = jnp.where(plane(1) > 0.5, plane(0), 0.0)
+        gram_ref[1, here, :] = plane(2)
+        gram_ref[2, here, :] = plane(3)
+    for copy in range(still_ref.shape[0]):
+        still_ref[copy] = gram_ref[...]
     edge_ref[...] = edge_of(lambda i: rows_ref[i - SUB], range(SUB, rows + SUB), cols, lat)
 
 
@@ -190,32 +205,25 @@
     )
 
 
-def gathered_near(mine_ref, other_ref, field):
-    loops = mine_ref.shape[0]
-    parts = []
-    for shift in (loops - 1, 0, 1):
-        at = lax.rem(lax.axis_index("loop") + shift, loops)
-        parts.append(jnp.concatenate([mine_ref[at, field], other_ref[at, field]], axis=1))
-    return jnp.concatenate(parts, axis=0)
-
-
-def plan_kernel(mine_ref, other_ref, faces_ref, near_ref, plan_ref):
+def surface_outflow(value, to_below, to_above, to_right, to_left):
+    height, width = value.shape
+    result = to_right * (value - pltpu.roll(value, width - 1, 1))
+    result = result + to_left * (value - pltpu.roll(value, 1, 1))
+    result = result + to_below * (value - pltpu.roll(value, height - 1, 0))
+    return result + to_above * (value - pltpu.roll(value, 1, 0))
+
+
+def plan_kernel(mine_ref, other_ref, faces_ref, plan_ref):
     loops, _, rows, cols = mine_ref.shape
     closed = closed_lane(cols)
     for at, face in enumerate(surface_faces(gathered(mine_ref, other_ref, 0), closed)):
         faces_ref[at] = SURFACE_GAIN * face
     for field in (1, 2):
         faces_ref[3 + field] = gathered(mine_ref, other_ref, field)
-    spread = gathered_near(mine_ref, other_ref, 0)
-    for at, face in enumerate(surface_faces(spread, closed)):
-        near_ref[at] = face
-    near_ref[4] = jnp.where(spread > 0.0, gathered_near(mine_ref, other_ref, 3), 0.0)
-    near_ref[5] = jnp.where(spread > 0.0, 1.0, 0.0)
-
     count = plan_ref.shape[0] // 2
-    gram = mine_ref[0, 4] + other_ref[0, 4]
+    gram = mine_ref[0, 3] + other_ref[0, 3]
     for i in range(1, loops):
-        gram = gram + (mine_ref[i, 4] + other_ref[i, 4])
+        gram = gram + (mine_ref[i, 3] + other_ref[i, 3])
     wide = (count, cols)
     step_change = [jnp.broadcast_to(gram[:, i : i + 1], wide) for i in range(count)]
     change_change = [
@@ -244,13 +252,14 @@
 
 
 def border_kernel(
-    levels, padded, edge_ref, low_ref, high_ref, hist_ref, out_ref, halo_ref
+    levels, padded, edge_ref, low_ref, high_ref, rows_ref, hist_ref, out_ref, halo_ref
 ):
     planes, cols = edge_ref.shape
-    rows = hist_ref.shape[0]
-    pairs = hist_ref.shape[1] // 2
+    rows, pairs, _ = hist_ref.shape
     lat = lax.axis_index("lat")
-    near, second = state_rows(levels)
+    near, second, surface, distant = row_layout(levels, pairs)
+    hist = SUB * near
+    far = hist + SUB * pairs
     rest = jnp.zeros((padded - levels, cols), F32)
     for i in range(2 * SUB):
         ref = low_ref if i < SUB else high_ref
@@ -263,70 +272,101 @@
     out_ref[pl.ds(0, planes), :] = total + edge_of(
         lambda i: halo_ref[i - rows], range(rows + SUB, rows + 2 * SUB), cols, lat
     )
-    start = SUB * near
-    far = start + SUB * 2 * pairs
-    ahead = REACH - SUB
-    apart = planes
-    joint = apart + (rows + 2 * REACH) * pairs
-    for i in range(rows + 2 * REACH):
-        at = i - REACH
-        target = pl.ds(apart + i * pairs, pairs)
-        if at < -SUB:
-            out_ref[target, :] = low_ref[pl.ds(far + i * pairs, pairs), :]
-            continue
-        if at >= rows + SUB:
-            out_ref[target, :] = high_ref[pl.ds(far + (at - rows - SUB) * pairs, pairs), :]
-            continue
-        if at < 0:
-            ref, here = low_ref, start + (at + SUB) * 2 * pairs
-        elif at < rows:
-            ref, here = hist_ref.at[at], 0
+    tall = 3 * rows
+    fields = planes + (rows + 2 * REACH) * pairs
+    out_ref[pl.ds(fields, 8 * tall), :] = jnp.zeros((8 * tall, cols), F32)
+    for at in range(-REACH, rows + REACH):
+        if 0 <= at < rows:
+            ref, apart = hist_ref.at[at], 0
+        elif -SUB <= at < rows + SUB:
+            ref, index = (low_ref, at + SUB) if at < 0 else (high_ref, at - rows)
+            apart = hist + index * pairs
         else:
-            ref, here = high_ref, start + (at - rows) * 2 * pairs
-        out_ref[target, :] = ref[pl.ds(here, pairs), :]
-        target = pl.ds(joint + (i - ahead) * pairs, pairs)
-        out_ref[target, :] = ref[pl.ds(here + pairs, pairs), :]
-
-
-def basis_kernel(planes, rows, pairs, mine_ref, other_ref, still_ref, still_other_ref, out_ref, *work):
+            ref, index = (low_ref, at + REACH) if at < 0 else (high_ref, at - rows - SUB)
+            apart = far + index * distant
+        out_ref[pl.ds(planes + (at + REACH) * pairs, pairs), :] = ref[pl.ds(apart, pairs), :]
+        if 0 <= at < rows:
+            ref = rows_ref.at[at]
+            places = {0: levels, 6: 0, 7: padded, 5: padded + levels}
+            places.update({1 + field: levels + 2 + field for field in range(4)})
+            limit = levels + 1
+        elif -SUB <= at < rows + SUB:
+            start = index * near
+            places = {0: start + levels, 6: start, 7: start + second}
+            places.update({1 + field: start + surface + field for field in range(5)})
+            limit = start + levels + 1
+        else:
+            places = {0: apart + pairs, 6: apart + pairs + 1, 7: apart + pairs + 2}
+            limit = None
+        for field, place in places.items():
+            value = ref[pl.ds(place, 1), :]
+            if field == 0 and limit is not None:
+                value = jnp.where(ref[pl.ds(limit, 1), :] > 0.5, value, 0.0)
+            out_ref[pl.ds(fields + field * tall + at + rows, 1), :] = value
+
+
+def basis_kernel(
+    planes, rows, pairs, mine_ref, other_ref, step_ref, change_ref, _,
+    out_ref, near_ref, base_ref, first_ref, *work
+):
     cols = mine_ref.shape[1]
     width = 2 * cols
-    loops = still_ref.shape[0]
     tall = rows + 2 * REACH
     ahead = REACH - SUB
+    high = 3 * rows
     apart = planes
-    joint = apart + tall * pairs
-    opened = iota((1, width), 1) != closed_lane(cols)
+    fields = apart + tall * pairs
+    closed = closed_lane(cols)
+    opened = iota((1, width), 1) != closed
 
     def wide(at, size):
         return jnp.concatenate([mine_ref[pl.ds(at, size), :], other_ref[pl.ds(at, size), :]], axis=1)
 
-    near = [lax.rem(lax.axis_index("loop") + shift, loops) for shift in (loops - 1, 0, 1)]
-
-    def still(field, i):
-        block, row = divmod(i - REACH + rows, rows)
-        return jnp.concatenate(
-            [
-                ref[near[block], field, pl.ds(row, 1), :]
-                for ref in (still_ref, still_other_ref)
-            ],
-            axis=1,
-        )
-
     def left(value):
         return pltpu.roll(value, width - 1, 1)
 
     def right(value):
         return pltpu.roll(value, 1, 1)
 
-    spread = [still(0, i) for i in range(tall)]
+    def field(at):
+        return wide(fields + at * high, high)
+
+    def field_row(at, i):
+        return wide(fields + at * high + i - REACH + rows, 1)
+
+    faces = surface_faces(field(0), closed)
+    for at in range(4):
+        near_ref[at] = faces[at]
+    sea = jnp.where(field(0) > 0.0, 1.0, 0.0)
+    weight = field(3)
+    near_ref[4] = weight * sea
+    near_ref[5] = sea
+    value = [field(6), field(7)]
+    for sweep in range(SUB):
+        value = [part - surface_outflow(part, *faces) for part in value]
+    value = [weight * (value[0] - field(4)), weight * (value[1] - field(5))]
+    for sweep in range(SUB):
+        value = [part - surface_outflow(part, *faces) for part in value]
+    base = [(part * sea)[rows : 2 * rows, :cols] for part in value]
+    for tracer in range(2):
+        base_ref[tracer] = base[tracer]
+    lane = iota((1, cols), 1)
+    for i in range(pairs // 2):
+        total = jnp.zeros((1, cols), F32)
+        for at, ref in ((0, step_ref), (cols // 2, change_ref)):
+            part = ref[i, pl.ds(0, rows), :] * base[0] + ref[i, pl.ds(rows, rows), :] * base[1]
+            part = jnp.sum(part, axis=(0, 1), keepdims=True)
+            total = total + jnp.where(lane == at, part, 0.0)
+        first_ref[pl.ds(i, 1), :] = total
+
+    spread = [field_row(0, i) for i in range(tall)]
     to_right = [faces_between(value, left(value), opened) for value in spread]
     to_left = [right(value) for value in to_right]
     to_below = [faces_between(spread[i], spread[i + 1]) for i in range(tall - 1)]
     inner = range(ahead, tall - ahead)
-    damping = {i: (still(1, i) - SHIFT) * (1.0 / SPAN) for i in inner}
-    response_weight = {i: still(2, i) for i in inner}
-    weight = {i: still(3, i) for i in inner}
+    damping = {i: (field_row(1, i) - SHIFT) * (1.0 / SPAN) for i in inner}
+    response_weight = {i: field_row(2, i) for i in inner}
+    weight = {i: field_row(3, i) for i in inner}
     gain = SURFACE_GAIN / SPAN
 
     def outflow(get, i):
@@ -354,25 +394,18 @@
     def start_apart(i):
         return wide(apart + i * pairs, pairs)
 
-    def start_joint(i):
-        return wide(joint + (i - ahead) * pairs, pairs)
-
-    both = (start_apart, start_joint)
+    get = start_apart
     for sweep in range(SUB):
-        both = (
-            mixed(both[0], work[sweep], REACH - 1 - sweep),
-            mixed(both[1], work[SUB + sweep], SUB - 1 - sweep),
-        )
-    keep(0, both[1])
+        get = mixed(get, work[sweep], REACH - 1 - sweep)
     reach = REACH - SUB
-    powers = [both[0]]
+    powers = [get]
     for power in range(1, ITERS):
-        powers.append(applied(powers[-1], work[2 * SUB + power - 1], reach - power))
+        powers.append(applied(powers[-1], work[SUB + power - 1], reach - power))
     for power in range(ITERS):
-        keep(1 + power, powers[power])
+        keep(power, powers[power])
     reach = ITERS - 1
-    slot = 1 + ITERS
-    at = 2 * SUB + ITERS - 1
+    slot = ITERS
+    at = SUB + ITERS - 1
     chains = []
     for factor, power in [(weight, 0)] + [(response_weight, power) for power in range(ITERS)]:
         get = powers[power]
@@ -440,7 +473,7 @@
 
 def fields_kernel(
     levels, padded, scale,
-    rows_ref, main_ref, edge_ref, other_ref, weight_ref, observed_ref, basis_ref, still_ref,
+    rows_ref, main_ref, edge_ref, other_ref, weight_ref, observed_ref, basis_ref, first_ref,
     mixed_ref, fields_ref, part_ref,
 ):
     rows, _, cols = rows_ref.shape
@@ -523,64 +556,59 @@
         part_ref[1, here, :] = jnp.sum(
             jnp.where(wet, misfit[1] - misfit[0], 0.0), axis=0, keepdims=True
         )
-        part_ref[2, here, :] = misfit[0][0:1]
-        part_ref[3, here, :] = misfit[1][0:1]
     sums = [None] * FUNCTIONALS
 
     def add(at, slot, row, factor):
         value = basis_ref[slot, row] * factor
         sums[at] = value if sums[at] is None else sums[at] + value
 
-    chain = 1 + ITERS
     for row in range(rows):
         here = pl.ds(row, 1)
-        get = lambda field: part_ref[field, here, :]
-        still = lambda field: still_ref[field, here, :]
-        surface, base = get(0), get(1)
-        add(0, 0, row, 0.5 * (get(2) + get(3)))
-        add(0, 1, row, 0.5 * (get(2) - get(3)))
-        add(1, 1, row, still(3) * surface)
+        surface, base = part_ref[0, here, :], part_ref[1, here, :]
+        fixed = lambda plane: rows_ref[row, pl.ds(levels + plane, 1), :]
+        add(1, 0, row, fixed(4) * surface)
         for power in range(1, ITERS):
-            add(1 + power, chain + power - 1, row, surface)
+            add(1 + power, ITERS + power - 1, row, surface)
         for j in range(ITERS):
-            add(1 + ITERS + j, 1 + j, row, base)
+            add(1 + ITERS + j, j, row, base)
             at = 1 + 2 * ITERS + j * ITERS
-            add(at, 1 + j, row, still(2) * surface)
+            add(at, j, row, fixed(3) * surface)
             for power in range(1, ITERS):
-                add(at + power, chain + (1 + j) * (ITERS - 1) + power - 1, row, surface)
+                add(at + power, ITERS + (1 + j) * (ITERS - 1) + power - 1, row, surface)
     half = pairs // 2
-    total = jnp.zeros((half, cols), F32)
-    for at in range(FUNCTIONALS):
+    total = first_ref[...]
+    for at in range(1, FUNCTIONALS):
         value = jnp.sum(sums[at], axis=1, keepdims=True)
         total = total + jnp.where(lane == at, value[:half], 0.0)
         total = total + jnp.where(lane == cols // 2 + at, value[half:], 0.0)
-    part_ref[4] = total
+    part_ref[2] = total
     for copy in range(fields_ref.shape[0]):
         fields_ref[copy] = part_ref[...]
 
 
 def solve_kernel(
     levels, scale,
-    mine_ref, other_ref, faces_ref, near_ref, plan_ref, mixed_ref, depth_ref, step_ref, change_ref,
-    state_ref, gradient_ref, direction_ref, kept_ref,
+    mine_ref, other_ref, faces_ref, near_ref, base_ref, plan_ref, mixed_ref, depth_ref, step_ref,
+    change_ref, state_ref, gradient_ref, direction_ref, kept_ref,
 ):
     loops, _, rows, cols = mine_ref.shape
     loop = lax.axis_index("loop")
 
     def total(value):
-        return jnp.sum(value, axis=(0, 1), keepdims=True)
-
-    def outflow(value, to_below, to_above, to_right, to_left):
-        height, width = value.shape
-        result = to_right * (value - pltpu.roll(value, width - 1, 1))
-        result = result + to_left * (value - pltpu.roll(value, 1, 1))
-        result = result + to_below * (value - pltpu.roll(value, height - 1, 0))
-        return result + to_above * (value - pltpu.roll(value, 1, 0))
+        parts = [
+            value[i * rows : (i + 1) * rows, j * cols : (j + 1) * cols]
+            for i in range(loops)
+            for j in range(2)
+        ]
+        while len(parts) > 1:
+            half = (len(parts) + 1) // 2
+            parts = [a + b for a, b in zip(parts, parts[half:])] + parts[len(parts) - half : half]
+        return jnp.sum(jnp.sum(parts[0], axis=1, keepdims=True), axis=0, keepdims=True)
 
     count = step_ref.shape[0]
-    inner = mine_ref[0, 4] + other_ref[0, 4]
+    inner = mine_ref[0, 2] + other_ref[0, 2]
     for i in range(1, loops):
-        inner = inner + (mine_ref[i, 4] + other_ref[i, 4])
+        inner = inner + (mine_ref[i, 2] + other_ref[i, 2])
     plan = plan_ref[...]
     shifted = pltpu.roll(inner, cols // 2, 1)
     linear = None
@@ -603,7 +631,7 @@
         search_of = [one]
         solution_of = []
         for sweep in range(ITERS):
-            image = damping * search + outflow(search, *gained)
+            image = damping * search + surface_outflow(search, *gained)
             alpha = norm_now / total(search * image)
             solution = solution + alpha * search
             solution_of = add_up(solution_of, alpha, search_of)
@@ -627,20 +655,25 @@
                 result[at] = value if result[at] is None else result[at] + value
         return result
 
-    def keep(slot, value):
+    def near(slot, value):
         for i in range(loops):
             kept_ref[slot, i] = value[i * rows : (i + 1) * rows]
-
-    def kept_around(slot):
         return jnp.concatenate(
             [kept_ref[slot, lax.rem(loop + shift, loops)] for shift in (loops - 1, 0, 1)], axis=0
         )
 
     elevation, elevation_of = conjugate(gathered(mine_ref, other_ref, 0))
-    keep(0, elevation)
     pressure = gathered(mine_ref, other_ref, 1) + faces_ref[5] * elevation
+    elevation = near(0, elevation)
+    depth = depth_ref[...]
+    here = elevation[rows : 2 * rows, :cols]
+    for level in range(levels):
+        at = pl.ds(level * rows, rows)
+        change = jnp.where(level < depth, here, 0.0)
+        state_ref[0, at, :] = mixed_ref[0, at, :] - change
+        state_ref[1, at, :] = mixed_ref[1, at, :] + change
     response, response_of = conjugate(pressure)
-    keep(1, response)
+    response = near(1, response)
 
     lane = iota((1, cols), 1)
     factor = jnp.where(lane == 0, 1.0, 0.0)
@@ -656,20 +689,15 @@
         jnp.broadcast_to(weights[i : i + 1], (rows, cols)) for i in range(2 * count)
     ]
 
-    elevation = kept_around(0)
-    lowered = near_ref[4] * elevation
     sea = near_ref[5]
-    raised = (scale * sea) * kept_around(1)
-    near = [near_ref[i] for i in range(4)]
-    carried = [
-        gathered_near(mine_ref, other_ref, 2) - lowered + raised,
-        gathered_near(mine_ref, other_ref, 3) + lowered - raised,
-    ]
+    carried = near_ref[4] * elevation - (scale * sea) * response
+    faces = [near_ref[i] for i in range(4)]
     for sweep in range(SUB):
-        carried = [value - outflow(value, *near) for value in carried]
+        carried = carried - surface_outflow(carried, *faces)
+    carried = (sea * carried)[rows : 2 * rows, :cols]
     for tracer in range(2):
         at = pl.ds(tracer * rows, rows)
-        gradient = jnp.where(sea > 0.0, carried[tracer], 0.0)[rows : 2 * rows, :cols]
+        gradient = base_ref[tracer] - carried if tracer == 0 else base_ref[tracer] + carried
         gradient_ref[tracer] = gradient
         value = gamma * gradient
         for i in range(count):
@@ -677,21 +705,13 @@
             value = value + weights[count + i] * change_ref[i, at, :]
         direction_ref[tracer] = value
 
-    depth = depth_ref[...]
-    here = elevation[rows : 2 * rows, :cols]
-    for level in range(levels):
-        at = pl.ds(level * rows, rows)
-        change = jnp.where(level < depth, here, 0.0)
-        state_ref[0, at, :] = mixed_ref[0, at, :] - change
-        state_ref[1, at, :] = mixed_ref[1, at, :] + change
-
 
 def on_device(
     state, observed, weight, control, depth_index, diffusivity, damping, history_step, history_change
 ):
     _, levels, rows, cols = state.shape
     count = history_step.shape[0]
-    padded = round_up(levels + 2, 8)
+    padded = round_up(levels + 6, 8)
     planes = 2 * padded
     loops = lax.axis_size("loop")
     lats = lax.axis_size("lat")
@@ -707,17 +727,18 @@
     pairs = 2 * count
     inputs = (
         state, control, depth_index, diffusivity,
-        history_step.reshape(-1, cols), history_change.reshape(-1, cols),
+        history_step.reshape(-1, cols), history_change.reshape(-1, cols), damping, weight, observed,
     )
-    states = SUB * state_rows(levels)[0]
-    sent = (states + (SUB + REACH) * pairs, cols)
-    shapes = ((rows, planes, cols), (rows, 2 * pairs, cols), sent, sent)
+    held = [x.shape for x in inputs[:-1]] + [(2, rows, cols)]
+    near, _, _, distant = row_layout(levels, pairs)
+    sent = (round_up(SUB * (near + pairs) + (REACH - SUB) * distant, 8), cols)
+    shapes = ((rows, planes, cols), (rows, pairs, cols), sent, sent)
     packed, hist, up, down = pl.pallas_call(
         functools.partial(pack_kernel, levels, padded),
         out_shape=[jax.ShapeDtypeStruct(shape, F32) for shape in shapes],
         in_specs=[pl.BlockSpec(memory_space=pltpu.HBM)] * len(inputs),
         out_specs=[VMEM] * len(shapes),
-        scratch_shapes=[pltpu.VMEM(x.shape, x.dtype) for x in inputs]
+        scratch_shapes=[pltpu.VMEM(shape, x.dtype) for shape, x in zip(held, inputs)]
         + [pltpu.SemaphoreType.DMA((len(inputs),))],
         compiler_params=pltpu.CompilerParams(vmem_limit_bytes=VMEM_BYTES),
         name="pack",
@@ -727,27 +748,24 @@
     swap = [(0, 1), (1, 0)]
     low = lax.ppermute(up, "loop", forward)
     high = lax.ppermute(down, "loop", backward)
-    edge, still, still_own, _ = call(
-        pairs_kernel,
-        [(planes, cols), (loops, 5, rows, cols), (5, rows, cols), (count, cols)],
+    edge, still, depth, _ = call(
+        functools.partial(pairs_kernel, levels),
+        [(planes, cols), (loops, 4, rows, cols), (rows, cols), (4, rows, cols)],
         name="pairs",
-    )(packed, step, change, depth_index, diffusivity, damping, weight)
+    )(packed, step, change)
     still = lax.all_to_all(still, "loop", 0, 0)
     still_other = lax.ppermute(still, "lat", swap)
     height = loops * rows
     large = VMEM_BYTES if loops <= 16 else 2 * VMEM_BYTES
-    faces, near, plan = call(
-        plan_kernel,
-        [(6, height, 2 * cols), (6, 3 * rows, 2 * cols), (pairs, cols)],
-        vmem=large,
-        name="plan",
+    faces, plan = call(
+        plan_kernel, [(6, height, 2 * cols), (pairs, cols)], vmem=large, name="plan"
     )(still, still_other)
-    swapped = planes + (rows + 2 * REACH + rows + 2 * SUB) * pairs
+    swapped = planes + (rows + 2 * REACH) * pairs + 8 * 3 * rows
     border, halo = call(
         functools.partial(border_kernel, levels, padded),
         [(swapped, cols), (2 * SUB, planes, cols)],
         name="border",
-    )(edge, low, high, hist)
+    )(edge, low, high, packed, hist)
     other = lax.ppermute(border, "lat", swap)
     tall = rows + 2 * SUB
     (mixed,) = call(
@@ -758,28 +776,38 @@
         name="mix",
     )(packed, halo)
     chains = 1 + ITERS
-    buffers = 2 * SUB + ITERS - 1 + chains * (ITERS - 1)
-    (basis,) = call(
+    buffers = SUB + ITERS - 1 + chains * (ITERS - 1)
+    shapes = (
+        (ITERS + chains * (ITERS - 1), rows, pairs, cols),
+        (6, 3 * rows, 2 * cols),
+        (2, rows, cols),
+        (count, cols),
+    )
+    basis, around, base, first = pl.pallas_call(
         functools.partial(basis_kernel, planes, rows, pairs),
-        [(1 + ITERS + chains * (ITERS - 1), rows, pairs, cols)],
-        scratch=[pltpu.VMEM((rows + 2 * REACH, pairs, 2 * cols), F32)] * buffers,
+        out_shape=[jax.ShapeDtypeStruct(shape, F32) for shape in shapes],
+        in_specs=[VMEM] * 4 + [pl.BlockSpec(memory_space=pl.ANY)],
+        out_specs=[VMEM] * len(shapes),
+        scratch_shapes=[pltpu.VMEM((rows + 2 * REACH, pairs, 2 * cols), F32)] * buffers,
+        compiler_params=pltpu.CompilerParams(vmem_limit_bytes=VMEM_BYTES),
         name="basis",
-    )(border, other, still, still_other)
+    )(border, other, step, change, still_other)
     mixed, fields = call(
         functools.partial(fields_kernel, levels, padded, scale),
-        [flat, (loops, 5, rows, cols)],
-        scratch=[pltpu.VMEM((5, rows, cols), F32)],
+        [flat, (loops, 3, rows, cols)],
+        scratch=[pltpu.VMEM((3, rows, cols), F32)],
         name="fields",
-    )(packed, mixed, border, other, weight, observed, basis, still_own)
+    )(packed, mixed, border, other, weight, observed, basis, first)
     mine = lax.all_to_all(fields, "loop", 0, 0)
     theirs = lax.ppermute(mine, "lat", swap)
+    shapes = (flat, (2, rows, cols), (2, rows, cols))
     state_next, gradient, direction = call(
         functools.partial(solve_kernel, levels, scale),
-        [flat, (2, rows, cols), (2, rows, cols)],
+        shapes,
         scratch=[pltpu.VMEM((2, loops, rows, 2 * cols), F32)],
         vmem=large,
         name="solve",
-    )(mine, theirs, faces, near, plan, mixed, depth_index, step, change)
+    )(mine, theirs, faces, around, base, plan, mixed, depth, step, change)
     return (state_next.reshape(2, levels, rows, cols), gradient, direction)
 
 

time: 40.7 us -> 38.9 us (0.956)
  blocking collectives: 11.9 us -> 10.8 us
    ppermute x1, waiting for transfers between devices: 3.93 us -> 2.77 us  [on_device(): low = lax.ppermute(up, 'loop', forward)]
    all_to_all x1, blocking collectives: 11.9 us -> 10.8 us  [on_device(): mine = lax.all_to_all(fields, 'loop', 0, 0)]
    all_to_all x1, waiting for transfers between devices: 0.93 us -> 1.7 us  [on_device(): still = lax.all_to_all(still, 'loop', 0, 0)]
    pallas_call x4, Pallas kernels: 5.94 us -> 5.52 us  [the longest x1 2.58 us: on_device(): call(functools.partial(solve_kernel, levels, scale), shapes, scratch=[plt...]
where the time goes in v7:
time: 38.9 us; the launch traced here: 38.6 us
  blocking collectives  10.8 us (28%)
  starting transfers between devices  9.54 us (25%)
  Pallas kernels  9.21 us (24%)
  waiting for transfers between devices  8.26 us (21%)
  between operations  0.74 us (2%)
    all_to_all x1, blocking collectives, on_device(): mine = lax.all_to_all(fields, 'loop', 0, 0)  10.8 us
    all_to_all x1, starting transfers between devices, on_device(): still = lax.all_to_all(still, 'loop', 0, 0)  3.37 us
    ppermute x1, starting transfers between devices, on_device(): high = lax.ppermute(down, 'loop', backward)  3.1 us
    ppermute x1, starting transfers between devices, on_device(): low = lax.ppermute(up, 'loop', forward)  2.99 us
    ppermute x1, waiting for transfers between devices, on_device(): low = lax.ppermute(up, 'loop', forward)  2.77 us
    pallas_call x1, Pallas kernels, on_device(): call(functools.partial(solve_kernel, levels, scale), shapes, scratch=[plt...  2.58 us
    ppermute x1, waiting for transfers between devices, on_device(): high = lax.ppermute(down, 'loop', backward)  2.51 us
    pallas_call x1, Pallas kernels, on_device(): pl.pallas_call(functools.partial(basis_kernel, planes, rows, pairs), out_...  1.82 us
  transfers between devices with their start and end apart: 6, of which 5 were waited for; matrix products, arithmetic and copies ran while one was open for 0% of the time, Pallas kernels for 6%

profile of v7, /device:TPU:0, one launch (start us, length us, event | category | flops | bytes accessed | tf_op | source)
XLA Modules:
  0.0 38.6 jit_solution(4932919507653640360)
XLA Ops:
  0.6 0.0 copy-start.1
  0.7 1.5 %pack.1 = (f32[8,112,128]{2,1,0:T(8,128)S(1)}, f32[8,16,128]{2,1,0:T(8,128)S(1)}, f32[448,128]{1,0:T(8,128)S(1)}, f32[448,128]{1,0:T(8,128)S(1)}) custom-call(f32[2,400,128]{2,1,0:T(8,128)} %bitcast.20, f32[2,8,128]{2,1,0:T(8,128)} %refs_1_.1, s32[8,128]{1,0:T(8,128)} %refs_2_.1, f32[8,128]{1,0:T(8,128)} %refs_3_.1, f32[128,128]{1,0:T(8,128)} %bitcast.10, ...), custom_call_target="tpu_custom_call" | custom-call | tf_op jit(solution)/shard_map/pack/pallas_call | solution.py:736
  2.1 3.0 %collective-permute-start = (f32[448,128]{1,0:T(8,128)S(1)}, f32[448,128]{1,0:T(8,128)S(1)}, u32[]{:S(2)}, u32[]{:S(2)}) collective-permute-start(f32[448,128]{1,0:T(8,128)S(1)} %get-tuple-element.25), channel_id=1, source_target_pairs={{0,2},{2,4},{4,6},{6,8},{8,10},{10,12},{12,14},{14,0},{1,3},{3,5},... | collective-permute-start | bytes 688136 | tf_op jit(solution)/shard_map/ppermute | solution.py:749
  5.1 3.1 %collective-permute-start.1 = (f32[448,128]{1,0:T(8,128)S(1)}, f32[448,128]{1,0:T(8,128)S(1)}, u32[]{:S(2)}, u32[]{:S(2)}) collective-permute-start(f32[448,128]{1,0:T(8,128)S(1)} %get-tuple-element.26), channel_id=1, source_target_pairs={{2,0},{4,2},{6,4},{8,6},{10,8},{12,10},{14,12},{0,14},{3,1},{5,3},... | collective-permute-start | bytes 688136 | tf_op jit(solution)/shard_map/ppermute | solution.py:750
  8.2 0.9 %pairs.1 = (f32[112,128]{1,0:T(8,128)S(1)}, f32[8,4,8,128]{3,2,1,0:T(8,128)}, f32[8,128]{1,0:T(8,128)S(1)}, f32[4,8,128]{2,1,0:T(8,128)}) custom-call(f32[8,112,128]{2,1,0:T(8,128)S(1)} %get-tuple-element.23.rows_ref, f32[8,16,128]{2,1,0:T(8,128)S(1)} %bitcast.11, f32[8,16,128]{2,1,0:T(8,128)S(1)} %bitcast.15), custom_call_target="tpu_custom_call" | custom-call | tf_op jit(solution)/shard_map/pairs/pallas_call | solution.py:751
  9.1 3.4 %all-to-all-start = ((f32[8,4,8,128]{3,2,1,0:T(8,128)}), f32[8,4,8,128]{3,2,1,0:T(8,128)S(1)}, u32[]{:S(2)}, u32[]{:S(2)}) async-start(f32[8,4,8,128]{3,2,1,0:T(8,128)} %get-tuple-element.30), calls=%async_computation | async-start | bytes 262144 | tf_op jit(solution)/shard_map/all_to_all | solution.py:756
  12.5 2.8 %collective-permute-done.low_ref = f32[448,128]{1,0:T(8,128)S(1)} collective-permute-done((f32[448,128]{1,0:T(8,128)S(1)}, f32[448,128]{1,0:T(8,128)S(1)}, u32[]{:S(2)}, u32[]{:S(2)}) %collective-permute-start) | collective-permute-done | bytes 229408 | tf_op jit(solution)/shard_map/ppermute | solution.py:749
  15.3 2.5 %collective-permute-done.1.high_ref = f32[448,128]{1,0:T(8,128)S(1)} collective-permute-done((f32[448,128]{1,0:T(8,128)S(1)}, f32[448,128]{1,0:T(8,128)S(1)}, u32[]{:S(2)}, u32[]{:S(2)}) %collective-permute-start.1) | collective-permute-done | bytes 229408 | tf_op jit(solution)/shard_map/ppermute | solution.py:750
  17.8 0.2 border.1
  18.0 0.1 collective-permute-start.2
  18.1 1.7 %all-to-all-done.mine_ref = f32[8,4,8,128]{3,2,1,0:T(8,128)S(1)} async-done(((f32[8,4,8,128]{3,2,1,0:T(8,128)}), f32[8,4,8,128]{3,2,1,0:T(8,128)S(1)}, u32[]{:S(2)}, u32[]{:S(2)}) %all-to-all-start) | async-done | bytes 131104 | tf_op jit(solution)/shard_map/all_to_all | solution.py:756
  19.8 0.0 collective-permute-start.3
  19.8 1.1 %mix.1.main_ref = f32[8,112,128]{2,1,0:T(8,128)S(1)} custom-call(f32[8,112,128]{2,1,0:T(8,128)S(1)} %get-tuple-element.23.rows_ref, f32[6,112,128]{2,1,0:T(8,128)S(1)} %get-tuple-element.28.halo_ref), custom_call_target="tpu_custom_call" | custom-call | tf_op jit(solution)/shard_map/mix/pallas_call | solution.py:771
  20.9 0.0 copy-start
  21.0 0.0 copy-start.3
  21.0 0.2 collective-permute-done.3._.other_ref
  21.2 0.0 collective-permute-done.2.other_ref
  21.2 1.8 %basis.1 = (f32[11,8,16,128]{3,2,1,0:T(8,128)S(1)}, f32[6,24,256]{2,1,0:T(8,128)S(1)}, f32[2,8,128]{2,1,0:T(8,128)S(1)}, f32[8,128]{1,0:T(8,128)S(1)}) custom-call(f32[656,128]{1,0:T(8,128)S(1)} %get-tuple-element.29.mine_ref.edge_ref, f32[656,128]{1,0:T(8,128)S(1)} %collective-permute-done.2.other_ref, f32[8,16,128]{2,1,0:T(8,128)S(1)} %bitcast.12, ...), custom_call_target="tpu_custom_call" | custom-call | tf_op jit(solution)/shard_map/basis/pallas_call | solution.py:786
  23.0 0.9 %fields.1 = (f32[2,400,128]{2,1,0:T(8,128)S(1)}, f32[8,3,8,128]{3,2,1,0:T(8,128)S(1)}) custom-call(f32[8,112,128]{2,1,0:T(8,128)S(1)} %get-tuple-element.23.rows_ref, f32[8,112,128]{2,1,0:T(8,128)S(1)} %mix.1.main_ref, f32[656,128]{1,0:T(8,128)S(1)} %get-tuple-element.29.mine_ref.edge_ref, f32[656,128]{1,0:T(8,128)S(1)} %collective-permute-done.2.other_ref, ...), custom_call_target="tpu_custom_call" | custom-call | tf_op jit(solution)/shard_map/fields/pallas_call | solution.py:795
  23.9 10.8 %all_to_all.10.mine_ref = f32[8,3,8,128]{3,2,1,0:T(8,128)S(1)} all-to-all(f32[8,3,8,128]{3,2,1,0:T(8,128)S(1)} %get-tuple-element.33), channel_id=1, replica_groups=mesh['members'=2,'loop'=8,'lat'=2] {'loop'}, dimensions={0} | all-to-all | bytes 196608 | tf_op jit(solution)/shard_map/all_to_all | solution.py:801
  34.7 0.0 collective-permute-start.4
  34.7 0.2 plan.1
  34.9 1.1 %collective-permute-done.4.other_ref = f32[8,3,8,128]{3,2,1,0:T(8,128)S(1)} collective-permute-done((f32[8,3,8,128]{3,2,1,0:T(8,128)S(1)}, f32[8,3,8,128]{3,2,1,0:T(8,128)S(1)}, u32[]{:S(2)}, u32[]{:S(2)}) %collective-permute-start.4) | collective-permute-done | bytes 98336 | tf_op jit(solution)/shard_map/ppermute | solution.py:802
  36.0 2.6 %solve.1 = (f32[2,400,128]{2,1,0:T(8,128)}, f32[2,8,128]{2,1,0:T(8,128)}, f32[2,8,128]{2,1,0:T(8,128)}) custom-call(f32[8,3,8,128]{3,2,1,0:T(8,128)S(1)} %all_to_all.10.mine_ref, f32[8,3,8,128]{3,2,1,0:T(8,128)S(1)} %collective-permute-done.4.other_ref, f32[6,64,256]{2,1,0:T(8,128)S(1)} %get-tuple-element.34.faces_ref, ...), custom_call_target="tpu_custom_call" | custom-call | tf_op jit(solution)/shard_map/solve/pallas_call | solution.py:804
  (5 shorter events, 0.0 us)
Async XLA Ops:
  0.6 7.6 %copy-start.1 = (f32[8,2,8,128]{3,2,1,0:T(8,128)S(1)}, f32[8,2,8,128]{3,2,1,0:T(8,128)}, u32[]{:S(2)}) copy-start(f32[8,2,8,128]{3,2,1,0:T(8,128)} %param.16) | copy-start | bytes 196612
  0.6 7.6 %copy-start.2 = (f32[8,2,8,128]{3,2,1,0:T(8,128)S(1)}, f32[8,2,8,128]{3,2,1,0:T(8,128)}, u32[]{:S(2)}) copy-start(f32[8,2,8,128]{3,2,1,0:T(8,128)} %param.17) | copy-start | bytes 196612
  2.1 13.2 %collective-permute-start = (f32[448,128]{1,0:T(8,128)S(1)}, f32[448,128]{1,0:T(8,128)S(1)}, u32[]{:S(2)}, u32[]{:S(2)}) collective-permute-start(f32[448,128]{1,0:T(8,128)S(1)} %get-tuple-element.25), channel_id=1, source_target_pairs={{0,2},{2,4},{4,6},{6,8},{8,10},{10,12},{12,14},{14,0},{1,3},{3,5},... | collective-permute-start | bytes 688136 | tf_op jit(solution)/shard_map/ppermute | solution.py:749
  5.1 12.7 %collective-permute-start.1 = (f32[448,128]{1,0:T(8,128)S(1)}, f32[448,128]{1,0:T(8,128)S(1)}, u32[]{:S(2)}, u32[]{:S(2)}) collective-permute-start(f32[448,128]{1,0:T(8,128)S(1)} %get-tuple-element.26), channel_id=1, source_target_pairs={{2,0},{4,2},{6,4},{8,6},{10,8},{12,10},{14,12},{0,14},{3,1},{5,3},... | collective-permute-start | bytes 688136 | tf_op jit(solution)/shard_map/ppermute | solution.py:750
  9.1 10.7 %all-to-all-start = ((f32[8,4,8,128]{3,2,1,0:T(8,128)}), f32[8,4,8,128]{3,2,1,0:T(8,128)S(1)}, u32[]{:S(2)}, u32[]{:S(2)}) async-start(f32[8,4,8,128]{3,2,1,0:T(8,128)} %get-tuple-element.30), calls=%async_computation | async-start | bytes 262144 | tf_op jit(solution)/shard_map/all_to_all | solution.py:756
  18.0 3.1 %collective-permute-start.2 = (f32[656,128]{1,0:T(8,128)S(1)}, f32[656,128]{1,0:T(8,128)S(1)}, u32[]{:S(2)}, u32[]{:S(2)}) collective-permute-start(f32[656,128]{1,0:T(8,128)S(1)} %get-tuple-element.29.mine_ref.edge_ref), channel_id=1, source_target_pairs={{0,1},{1,0},{2,3},{3,2},{4,5},{5,4},{6,7},{7,6},{8,9},{9,8},{10,11... | collective-permute-start | bytes 1007624 | tf_op jit(solution)/shard_map/ppermute | solution.py:769
  19.8 1.3 %collective-permute-start.3 = (f32[8,4,8,128]{3,2,1,0:T(8,128)S(1)}, f32[8,4,8,128]{3,2,1,0:T(8,128)S(1)}, u32[]{:S(2)}, u32[]{:S(2)}) collective-permute-start(f32[8,4,8,128]{3,2,1,0:T(8,128)S(1)} %all-to-all-done.mine_ref), channel_id=1, source_target_pairs={{0,1},{1,0},{2,3},{3,2},{4,5},{5,4},{6,7},{7,6},{8,9},{9,8},{10,11... | collective-permute-start | bytes 393224 | tf_op jit(solution)/shard_map/ppermute | solution.py:757
  20.9 2.0 %copy-start = (f32[2,50,8,128]{3,2,1,0:T(8,128)S(1)}, f32[2,50,8,128]{3,2,1,0:T(8,128)}, u32[]{:S(2)}) copy-start(f32[2,50,8,128]{3,2,1,0:T(8,128)} %param.10) | copy-start | bytes 1228804
  21.0 2.0 %copy-start.3 = (f32[50,8,128]{2,1,0:T(8,128)S(1)}, f32[50,8,128]{2,1,0:T(8,128)}, u32[]{:S(2)}) copy-start(f32[50,8,128]{2,1,0:T(8,128)} %param.11) | copy-start | bytes 614404
  34.7 1.3 %collective-permute-start.4 = (f32[8,3,8,128]{3,2,1,0:T(8,128)S(1)}, f32[8,3,8,128]{3,2,1,0:T(8,128)S(1)}, u32[]{:S(2)}, u32[]{:S(2)}) collective-permute-start(f32[8,3,8,128]{3,2,1,0:T(8,128)S(1)} %all_to_all.10.mine_ref), channel_id=1, source_target_pairs={{0,1},{1,0},{2,3},{3,2},{4,5},{5,4},{6,7},{7,6},{8,9},{9,8},{10,11... | collective-permute-start | bytes 294920 | tf_op jit(solution)/shard_map/ppermute | solution.py:802

commit v8 on v7

--- a/solution.py
+++ b/solution.py
@@ -11,6 +11,7 @@
 SUB = 3
 SURFACE_GAIN = 5.0
 SLOT = 8
+WIDE_SLOT = 16
 REACH = SUB + 2 * (ITERS - 1)
 SHIFT = 5.0
 SPAN = 5.0
@@ -40,15 +41,17 @@
     return lax.broadcasted_iota(jnp.int32, shape, dim)
 
 
-def row_layout(levels, pairs):
-    second = levels + 2
-    surface = second + levels
-    return surface + 5, second, surface, pairs + 3
+def state_rows(levels):
+    return 2 * levels + 2, levels + 2
+
+
+def hist_rows(pairs):
+    return pairs + 8, pairs + 3
 
 
 def pack_kernel(levels, padded, *refs):
-    sources, outs, targets, sems = refs[:9], refs[9:13], refs[13:22], refs[22]
-    rows_ref, hist_ref, up_ref, down_ref = outs
+    sources, outs, targets, sems = refs[:9], refs[9:15], refs[15:24], refs[24]
+    rows_ref, hist_ref = outs[:2]
     rows, cols = targets[2].shape
     copies = []
     for at, (source, target) in enumerate(zip(sources, targets)):
@@ -65,9 +68,8 @@
     ) = targets
     count = step_ref.shape[0] // (2 * rows)
     pairs = 2 * count
-    near, second, surface, distant = row_layout(levels, pairs)
-    hist = SUB * near
-    far = hist + SUB * pairs
+    near, second = state_rows(levels)
+    close, distant = hist_rows(pairs)
     depth = depth_ref[...].astype(F32)
     spread = spread_ref[...]
     wet = depth > 0.5
@@ -81,59 +83,65 @@
         observed_ref[0],
         observed_ref[1],
     ]
-    for ref in (up_ref, down_ref):
-        ref[pl.ds(ref.shape[0] - 8, 8), :] = jnp.zeros((8, cols), F32)
-
-    def near_of(row):
-        if row < SUB:
-            return [(down_ref, row)]
-        return [(up_ref, row - rows + SUB)] if row >= rows - SUB else []
-
-    def far_of(row):
-        result = []
-        if SUB <= row < REACH:
-            result.append((down_ref, far + (row - SUB) * distant))
-        if rows - REACH <= row < rows - SUB:
-            result.append((up_ref, far + (row - rows + REACH) * distant))
-        return result
-
     for row in range(rows):
         here = slice(row, row + 1)
-        targets = [(hist_ref.at[row], 0)]
-        targets += [(ref, hist + at * pairs) for ref, at in near_of(row)] + far_of(row)
         for which, ref in enumerate((step_ref, change_ref)):
             both = [ref[pl.ds(tracer * rows + row, count, stride=2 * rows), :] for tracer in range(2)]
             apart = jnp.where(wet[here], both[0] - both[1], 0.0)
-            for target, at in targets:
-                target[pl.ds(at + which * count, count), :] = apart
-        for target, at in far_of(row):
-            target[pl.ds(at + pairs, 1), :] = jnp.where(wet[here], spread[here], 0.0)
-        for target, at in near_of(row):
-            for field in range(5):
-                target[pl.ds(at * near + surface + field, 1), :] = fields[field][here]
+            hist_ref[row, pl.ds(which * count, count), :] = apart
     for copy in copies[:2]:
         copy.wait()
     first = iota((levels, cols), 0) == 0
     rest = jnp.zeros((padded - levels, cols), F32)
     for row in range(rows):
         here = slice(row, row + 1)
-        targets = [(rows_ref.at[row], 0, padded)]
-        targets += [(ref, at * near, second) for ref, at in near_of(row)]
         for tracer in range(2):
             lift = jnp.where(wet[here], control_ref[tracer, here, :], 0.0)
             value = state_ref[tracer, pl.ds(row, levels, stride=rows), :]
             value = value + jnp.where(first, lift, 0.0)
-            for target, at, offset in targets:
-                target[pl.ds(at + tracer * offset, levels), :] = value
-            for target, at in far_of(row):
-                target[pl.ds(at + pairs + 1 + tracer, 1), :] = value[0:1]
+            rows_ref[row, pl.ds(tracer * padded, levels), :] = value
             rows_ref[row, pl.ds(tracer * padded + levels, padded - levels), :] = rest
-        for target, at, _ in targets:
-            target[pl.ds(at + levels, 1), :] = spread[here]
-            target[pl.ds(at + levels + 1, 1), :] = depth[here]
-        for field in range(4):
-            rows_ref[row, pl.ds(levels + 2 + field, 1), :] = fields[field][here]
+        for field, value in enumerate([spread, depth] + fields[:4]):
+            rows_ref[row, pl.ds(levels + field, 1), :] = value[here]
         rows_ref[row, pl.ds(padded + levels, 1), :] = fields[4][here]
+
+    even = lax.rem(lax.axis_index("loop"), 2) == 0
+
+    def put(refs, at, upper, lower):
+        here = pl.ds(at, upper.shape[0])
+        refs[0][here, :] = jnp.where(even, upper, lower)
+        refs[1][here, :] = jnp.where(even, lower, upper)
+
+    def fill(refs, last):
+        if last < refs[0].shape[0]:
+            rest = jnp.zeros((refs[0].shape[0] - last, cols), F32)
+            put(refs, last, rest, rest)
+
+    masked = jnp.where(wet, spread, 0.0)
+    for at in range(REACH):
+        far = at < REACH - SUB
+        index = at if far else at - (REACH - SUB)
+        upper = rows - REACH + at if far else rows - SUB + index
+        lower = SUB + index if far else index
+        start = SUB * close + index * distant if far else index * close
+        put(outs[2:4], start, hist_ref[upper], hist_ref[lower])
+        start = start + pairs
+        put(outs[2:4], start, masked[upper : upper + 1], masked[lower : lower + 1])
+        for tracer in range(2):
+            here = pl.ds(tracer * padded, 1)
+            put(outs[2:4], start + 1 + tracer, rows_ref[upper, here, :], rows_ref[lower, here, :])
+        if not far:
+            here = pl.ds(levels + 2, 4)
+            put(outs[2:4], start + 3, rows_ref[upper, here, :], rows_ref[lower, here, :])
+            here = pl.ds(padded + levels, 1)
+            put(outs[2:4], start + 7, rows_ref[upper, here, :], rows_ref[lower, here, :])
+    fill(outs[2:4], SUB * close + (REACH - SUB) * distant)
+    for at in range(SUB):
+        upper, lower = rows - SUB + at, at
+        for start, size, place in ((0, levels + 2, 0), (padded, levels, second)):
+            here = pl.ds(start, size)
+            put(outs[4:6], at * near + place, rows_ref[upper, here, :], rows_ref[lower, here, :])
+    fill(outs[4:6], SUB * near)
 
 
 def edge_of(rows_of, indices, cols, lat):
@@ -149,13 +157,13 @@
     return total
 
 
-def pairs_kernel(levels, rows_ref, step_ref, change_ref, edge_ref, still_ref, depth_ref, gram_ref):
+def pairs_kernel(levels, rows_ref, step_ref, change_ref, edge_ref, depth_ref, fixed_ref):
     rows, _, cols = rows_ref.shape
     lat = lax.axis_index("lat")
     count = step_ref.shape[0]
     lane = iota((1, cols), 1)
     gram = [jnp.zeros((1, cols), F32) for _ in range(count)]
-    at = 0
+    at = FUNCTIONALS
     for left_ref in (step_ref, change_ref):
         for i in range(count):
             for j in range(i, count):
@@ -165,16 +173,14 @@
                     gram[j] = gram[j] + jnp.where(lane == at + i, value, 0.0)
         at += count
     for i in range(count):
-        gram_ref[3, pl.ds(i, 1), :] = gram[i]
+        fixed_ref[3, pl.ds(i, 1), :] = gram[i]
     for row in range(rows):
         plane = lambda at: rows_ref[row, pl.ds(levels + at, 1), :]
         here = pl.ds(row, 1)
         depth_ref[here, :] = plane(1)
-        gram_ref[0, here, :] = jnp.where(plane(1) > 0.5, plane(0), 0.0)
-        gram_ref[1, here, :] = plane(2)
-        gram_ref[2, here, :] = plane(3)
-    for copy in range(still_ref.shape[0]):
-        still_ref[copy] = gram_ref[...]
+        fixed_ref[0, here, :] = jnp.where(plane(1) > 0.5, plane(0), 0.0)
+        fixed_ref[1, here, :] = plane(2)
+        fixed_ref[2, here, :] = plane(3)
     edge_ref[...] = edge_of(lambda i: rows_ref[i - SUB], range(SUB, rows + SUB), cols, lat)
 
 
@@ -216,19 +222,20 @@
 def plan_kernel(mine_ref, other_ref, faces_ref, plan_ref):
     loops, _, rows, cols = mine_ref.shape
     closed = closed_lane(cols)
-    for at, face in enumerate(surface_faces(gathered(mine_ref, other_ref, 0), closed)):
+    for at, face in enumerate(surface_faces(gathered(mine_ref, other_ref, 3), closed)):
         faces_ref[at] = SURFACE_GAIN * face
-    for field in (1, 2):
-        faces_ref[3 + field] = gathered(mine_ref, other_ref, field)
+    for field in (4, 5):
+        faces_ref[field] = gathered(mine_ref, other_ref, field)
     count = plan_ref.shape[0] // 2
-    gram = mine_ref[0, 3] + other_ref[0, 3]
+    gram = mine_ref[0, 2] + other_ref[0, 2]
     for i in range(1, loops):
-        gram = gram + (mine_ref[i, 3] + other_ref[i, 3])
+        gram = gram + (mine_ref[i, 2] + other_ref[i, 2])
     wide = (count, cols)
-    step_change = [jnp.broadcast_to(gram[:, i : i + 1], wide) for i in range(count)]
-    change_change = [
-        jnp.broadcast_to(gram[:, count + i : count + i + 1], wide) for i in range(count)
+    tables = [
+        jnp.broadcast_to(gram[:, i : i + 1], wide)
+        for i in range(FUNCTIONALS, FUNCTIONALS + 2 * count)
     ]
+    step_change, change_change = tables[:count], tables[count:]
     last = count - 1
     gamma = step_change[last][last:] / change_change[last][last:]
     rho = [1.0 / step_change[i][i : i + 1] for i in range(count)]
@@ -251,62 +258,92 @@
     plan_ref[pl.ds(0, 1), :] = jnp.where(at, -gamma, plan_ref[pl.ds(0, 1), :])
 
 
-def border_kernel(
-    levels, padded, edge_ref, low_ref, high_ref, rows_ref, hist_ref, out_ref, halo_ref
-):
+def received(first_ref, second_ref):
+    even = lax.rem(lax.axis_index("loop"), 2) == 0
+
+    def low(at, size):
+        here = pl.ds(at, size)
+        return jnp.where(even, second_ref[here, :], first_ref[here, :])
+
+    def high(at, size):
+        here = pl.ds(at, size)
+        return jnp.where(even, first_ref[here, :], second_ref[here, :])
+
+    return low, high
+
+
+def halo_kernel(levels, padded, rows, edge_ref, first_ref, second_ref, _, out_ref, halo_ref):
     planes, cols = edge_ref.shape
-    rows, pairs, _ = hist_ref.shape
     lat = lax.axis_index("lat")
-    near, second, surface, distant = row_layout(levels, pairs)
-    hist = SUB * near
-    far = hist + SUB * pairs
+    near, second = state_rows(levels)
     rest = jnp.zeros((padded - levels, cols), F32)
+    low, high = received(first_ref, second_ref)
     for i in range(2 * SUB):
-        ref = low_ref if i < SUB else high_ref
+        get = low if i < SUB else high
         at = i % SUB * near
         halo_ref[i, pl.ds(levels, padded - levels), :] = rest
         halo_ref[i, pl.ds(padded + levels, padded - levels), :] = rest
-        halo_ref[i, pl.ds(0, levels + 2), :] = ref[pl.ds(at, levels + 2), :]
-        halo_ref[i, pl.ds(padded, levels), :] = ref[pl.ds(at + second, levels), :]
+        halo_ref[i, pl.ds(0, levels + 2), :] = get(at, levels + 2)
+        halo_ref[i, pl.ds(padded, levels), :] = get(at + second, levels)
     total = edge_ref[...] + edge_of(lambda i: halo_ref[i], range(SUB), cols, lat)
-    out_ref[pl.ds(0, planes), :] = total + edge_of(
+    out_ref[...] = total + edge_of(
         lambda i: halo_ref[i - rows], range(rows + SUB, rows + 2 * SUB), cols, lat
     )
+
+
+def border_kernel(levels, padded, first_ref, second_ref, rows_ref, hist_ref, out_ref, swap_ref):
+    rows, pairs, cols = hist_ref.shape
+    close, distant = hist_rows(pairs)
+    low, high = received(first_ref, second_ref)
     tall = 3 * rows
-    fields = planes + (rows + 2 * REACH) * pairs
+    fields = (rows + 2 * REACH) * pairs
     out_ref[pl.ds(fields, 8 * tall), :] = jnp.zeros((8 * tall, cols), F32)
+    lane = iota((1, cols), 1)
+    place = lane % WIDE_SLOT - REACH * lax.axis_index("lat")
+    sent = (place >= 0) & (place < REACH)
+    slots = cols // WIDE_SLOT
+    groups = [None] * slot_groups(rows, cols)
     for at in range(-REACH, rows + REACH):
+        get = low if at < 0 else high
         if 0 <= at < rows:
-            ref, apart = hist_ref.at[at], 0
-        elif -SUB <= at < rows + SUB:
-            ref, index = (low_ref, at + SUB) if at < 0 else (high_ref, at - rows)
-            apart = hist + index * pairs
-        else:
-            ref, index = (low_ref, at + REACH) if at < 0 else (high_ref, at - rows - SUB)
-            apart = far + index * distant
-        out_ref[pl.ds(planes + (at + REACH) * pairs, pairs), :] = ref[pl.ds(apart, pairs), :]
-        if 0 <= at < rows:
-            ref = rows_ref.at[at]
+            own = rows_ref.at[at]
+            get = lambda place, size: own[pl.ds(place, size), :]
+            apart = hist_ref[at]
             places = {0: levels, 6: 0, 7: padded, 5: padded + levels}
             places.update({1 + field: levels + 2 + field for field in range(4)})
-            limit = levels + 1
         elif -SUB <= at < rows + SUB:
-            start = index * near
-            places = {0: start + levels, 6: start, 7: start + second}
-            places.update({1 + field: start + surface + field for field in range(5)})
-            limit = start + levels + 1
+            start = (at + SUB if at < 0 else at - rows) * close
+            apart = get(start, pairs)
+            start = start + pairs
+            places = {0: start, 6: start + 1, 7: start + 2}
+            places.update({1 + field: start + 3 + field for field in range(5)})
         else:
-            places = {0: apart + pairs, 6: apart + pairs + 1, 7: apart + pairs + 2}
-            limit = None
+            start = SUB * close + (at + REACH if at < 0 else at - rows - SUB) * distant
+            apart = get(start, pairs)
+            start = start + pairs
+            places = {0: start, 6: start + 1, 7: start + 2}
+        out_ref[pl.ds((at + REACH) * pairs, pairs), :] = apart
+        group, slot = divmod(at + REACH, slots)
+        moved = pltpu.roll(apart, WIDE_SLOT * slot + REACH, 1)
+        moved = jnp.where(sent & (lane // WIDE_SLOT == slot), moved, 0.0)
+        groups[group] = moved if groups[group] is None else groups[group] + moved
         for field, place in places.items():
-            value = ref[pl.ds(place, 1), :]
-            if field == 0 and limit is not None:
-                value = jnp.where(ref[pl.ds(limit, 1), :] > 0.5, value, 0.0)
+            value = get(place, 1)
+            if field == 0 and 0 <= at < rows:
+                value = jnp.where(get(levels + 1, 1) > 0.5, value, 0.0)
             out_ref[pl.ds(fields + field * tall + at + rows, 1), :] = value
+    for at, group in enumerate(groups):
+        swap_ref[pl.ds(at * pairs, pairs), :] = group
+    swap_ref[pl.ds(len(groups) * pairs, 8 * tall), :] = out_ref[pl.ds(fields, 8 * tall), :]
+
+
+def slot_groups(rows, cols):
+    slots = cols // WIDE_SLOT
+    return (rows + 2 * REACH + slots - 1) // slots
 
 
 def basis_kernel(
-    planes, rows, pairs, mine_ref, other_ref, step_ref, change_ref, _,
+    rows, pairs, mine_ref, other_ref, step_ref, change_ref,
     out_ref, near_ref, base_ref, first_ref, *work
 ):
     cols = mine_ref.shape[1]
@@ -314,13 +351,18 @@
     tall = rows + 2 * REACH
     ahead = REACH - SUB
     high = 3 * rows
-    apart = planes
-    fields = apart + tall * pairs
+    fields = tall * pairs
     closed = closed_lane(cols)
     opened = iota((1, width), 1) != closed
+    slots = cols // WIDE_SLOT
+    other_fields = slot_groups(rows, cols) * pairs
+    lane = iota((1, cols), 1)
+    start = jnp.where(lax.axis_index("lat") == 0, 0, cols - REACH)
+    at_border = (lane >= start) & (lane < start + REACH)
 
     def wide(at, size):
-        return jnp.concatenate([mine_ref[pl.ds(at, size), :], other_ref[pl.ds(at, size), :]], axis=1)
+        there = pl.ds(at - fields + other_fields, size)
+        return jnp.concatenate([mine_ref[pl.ds(at, size), :], other_ref[there, :]], axis=1)
 
     def left(value):
         return pltpu.roll(value, width - 1, 1)
@@ -350,7 +392,6 @@
     base = [(part * sea)[rows : 2 * rows, :cols] for part in value]
     for tracer in range(2):
         base_ref[tracer] = base[tracer]
-    lane = iota((1, cols), 1)
     for i in range(pairs // 2):
         total = jnp.zeros((1, cols), F32)
         for at, ref in ((0, step_ref), (cols // 2, change_ref)):
@@ -391,10 +432,13 @@
         for i in range(rows):
             out_ref[slot, i] = get(i + REACH)[:, :cols]
 
-    def start_apart(i):
-        return wide(apart + i * pairs, pairs)
-
-    get = start_apart
+    for i in range(tall):
+        group, slot = divmod(i, slots)
+        there = other_ref[pl.ds(group * pairs, pairs), :]
+        there = pltpu.roll(there, (cols - WIDE_SLOT * slot - REACH) % cols, 1)
+        work[-1][i, :, :cols] = mine_ref[pl.ds(i * pairs, pairs), :]
+        work[-1][i, :, cols:] = jnp.where(at_border, there, 0.0)
+    get = lambda i: work[-1][i]
     for sweep in range(SUB):
         get = mixed(get, work[sweep], REACH - 1 - sweep)
     reach = REACH - SUB
@@ -473,7 +517,7 @@
 
 def fields_kernel(
     levels, padded, scale,
-    rows_ref, main_ref, edge_ref, other_ref, weight_ref, observed_ref, basis_ref, first_ref,
+    rows_ref, main_ref, edge_ref, other_ref, weight_ref, observed_ref, basis_ref, first_ref, fixed_ref,
     mixed_ref, fields_ref, part_ref,
 ):
     rows, _, cols = rows_ref.shape
@@ -576,12 +620,14 @@
             for power in range(1, ITERS):
                 add(at + power, ITERS + (1 + j) * (ITERS - 1) + power - 1, row, surface)
     half = pairs // 2
-    total = first_ref[...]
+    total = first_ref[...] + fixed_ref[3]
     for at in range(1, FUNCTIONALS):
         value = jnp.sum(sums[at], axis=1, keepdims=True)
         total = total + jnp.where(lane == at, value[:half], 0.0)
         total = total + jnp.where(lane == cols // 2 + at, value[half:], 0.0)
     part_ref[2] = total
+    for field in range(3):
+        part_ref[3 + field] = fixed_ref[field]
     for copy in range(fields_ref.shape[0]):
         fields_ref[copy] = part_ref[...]
 
@@ -730,10 +776,11 @@
         history_step.reshape(-1, cols), history_change.reshape(-1, cols), damping, weight, observed,
     )
     held = [x.shape for x in inputs[:-1]] + [(2, rows, cols)]
-    near, _, _, distant = row_layout(levels, pairs)
-    sent = (round_up(SUB * (near + pairs) + (REACH - SUB) * distant, 8), cols)
-    shapes = ((rows, planes, cols), (rows, pairs, cols), sent, sent)
-    packed, hist, up, down = pl.pallas_call(
+    close, distant = hist_rows(pairs)
+    sent_hist = (round_up(SUB * close + (REACH - SUB) * distant, 8), cols)
+    sent = (round_up(SUB * state_rows(levels)[0], 8), cols)
+    shapes = ((rows, planes, cols), (rows, pairs, cols), sent_hist, sent_hist, sent, sent)
+    packed, hist, first_hist, second_hist, first, second = pl.pallas_call(
         functools.partial(pack_kernel, levels, padded),
         out_shape=[jax.ShapeDtypeStruct(shape, F32) for shape in shapes],
         in_specs=[pl.BlockSpec(memory_space=pltpu.HBM)] * len(inputs),
@@ -743,30 +790,53 @@
         compiler_params=pltpu.CompilerParams(vmem_limit_bytes=VMEM_BYTES),
         name="pack",
     )(*(pltpu.with_memory_space_constraint(x, pltpu.HBM) for x in inputs))
-    forward = [(i, (i + 1) % loops) for i in range(loops)]
-    backward = [(target, source) for source, target in forward]
+    partner = [(i, i ^ 1) for i in range(loops)]
+    following = [(i, (i - 1 + 2 * (i % 2)) % loops) for i in range(loops)]
     swap = [(0, 1), (1, 0)]
-    low = lax.ppermute(up, "loop", forward)
-    high = lax.ppermute(down, "loop", backward)
-    edge, still, depth, _ = call(
+    first_hist = lax.ppermute(first_hist, "loop", partner)
+    second_hist = lax.ppermute(second_hist, "loop", following)
+    first = lax.ppermute(first, "loop", partner)
+    second = lax.ppermute(second, "loop", following)
+    edge, depth, fixed = call(
         functools.partial(pairs_kernel, levels),
-        [(planes, cols), (loops, 4, rows, cols), (rows, cols), (4, rows, cols)],
+        [(planes, cols), (rows, cols), (4, rows, cols)],
         name="pairs",
     )(packed, step, change)
-    still = lax.all_to_all(still, "loop", 0, 0)
-    still_other = lax.ppermute(still, "lat", swap)
     height = loops * rows
     large = VMEM_BYTES if loops <= 16 else 2 * VMEM_BYTES
-    faces, plan = call(
-        plan_kernel, [(6, height, 2 * cols), (pairs, cols)], vmem=large, name="plan"
-    )(still, still_other)
-    swapped = planes + (rows + 2 * REACH) * pairs + 8 * 3 * rows
-    border, halo = call(
+    fields = 8 * 3 * rows
+    border, border_other = call(
         functools.partial(border_kernel, levels, padded),
-        [(swapped, cols), (2 * SUB, planes, cols)],
+        [
+            ((rows + 2 * REACH) * pairs + fields, cols),
+            (slot_groups(rows, cols) * pairs + fields, cols),
+        ],
         name="border",
-    )(edge, low, high, packed, hist)
-    other = lax.ppermute(border, "lat", swap)
+    )(first_hist, second_hist, packed, hist)
+    border_other = lax.ppermute(border_other, "lat", swap)
+    chains = 1 + ITERS
+    buffers = SUB + ITERS + chains * (ITERS - 1)
+    shapes = (
+        (ITERS + chains * (ITERS - 1), rows, pairs, cols),
+        (6, 3 * rows, 2 * cols),
+        (2, rows, cols),
+        (count, cols),
+    )
+    basis, around, base, near_start = pl.pallas_call(
+        functools.partial(basis_kernel, rows, pairs),
+        out_shape=[jax.ShapeDtypeStruct(shape, F32) for shape in shapes],
+        in_specs=[VMEM] * 4,
+        out_specs=[VMEM] * len(shapes),
+        scratch_shapes=[pltpu.VMEM((rows + 2 * REACH, pairs, 2 * cols), F32)] * buffers,
+        compiler_params=pltpu.CompilerParams(vmem_limit_bytes=VMEM_BYTES),
+        name="basis",
+    )(border, border_other, step, change)
+    edge, halo = call(
+        functools.partial(halo_kernel, levels, padded, rows),
+        [(planes, cols), (2 * SUB, planes, cols)],
+        name="halo",
+    )(edge, first, second, near_start)
+    other = lax.ppermute(edge, "lat", swap)
     tall = rows + 2 * SUB
     (mixed,) = call(
         functools.partial(mix_kernel, levels, padded),
@@ -775,31 +845,17 @@
         + [pltpu.VMEM((tall, planes, cols), F32)] * 2,
         name="mix",
     )(packed, halo)
-    chains = 1 + ITERS
-    buffers = SUB + ITERS - 1 + chains * (ITERS - 1)
-    shapes = (
-        (ITERS + chains * (ITERS - 1), rows, pairs, cols),
-        (6, 3 * rows, 2 * cols),
-        (2, rows, cols),
-        (count, cols),
-    )
-    basis, around, base, first = pl.pallas_call(
-        functools.partial(basis_kernel, planes, rows, pairs),
-        out_shape=[jax.ShapeDtypeStruct(shape, F32) for shape in shapes],
-        in_specs=[VMEM] * 4 + [pl.BlockSpec(memory_space=pl.ANY)],
-        out_specs=[VMEM] * len(shapes),
-        scratch_shapes=[pltpu.VMEM((rows + 2 * REACH, pairs, 2 * cols), F32)] * buffers,
-        compiler_params=pltpu.CompilerParams(vmem_limit_bytes=VMEM_BYTES),
-        name="basis",
-    )(border, other, step, change, still_other)
     mixed, fields = call(
         functools.partial(fields_kernel, levels, padded, scale),
-        [flat, (loops, 3, rows, cols)],
-        scratch=[pltpu.VMEM((3, rows, cols), F32)],
+        [flat, (loops, 6, rows, cols)],
+        scratch=[pltpu.VMEM((6, rows, cols), F32)],
         name="fields",
-    )(packed, mixed, border, other, weight, observed, basis, first)
+    )(packed, mixed, edge, other, weight, observed, basis, near_start, fixed)
     mine = lax.all_to_all(fields, "loop", 0, 0)
     theirs = lax.ppermute(mine, "lat", swap)
+    faces, plan = call(
+        plan_kernel, [(6, height, 2 * cols), (pairs, cols)], vmem=large, name="plan"
+    )(mine, theirs)
     shapes = (flat, (2, rows, cols), (2, rows, cols))
     state_next, gradient, direction = call(
         functools.partial(solve_kernel, levels, scale),

time: 38.9 us -> 37.6 us (0.967)
  waiting for transfers between devices: 8.26 us -> 6.28 us
  blocking collectives: 10.8 us -> 12.2 us
  starting transfers between devices: 9.54 us -> 8.63 us
  local copies, waits for them, and re-layouts: 0.02 us -> 0.67 us
    all_to_all x1 -> x0, starting transfers between devices: 3.37 us -> none  [on_device(): still = lax.all_to_all(still, 'loop', 0, 0)]
    ppermute x4 -> x6, starting transfers between devices: 6.17 us -> 8.63 us  [the longest x1 3.57 us: on_device(): second_hist = lax.ppermute(second_hist, 'loop', following)]
    all_to_all x1 -> x0, waiting for transfers between devices: 1.7 us -> none  [on_device(): still = lax.all_to_all(still, 'loop', 0, 0)]
    all_to_all x1, blocking collectives: 10.8 us -> 12.2 us  [on_device(): mine = lax.all_to_all(fields, 'loop', 0, 0)]
    unnamed x8, local copies, waits for them, and re-layouts: 0.02 us -> 0.67 us
    ppermute x4 -> x6, waiting for transfers between devices: 5.48 us -> 4.84 us  [the longest x1 2.76 us: on_device(): first = lax.ppermute(first, 'loop', partner)]
    pallas_call x3 -> x4, Pallas kernels: 2.95 us -> 2.47 us  [the longest x1 1.86 us: on_device(): pl.pallas_call(functools.partial(basis_kernel, rows, pairs), out_shape=[j...]
  transfers between devices with their start and end apart: 6 -> 7, of which waited for: 5 -> 4; matrix products, arithmetic and copies ran while one was open for 0% -> 0% of each run, Pallas kernels for 6% -> 9%
where the time goes in v8:
time: 37.6 us; the launch traced here: 37.4 us
  blocking collectives  12.2 us (32%)
  Pallas kernels  8.85 us (24%)
  starting transfers between devices  8.63 us (23%)
  waiting for transfers between devices  6.28 us (17%)
  between operations  0.74 us (2%)
  local copies, waits for them, and re-layouts  0.67 us (2%)
    all_to_all x1, blocking collectives, on_device(): mine = lax.all_to_all(fields, 'loop', 0, 0)  12.2 us
    ppermute x1, starting transfers between devices, on_device(): second_hist = lax.ppermute(second_hist, 'loop', following)  3.57 us
    ppermute x1, starting transfers between devices, on_device(): first_hist = lax.ppermute(first_hist, 'loop', partner)  3 us
    ppermute x1, waiting for transfers between devices, on_device(): first = lax.ppermute(first, 'loop', partner)  2.76 us
    pallas_call x1, Pallas kernels, on_device(): call(functools.partial(solve_kernel, levels, scale), shapes, scratch=[plt...  2.59 us
    ppermute x1, starting transfers between devices, on_device(): second = lax.ppermute(second, 'loop', following)  1.91 us
    pallas_call x1, Pallas kernels, on_device(): pl.pallas_call(functools.partial(basis_kernel, rows, pairs), out_shape=[j...  1.86 us
    ppermute x1, waiting for transfers between devices, on_device(): second_hist = lax.ppermute(second_hist, 'loop', following)  1.71 us
  transfers between devices with their start and end apart: 7, of which 4 were waited for; matrix products, arithmetic and copies ran while one was open for 0% of the time, Pallas kernels for 9%

profile of v8, /device:TPU:0, one launch (start us, length us, event | category | flops | bytes accessed | tf_op | source)
XLA Modules:
  0.0 37.4 jit_solution(17337917954622783309)
XLA Ops:
  0.6 1.5 %pack.1 = (f32[8,112,128]{2,1,0:T(8,128)S(1)}, f32[8,16,128]{2,1,0:T(8,128)S(1)}, f32[152,128]{1,0:T(8,128)S(1)}, f32[152,128]{1,0:T(8,128)S(1)}, f32[312,128]{1,0:T(8,128)S(1)}, /*index=5*/f32[312,128]{1,0:T(8,128)S(1)}) custom-call(f32[2,400,128]{2,1,0:T(8,128)} %bitcast.20, f32[2,8,128]{2,1,0:T(8,128)} %refs_1_.1, s32[8,128]{1,0:T(8,128)} %refs_2_.1, ...), custom_call_target="tpu_custom_call" | custom-call | tf_op jit(solution)/shard_map/pack/pallas_call | solution.py:783
  2.1 3.0 %collective-permute-start.2 = (f32[152,128]{1,0:T(8,128)S(1)}, f32[152,128]{1,0:T(8,128)S(1)}, u32[]{:S(2)}, u32[]{:S(2)}) collective-permute-start(f32[152,128]{1,0:T(8,128)S(1)} %get-tuple-element.31), channel_id=1, source_target_pairs={{0,2},{2,0},{4,6},{6,4},{8,10},{10,8},{12,14},{14,12},{1,3},{3,1},... | collective-permute-start | bytes 233480 | tf_op jit(solution)/shard_map/ppermute | solution.py:796
  5.1 3.6 %collective-permute-start.3 = (f32[152,128]{1,0:T(8,128)S(1)}, f32[152,128]{1,0:T(8,128)S(1)}, u32[]{:S(2)}, u32[]{:S(2)}) collective-permute-start(f32[152,128]{1,0:T(8,128)S(1)} %get-tuple-element.32), channel_id=1, source_target_pairs={{0,14},{2,4},{4,2},{6,8},{8,6},{10,12},{12,10},{14,0},{1,15},{3,5}... | collective-permute-start | bytes 233480 | tf_op jit(solution)/shard_map/ppermute | solution.py:797
  8.7 0.0 collective-permute-start
  8.7 1.9 %collective-permute-start.1 = (f32[312,128]{1,0:T(8,128)S(1)}, f32[312,128]{1,0:T(8,128)S(1)}, u32[]{:S(2)}, u32[]{:S(2)}) collective-permute-start(f32[312,128]{1,0:T(8,128)S(1)} %get-tuple-element.30), channel_id=1, source_target_pairs={{0,14},{2,4},{4,2},{6,8},{8,6},{10,12},{12,10},{14,0},{1,15},{3,5}... | collective-permute-start | bytes 479240 | tf_op jit(solution)/shard_map/ppermute | solution.py:799
  10.6 1.7 %collective-permute-done.3.second_ref = f32[152,128]{1,0:T(8,128)S(1)} collective-permute-done((f32[152,128]{1,0:T(8,128)S(1)}, f32[152,128]{1,0:T(8,128)S(1)}, u32[]{:S(2)}, u32[]{:S(2)}) %collective-permute-start.3) | collective-permute-done | bytes 77856 | tf_op jit(solution)/shard_map/ppermute | solution.py:797
  12.3 0.1 border.1
  12.5 0.1 collective-permute-start.4
  12.5 0.6 %copy-done.1 = f32[8,2,8,128]{3,2,1,0:T(8,128)S(1)} copy-done((f32[8,2,8,128]{3,2,1,0:T(8,128)S(1)}, f32[8,2,8,128]{3,2,1,0:T(8,128)}, u32[]{:S(2)}) %copy-start.1) | copy-done | bytes 65560
  13.2 0.0 copy-done.2
  13.2 0.3 pairs.1
  13.5 0.4 collective-permute-done.4.other_ref
  13.9 1.9 %basis.1 = (f32[11,8,16,128]{3,2,1,0:T(8,128)S(1)}, f32[6,24,256]{2,1,0:T(8,128)S(1)}, f32[2,8,128]{2,1,0:T(8,128)S(1)}, f32[8,128]{1,0:T(8,128)S(1)}) custom-call(f32[544,128]{1,0:T(8,128)S(1)} %get-tuple-element.34.mine_ref, f32[240,128]{1,0:T(8,128)S(1)} %collective-permute-done.4.other_ref, f32[8,16,128]{2,1,0:T(8,128)S(1)} %bitcast.12, ...), custom_call_target="tpu_custom_call" | custom-call | tf_op jit(solution)/shard_map/basis/pallas_call | solution.py:825
  15.7 2.8 %collective-permute-done.first_ref = f32[312,128]{1,0:T(8,128)S(1)} collective-permute-done((f32[312,128]{1,0:T(8,128)S(1)}, f32[312,128]{1,0:T(8,128)S(1)}, u32[]{:S(2)}, u32[]{:S(2)}) %collective-permute-start) | collective-permute-done | bytes 159776 | tf_op jit(solution)/shard_map/ppermute | solution.py:798
  18.5 0.2 halo.1
  18.7 0.1 collective-permute-start.5
  18.8 0.0 copy-start
  18.8 0.0 copy-start.3
  18.8 1.2 %mix.1.main_ref = f32[8,112,128]{2,1,0:T(8,128)S(1)} custom-call(f32[8,112,128]{2,1,0:T(8,128)S(1)} %get-tuple-element.27.rows_ref, f32[6,112,128]{2,1,0:T(8,128)S(1)} %get-tuple-element.37.halo_ref), custom_call_target="tpu_custom_call" | custom-call | tf_op jit(solution)/shard_map/mix/pallas_call | solution.py:841
  20.0 0.9 %fields.1 = (f32[2,400,128]{2,1,0:T(8,128)S(1)}, f32[8,6,8,128]{3,2,1,0:T(8,128)S(1)}) custom-call(f32[8,112,128]{2,1,0:T(8,128)S(1)} %get-tuple-element.27.rows_ref, f32[8,112,128]{2,1,0:T(8,128)S(1)} %mix.1.main_ref, f32[112,128]{1,0:T(8,128)S(1)} %get-tuple-element.38.edge_ref, f32[112,128]{1,0:T(8,128)S(1)} %collective-permute-done.5.other_ref, ...), custom_call_target="tpu_custom_call" | custom-call | tf_op jit(solution)/shard_map/fields/pallas_call | solution.py:848
  20.9 12.2 %all_to_all.5.mine_ref = f32[8,6,8,128]{3,2,1,0:T(8,128)S(1)} all-to-all(f32[8,6,8,128]{3,2,1,0:T(8,128)S(1)} %get-tuple-element.41), channel_id=1, replica_groups=mesh['members'=2,'loop'=8,'lat'=2] {'loop'}, dimensions={0} | all-to-all | bytes 393216 | tf_op jit(solution)/shard_map/all_to_all | solution.py:854
  33.2 1.4 %collective-permute-done.6.other_ref = f32[8,6,8,128]{3,2,1,0:T(8,128)S(1)} collective-permute-done((f32[8,6,8,128]{3,2,1,0:T(8,128)S(1)}, f32[8,6,8,128]{3,2,1,0:T(8,128)S(1)}, u32[]{:S(2)}, u32[]{:S(2)}) %collective-permute-start.6) | collective-permute-done | bytes 196640 | tf_op jit(solution)/shard_map/ppermute | solution.py:855
  34.6 0.2 plan.1
  34.8 2.6 %solve.1 = (f32[2,400,128]{2,1,0:T(8,128)}, f32[2,8,128]{2,1,0:T(8,128)}, f32[2,8,128]{2,1,0:T(8,128)}) custom-call(f32[8,6,8,128]{3,2,1,0:T(8,128)S(1)} %all_to_all.5.mine_ref, f32[8,6,8,128]{3,2,1,0:T(8,128)S(1)} %collective-permute-done.6.other_ref, f32[6,64,256]{2,1,0:T(8,128)S(1)} %get-tuple-element.42.faces_ref, ...), custom_call_target="tpu_custom_call" | custom-call | tf_op jit(solution)/shard_map/solve/pallas_call | solution.py:860
  (8 shorter events, 0.0 us)
Async XLA Ops:
  2.1 8.5 %collective-permute-start.2 = (f32[152,128]{1,0:T(8,128)S(1)}, f32[152,128]{1,0:T(8,128)S(1)}, u32[]{:S(2)}, u32[]{:S(2)}) collective-permute-start(f32[152,128]{1,0:T(8,128)S(1)} %get-tuple-element.31), channel_id=1, source_target_pairs={{0,2},{2,0},{4,6},{6,4},{8,10},{10,8},{12,14},{14,12},{1,3},{3,1},... | collective-permute-start | bytes 233480 | tf_op jit(solution)/shard_map/ppermute | solution.py:796
  5.1 7.2 %collective-permute-start.3 = (f32[152,128]{1,0:T(8,128)S(1)}, f32[152,128]{1,0:T(8,128)S(1)}, u32[]{:S(2)}, u32[]{:S(2)}) collective-permute-start(f32[152,128]{1,0:T(8,128)S(1)} %get-tuple-element.32), channel_id=1, source_target_pairs={{0,14},{2,4},{4,2},{6,8},{8,6},{10,12},{12,10},{14,0},{1,15},{3,5}... | collective-permute-start | bytes 233480 | tf_op jit(solution)/shard_map/ppermute | solution.py:797
  8.7 9.8 %collective-permute-start = (f32[312,128]{1,0:T(8,128)S(1)}, f32[312,128]{1,0:T(8,128)S(1)}, u32[]{:S(2)}, u32[]{:S(2)}) collective-permute-start(f32[312,128]{1,0:T(8,128)S(1)} %get-tuple-element.29), channel_id=1, source_target_pairs={{0,2},{2,0},{4,6},{6,4},{8,10},{10,8},{12,14},{14,12},{1,3},{3,1},... | collective-permute-start | bytes 479240 | tf_op jit(solution)/shard_map/ppermute | solution.py:798
  8.7 9.8 %collective-permute-start.1 = (f32[312,128]{1,0:T(8,128)S(1)}, f32[312,128]{1,0:T(8,128)S(1)}, u32[]{:S(2)}, u32[]{:S(2)}) collective-permute-start(f32[312,128]{1,0:T(8,128)S(1)} %get-tuple-element.30), channel_id=1, source_target_pairs={{0,14},{2,4},{4,2},{6,8},{8,6},{10,12},{12,10},{14,0},{1,15},{3,5}... | collective-permute-start | bytes 479240 | tf_op jit(solution)/shard_map/ppermute | solution.py:799
  12.3 0.8 %copy-start.1 = (f32[8,2,8,128]{3,2,1,0:T(8,128)S(1)}, f32[8,2,8,128]{3,2,1,0:T(8,128)}, u32[]{:S(2)}) copy-start(f32[8,2,8,128]{3,2,1,0:T(8,128)} %param.16) | copy-start | bytes 196612
  12.3 0.9 %copy-start.2 = (f32[8,2,8,128]{3,2,1,0:T(8,128)S(1)}, f32[8,2,8,128]{3,2,1,0:T(8,128)}, u32[]{:S(2)}) copy-start(f32[8,2,8,128]{3,2,1,0:T(8,128)} %param.17) | copy-start | bytes 196612
  12.5 1.4 %collective-permute-start.4 = (f32[240,128]{1,0:T(8,128)S(1)}, f32[240,128]{1,0:T(8,128)S(1)}, u32[]{:S(2)}, u32[]{:S(2)}) collective-permute-start(f32[240,128]{1,0:T(8,128)S(1)} %get-tuple-element.35), channel_id=1, source_target_pairs={{0,1},{1,0},{2,3},{3,2},{4,5},{5,4},{6,7},{7,6},{8,9},{9,8},{10,11... | collective-permute-start | bytes 368648 | tf_op jit(solution)/shard_map/ppermute | solution.py:816
  18.7 1.3 %collective-permute-start.5 = (f32[112,128]{1,0:T(8,128)S(1)}, f32[112,128]{1,0:T(8,128)S(1)}, u32[]{:S(2)}, u32[]{:S(2)}) collective-permute-start(f32[112,128]{1,0:T(8,128)S(1)} %get-tuple-element.38.edge_ref), channel_id=1, source_target_pairs={{0,1},{1,0},{2,3},{3,2},{4,5},{5,4},{6,7},{7,6},{8,9},{9,8},{10,11... | collective-permute-start | bytes 172040 | tf_op jit(solution)/shard_map/ppermute | solution.py:839
  18.8 1.3 %copy-start = (f32[2,50,8,128]{3,2,1,0:T(8,128)S(1)}, f32[2,50,8,128]{3,2,1,0:T(8,128)}, u32[]{:S(2)}) copy-start(f32[2,50,8,128]{3,2,1,0:T(8,128)} %param.10) | copy-start | bytes 1228804
  18.8 1.3 %copy-start.3 = (f32[50,8,128]{2,1,0:T(8,128)S(1)}, f32[50,8,128]{2,1,0:T(8,128)}, u32[]{:S(2)}) copy-start(f32[50,8,128]{2,1,0:T(8,128)} %param.11) | copy-start | bytes 614404
  33.2 1.4 %collective-permute-start.6 = (f32[8,6,8,128]{3,2,1,0:T(8,128)S(1)}, f32[8,6,8,128]{3,2,1,0:T(8,128)S(1)}, u32[]{:S(2)}, u32[]{:S(2)}) collective-permute-start(f32[8,6,8,128]{3,2,1,0:T(8,128)S(1)} %all_to_all.5.mine_ref), channel_id=1, source_target_pairs={{0,1},{1,0},{2,3},{3,2},{4,5},{5,4},{6,7},{7,6},{8,9},{9,8},{10,11... | collective-permute-start | bytes 589832 | tf_op jit(solution)/shard_map/ppermute | solution.py:855

commit v9 on v8

--- a/solution.py
+++ b/solution.py
@@ -12,6 +12,8 @@
 SURFACE_GAIN = 5.0
 SLOT = 8
 WIDE_SLOT = 16
+FOLD = SLOT * SUB
+SWAP_ROWS = 240
 REACH = SUB + 2 * (ITERS - 1)
 SHIFT = 5.0
 SPAN = 5.0
@@ -135,7 +137,18 @@
             put(outs[2:4], start + 3, rows_ref[upper, here, :], rows_ref[lower, here, :])
             here = pl.ds(padded + levels, 1)
             put(outs[2:4], start + 7, rows_ref[upper, here, :], rows_ref[lower, here, :])
-    fill(outs[2:4], SUB * close + (REACH - SUB) * distant)
+    last = SUB * close + (REACH - SUB) * distant
+    folds = outs[2].shape[0] - FOLD
+    if last < folds:
+        rest = jnp.zeros((folds - last, cols), F32)
+        put(outs[2:4], last, rest, rest)
+    lat = lax.axis_index("lat")
+    put(
+        outs[2:4],
+        folds,
+        folded(edge_of(lambda i: rows_ref[rows - SUB + i], range(SUB), cols, lat)),
+        folded(edge_of(lambda i: rows_ref[i], range(SUB), cols, lat)),
+    )
     for at in range(SUB):
         upper, lower = rows - SUB + at, at
         for start, size, place in ((0, levels + 2, 0), (padded, levels, second)):
@@ -157,8 +170,76 @@
     return total
 
 
-def pairs_kernel(levels, rows_ref, step_ref, change_ref, edge_ref, depth_ref, fixed_ref):
+def folded(edge):
+    planes, cols = edge.shape
+    total = None
+    for at, start in enumerate(range(0, planes, FOLD)):
+        size = min(FOLD, planes - start)
+        part = pltpu.roll(edge[start : start + size], FOLD * at, 1)
+        if size < FOLD:
+            part = jnp.concatenate([part, jnp.zeros((FOLD - size, cols), F32)], axis=0)
+        total = part if total is None else total + part
+    return total
+
+
+def unfolded(fold, planes, lane_at):
+    cols = fold.shape[1]
+    lane = iota((1, cols), 1)
+    here = (lane >= lane_at) & (lane < lane_at + FOLD)
+    parts = []
+    for at, start in enumerate(range(0, planes, FOLD)):
+        part = pltpu.roll(fold, (lane_at - FOLD * at) % cols, 1)
+        parts.append(jnp.where(here, part, 0.0)[: min(FOLD, planes - start)])
+    return jnp.concatenate(parts, axis=0)
+
+
+def level_face(levels, depth_here, depth_there, spread_here, spread_there):
+    opened = levels < jnp.minimum(depth_here, depth_there)
+    return jnp.where(opened, 0.5 * (spread_here + spread_there), 0.0)
+
+
+def side_faces(level, depth, spread):
+    cols = depth.shape[1]
+    lane = iota((1, cols), 1)
+    result = []
+    for by, inside in ((cols - 1, lane < cols - 1), (1, lane > 0)):
+        there = jnp.where(inside, pltpu.roll(depth, by, 1), 0.0)
+        result.append(level_face(level, depth, there, spread, pltpu.roll(spread, by, 1)))
+    return result
+
+
+def mixed_row(get, faces, i, at):
+    below, above, right, left = faces
+    centre = get(i)[at, :]
+    cols = centre.shape[1]
+    total = centre + below * (get(i + 1)[at, :] - centre)
+    total = total + above * (get(i - 1)[at, :] - centre)
+    total = total + right * (pltpu.roll(centre, cols - 1, 1) - centre)
+    return total + left * (pltpu.roll(centre, 1, 1) - centre)
+
+
+def pairs_kernel(
+    levels, padded, rows_ref, step_ref, change_ref, edge_ref, depth_ref, fixed_ref, face_ref, inner_ref
+):
     rows, _, cols = rows_ref.shape
+    level = iota((padded, cols), 0).astype(F32)
+    spreads = [rows_ref[i, pl.ds(levels, 1), :] for i in range(rows)]
+    depths = [rows_ref[i, pl.ds(levels + 1, 1), :] for i in range(rows)]
+    for i in range(rows):
+        if i + 1 < rows:
+            face_ref[0, i] = level_face(level, depths[i], depths[i + 1], spreads[i], spreads[i + 1])
+        face_ref[1, i], face_ref[2, i] = side_faces(level, depths[i], spreads[i])
+    face_ref[0, rows - 1] = jnp.zeros((padded, cols), F32)
+    for sweep in range(SUB):
+        source = rows_ref if sweep == 0 else inner_ref.at[sweep - 1]
+        for i in range(rows):
+            for tracer in range(2):
+                at = pl.ds(tracer * padded, padded)
+                if sweep < i < rows - 1 - sweep:
+                    faces = face_ref[0, i], face_ref[0, i - 1], face_ref[1, i], face_ref[2, i]
+                    inner_ref[sweep, i, at, :] = mixed_row(lambda j: source.at[j], faces, i, at)
+                else:
+                    inner_ref[sweep, i, at, :] = jnp.zeros((padded, cols), F32)
     lat = lax.axis_index("lat")
     count = step_ref.shape[0]
     lane = iota((1, cols), 1)
@@ -272,26 +353,9 @@
     return low, high
 
 
-def halo_kernel(levels, padded, rows, edge_ref, first_ref, second_ref, _, out_ref, halo_ref):
-    planes, cols = edge_ref.shape
-    lat = lax.axis_index("lat")
-    near, second = state_rows(levels)
-    rest = jnp.zeros((padded - levels, cols), F32)
-    low, high = received(first_ref, second_ref)
-    for i in range(2 * SUB):
-        get = low if i < SUB else high
-        at = i % SUB * near
-        halo_ref[i, pl.ds(levels, padded - levels), :] = rest
-        halo_ref[i, pl.ds(padded + levels, padded - levels), :] = rest
-        halo_ref[i, pl.ds(0, levels + 2), :] = get(at, levels + 2)
-        halo_ref[i, pl.ds(padded, levels), :] = get(at + second, levels)
-    total = edge_ref[...] + edge_of(lambda i: halo_ref[i], range(SUB), cols, lat)
-    out_ref[...] = total + edge_of(
-        lambda i: halo_ref[i - rows], range(rows + SUB, rows + 2 * SUB), cols, lat
-    )
-
-
-def border_kernel(levels, padded, first_ref, second_ref, rows_ref, hist_ref, out_ref, swap_ref):
+def border_kernel(
+    levels, padded, edge_ref, first_ref, second_ref, rows_ref, hist_ref, out_ref, swap_ref
+):
     rows, pairs, cols = hist_ref.shape
     close, distant = hist_rows(pairs)
     low, high = received(first_ref, second_ref)
@@ -334,7 +398,26 @@
             out_ref[pl.ds(fields + field * tall + at + rows, 1), :] = value
     for at, group in enumerate(groups):
         swap_ref[pl.ds(at * pairs, pairs), :] = group
-    swap_ref[pl.ds(len(groups) * pairs, 8 * tall), :] = out_ref[pl.ds(fields, 8 * tall), :]
+    total = None
+    for field in range(8):
+        moved = pltpu.roll(
+            out_ref[pl.ds(fields + field * tall, tall), :], WIDE_SLOT * field + REACH, 1
+        )
+        moved = jnp.where(sent & (lane // WIDE_SLOT == field), moved, 0.0)
+        total = moved if total is None else total + moved
+    at = len(groups) * pairs
+    swap_ref[pl.ds(at, tall), :] = total
+    at = at + tall
+    planes = edge_ref.shape[0]
+    folds = first_ref.shape[0] - FOLD
+    before = unfolded(low(folds, FOLD), planes, 0)
+    after = unfolded(high(folds, FOLD), planes, SLOT * (rows + SUB))
+    swap_ref[pl.ds(at, planes), :] = edge_ref[...] + (before + after)
+    at = at + planes
+    if at < swap_ref.shape[0]:
+        swap_ref[pl.ds(at, swap_ref.shape[0] - at), :] = jnp.zeros(
+            (swap_ref.shape[0] - at, cols), F32
+        )
 
 
 def slot_groups(rows, cols):
@@ -356,13 +439,19 @@
     opened = iota((1, width), 1) != closed
     slots = cols // WIDE_SLOT
     other_fields = slot_groups(rows, cols) * pairs
+    beside_ref = work[-2]
     lane = iota((1, cols), 1)
     start = jnp.where(lax.axis_index("lat") == 0, 0, cols - REACH)
     at_border = (lane >= start) & (lane < start + REACH)
 
+    packed = other_ref[pl.ds(other_fields, high), :]
+    for at in range(8):
+        there = pltpu.roll(packed, (cols - WIDE_SLOT * at - REACH) % cols, 1)
+        beside_ref[pl.ds(at * high, high), :] = jnp.where(at_border, there, 0.0)
+
     def wide(at, size):
-        there = pl.ds(at - fields + other_fields, size)
-        return jnp.concatenate([mine_ref[pl.ds(at, size), :], other_ref[there, :]], axis=1)
+        there = pl.ds(at - fields, size)
+        return jnp.concatenate([mine_ref[pl.ds(at, size), :], beside_ref[there, :]], axis=1)
 
     def left(value):
         return pltpu.roll(value, width - 1, 1)
@@ -462,66 +551,81 @@
 
 
 def mix_kernel(
-    levels, padded, rows_ref, halo_ref, out_ref, face_ref, here_ref, there_ref
+    levels, padded, rows_ref, first_ref, second_ref, own_face_ref, inner_ref, _,
+    out_ref, face_ref, outer_ref, halo_ref
 ):
     rows, _, cols = rows_ref.shape
-    lane = iota((1, cols), 1)
     count = rows + 2 * SUB
+    near, second = state_rows(levels)
+    rest = jnp.zeros((padded - levels, cols), F32)
+    low, high = received(first_ref, second_ref)
+    for i in range(2 * SUB):
+        get = low if i < SUB else high
+        at = i % SUB * near
+        halo_ref[i, pl.ds(levels, padded - levels), :] = rest
+        halo_ref[i, pl.ds(padded + levels, padded - levels), :] = rest
+        halo_ref[i, pl.ds(0, levels + 2), :] = get(at, levels + 2)
+        halo_ref[i, pl.ds(padded, levels), :] = get(at + second, levels)
     level = iota((padded, cols), 0).astype(F32)
 
-    def left(value):
-        return pltpu.roll(value, cols - 1, 1)
-
-    def right(value):
-        return pltpu.roll(value, 1, 1)
-
-    def source(i):
+    def state_row(i):
         if i < SUB:
             return halo_ref.at[i]
-        if i < SUB + rows:
-            return rows_ref.at[i - SUB]
-        return halo_ref.at[i - rows]
-
-    def face(depth_here, depth_there, spread_here, spread_there):
-        opened = level < jnp.minimum(depth_here, depth_there)
-        return jnp.where(opened, 0.5 * (spread_here + spread_there), 0.0)
-
-    spreads = [source(i)[pl.ds(levels, 1), :] for i in range(count)]
-    depths = [source(i)[pl.ds(levels + 1, 1), :] for i in range(count)]
+        return rows_ref.at[i - SUB] if i < SUB + rows else halo_ref.at[i - rows]
+
+    def face(kind, i):
+        last = SUB + rows - (1 if kind == 0 else 0)
+        return own_face_ref[kind, i - SUB] if SUB <= i < last else face_ref[kind, i]
+
+    spreads = [state_row(i)[pl.ds(levels, 1), :] for i in range(count)]
+    depths = [state_row(i)[pl.ds(levels + 1, 1), :] for i in range(count)]
     for i in range(count - 1):
-        face_ref[0, i] = face(depths[i], depths[i + 1], spreads[i], spreads[i + 1])
-    for i in range(1, count - 1):
-        there = jnp.where(lane < cols - 1, left(depths[i]), 0.0)
-        face_ref[1, i] = face(depths[i], there, spreads[i], left(spreads[i]))
-        there = jnp.where(lane > 0, right(depths[i]), 0.0)
-        face_ref[2, i] = face(depths[i], there, spreads[i], right(spreads[i]))
+        if not SUB <= i < SUB + rows - 1:
+            face_ref[0, i] = level_face(level, depths[i], depths[i + 1], spreads[i], spreads[i + 1])
+        if i > 0 and not SUB <= i < SUB + rows:
+            face_ref[1, i], face_ref[2, i] = side_faces(level, depths[i], spreads[i])
+
+    def after(sweep):
+        def get(i):
+            if sweep == 0:
+                return state_row(i)
+            if SUB + sweep <= i < SUB + rows - sweep:
+                return inner_ref.at[sweep - 1, i - SUB]
+            return outer_ref.at[sweep - 1, i]
+
+        return get
 
     for sweep in range(1, SUB + 1):
-        target = here_ref if sweep % 2 else there_ref
         for i in range(sweep, count - sweep):
-            def field(at):
-                if sweep == 1:
-                    return source(at)
-                return (there_ref if sweep % 2 else here_ref).at[at]
-
-            into = out_ref.at[i - SUB] if sweep == SUB else target.at[i]
+            done = SUB + sweep <= i < SUB + rows - sweep
+            if done and sweep < SUB:
+                continue
+            into = out_ref.at[i - SUB] if sweep == SUB else outer_ref.at[sweep - 1, i]
             for tracer in range(2):
                 at = pl.ds(tracer * padded, padded)
-                centre = field(i)[at, :]
-                total = centre + face_ref[0, i] * (field(i + 1)[at, :] - centre)
-                total = total + face_ref[0, i - 1] * (field(i - 1)[at, :] - centre)
-                total = total + face_ref[1, i] * (left(centre) - centre)
-                total = total + face_ref[2, i] * (right(centre) - centre)
-                into[at, :] = total
-
-
-def fields_kernel(
-    levels, padded, scale,
-    rows_ref, main_ref, edge_ref, other_ref, weight_ref, observed_ref, basis_ref, first_ref, fixed_ref,
-    mixed_ref, fields_ref, part_ref,
-):
-    rows, _, cols = rows_ref.shape
-    pairs = basis_ref.shape[2]
+                if done:
+                    into[at, :] = inner_ref[sweep - 1, i - SUB, at, :]
+                else:
+                    faces = face(0, i), face(0, i - 1), face(1, i), face(2, i)
+                    into[at, :] = mixed_row(after(sweep - 1), faces, i, at)
+
+
+def hold_kernel(weight_hbm, observed_hbm, weight_ref, observed_ref, sems):
+    copies = [
+        pltpu.make_async_copy(weight_hbm, weight_ref, sems.at[0]),
+        pltpu.make_async_copy(observed_hbm, observed_ref, sems.at[1]),
+    ]
+    for copy in copies:
+        copy.start()
+    for copy in copies:
+        copy.wait()
+
+
+def strip_kernel(levels, padded, edge_at, mine_ref, other_ref, _, out_ref):
+    cols = mine_ref.shape[1]
+    planes = 2 * padded
+    edge_ref = mine_ref.at[pl.ds(edge_at, planes)]
+    other_ref = other_ref.at[pl.ds(edge_at, planes)]
     lat = lax.axis_index("lat")
     lane = iota((1, cols), 1)
     place = lane % SLOT
@@ -554,8 +658,6 @@
     over_high = jnp.where(out_of_high, to_left, 0.0)
     own_right = jnp.where(place == SUB - 1, 0.0, to_right)
     own_left = jnp.where(place == SUB, 0.0, to_left)
-    start = jnp.where(lat == 0, cols - SUB, 0)
-    at_border = (lane >= start) & (lane < start + SUB)
 
     def spread_out(value, east, west):
         before, after = right(value), left(value)
@@ -580,12 +682,37 @@
             if sweep < SUB:
                 parts[tracer] = spread_out(part, to_right, to_left)
 
+    for tracer in range(2):
+        out_ref[pl.ds(tracer * padded, padded), :] = extras[tracer]
+
+
+def fields_kernel(
+    levels, padded, scale,
+    rows_ref, main_ref, extra_ref, weight_ref, observed_ref, basis_ref, first_ref, fixed_ref,
+    mixed_ref, fields_ref, part_ref,
+):
+    rows, _, cols = rows_ref.shape
+    pairs = basis_ref.shape[2]
+    lat = lax.axis_index("lat")
+    lane = iota((1, cols), 1)
+    place = lane % SLOT
+    level = iota((padded, cols), 0).astype(F32)
+
+    def left(value, by=1):
+        return pltpu.roll(value, (cols - by) % cols, 1)
+
+    def right(value, by=1):
+        return pltpu.roll(value, by, 1)
+
+    start = jnp.where(lat == 0, cols - SUB, 0)
+    at_border = (lane >= start) & (lane < start + SUB)
+
     for row in range(rows):
         i = row + SUB
         at = pl.ds(row, levels, stride=rows)
         mixed = []
         for tracer in range(2):
-            border = jnp.where(at_border, left(extras[tracer], SLOT * i + SUB), 0.0)
+            border = jnp.where(at_border, left(extra_ref[pl.ds(tracer * padded, padded), :], SLOT * i + SUB), 0.0)
             mixed.append((main_ref[row, pl.ds(tracer * padded, padded), :] + border)[:levels])
         wet = level[:levels] < rows_ref[row, pl.ds(levels + 1, 1), :]
         weight = weight_ref[at, :]
@@ -777,7 +904,7 @@
     )
     held = [x.shape for x in inputs[:-1]] + [(2, rows, cols)]
     close, distant = hist_rows(pairs)
-    sent_hist = (round_up(SUB * close + (REACH - SUB) * distant, 8), cols)
+    sent_hist = (round_up(SUB * close + (REACH - SUB) * distant, 8) + FOLD, cols)
     sent = (round_up(SUB * state_rows(levels)[0], 8), cols)
     shapes = ((rows, planes, cols), (rows, pairs, cols), sent_hist, sent_hist, sent, sent)
     packed, hist, first_hist, second_hist, first, second = pl.pallas_call(
@@ -797,23 +924,43 @@
     second_hist = lax.ppermute(second_hist, "loop", following)
     first = lax.ppermute(first, "loop", partner)
     second = lax.ppermute(second, "loop", following)
-    edge, depth, fixed = call(
-        functools.partial(pairs_kernel, levels),
-        [(planes, cols), (rows, cols), (4, rows, cols)],
+    edge, depth, fixed, own_face, inner = call(
+        functools.partial(pairs_kernel, levels, padded),
+        [
+            (planes, cols), (rows, cols), (4, rows, cols), (3, rows, padded, cols),
+            (SUB, rows, planes, cols),
+        ],
         name="pairs",
     )(packed, step, change)
     height = loops * rows
     large = VMEM_BYTES if loops <= 16 else 2 * VMEM_BYTES
     fields = 8 * 3 * rows
-    border, border_other = call(
+    fields = 8 * 3 * rows
+    edge_at = slot_groups(rows, cols) * pairs + 3 * rows
+    border, border_mine = call(
         functools.partial(border_kernel, levels, padded),
-        [
-            ((rows + 2 * REACH) * pairs + fields, cols),
-            (slot_groups(rows, cols) * pairs + fields, cols),
-        ],
+        [((rows + 2 * REACH) * pairs + fields, cols), (max(SWAP_ROWS, edge_at + planes), cols)],
         name="border",
-    )(first_hist, second_hist, packed, hist)
-    border_other = lax.ppermute(border_other, "lat", swap)
+    )(edge, first_hist, second_hist, packed, hist)
+    border_other = lax.ppermute(border_mine, "lat", swap)
+    held_weight, held_observed = pl.pallas_call(
+        hold_kernel,
+        out_shape=[jax.ShapeDtypeStruct(x.shape, F32) for x in (weight, observed)],
+        in_specs=[pl.BlockSpec(memory_space=pltpu.HBM)] * 2,
+        out_specs=[VMEM] * 2,
+        scratch_shapes=[pltpu.SemaphoreType.DMA((2,))],
+        compiler_params=pltpu.CompilerParams(vmem_limit_bytes=VMEM_BYTES),
+        name="hold",
+    )(*(pltpu.with_memory_space_constraint(x, pltpu.HBM) for x in (weight, observed)))
+    (extra,) = pl.pallas_call(
+        functools.partial(strip_kernel, levels, padded, edge_at),
+        out_shape=[jax.ShapeDtypeStruct((planes, cols), F32)],
+        in_specs=[VMEM] * 2 + [pl.BlockSpec(memory_space=pl.ANY)],
+        out_specs=[VMEM],
+        compiler_params=pltpu.CompilerParams(vmem_limit_bytes=VMEM_BYTES),
+        name="strip",
+    )(border_mine, border_other, held_weight)
+    fields_height = fields
     chains = 1 + ITERS
     buffers = SUB + ITERS + chains * (ITERS - 1)
     shapes = (
@@ -827,30 +974,31 @@
         out_shape=[jax.ShapeDtypeStruct(shape, F32) for shape in shapes],
         in_specs=[VMEM] * 4,
         out_specs=[VMEM] * len(shapes),
-        scratch_shapes=[pltpu.VMEM((rows + 2 * REACH, pairs, 2 * cols), F32)] * buffers,
+        scratch_shapes=[pltpu.VMEM((rows + 2 * REACH, pairs, 2 * cols), F32)] * (buffers - 1)
+        + [
+            pltpu.VMEM((fields_height, cols), F32),
+            pltpu.VMEM((rows + 2 * REACH, pairs, 2 * cols), F32),
+        ],
         compiler_params=pltpu.CompilerParams(vmem_limit_bytes=VMEM_BYTES),
         name="basis",
     )(border, border_other, step, change)
-    edge, halo = call(
-        functools.partial(halo_kernel, levels, padded, rows),
-        [(planes, cols), (2 * SUB, planes, cols)],
-        name="halo",
-    )(edge, first, second, near_start)
-    other = lax.ppermute(edge, "lat", swap)
     tall = rows + 2 * SUB
     (mixed,) = call(
         functools.partial(mix_kernel, levels, padded),
         [(rows, planes, cols)],
-        scratch=[pltpu.VMEM((3, tall, padded, cols), F32)]
-        + [pltpu.VMEM((tall, planes, cols), F32)] * 2,
+        scratch=[
+            pltpu.VMEM((3, tall, padded, cols), F32),
+            pltpu.VMEM((SUB - 1, tall, planes, cols), F32),
+            pltpu.VMEM((2 * SUB, planes, cols), F32),
+        ],
         name="mix",
-    )(packed, halo)
+    )(packed, first, second, own_face, inner, near_start)
     mixed, fields = call(
         functools.partial(fields_kernel, levels, padded, scale),
         [flat, (loops, 6, rows, cols)],
         scratch=[pltpu.VMEM((6, rows, cols), F32)],
         name="fields",
-    )(packed, mixed, edge, other, weight, observed, basis, near_start, fixed)
+    )(packed, mixed, extra, held_weight, held_observed, basis, near_start, fixed)
     mine = lax.all_to_all(fields, "loop", 0, 0)
     theirs = lax.ppermute(mine, "lat", swap)
     faces, plan = call(

time: 37.6 us -> 37.3 us (level)
  waiting for transfers between devices: 6.28 us -> 3.27 us
  Pallas kernels: 8.85 us -> 10.2 us
  local copies, waits for them, and re-layouts: 0.67 us -> 1.68 us
  blocking collectives: 12.2 us -> 12.6 us
    pallas_call x2 -> x3, Pallas kernels: 0.49 us -> 2.38 us  [the longest x1 1.13 us: on_device(): pl.pallas_call(hold_kernel, out_shape=[jax.ShapeDtypeStruct(x.shape, F32)...]
    ppermute x1, waiting for transfers between devices: 1.71 us -> 0.01 us  [on_device(): second_hist = lax.ppermute(second_hist, 'loop', following)]
    ppermute x1, waiting for transfers between devices: 2.76 us -> 1.64 us  [on_device(): first = lax.ppermute(first, 'loop', partner)]
    unnamed x8 -> x6, local copies, waits for them, and re-layouts: 0.67 us -> 1.68 us
    pallas_call x1, Pallas kernels: 0.88 us -> 0.42 us  [on_device(): call(functools.partial(fields_kernel, levels, padded, scale), [flat, (loo...]
    pallas_call x1, Pallas kernels: 1.22 us -> 0.78 us  [on_device(): call(functools.partial(mix_kernel, levels, padded), [(rows, planes, cols)...]
    all_to_all x1, blocking collectives: 12.2 us -> 12.6 us  [on_device(): mine = lax.all_to_all(fields, 'loop', 0, 0)]
  transfers between devices with their start and end apart: 7 -> 6, of which waited for: 4 -> 3; matrix products, arithmetic and copies ran while one was open for 0% -> 0% of each run, Pallas kernels for 9% -> 12%
where the time goes in v9:
time: 37.3 us; the launch traced here: 37 us
  blocking collectives  12.6 us (34%)
  Pallas kernels  10.2 us (27%)
  starting transfers between devices  8.56 us (23%)
  waiting for transfers between devices  3.27 us (9%)
  local copies, waits for them, and re-layouts  1.68 us (5%)
  between operations  0.73 us (2%)
    all_to_all x1, blocking collectives, on_device(): mine = lax.all_to_all(fields, 'loop', 0, 0)  12.6 us
    ppermute x1, starting transfers between devices, on_device(): second_hist = lax.ppermute(second_hist, 'loop', following)  3.57 us
    ppermute x1, starting transfers between devices, on_device(): first_hist = lax.ppermute(first_hist, 'loop', partner)  3 us
    pallas_call x1, Pallas kernels, on_device(): call(functools.partial(solve_kernel, levels, scale), shapes, scratch=[plt...  2.59 us
    pallas_call x1, Pallas kernels, on_device(): pl.pallas_call(functools.partial(basis_kernel, rows, pairs), out_shape=[j...  1.91 us
    ppermute x1, starting transfers between devices, on_device(): second = lax.ppermute(second, 'loop', following)  1.91 us
    unnamed x6, local copies, waits for them, and re-layouts  1.68 us
    pallas_call x1, Pallas kernels, on_device(): pl.pallas_call(functools.partial(pack_kernel, levels, padded), out_shape=...  1.65 us
  transfers between devices with their start and end apart: 6, of which 3 were waited for; matrix products, arithmetic and copies ran while one was open for 0% of the time, Pallas kernels for 12%

profile of v9, /device:TPU:0, one launch (start us, length us, event | category | flops | bytes accessed | tf_op | source)
XLA Modules:
  0.0 37.0 jit_solution(18105905744934767294)
XLA Ops:
  0.6 0.0 copy-start.1
  0.6 1.7 %pack.1 = (f32[8,112,128]{2,1,0:T(8,128)S(1)}, f32[8,16,128]{2,1,0:T(8,128)S(1)}, f32[176,128]{1,0:T(8,128)S(1)}, f32[176,128]{1,0:T(8,128)S(1)}, f32[312,128]{1,0:T(8,128)S(1)}, /*index=5*/f32[312,128]{1,0:T(8,128)S(1)}) custom-call(f32[2,400,128]{2,1,0:T(8,128)} %bitcast.20, f32[2,8,128]{2,1,0:T(8,128)} %refs_1_.1, s32[8,128]{1,0:T(8,128)} %refs_2_.1, ...), custom_call_target="tpu_custom_call" | custom-call | tf_op jit(solution)/shard_map/pack/pallas_call | solution.py:910
  2.3 3.0 %collective-permute-start.2 = (f32[176,128]{1,0:T(8,128)S(1)}, f32[176,128]{1,0:T(8,128)S(1)}, u32[]{:S(2)}, u32[]{:S(2)}) collective-permute-start(f32[176,128]{1,0:T(8,128)S(1)} %get-tuple-element.35), channel_id=1, source_target_pairs={{0,2},{2,0},{4,6},{6,4},{8,10},{10,8},{12,14},{14,12},{1,3},{3,1},... | collective-permute-start | bytes 270344 | tf_op jit(solution)/shard_map/ppermute | solution.py:923
  5.3 3.6 %collective-permute-start.3 = (f32[176,128]{1,0:T(8,128)S(1)}, f32[176,128]{1,0:T(8,128)S(1)}, u32[]{:S(2)}, u32[]{:S(2)}) collective-permute-start(f32[176,128]{1,0:T(8,128)S(1)} %get-tuple-element.36), channel_id=1, source_target_pairs={{0,14},{2,4},{4,2},{6,8},{8,6},{10,12},{12,10},{14,0},{1,15},{3,5}... | collective-permute-start | bytes 270344 | tf_op jit(solution)/shard_map/ppermute | solution.py:924
  8.9 0.0 collective-permute-start
  8.9 1.9 %collective-permute-start.1 = (f32[312,128]{1,0:T(8,128)S(1)}, f32[312,128]{1,0:T(8,128)S(1)}, u32[]{:S(2)}, u32[]{:S(2)}) collective-permute-start(f32[312,128]{1,0:T(8,128)S(1)} %get-tuple-element.31), channel_id=1, source_target_pairs={{0,14},{2,4},{4,2},{6,8},{8,6},{10,12},{12,10},{14,0},{1,15},{3,5}... | collective-permute-start | bytes 479240 | tf_op jit(solution)/shard_map/ppermute | solution.py:926
  10.8 0.8 %copy-done = f32[8,2,8,128]{3,2,1,0:T(8,128)S(1)} copy-done((f32[8,2,8,128]{3,2,1,0:T(8,128)S(1)}, f32[8,2,8,128]{3,2,1,0:T(8,128)}, u32[]{:S(2)}) %copy-start) | copy-done | bytes 65560
  11.6 0.8 %copy-done.2 = f32[8,2,8,128]{3,2,1,0:T(8,128)S(1)} copy-done((f32[8,2,8,128]{3,2,1,0:T(8,128)S(1)}, f32[8,2,8,128]{3,2,1,0:T(8,128)}, u32[]{:S(2)}) %copy-start.2) | copy-done | bytes 65560
  12.5 0.8 %pairs.1 = (f32[112,128]{1,0:T(8,128)S(1)}, f32[8,128]{1,0:T(8,128)S(1)}, f32[4,8,128]{2,1,0:T(8,128)S(1)}, f32[3,8,56,128]{3,2,1,0:T(8,128)S(1)}, f32[3,8,112,128]{3,2,1,0:T(8,128)S(1)}) custom-call(f32[8,112,128]{2,1,0:T(8,128)S(1)} %get-tuple-element.29.rows_ref, f32[8,16,128]{2,1,0:T(8,128)S(1)} %bitcast.9, f32[8,16,128]{2,1,0:T(8,128)S(1)} %bitcast.13), custom_call_target="tpu_custom_call" | custom-call | tf_op jit(solution)/shard_map/pairs/pallas_call | solution.py:927
  13.3 0.0 collective-permute-done.3.second_ref
  13.3 0.2 border.1
  13.5 0.1 collective-permute-start.4
  13.6 1.1 %hold.1 = (f32[400,128]{1,0:T(8,128)S(1)}, f32[2,400,128]{2,1,0:T(8,128)S(1)}) custom-call(f32[400,128]{1,0:T(8,128)} %bitcast.19, f32[2,400,128]{2,1,0:T(8,128)} %bitcast.17), custom_call_target="tpu_custom_call" | custom-call | tf_op jit(solution)/shard_map/hold/pallas_call | solution.py:946
  14.7 0.2 collective-permute-done.4.other_ref
  14.9 1.9 %basis.1 = (f32[11,8,16,128]{3,2,1,0:T(8,128)S(1)}, f32[6,24,256]{2,1,0:T(8,128)S(1)}, f32[2,8,128]{2,1,0:T(8,128)S(1)}, f32[8,128]{1,0:T(8,128)S(1)}) custom-call(f32[544,128]{1,0:T(8,128)S(1)} %get-tuple-element.38.mine_ref, f32[240,128]{1,0:T(8,128)S(1)} %collective-permute-done.4.other_ref, f32[8,16,128]{2,1,0:T(8,128)S(1)} %bitcast.10, ...), custom_call_target="tpu_custom_call" | custom-call | tf_op jit(solution)/shard_map/basis/pallas_call | solution.py:972
  16.8 0.4 %strip.1.extra_ref = f32[112,128]{1,0:T(8,128)S(1)} custom-call(f32[240,128]{1,0:T(8,128)S(1)} %get-tuple-element.39.mine_ref, f32[240,128]{1,0:T(8,128)S(1)} %collective-permute-done.4.other_ref, f32[400,128]{1,0:T(8,128)S(1)} %get-tuple-element.41._.weight_ref), custom_call_target="tpu_custom_call" | custom-call | tf_op jit(solution)/shard_map/strip/pallas_call | solution.py:955
  17.3 1.6 %collective-permute-done.first_ref = f32[312,128]{1,0:T(8,128)S(1)} collective-permute-done((f32[312,128]{1,0:T(8,128)S(1)}, f32[312,128]{1,0:T(8,128)S(1)}, u32[]{:S(2)}, u32[]{:S(2)}) %collective-permute-start) | collective-permute-done | bytes 159776 | tf_op jit(solution)/shard_map/ppermute | solution.py:925
  18.9 0.8 %mix.1.main_ref = f32[8,112,128]{2,1,0:T(8,128)S(1)} custom-call(f32[8,112,128]{2,1,0:T(8,128)S(1)} %get-tuple-element.29.rows_ref, f32[312,128]{1,0:T(8,128)S(1)} %collective-permute-done.first_ref, f32[312,128]{1,0:T(8,128)S(1)} %collective-permute-done.1.second_ref, f32[3,8,56,128]{3,2,1,0:T(8,128)S(1)} %get-tuple-element.32.own_face_ref, ...), custom_call_target="tpu_custom_call" | custom-call | tf_op jit(solution)/shard_map/mix/pallas_call | solution.py:986
  19.7 0.4 %fields.1 = (f32[2,400,128]{2,1,0:T(8,128)S(1)}, f32[8,6,8,128]{3,2,1,0:T(8,128)S(1)}) custom-call(f32[8,112,128]{2,1,0:T(8,128)S(1)} %get-tuple-element.29.rows_ref, f32[8,112,128]{2,1,0:T(8,128)S(1)} %mix.1.main_ref, f32[112,128]{1,0:T(8,128)S(1)} %strip.1.extra_ref, f32[400,128]{1,0:T(8,128)S(1)} %get-tuple-element.41._.weight_ref, ...), custom_call_target="tpu_custom_call" | custom-call | tf_op jit(solution)/shard_map/fields/pallas_call | solution.py:996
  20.2 12.6 %all_to_all.5.mine_ref = f32[8,6,8,128]{3,2,1,0:T(8,128)S(1)} all-to-all(f32[8,6,8,128]{3,2,1,0:T(8,128)S(1)} %get-tuple-element.45), channel_id=1, replica_groups=mesh['members'=2,'loop'=8,'lat'=2] {'loop'}, dimensions={0} | all-to-all | bytes 393216 | tf_op jit(solution)/shard_map/all_to_all | solution.py:1002
  32.8 0.0 collective-permute-start.5
  32.8 1.4 %collective-permute-done.5.other_ref = f32[8,6,8,128]{3,2,1,0:T(8,128)S(1)} collective-permute-done((f32[8,6,8,128]{3,2,1,0:T(8,128)S(1)}, f32[8,6,8,128]{3,2,1,0:T(8,128)S(1)}, u32[]{:S(2)}, u32[]{:S(2)}) %collective-permute-start.5) | collective-permute-done | bytes 196640 | tf_op jit(solution)/shard_map/ppermute | solution.py:1003
  34.2 0.2 plan.1
  34.5 2.6 %solve.1 = (f32[2,400,128]{2,1,0:T(8,128)}, f32[2,8,128]{2,1,0:T(8,128)}, f32[2,8,128]{2,1,0:T(8,128)}) custom-call(f32[8,6,8,128]{3,2,1,0:T(8,128)S(1)} %all_to_all.5.mine_ref, f32[8,6,8,128]{3,2,1,0:T(8,128)S(1)} %collective-permute-done.5.other_ref, f32[6,64,256]{2,1,0:T(8,128)S(1)} %get-tuple-element.46.faces_ref, ...), custom_call_target="tpu_custom_call" | custom-call | tf_op jit(solution)/shard_map/solve/pallas_call | solution.py:1008
  (5 shorter events, 0.0 us)
Async XLA Ops:
  0.6 14.3 %copy-start.1 = (f32[8,2,8,128]{3,2,1,0:T(8,128)S(1)}, f32[8,2,8,128]{3,2,1,0:T(8,128)}, u32[]{:S(2)}) copy-start(f32[8,2,8,128]{3,2,1,0:T(8,128)} %param.16) | copy-start | bytes 196612
  2.3 11.0 %collective-permute-start.2 = (f32[176,128]{1,0:T(8,128)S(1)}, f32[176,128]{1,0:T(8,128)S(1)}, u32[]{:S(2)}, u32[]{:S(2)}) collective-permute-start(f32[176,128]{1,0:T(8,128)S(1)} %get-tuple-element.35), channel_id=1, source_target_pairs={{0,2},{2,0},{4,6},{6,4},{8,10},{10,8},{12,14},{14,12},{1,3},{3,1},... | collective-permute-start | bytes 270344 | tf_op jit(solution)/shard_map/ppermute | solution.py:923
  5.3 8.0 %collective-permute-start.3 = (f32[176,128]{1,0:T(8,128)S(1)}, f32[176,128]{1,0:T(8,128)S(1)}, u32[]{:S(2)}, u32[]{:S(2)}) collective-permute-start(f32[176,128]{1,0:T(8,128)S(1)} %get-tuple-element.36), channel_id=1, source_target_pairs={{0,14},{2,4},{4,2},{6,8},{8,6},{10,12},{12,10},{14,0},{1,15},{3,5}... | collective-permute-start | bytes 270344 | tf_op jit(solution)/shard_map/ppermute | solution.py:924
  8.9 10.0 %collective-permute-start = (f32[312,128]{1,0:T(8,128)S(1)}, f32[312,128]{1,0:T(8,128)S(1)}, u32[]{:S(2)}, u32[]{:S(2)}) collective-permute-start(f32[312,128]{1,0:T(8,128)S(1)} %get-tuple-element.30), channel_id=1, source_target_pairs={{0,2},{2,0},{4,6},{6,4},{8,10},{10,8},{12,14},{14,12},{1,3},{3,1},... | collective-permute-start | bytes 479240 | tf_op jit(solution)/shard_map/ppermute | solution.py:925
  8.9 10.0 %collective-permute-start.1 = (f32[312,128]{1,0:T(8,128)S(1)}, f32[312,128]{1,0:T(8,128)S(1)}, u32[]{:S(2)}, u32[]{:S(2)}) collective-permute-start(f32[312,128]{1,0:T(8,128)S(1)} %get-tuple-element.31), channel_id=1, source_target_pairs={{0,14},{2,4},{4,2},{6,8},{8,6},{10,12},{12,10},{14,0},{1,15},{3,5}... | collective-permute-start | bytes 479240 | tf_op jit(solution)/shard_map/ppermute | solution.py:926
  10.8 0.8 %copy-start = (f32[8,2,8,128]{3,2,1,0:T(8,128)S(1)}, f32[8,2,8,128]{3,2,1,0:T(8,128)}, u32[]{:S(2)}) copy-start(f32[8,2,8,128]{3,2,1,0:T(8,128)} %param.16) | copy-start | bytes 196612
  11.6 0.8 %copy-start.2 = (f32[8,2,8,128]{3,2,1,0:T(8,128)S(1)}, f32[8,2,8,128]{3,2,1,0:T(8,128)}, u32[]{:S(2)}) copy-start(f32[8,2,8,128]{3,2,1,0:T(8,128)} %param.17) | copy-start | bytes 196612
  13.5 1.4 %collective-permute-start.4 = (f32[240,128]{1,0:T(8,128)S(1)}, f32[240,128]{1,0:T(8,128)S(1)}, u32[]{:S(2)}, u32[]{:S(2)}) collective-permute-start(f32[240,128]{1,0:T(8,128)S(1)} %get-tuple-element.39.mine_ref), channel_id=1, source_target_pairs={{0,1},{1,0},{2,3},{3,2},{4,5},{5,4},{6,7},{7,6},{8,9},{9,8},{10,11... | collective-permute-start | bytes 368648 | tf_op jit(solution)/shard_map/ppermute | solution.py:945
  32.8 1.4 %collective-permute-start.5 = (f32[8,6,8,128]{3,2,1,0:T(8,128)S(1)}, f32[8,6,8,128]{3,2,1,0:T(8,128)S(1)}, u32[]{:S(2)}, u32[]{:S(2)}) collective-permute-start(f32[8,6,8,128]{3,2,1,0:T(8,128)S(1)} %all_to_all.5.mine_ref), channel_id=1, source_target_pairs={{0,1},{1,0},{2,3},{3,2},{4,5},{5,4},{6,7},{7,6},{8,9},{9,8},{10,11... | collective-permute-start | bytes 589832 | tf_op jit(solution)/shard_map/ppermute | solution.py:1003

commit v10 on v9

--- a/solution.py
+++ b/solution.py
@@ -52,8 +52,9 @@
 
 
 def pack_kernel(levels, padded, *refs):
-    sources, outs, targets, sems = refs[:9], refs[9:15], refs[15:24], refs[24]
+    sources, outs, targets, sems = refs[:9], refs[9:15], refs[15:22], refs[22]
     rows_ref, hist_ref = outs[:2]
+    targets = targets[:4] + outs[4:6] + targets[4:]
     rows, cols = targets[2].shape
     copies = []
     for at, (source, target) in enumerate(zip(sources, targets)):
@@ -70,7 +71,6 @@
     ) = targets
     count = step_ref.shape[0] // (2 * rows)
     pairs = 2 * count
-    near, second = state_rows(levels)
     close, distant = hist_rows(pairs)
     depth = depth_ref[...].astype(F32)
     spread = spread_ref[...]
@@ -114,11 +114,6 @@
         refs[0][here, :] = jnp.where(even, upper, lower)
         refs[1][here, :] = jnp.where(even, lower, upper)
 
-    def fill(refs, last):
-        if last < refs[0].shape[0]:
-            rest = jnp.zeros((refs[0].shape[0] - last, cols), F32)
-            put(refs, last, rest, rest)
-
     masked = jnp.where(wet, spread, 0.0)
     for at in range(REACH):
         far = at < REACH - SUB
@@ -149,12 +144,6 @@
         folded(edge_of(lambda i: rows_ref[rows - SUB + i], range(SUB), cols, lat)),
         folded(edge_of(lambda i: rows_ref[i], range(SUB), cols, lat)),
     )
-    for at in range(SUB):
-        upper, lower = rows - SUB + at, at
-        for start, size, place in ((0, levels + 2, 0), (padded, levels, second)):
-            here = pl.ds(start, size)
-            put(outs[4:6], at * near + place, rows_ref[upper, here, :], rows_ref[lower, here, :])
-    fill(outs[4:6], SUB * near)
 
 
 def edge_of(rows_of, indices, cols, lat):
@@ -219,9 +208,25 @@
 
 
 def pairs_kernel(
-    levels, padded, rows_ref, step_ref, change_ref, edge_ref, depth_ref, fixed_ref, face_ref, inner_ref
+    levels, padded, rows_ref, step_ref, change_ref,
+    first_ref, second_ref, edge_ref, depth_ref, fixed_ref, face_ref, inner_ref,
 ):
     rows, _, cols = rows_ref.shape
+    even = lax.rem(lax.axis_index("loop"), 2) == 0
+    near, second = state_rows(levels)
+
+    def put(at, upper, lower):
+        here = pl.ds(at, upper.shape[0])
+        first_ref[here, :] = jnp.where(even, upper, lower)
+        second_ref[here, :] = jnp.where(even, lower, upper)
+
+    for i in range(SUB):
+        for start, size, place in ((0, levels + 2, 0), (padded, levels, second)):
+            here = pl.ds(start, size)
+            put(i * near + place, rows_ref[rows - SUB + i, here, :], rows_ref[i, here, :])
+    if SUB * near < first_ref.shape[0]:
+        rest = jnp.zeros((first_ref.shape[0] - SUB * near, cols), F32)
+        put(SUB * near, rest, rest)
     level = iota((padded, cols), 0).astype(F32)
     spreads = [rows_ref[i, pl.ds(levels, 1), :] for i in range(rows)]
     depths = [rows_ref[i, pl.ds(levels + 1, 1), :] for i in range(rows)]
@@ -894,8 +899,6 @@
     state = state.reshape(flat)
     observed = observed.reshape(flat)
     weight = weight.reshape(flat[1:])
-    step = history_step.reshape(count, 2 * rows, cols)
-    change = history_change.reshape(count, 2 * rows, cols)
 
     pairs = 2 * count
     inputs = (
@@ -906,13 +909,16 @@
     close, distant = hist_rows(pairs)
     sent_hist = (round_up(SUB * close + (REACH - SUB) * distant, 8) + FOLD, cols)
     sent = (round_up(SUB * state_rows(levels)[0], 8), cols)
-    shapes = ((rows, planes, cols), (rows, pairs, cols), sent_hist, sent_hist, sent, sent)
-    packed, hist, first_hist, second_hist, first, second = pl.pallas_call(
+    stored = (2 * count * rows, cols)
+    shapes = ((rows, planes, cols), (rows, pairs, cols), sent_hist, sent_hist, stored, stored)
+    packed, hist, first_hist, second_hist, step, change = pl.pallas_call(
         functools.partial(pack_kernel, levels, padded),
         out_shape=[jax.ShapeDtypeStruct(shape, F32) for shape in shapes],
         in_specs=[pl.BlockSpec(memory_space=pltpu.HBM)] * len(inputs),
         out_specs=[VMEM] * len(shapes),
-        scratch_shapes=[pltpu.VMEM(shape, x.dtype) for shape, x in zip(held, inputs)]
+        scratch_shapes=[
+            pltpu.VMEM(shape, x.dtype) for at, (shape, x) in enumerate(zip(held, inputs)) if at not in (4, 5)
+        ]
         + [pltpu.SemaphoreType.DMA((len(inputs),))],
         compiler_params=pltpu.CompilerParams(vmem_limit_bytes=VMEM_BYTES),
         name="pack",
@@ -921,17 +927,19 @@
     following = [(i, (i - 1 + 2 * (i % 2)) % loops) for i in range(loops)]
     swap = [(0, 1), (1, 0)]
     first_hist = lax.ppermute(first_hist, "loop", partner)
+    step = step.reshape(count, 2 * rows, cols)
+    change = change.reshape(count, 2 * rows, cols)
     second_hist = lax.ppermute(second_hist, "loop", following)
-    first = lax.ppermute(first, "loop", partner)
-    second = lax.ppermute(second, "loop", following)
-    edge, depth, fixed, own_face, inner = call(
+    first, second, edge, depth, fixed, own_face, inner = call(
         functools.partial(pairs_kernel, levels, padded),
         [
-            (planes, cols), (rows, cols), (4, rows, cols), (3, rows, padded, cols),
+            sent, sent, (planes, cols), (rows, cols), (4, rows, cols), (3, rows, padded, cols),
             (SUB, rows, planes, cols),
         ],
         name="pairs",
     )(packed, step, change)
+    first = lax.ppermute(first, "loop", partner)
+    second = lax.ppermute(second, "loop", following)
     height = loops * rows
     large = VMEM_BYTES if loops <= 16 else 2 * VMEM_BYTES
     fields = 8 * 3 * rows

time: 37.3 us -> 36.1 us (0.968)
  waiting for transfers between devices: 3.27 us -> 5.37 us
  local copies, waits for them, and re-layouts: 1.68 us -> 0 us
  blocking collectives: 12.6 us -> 11.1 us
    unnamed x6 -> x0, local copies, waits for them, and re-layouts: 1.68 us -> none
    all_to_all x1, blocking collectives: 12.6 us -> 11.1 us  [on_device(): mine = lax.all_to_all(fields, 'loop', 0, 0)]
    ppermute x1, waiting for transfers between devices: 1.64 us -> 2.77 us  [on_device(): first = lax.ppermute(first, 'loop', partner)]
    ppermute x1, waiting for transfers between devices: 0.01 us -> 0.97 us  [on_device(): second_hist = lax.ppermute(second_hist, 'loop', following)]
  transfers between devices with their start and end apart: 6 -> 6, of which waited for: 3 -> 4; matrix products, arithmetic and copies ran while one was open for 0% -> 0% of each run, Pallas kernels for 12% -> 12%
where the time goes in v10:
time: 36.1 us; the launch traced here: 35.9 us
  blocking collectives  11.1 us (31%)
  Pallas kernels  10.1 us (28%)
  starting transfers between devices  8.62 us (24%)
  waiting for transfers between devices  5.37 us (15%)
  between operations  0.71 us (2%)
    all_to_all x1, blocking collectives, on_device(): mine = lax.all_to_all(fields, 'loop', 0, 0)  11.1 us
    ppermute x1, starting transfers between devices, on_device(): second_hist = lax.ppermute(second_hist, 'loop', following)  3.57 us
    ppermute x1, starting transfers between devices, on_device(): first_hist = lax.ppermute(first_hist, 'loop', partner)  3 us
    ppermute x1, waiting for transfers between devices, on_device(): first = lax.ppermute(first, 'loop', partner)  2.77 us
    pallas_call x1, Pallas kernels, on_device(): call(functools.partial(solve_kernel, levels, scale), shapes, scratch=[plt...  2.59 us
    pallas_call x1, Pallas kernels, on_device(): pl.pallas_call(functools.partial(basis_kernel, rows, pairs), out_shape=[j...  1.91 us
    ppermute x1, starting transfers between devices, on_device(): second = lax.ppermute(second, 'loop', following)  1.9 us
    pallas_call x1, Pallas kernels, on_device(): pl.pallas_call(functools.partial(pack_kernel, levels, padded), out_shape=...  1.62 us
  transfers between devices with their start and end apart: 6, of which 4 were waited for; matrix products, arithmetic and copies ran while one was open for 0% of the time, Pallas kernels for 12%

profile of v10, /device:TPU:0, one launch (start us, length us, event | category | flops | bytes accessed | tf_op | source)
XLA Modules:
  0.0 35.9 jit_solution(15303917513596206188)
XLA Ops:
  0.6 1.6 %pack.1 = (f32[8,112,128]{2,1,0:T(8,128)S(1)}, f32[8,16,128]{2,1,0:T(8,128)S(1)}, f32[176,128]{1,0:T(8,128)S(1)}, f32[176,128]{1,0:T(8,128)S(1)}, f32[128,128]{1,0:T(8,128)S(1)}, /*index=5*/f32[128,128]{1,0:T(8,128)S(1)}) custom-call(f32[2,400,128]{2,1,0:T(8,128)} %bitcast.18, f32[2,8,128]{2,1,0:T(8,128)} %refs_1_.1, s32[8,128]{1,0:T(8,128)} %refs_2_.1, ...), custom_call_target="tpu_custom_call" | custom-call | tf_op jit(solution)/shard_map/pack/pallas_call | solution.py:914
  2.3 3.0 %collective-permute-start.2 = (f32[176,128]{1,0:T(8,128)S(1)}, f32[176,128]{1,0:T(8,128)S(1)}, u32[]{:S(2)}, u32[]{:S(2)}) collective-permute-start(f32[176,128]{1,0:T(8,128)S(1)} %get-tuple-element.39), channel_id=1, source_target_pairs={{0,2},{2,0},{4,6},{6,4},{8,10},{10,8},{12,14},{14,12},{1,3},{3,1},... | collective-permute-start | bytes 270344 | tf_op jit(solution)/shard_map/ppermute | solution.py:929
  5.3 3.6 %collective-permute-start.3 = (f32[176,128]{1,0:T(8,128)S(1)}, f32[176,128]{1,0:T(8,128)S(1)}, u32[]{:S(2)}, u32[]{:S(2)}) collective-permute-start(f32[176,128]{1,0:T(8,128)S(1)} %get-tuple-element.40), channel_id=1, source_target_pairs={{0,14},{2,4},{4,2},{6,8},{8,6},{10,12},{12,10},{14,0},{1,15},{3,5}... | collective-permute-start | bytes 270344 | tf_op jit(solution)/shard_map/ppermute | solution.py:932
  8.8 0.8 %pairs.1 = (f32[312,128]{1,0:T(8,128)S(1)}, f32[312,128]{1,0:T(8,128)S(1)}, f32[112,128]{1,0:T(8,128)S(1)}, f32[8,128]{1,0:T(8,128)S(1)}, f32[4,8,128]{2,1,0:T(8...) custom-call(f32[8,112,128]{2,1,0:T(8,128)S(1)} %get-tuple-element.31.rows_ref, ...), custom_call_target="tpu_custom_call" | custom-call | tf_op jit(solution)/shard_map/pairs/pallas_call | solution.py:933
  9.6 0.1 collective-permute-start
  9.7 1.9 %collective-permute-start.1 = (f32[312,128]{1,0:T(8,128)S(1)}, f32[312,128]{1,0:T(8,128)S(1)}, u32[]{:S(2)}, u32[]{:S(2)}) collective-permute-start(f32[312,128]{1,0:T(8,128)S(1)} %get-tuple-element.35), channel_id=1, source_target_pairs={{0,14},{2,4},{4,2},{6,8},{8,6},{10,12},{12,10},{14,0},{1,15},{3,5}... | collective-permute-start | bytes 479240 | tf_op jit(solution)/shard_map/ppermute | solution.py:942
  11.6 0.0 collective-permute-done.2.first_ref
  11.6 1.0 %collective-permute-done.3.second_ref = f32[176,128]{1,0:T(8,128)S(1)} collective-permute-done((f32[176,128]{1,0:T(8,128)S(1)}, f32[176,128]{1,0:T(8,128)S(1)}, u32[]{:S(2)}, u32[]{:S(2)}) %collective-permute-start.3) | collective-permute-done | bytes 90144 | tf_op jit(solution)/shard_map/ppermute | solution.py:932
  12.6 0.2 border.1
  12.8 0.1 collective-permute-start.4
  12.9 1.1 %hold.1 = (f32[400,128]{1,0:T(8,128)S(1)}, f32[2,400,128]{2,1,0:T(8,128)S(1)}) custom-call(f32[400,128]{1,0:T(8,128)} %bitcast.17, f32[2,400,128]{2,1,0:T(8,128)} %bitcast.15), custom_call_target="tpu_custom_call" | custom-call | tf_op jit(solution)/shard_map/hold/pallas_call | solution.py:954
  14.0 0.2 collective-permute-done.4.other_ref
  14.2 1.9 %basis.1 = (f32[11,8,16,128]{3,2,1,0:T(8,128)S(1)}, f32[6,24,256]{2,1,0:T(8,128)S(1)}, f32[2,8,128]{2,1,0:T(8,128)S(1)}, f32[8,128]{1,0:T(8,128)S(1)}) custom-call(f32[544,128]{1,0:T(8,128)S(1)} %get-tuple-element.42.mine_ref, f32[240,128]{1,0:T(8,128)S(1)} %collective-permute-done.4.other_ref, f32[8,16,128]{2,1,0:T(8,128)S(1)} %bitcast.9, ...), custom_call_target="tpu_custom_call" | custom-call | tf_op jit(solution)/shard_map/basis/pallas_call | solution.py:980
  16.1 0.4 %strip.1.extra_ref = f32[112,128]{1,0:T(8,128)S(1)} custom-call(f32[240,128]{1,0:T(8,128)S(1)} %get-tuple-element.43.mine_ref, f32[240,128]{1,0:T(8,128)S(1)} %collective-permute-done.4.other_ref, f32[400,128]{1,0:T(8,128)S(1)} %get-tuple-element.45._.weight_ref), custom_call_target="tpu_custom_call" | custom-call | tf_op jit(solution)/shard_map/strip/pallas_call | solution.py:963
  16.6 2.8 %collective-permute-done.first_ref = f32[312,128]{1,0:T(8,128)S(1)} collective-permute-done((f32[312,128]{1,0:T(8,128)S(1)}, f32[312,128]{1,0:T(8,128)S(1)}, u32[]{:S(2)}, u32[]{:S(2)}) %collective-permute-start) | collective-permute-done | bytes 159776 | tf_op jit(solution)/shard_map/ppermute | solution.py:941
  19.3 0.0 collective-permute-done.1.second_ref
  19.3 0.8 %mix.1.main_ref = f32[8,112,128]{2,1,0:T(8,128)S(1)} custom-call(f32[8,112,128]{2,1,0:T(8,128)S(1)} %get-tuple-element.31.rows_ref, f32[312,128]{1,0:T(8,128)S(1)} %collective-permute-done.first_ref, f32[312,128]{1,0:T(8,128)S(1)} %collective-permute-done.1.second_ref, f32[3,8,56,128]{3,2,1,0:T(8,128)S(1)} %get-tuple-element.36.own_face_ref, ...), custom_call_target="tpu_custom_call" | custom-call | tf_op jit(solution)/shard_map/mix/pallas_call | solution.py:994
  20.1 0.4 %fields.1 = (f32[2,400,128]{2,1,0:T(8,128)S(1)}, f32[8,6,8,128]{3,2,1,0:T(8,128)S(1)}) custom-call(f32[8,112,128]{2,1,0:T(8,128)S(1)} %get-tuple-element.31.rows_ref, f32[8,112,128]{2,1,0:T(8,128)S(1)} %mix.1.main_ref, f32[112,128]{1,0:T(8,128)S(1)} %strip.1.extra_ref, f32[400,128]{1,0:T(8,128)S(1)} %get-tuple-element.45._.weight_ref, ...), custom_call_target="tpu_custom_call" | custom-call | tf_op jit(solution)/shard_map/fields/pallas_call | solution.py:1004
  20.5 11.1 %all_to_all.5.mine_ref = f32[8,6,8,128]{3,2,1,0:T(8,128)S(1)} all-to-all(f32[8,6,8,128]{3,2,1,0:T(8,128)S(1)} %get-tuple-element.49), channel_id=1, replica_groups=mesh['members'=2,'loop'=8,'lat'=2] {'loop'}, dimensions={0} | all-to-all | bytes 393216 | tf_op jit(solution)/shard_map/all_to_all | solution.py:1010
  31.7 0.0 collective-permute-start.5
  31.7 1.4 %collective-permute-done.5.other_ref = f32[8,6,8,128]{3,2,1,0:T(8,128)S(1)} collective-permute-done((f32[8,6,8,128]{3,2,1,0:T(8,128)S(1)}, f32[8,6,8,128]{3,2,1,0:T(8,128)S(1)}, u32[]{:S(2)}, u32[]{:S(2)}) %collective-permute-start.5) | collective-permute-done | bytes 196640 | tf_op jit(solution)/shard_map/ppermute | solution.py:1011
  33.1 0.2 plan.1
  33.3 2.6 %solve.1 = (f32[2,400,128]{2,1,0:T(8,128)}, f32[2,8,128]{2,1,0:T(8,128)}, f32[2,8,128]{2,1,0:T(8,128)}) custom-call(f32[8,6,8,128]{3,2,1,0:T(8,128)S(1)} %all_to_all.5.mine_ref, f32[8,6,8,128]{3,2,1,0:T(8,128)S(1)} %collective-permute-done.5.other_ref, f32[6,64,256]{2,1,0:T(8,128)S(1)} %get-tuple-element.50.faces_ref, ...), custom_call_target="tpu_custom_call" | custom-call | tf_op jit(solution)/shard_map/solve/pallas_call | solution.py:1016
Async XLA Ops:
  2.3 9.4 %collective-permute-start.2 = (f32[176,128]{1,0:T(8,128)S(1)}, f32[176,128]{1,0:T(8,128)S(1)}, u32[]{:S(2)}, u32[]{:S(2)}) collective-permute-start(f32[176,128]{1,0:T(8,128)S(1)} %get-tuple-element.39), channel_id=1, source_target_pairs={{0,2},{2,0},{4,6},{6,4},{8,10},{10,8},{12,14},{14,12},{1,3},{3,1},... | collective-permute-start | bytes 270344 | tf_op jit(solution)/shard_map/ppermute | solution.py:929
  5.3 7.3 %collective-permute-start.3 = (f32[176,128]{1,0:T(8,128)S(1)}, f32[176,128]{1,0:T(8,128)S(1)}, u32[]{:S(2)}, u32[]{:S(2)}) collective-permute-start(f32[176,128]{1,0:T(8,128)S(1)} %get-tuple-element.40), channel_id=1, source_target_pairs={{0,14},{2,4},{4,2},{6,8},{8,6},{10,12},{12,10},{14,0},{1,15},{3,5}... | collective-permute-start | bytes 270344 | tf_op jit(solution)/shard_map/ppermute | solution.py:932
  9.6 9.7 %collective-permute-start = (f32[312,128]{1,0:T(8,128)S(1)}, f32[312,128]{1,0:T(8,128)S(1)}, u32[]{:S(2)}, u32[]{:S(2)}) collective-permute-start(f32[312,128]{1,0:T(8,128)S(1)} %get-tuple-element.34), channel_id=1, source_target_pairs={{0,2},{2,0},{4,6},{6,4},{8,10},{10,8},{12,14},{14,12},{1,3},{3,1},... | collective-permute-start | bytes 479240 | tf_op jit(solution)/shard_map/ppermute | solution.py:941
  9.7 9.6 %collective-permute-start.1 = (f32[312,128]{1,0:T(8,128)S(1)}, f32[312,128]{1,0:T(8,128)S(1)}, u32[]{:S(2)}, u32[]{:S(2)}) collective-permute-start(f32[312,128]{1,0:T(8,128)S(1)} %get-tuple-element.35), channel_id=1, source_target_pairs={{0,14},{2,4},{4,2},{6,8},{8,6},{10,12},{12,10},{14,0},{1,15},{3,5}... | collective-permute-start | bytes 479240 | tf_op jit(solution)/shard_map/ppermute | solution.py:942
  12.8 1.4 %collective-permute-start.4 = (f32[240,128]{1,0:T(8,128)S(1)}, f32[240,128]{1,0:T(8,128)S(1)}, u32[]{:S(2)}, u32[]{:S(2)}) collective-permute-start(f32[240,128]{1,0:T(8,128)S(1)} %get-tuple-element.43.mine_ref), channel_id=1, source_target_pairs={{0,1},{1,0},{2,3},{3,2},{4,5},{5,4},{6,7},{7,6},{8,9},{9,8},{10,11... | collective-permute-start | bytes 368648 | tf_op jit(solution)/shard_map/ppermute | solution.py:953
  31.7 1.4 %collective-permute-start.5 = (f32[8,6,8,128]{3,2,1,0:T(8,128)S(1)}, f32[8,6,8,128]{3,2,1,0:T(8,128)S(1)}, u32[]{:S(2)}, u32[]{:S(2)}) collective-permute-start(f32[8,6,8,128]{3,2,1,0:T(8,128)S(1)} %all_to_all.5.mine_ref), channel_id=1, source_target_pairs={{0,1},{1,0},{2,3},{3,2},{4,5},{5,4},{6,7},{7,6},{8,9},{9,8},{10,11... | collective-permute-start | bytes 589832 | tf_op jit(solution)/shard_map/ppermute | solution.py:1011

commit v11 on v10

--- a/solution.py
+++ b/solution.py
@@ -44,11 +44,11 @@
 
 
 def state_rows(levels):
-    return 2 * levels + 2, levels + 2
+    return 2 * (levels - 1), levels - 1
 
 
 def hist_rows(pairs):
-    return pairs + 8, pairs + 3
+    return pairs + 9, pairs + 3
 
 
 def pack_kernel(levels, padded, *refs):
@@ -123,7 +123,8 @@
         start = SUB * close + index * distant if far else index * close
         put(outs[2:4], start, hist_ref[upper], hist_ref[lower])
         start = start + pairs
-        put(outs[2:4], start, masked[upper : upper + 1], masked[lower : lower + 1])
+        kind = masked if far else spread
+        put(outs[2:4], start, kind[upper : upper + 1], kind[lower : lower + 1])
         for tracer in range(2):
             here = pl.ds(tracer * padded, 1)
             put(outs[2:4], start + 1 + tracer, rows_ref[upper, here, :], rows_ref[lower, here, :])
@@ -132,6 +133,7 @@
             put(outs[2:4], start + 3, rows_ref[upper, here, :], rows_ref[lower, here, :])
             here = pl.ds(padded + levels, 1)
             put(outs[2:4], start + 7, rows_ref[upper, here, :], rows_ref[lower, here, :])
+            put(outs[2:4], start + 8, depth[upper : upper + 1], depth[lower : lower + 1])
     last = SUB * close + (REACH - SUB) * distant
     folds = outs[2].shape[0] - FOLD
     if last < folds:
@@ -221,7 +223,7 @@
         second_ref[here, :] = jnp.where(even, lower, upper)
 
     for i in range(SUB):
-        for start, size, place in ((0, levels + 2, 0), (padded, levels, second)):
+        for start, size, place in ((1, levels - 1, 0), (padded + 1, levels - 1, second)):
             here = pl.ds(start, size)
             put(i * near + place, rows_ref[rows - SUB + i, here, :], rows_ref[i, here, :])
     if SUB * near < first_ref.shape[0]:
@@ -374,8 +376,10 @@
     groups = [None] * slot_groups(rows, cols)
     for at in range(-REACH, rows + REACH):
         get = low if at < 0 else high
+        limit = None
         if 0 <= at < rows:
             own = rows_ref.at[at]
+            limit = levels + 1
             get = lambda place, size: own[pl.ds(place, size), :]
             apart = hist_ref[at]
             places = {0: levels, 6: 0, 7: padded, 5: padded + levels}
@@ -386,6 +390,7 @@
             start = start + pairs
             places = {0: start, 6: start + 1, 7: start + 2}
             places.update({1 + field: start + 3 + field for field in range(5)})
+            limit = start + 8
         else:
             start = SUB * close + (at + REACH if at < 0 else at - rows - SUB) * distant
             apart = get(start, pairs)
@@ -398,8 +403,8 @@
         groups[group] = moved if groups[group] is None else groups[group] + moved
         for field, place in places.items():
             value = get(place, 1)
-            if field == 0 and 0 <= at < rows:
-                value = jnp.where(get(levels + 1, 1) > 0.5, value, 0.0)
+            if field == 0 and limit is not None:
+                value = jnp.where(get(limit, 1) > 0.5, value, 0.0)
             out_ref[pl.ds(fields + field * tall + at + rows, 1), :] = value
     for at, group in enumerate(groups):
         swap_ref[pl.ds(at * pairs, pairs), :] = group
@@ -556,21 +561,28 @@
 
 
 def mix_kernel(
-    levels, padded, rows_ref, first_ref, second_ref, own_face_ref, inner_ref, _,
-    out_ref, face_ref, outer_ref, halo_ref
+    levels, padded, pairs, rows_ref, first_ref, second_ref, first_hist_ref, second_hist_ref,
+    own_face_ref, inner_ref, _, out_ref, face_ref, outer_ref, halo_ref
 ):
     rows, _, cols = rows_ref.shape
     count = rows + 2 * SUB
     near, second = state_rows(levels)
     rest = jnp.zeros((padded - levels, cols), F32)
-    low, high = received(first_ref, second_ref)
+    close, _ = hist_rows(pairs)
+    state_of = received(first_ref, second_ref)
+    hist_of = received(first_hist_ref, second_hist_ref)
     for i in range(2 * SUB):
-        get = low if i < SUB else high
         at = i % SUB * near
+        start = i % SUB * close + pairs
+        state, hist = state_of[i // SUB], hist_of[i // SUB]
         halo_ref[i, pl.ds(levels, padded - levels), :] = rest
         halo_ref[i, pl.ds(padded + levels, padded - levels), :] = rest
-        halo_ref[i, pl.ds(0, levels + 2), :] = get(at, levels + 2)
-        halo_ref[i, pl.ds(padded, levels), :] = get(at + second, levels)
+        halo_ref[i, pl.ds(0, 1), :] = hist(start + 1, 1)
+        halo_ref[i, pl.ds(1, levels - 1), :] = state(at, levels - 1)
+        halo_ref[i, pl.ds(levels, 1), :] = hist(start, 1)
+        halo_ref[i, pl.ds(levels + 1, 1), :] = hist(start + 8, 1)
+        halo_ref[i, pl.ds(padded, 1), :] = hist(start + 2, 1)
+        halo_ref[i, pl.ds(padded + 1, levels - 1), :] = state(at + second, levels - 1)
     level = iota((padded, cols), 0).astype(F32)
 
     def state_row(i):
@@ -992,7 +1004,7 @@
     )(border, border_other, step, change)
     tall = rows + 2 * SUB
     (mixed,) = call(
-        functools.partial(mix_kernel, levels, padded),
+        functools.partial(mix_kernel, levels, padded, pairs),
         [(rows, planes, cols)],
         scratch=[
             pltpu.VMEM((3, tall, padded, cols), F32),
@@ -1000,7 +1012,7 @@
             pltpu.VMEM((2 * SUB, planes, cols), F32),
         ],
         name="mix",
-    )(packed, first, second, own_face, inner, near_start)
+    )(packed, first, second, first_hist, second_hist, own_face, inner, near_start)
     mixed, fields = call(
         functools.partial(fields_kernel, levels, padded, scale),
         [flat, (loops, 6, rows, cols)],

time: 36.1 us -> 35.8 us (level)
  transfers between devices with their start and end apart: 6 -> 6, of which waited for: 4 -> 4; matrix products, arithmetic and copies ran while one was open for 0% -> 0% of each run, Pallas kernels for 12% -> 13%
where the time goes in v11:
time: 35.8 us; the launch traced here: 35.6 us
  blocking collectives  11.1 us (31%)
  Pallas kernels  10.1 us (28%)
  starting transfers between devices  8.62 us (24%)
  waiting for transfers between devices  5.02 us (14%)
  between operations  0.71 us (2%)
    all_to_all x1, blocking collectives, on_device(): mine = lax.all_to_all(fields, 'loop', 0, 0)  11.1 us
    ppermute x1, starting transfers between devices, on_device(): second_hist = lax.ppermute(second_hist, 'loop', following)  3.57 us
    ppermute x1, starting transfers between devices, on_device(): first_hist = lax.ppermute(first_hist, 'loop', partner)  3 us
    pallas_call x1, Pallas kernels, on_device(): call(functools.partial(solve_kernel, levels, scale), shapes, scratch=[plt...  2.59 us
    ppermute x1, waiting for transfers between devices, on_device(): first = lax.ppermute(first, 'loop', partner)  2.42 us
    pallas_call x1, Pallas kernels, on_device(): pl.pallas_call(functools.partial(basis_kernel, rows, pairs), out_shape=[j...  1.91 us
    ppermute x1, starting transfers between devices, on_device(): second = lax.ppermute(second, 'loop', following)  1.9 us
    pallas_call x1, Pallas kernels, on_device(): pl.pallas_call(functools.partial(pack_kernel, levels, padded), out_shape=...  1.61 us
  transfers between devices with their start and end apart: 6, of which 4 were waited for; matrix products, arithmetic and copies ran while one was open for 0% of the time, Pallas kernels for 13%

profile of v11, /device:TPU:0, one launch (start us, length us, event | category | flops | bytes accessed | tf_op | source)
XLA Modules:
  0.0 35.6 jit_solution(3227625426945528)
XLA Ops:
  0.6 1.6 %pack.1 = (f32[8,112,128]{2,1,0:T(8,128)S(1)}, f32[8,16,128]{2,1,0:T(8,128)S(1)}, f32[176,128]{1,0:T(8,128)S(1)}, f32[176,128]{1,0:T(8,128)S(1)}, f32[128,128]{1,0:T(8,128)S(1)}, /*index=5*/f32[128,128]{1,0:T(8,128)S(1)}) custom-call(f32[2,400,128]{2,1,0:T(8,128)} %bitcast.18, f32[2,8,128]{2,1,0:T(8,128)} %refs_1_.1, s32[8,128]{1,0:T(8,128)} %refs_2_.1, ...), custom_call_target="tpu_custom_call" | custom-call | tf_op jit(solution)/shard_map/pack/pallas_call | solution.py:926
  2.3 3.0 %collective-permute-start.2 = (f32[176,128]{1,0:T(8,128)S(1)}, f32[176,128]{1,0:T(8,128)S(1)}, u32[]{:S(2)}, u32[]{:S(2)}) collective-permute-start(f32[176,128]{1,0:T(8,128)S(1)} %get-tuple-element.36), channel_id=1, source_target_pairs={{0,2},{2,0},{4,6},{6,4},{8,10},{10,8},{12,14},{14,12},{1,3},{3,1},... | collective-permute-start | bytes 270344 | tf_op jit(solution)/shard_map/ppermute | solution.py:941
  5.3 3.6 %collective-permute-start.3 = (f32[176,128]{1,0:T(8,128)S(1)}, f32[176,128]{1,0:T(8,128)S(1)}, u32[]{:S(2)}, u32[]{:S(2)}) collective-permute-start(f32[176,128]{1,0:T(8,128)S(1)} %get-tuple-element.37), channel_id=1, source_target_pairs={{0,14},{2,4},{4,2},{6,8},{8,6},{10,12},{12,10},{14,0},{1,15},{3,5}... | collective-permute-start | bytes 270344 | tf_op jit(solution)/shard_map/ppermute | solution.py:944
  8.8 0.8 %pairs.1 = (f32[296,128]{1,0:T(8,128)S(1)}, f32[296,128]{1,0:T(8,128)S(1)}, f32[112,128]{1,0:T(8,128)S(1)}, f32[8,128]{1,0:T(8,128)S(1)}, f32[4,8,128]{2,1,0:T(8...) custom-call(f32[8,112,128]{2,1,0:T(8,128)S(1)} %get-tuple-element.31.rows_ref, ...), custom_call_target="tpu_custom_call" | custom-call | tf_op jit(solution)/shard_map/pairs/pallas_call | solution.py:945
  9.6 0.1 collective-permute-start
  9.7 1.9 %collective-permute-start.1 = (f32[296,128]{1,0:T(8,128)S(1)}, f32[296,128]{1,0:T(8,128)S(1)}, u32[]{:S(2)}, u32[]{:S(2)}) collective-permute-start(f32[296,128]{1,0:T(8,128)S(1)} %get-tuple-element.35), channel_id=1, source_target_pairs={{0,14},{2,4},{4,2},{6,8},{8,6},{10,12},{12,10},{14,0},{1,15},{3,5}... | collective-permute-start | bytes 454664 | tf_op jit(solution)/shard_map/ppermute | solution.py:954
  11.6 0.0 collective-permute-done.2.first_ref.first_hist_ref
  11.6 1.0 %collective-permute-done.3.second_ref.second_hist_ref = f32[176,128]{1,0:T(8,128)S(1)} collective-permute-done((f32[176,128]{1,0:T(8,128)S(1)}, f32[176,128]{1,0:T(8,128)S(1)}, u32[]{:S(2)}, u32[]{:S(2)}) %collective-permute-start.3) | collective-permute-done | bytes 90144 | tf_op jit(solution)/shard_map/ppermute | solution.py:944
  12.6 0.2 border.1
  12.8 0.1 collective-permute-start.4
  12.9 1.1 %hold.1 = (f32[400,128]{1,0:T(8,128)S(1)}, f32[2,400,128]{2,1,0:T(8,128)S(1)}) custom-call(f32[400,128]{1,0:T(8,128)} %bitcast.17, f32[2,400,128]{2,1,0:T(8,128)} %bitcast.15), custom_call_target="tpu_custom_call" | custom-call | tf_op jit(solution)/shard_map/hold/pallas_call | solution.py:966
  14.0 0.2 collective-permute-done.4.other_ref
  14.2 1.9 %basis.1 = (f32[11,8,16,128]{3,2,1,0:T(8,128)S(1)}, f32[6,24,256]{2,1,0:T(8,128)S(1)}, f32[2,8,128]{2,1,0:T(8,128)S(1)}, f32[8,128]{1,0:T(8,128)S(1)}) custom-call(f32[544,128]{1,0:T(8,128)S(1)} %get-tuple-element.42.mine_ref, f32[240,128]{1,0:T(8,128)S(1)} %collective-permute-done.4.other_ref, f32[8,16,128]{2,1,0:T(8,128)S(1)} %bitcast.9, ...), custom_call_target="tpu_custom_call" | custom-call | tf_op jit(solution)/shard_map/basis/pallas_call | solution.py:992
  16.1 0.4 %strip.1.extra_ref = f32[112,128]{1,0:T(8,128)S(1)} custom-call(f32[240,128]{1,0:T(8,128)S(1)} %get-tuple-element.43.mine_ref, f32[240,128]{1,0:T(8,128)S(1)} %collective-permute-done.4.other_ref, f32[400,128]{1,0:T(8,128)S(1)} %get-tuple-element.45._.weight_ref), custom_call_target="tpu_custom_call" | custom-call | tf_op jit(solution)/shard_map/strip/pallas_call | solution.py:975
  16.6 2.4 %collective-permute-done.first_ref = f32[296,128]{1,0:T(8,128)S(1)} collective-permute-done((f32[296,128]{1,0:T(8,128)S(1)}, f32[296,128]{1,0:T(8,128)S(1)}, u32[]{:S(2)}, u32[]{:S(2)}) %collective-permute-start) | collective-permute-done | bytes 151584 | tf_op jit(solution)/shard_map/ppermute | solution.py:953
  19.0 0.0 collective-permute-done.1.second_ref
  19.0 0.8 %mix.1.main_ref = f32[8,112,128]{2,1,0:T(8,128)S(1)} custom-call(f32[8,112,128]{2,1,0:T(8,128)S(1)} %get-tuple-element.31.rows_ref, f32[296,128]{1,0:T(8,128)S(1)} %collective-permute-done.first_ref, f32[296,128]{1,0:T(8,128)S(1)} %collective-permute-done.1.second_ref, f32[176,128]{1,0:T(8,128)S(1)} %collective-permute-done.2.first_ref.first_hist_ref, ...), custom_call_target="tpu_custom_call" | custom-call | tf_op jit(solution)/shard_map/mix/pallas_call | solution.py:1006
  19.8 0.4 %fields.1 = (f32[2,400,128]{2,1,0:T(8,128)S(1)}, f32[8,6,8,128]{3,2,1,0:T(8,128)S(1)}) custom-call(f32[8,112,128]{2,1,0:T(8,128)S(1)} %get-tuple-element.31.rows_ref, f32[8,112,128]{2,1,0:T(8,128)S(1)} %mix.1.main_ref, f32[112,128]{1,0:T(8,128)S(1)} %strip.1.extra_ref, f32[400,128]{1,0:T(8,128)S(1)} %get-tuple-element.45._.weight_ref, ...), custom_call_target="tpu_custom_call" | custom-call | tf_op jit(solution)/shard_map/fields/pallas_call | solution.py:1016
  20.2 11.1 %all_to_all.5.mine_ref = f32[8,6,8,128]{3,2,1,0:T(8,128)S(1)} all-to-all(f32[8,6,8,128]{3,2,1,0:T(8,128)S(1)} %get-tuple-element.49), channel_id=1, replica_groups=mesh['members'=2,'loop'=8,'lat'=2] {'loop'}, dimensions={0} | all-to-all | bytes 393216 | tf_op jit(solution)/shard_map/all_to_all | solution.py:1022
  31.4 0.0 collective-permute-start.5
  31.4 1.4 %collective-permute-done.5.other_ref = f32[8,6,8,128]{3,2,1,0:T(8,128)S(1)} collective-permute-done((f32[8,6,8,128]{3,2,1,0:T(8,128)S(1)}, f32[8,6,8,128]{3,2,1,0:T(8,128)S(1)}, u32[]{:S(2)}, u32[]{:S(2)}) %collective-permute-start.5) | collective-permute-done | bytes 196640 | tf_op jit(solution)/shard_map/ppermute | solution.py:1023
  32.8 0.2 plan.1
  33.0 2.6 %solve.1 = (f32[2,400,128]{2,1,0:T(8,128)}, f32[2,8,128]{2,1,0:T(8,128)}, f32[2,8,128]{2,1,0:T(8,128)}) custom-call(f32[8,6,8,128]{3,2,1,0:T(8,128)S(1)} %all_to_all.5.mine_ref, f32[8,6,8,128]{3,2,1,0:T(8,128)S(1)} %collective-permute-done.5.other_ref, f32[6,64,256]{2,1,0:T(8,128)S(1)} %get-tuple-element.50.faces_ref, ...), custom_call_target="tpu_custom_call" | custom-call | tf_op jit(solution)/shard_map/solve/pallas_call | solution.py:1028
Async XLA Ops:
  2.3 9.3 %collective-permute-start.2 = (f32[176,128]{1,0:T(8,128)S(1)}, f32[176,128]{1,0:T(8,128)S(1)}, u32[]{:S(2)}, u32[]{:S(2)}) collective-permute-start(f32[176,128]{1,0:T(8,128)S(1)} %get-tuple-element.36), channel_id=1, source_target_pairs={{0,2},{2,0},{4,6},{6,4},{8,10},{10,8},{12,14},{14,12},{1,3},{3,1},... | collective-permute-start | bytes 270344 | tf_op jit(solution)/shard_map/ppermute | solution.py:941
  5.3 7.3 %collective-permute-start.3 = (f32[176,128]{1,0:T(8,128)S(1)}, f32[176,128]{1,0:T(8,128)S(1)}, u32[]{:S(2)}, u32[]{:S(2)}) collective-permute-start(f32[176,128]{1,0:T(8,128)S(1)} %get-tuple-element.37), channel_id=1, source_target_pairs={{0,14},{2,4},{4,2},{6,8},{8,6},{10,12},{12,10},{14,0},{1,15},{3,5}... | collective-permute-start | bytes 270344 | tf_op jit(solution)/shard_map/ppermute | solution.py:944
  9.6 9.4 %collective-permute-start = (f32[296,128]{1,0:T(8,128)S(1)}, f32[296,128]{1,0:T(8,128)S(1)}, u32[]{:S(2)}, u32[]{:S(2)}) collective-permute-start(f32[296,128]{1,0:T(8,128)S(1)} %get-tuple-element.34), channel_id=1, source_target_pairs={{0,2},{2,0},{4,6},{6,4},{8,10},{10,8},{12,14},{14,12},{1,3},{3,1},... | collective-permute-start | bytes 454664 | tf_op jit(solution)/shard_map/ppermute | solution.py:953
  9.7 9.3 %collective-permute-start.1 = (f32[296,128]{1,0:T(8,128)S(1)}, f32[296,128]{1,0:T(8,128)S(1)}, u32[]{:S(2)}, u32[]{:S(2)}) collective-permute-start(f32[296,128]{1,0:T(8,128)S(1)} %get-tuple-element.35), channel_id=1, source_target_pairs={{0,14},{2,4},{4,2},{6,8},{8,6},{10,12},{12,10},{14,0},{1,15},{3,5}... | collective-permute-start | bytes 454664 | tf_op jit(solution)/shard_map/ppermute | solution.py:954
  12.8 1.4 %collective-permute-start.4 = (f32[240,128]{1,0:T(8,128)S(1)}, f32[240,128]{1,0:T(8,128)S(1)}, u32[]{:S(2)}, u32[]{:S(2)}) collective-permute-start(f32[240,128]{1,0:T(8,128)S(1)} %get-tuple-element.43.mine_ref), channel_id=1, source_target_pairs={{0,1},{1,0},{2,3},{3,2},{4,5},{5,4},{6,7},{7,6},{8,9},{9,8},{10,11... | collective-permute-start | bytes 368648 | tf_op jit(solution)/shard_map/ppermute | solution.py:965
  31.4 1.4 %collective-permute-start.5 = (f32[8,6,8,128]{3,2,1,0:T(8,128)S(1)}, f32[8,6,8,128]{3,2,1,0:T(8,128)S(1)}, u32[]{:S(2)}, u32[]{:S(2)}) collective-permute-start(f32[8,6,8,128]{3,2,1,0:T(8,128)S(1)} %all_to_all.5.mine_ref), channel_id=1, source_target_pairs={{0,1},{1,0},{2,3},{3,2},{4,5},{5,4},{6,7},{7,6},{8,9},{9,8},{10,11... | collective-permute-start | bytes 589832 | tf_op jit(solution)/shard_map/ppermute | solution.py:1023

commit v12 on v11

--- a/solution.py
+++ b/solution.py
@@ -58,6 +58,8 @@
     rows, cols = targets[2].shape
     copies = []
     for at, (source, target) in enumerate(zip(sources, targets)):
+        if at == 0:
+            target = target.at[:, pl.ds(0, source.shape[1]), :]
         if at == 8:
             source = source.at[:, pl.ds(0, rows), :]
         copies.append(pltpu.make_async_copy(source, target, sems.at[at]))
@@ -628,9 +630,10 @@
 
 
 def hold_kernel(weight_hbm, observed_hbm, weight_ref, observed_ref, sems):
+    size = weight_hbm.shape[0]
     copies = [
-        pltpu.make_async_copy(weight_hbm, weight_ref, sems.at[0]),
-        pltpu.make_async_copy(observed_hbm, observed_ref, sems.at[1]),
+        pltpu.make_async_copy(weight_hbm, weight_ref.at[pl.ds(0, size), :], sems.at[0]),
+        pltpu.make_async_copy(observed_hbm, observed_ref.at[:, pl.ds(0, size), :], sems.at[1]),
     ]
     for copy in copies:
         copy.start()
@@ -917,7 +920,8 @@
         state, control, depth_index, diffusivity,
         history_step.reshape(-1, cols), history_change.reshape(-1, cols), damping, weight, observed,
     )
-    held = [x.shape for x in inputs[:-1]] + [(2, rows, cols)]
+    whole = round_up(levels, 8) * rows
+    held = [(2, whole, cols)] + [x.shape for x in inputs[1:-1]] + [(2, rows, cols)]
     close, distant = hist_rows(pairs)
     sent_hist = (round_up(SUB * close + (REACH - SUB) * distant, 8) + FOLD, cols)
     sent = (round_up(SUB * state_rows(levels)[0], 8), cols)
@@ -965,7 +969,7 @@
     border_other = lax.ppermute(border_mine, "lat", swap)
     held_weight, held_observed = pl.pallas_call(
         hold_kernel,
-        out_shape=[jax.ShapeDtypeStruct(x.shape, F32) for x in (weight, observed)],
+        out_shape=[jax.ShapeDtypeStruct(shape, F32) for shape in ((whole, cols), (2, whole, cols))],
         in_specs=[pl.BlockSpec(memory_space=pltpu.HBM)] * 2,
         out_specs=[VMEM] * 2,
         scratch_shapes=[pltpu.SemaphoreType.DMA((2,))],
@@ -1015,7 +1019,7 @@
     )(packed, first, second, first_hist, second_hist, own_face, inner, near_start)
     mixed, fields = call(
         functools.partial(fields_kernel, levels, padded, scale),
-        [flat, (loops, 6, rows, cols)],
+        [(2, whole, cols), (loops, 6, rows, cols)],
         scratch=[pltpu.VMEM((6, rows, cols), F32)],
         name="fields",
     )(packed, mixed, extra, held_weight, held_observed, basis, near_start, fixed)

time: 35.8 us -> 35.8 us (level)
  no operation moved by 1% of the time
where the time goes in v12:
time: 35.8 us; the launch traced here: 35.6 us
  blocking collectives  11.1 us (31%)
  Pallas kernels  10.1 us (28%)
  starting transfers between devices  8.62 us (24%)
  waiting for transfers between devices  5 us (14%)
  between operations  0.71 us (2%)
    all_to_all x1, blocking collectives, on_device(): mine = lax.all_to_all(fields, 'loop', 0, 0)  11.1 us
    ppermute x1, starting transfers between devices, on_device(): second_hist = lax.ppermute(second_hist, 'loop', following)  3.57 us
    ppermute x1, starting transfers between devices, on_device(): first_hist = lax.ppermute(first_hist, 'loop', partner)  3 us
    pallas_call x1, Pallas kernels, on_device(): call(functools.partial(solve_kernel, levels, scale), shapes, scratch=[plt...  2.59 us
    ppermute x1, waiting for transfers between devices, on_device(): first = lax.ppermute(first, 'loop', partner)  2.42 us
    pallas_call x1, Pallas kernels, on_device(): pl.pallas_call(functools.partial(basis_kernel, rows, pairs), out_shape=[j...  1.91 us
    ppermute x1, starting transfers between devices, on_device(): second = lax.ppermute(second, 'loop', following)  1.9 us
    pallas_call x1, Pallas kernels, on_device(): pl.pallas_call(functools.partial(pack_kernel, levels, padded), out_shape=...  1.62 us
  transfers between devices with their start and end apart: 6, of which 4 were waited for; matrix products, arithmetic and copies ran while one was open for 0% of the time, Pallas kernels for 13%

profile of v12, /device:TPU:0, one launch (start us, length us, event | category | flops | bytes accessed | tf_op | source)
XLA Modules:
  0.0 35.6 jit_solution(17241423154950586905)
XLA Ops:
  0.6 1.6 %pack.1 = (f32[8,112,128]{2,1,0:T(8,128)S(1)}, f32[8,16,128]{2,1,0:T(8,128)S(1)}, f32[176,128]{1,0:T(8,128)S(1)}, f32[176,128]{1,0:T(8,128)S(1)}, f32[128,128]{1,0:T(8,128)S(1)}, /*index=5*/f32[128,128]{1,0:T(8,128)S(1)}) custom-call(f32[2,400,128]{2,1,0:T(8,128)} %bitcast.18, f32[2,8,128]{2,1,0:T(8,128)} %refs_1_.1, s32[8,128]{1,0:T(8,128)} %refs_2_.1, ...), custom_call_target="tpu_custom_call" | custom-call | tf_op jit(solution)/shard_map/pack/pallas_call | solution.py:930
  2.3 3.0 %collective-permute-start.2 = (f32[176,128]{1,0:T(8,128)S(1)}, f32[176,128]{1,0:T(8,128)S(1)}, u32[]{:S(2)}, u32[]{:S(2)}) collective-permute-start(f32[176,128]{1,0:T(8,128)S(1)} %get-tuple-element.36), channel_id=1, source_target_pairs={{0,2},{2,0},{4,6},{6,4},{8,10},{10,8},{12,14},{14,12},{1,3},{3,1},... | collective-permute-start | bytes 270344 | tf_op jit(solution)/shard_map/ppermute | solution.py:945
  5.3 3.6 %collective-permute-start.3 = (f32[176,128]{1,0:T(8,128)S(1)}, f32[176,128]{1,0:T(8,128)S(1)}, u32[]{:S(2)}, u32[]{:S(2)}) collective-permute-start(f32[176,128]{1,0:T(8,128)S(1)} %get-tuple-element.37), channel_id=1, source_target_pairs={{0,14},{2,4},{4,2},{6,8},{8,6},{10,12},{12,10},{14,0},{1,15},{3,5}... | collective-permute-start | bytes 270344 | tf_op jit(solution)/shard_map/ppermute | solution.py:948
  8.8 0.8 %pairs.1 = (f32[296,128]{1,0:T(8,128)S(1)}, f32[296,128]{1,0:T(8,128)S(1)}, f32[112,128]{1,0:T(8,128)S(1)}, f32[8,128]{1,0:T(8,128)S(1)}, f32[4,8,128]{2,1,0:T(8...) custom-call(f32[8,112,128]{2,1,0:T(8,128)S(1)} %get-tuple-element.31.rows_ref, ...), custom_call_target="tpu_custom_call" | custom-call | tf_op jit(solution)/shard_map/pairs/pallas_call | solution.py:949
  9.6 0.1 collective-permute-start
  9.7 1.9 %collective-permute-start.1 = (f32[296,128]{1,0:T(8,128)S(1)}, f32[296,128]{1,0:T(8,128)S(1)}, u32[]{:S(2)}, u32[]{:S(2)}) collective-permute-start(f32[296,128]{1,0:T(8,128)S(1)} %get-tuple-element.35), channel_id=1, source_target_pairs={{0,14},{2,4},{4,2},{6,8},{8,6},{10,12},{12,10},{14,0},{1,15},{3,5}... | collective-permute-start | bytes 454664 | tf_op jit(solution)/shard_map/ppermute | solution.py:958
  11.6 0.0 collective-permute-done.2.first_ref.first_hist_ref
  11.6 1.0 %collective-permute-done.3.second_ref.second_hist_ref = f32[176,128]{1,0:T(8,128)S(1)} collective-permute-done((f32[176,128]{1,0:T(8,128)S(1)}, f32[176,128]{1,0:T(8,128)S(1)}, u32[]{:S(2)}, u32[]{:S(2)}) %collective-permute-start.3) | collective-permute-done | bytes 90144 | tf_op jit(solution)/shard_map/ppermute | solution.py:948
  12.6 0.2 border.1
  12.8 0.1 collective-permute-start.4
  12.9 1.1 %hold.1 = (f32[448,128]{1,0:T(8,128)S(1)}, f32[2,448,128]{2,1,0:T(8,128)S(1)}) custom-call(f32[400,128]{1,0:T(8,128)} %bitcast.17, f32[2,400,128]{2,1,0:T(8,128)} %bitcast.15), custom_call_target="tpu_custom_call" | custom-call | tf_op jit(solution)/shard_map/hold/pallas_call | solution.py:970
  14.0 0.2 collective-permute-done.4.other_ref
  14.2 1.9 %basis.1 = (f32[11,8,16,128]{3,2,1,0:T(8,128)S(1)}, f32[6,24,256]{2,1,0:T(8,128)S(1)}, f32[2,8,128]{2,1,0:T(8,128)S(1)}, f32[8,128]{1,0:T(8,128)S(1)}) custom-call(f32[544,128]{1,0:T(8,128)S(1)} %get-tuple-element.42.mine_ref, f32[240,128]{1,0:T(8,128)S(1)} %collective-permute-done.4.other_ref, f32[8,16,128]{2,1,0:T(8,128)S(1)} %bitcast.9, ...), custom_call_target="tpu_custom_call" | custom-call | tf_op jit(solution)/shard_map/basis/pallas_call | solution.py:996
  16.1 0.4 %strip.1.extra_ref = f32[112,128]{1,0:T(8,128)S(1)} custom-call(f32[240,128]{1,0:T(8,128)S(1)} %get-tuple-element.43.mine_ref, f32[240,128]{1,0:T(8,128)S(1)} %collective-permute-done.4.other_ref, f32[448,128]{1,0:T(8,128)S(1)} %get-tuple-element.45._.weight_ref), custom_call_target="tpu_custom_call" | custom-call | tf_op jit(solution)/shard_map/strip/pallas_call | solution.py:979
  16.6 2.4 %collective-permute-done.first_ref = f32[296,128]{1,0:T(8,128)S(1)} collective-permute-done((f32[296,128]{1,0:T(8,128)S(1)}, f32[296,128]{1,0:T(8,128)S(1)}, u32[]{:S(2)}, u32[]{:S(2)}) %collective-permute-start) | collective-permute-done | bytes 151584 | tf_op jit(solution)/shard_map/ppermute | solution.py:957
  19.0 0.0 collective-permute-done.1.second_ref
  19.0 0.8 %mix.1.main_ref = f32[8,112,128]{2,1,0:T(8,128)S(1)} custom-call(f32[8,112,128]{2,1,0:T(8,128)S(1)} %get-tuple-element.31.rows_ref, f32[296,128]{1,0:T(8,128)S(1)} %collective-permute-done.first_ref, f32[296,128]{1,0:T(8,128)S(1)} %collective-permute-done.1.second_ref, f32[176,128]{1,0:T(8,128)S(1)} %collective-permute-done.2.first_ref.first_hist_ref, ...), custom_call_target="tpu_custom_call" | custom-call | tf_op jit(solution)/shard_map/mix/pallas_call | solution.py:1010
  19.8 0.4 %fields.1 = (f32[2,448,128]{2,1,0:T(8,128)S(1)}, f32[8,6,8,128]{3,2,1,0:T(8,128)S(1)}) custom-call(f32[8,112,128]{2,1,0:T(8,128)S(1)} %get-tuple-element.31.rows_ref, f32[8,112,128]{2,1,0:T(8,128)S(1)} %mix.1.main_ref, f32[112,128]{1,0:T(8,128)S(1)} %strip.1.extra_ref, f32[448,128]{1,0:T(8,128)S(1)} %get-tuple-element.45._.weight_ref, ...), custom_call_target="tpu_custom_call" | custom-call | tf_op jit(solution)/shard_map/fields/pallas_call | solution.py:1020
  20.2 11.1 %all_to_all.5.mine_ref = f32[8,6,8,128]{3,2,1,0:T(8,128)S(1)} all-to-all(f32[8,6,8,128]{3,2,1,0:T(8,128)S(1)} %get-tuple-element.49), channel_id=1, replica_groups=mesh['members'=2,'loop'=8,'lat'=2] {'loop'}, dimensions={0} | all-to-all | bytes 393216 | tf_op jit(solution)/shard_map/all_to_all | solution.py:1026
  31.4 0.0 collective-permute-start.5
  31.4 1.4 %collective-permute-done.5.other_ref = f32[8,6,8,128]{3,2,1,0:T(8,128)S(1)} collective-permute-done((f32[8,6,8,128]{3,2,1,0:T(8,128)S(1)}, f32[8,6,8,128]{3,2,1,0:T(8,128)S(1)}, u32[]{:S(2)}, u32[]{:S(2)}) %collective-permute-start.5) | collective-permute-done | bytes 196640 | tf_op jit(solution)/shard_map/ppermute | solution.py:1027
  32.8 0.2 plan.1
  33.0 2.6 %solve.1 = (f32[2,400,128]{2,1,0:T(8,128)}, f32[2,8,128]{2,1,0:T(8,128)}, f32[2,8,128]{2,1,0:T(8,128)}) custom-call(f32[8,6,8,128]{3,2,1,0:T(8,128)S(1)} %all_to_all.5.mine_ref, f32[8,6,8,128]{3,2,1,0:T(8,128)S(1)} %collective-permute-done.5.other_ref, f32[6,64,256]{2,1,0:T(8,128)S(1)} %get-tuple-element.50.faces_ref, ...), custom_call_target="tpu_custom_call" | custom-call | tf_op jit(solution)/shard_map/solve/pallas_call | solution.py:1032
Async XLA Ops:
  2.3 9.4 %collective-permute-start.2 = (f32[176,128]{1,0:T(8,128)S(1)}, f32[176,128]{1,0:T(8,128)S(1)}, u32[]{:S(2)}, u32[]{:S(2)}) collective-permute-start(f32[176,128]{1,0:T(8,128)S(1)} %get-tuple-element.36), channel_id=1, source_target_pairs={{0,2},{2,0},{4,6},{6,4},{8,10},{10,8},{12,14},{14,12},{1,3},{3,1},... | collective-permute-start | bytes 270344 | tf_op jit(solution)/shard_map/ppermute | solution.py:945
  5.3 7.3 %collective-permute-start.3 = (f32[176,128]{1,0:T(8,128)S(1)}, f32[176,128]{1,0:T(8,128)S(1)}, u32[]{:S(2)}, u32[]{:S(2)}) collective-permute-start(f32[176,128]{1,0:T(8,128)S(1)} %get-tuple-element.37), channel_id=1, source_target_pairs={{0,14},{2,4},{4,2},{6,8},{8,6},{10,12},{12,10},{14,0},{1,15},{3,5}... | collective-permute-start | bytes 270344 | tf_op jit(solution)/shard_map/ppermute | solution.py:948
  9.6 9.3 %collective-permute-start = (f32[296,128]{1,0:T(8,128)S(1)}, f32[296,128]{1,0:T(8,128)S(1)}, u32[]{:S(2)}, u32[]{:S(2)}) collective-permute-start(f32[296,128]{1,0:T(8,128)S(1)} %get-tuple-element.34), channel_id=1, source_target_pairs={{0,2},{2,0},{4,6},{6,4},{8,10},{10,8},{12,14},{14,12},{1,3},{3,1},... | collective-permute-start | bytes 454664 | tf_op jit(solution)/shard_map/ppermute | solution.py:957
  9.7 9.3 %collective-permute-start.1 = (f32[296,128]{1,0:T(8,128)S(1)}, f32[296,128]{1,0:T(8,128)S(1)}, u32[]{:S(2)}, u32[]{:S(2)}) collective-permute-start(f32[296,128]{1,0:T(8,128)S(1)} %get-tuple-element.35), channel_id=1, source_target_pairs={{0,14},{2,4},{4,2},{6,8},{8,6},{10,12},{12,10},{14,0},{1,15},{3,5}... | collective-permute-start | bytes 454664 | tf_op jit(solution)/shard_map/ppermute | solution.py:958
  12.8 1.4 %collective-permute-start.4 = (f32[240,128]{1,0:T(8,128)S(1)}, f32[240,128]{1,0:T(8,128)S(1)}, u32[]{:S(2)}, u32[]{:S(2)}) collective-permute-start(f32[240,128]{1,0:T(8,128)S(1)} %get-tuple-element.43.mine_ref), channel_id=1, source_target_pairs={{0,1},{1,0},{2,3},{3,2},{4,5},{5,4},{6,7},{7,6},{8,9},{9,8},{10,11... | collective-permute-start | bytes 368648 | tf_op jit(solution)/shard_map/ppermute | solution.py:969
  31.4 1.4 %collective-permute-start.5 = (f32[8,6,8,128]{3,2,1,0:T(8,128)S(1)}, f32[8,6,8,128]{3,2,1,0:T(8,128)S(1)}, u32[]{:S(2)}, u32[]{:S(2)}) collective-permute-start(f32[8,6,8,128]{3,2,1,0:T(8,128)S(1)} %all_to_all.5.mine_ref), channel_id=1, source_target_pairs={{0,1},{1,0},{2,3},{3,2},{4,5},{5,4},{6,7},{7,6},{8,9},{9,8},{10,11... | collective-permute-start | bytes 589832 | tf_op jit(solution)/shard_map/ppermute | solution.py:1027

commit v13 on v12

--- a/solution.py
+++ b/solution.py
@@ -309,7 +309,7 @@
     return result + to_above * (value - pltpu.roll(value, 1, 0))
 
 
-def plan_kernel(mine_ref, other_ref, faces_ref, plan_ref):
+def make_plan(mine_ref, other_ref, faces_ref, plan_ref):
     loops, _, rows, cols = mine_ref.shape
     closed = closed_lane(cols)
     for at, face in enumerate(surface_faces(gathered(mine_ref, other_ref, 3), closed)):
@@ -781,11 +781,12 @@
 
 def solve_kernel(
     levels, scale,
-    mine_ref, other_ref, faces_ref, near_ref, base_ref, plan_ref, mixed_ref, depth_ref, step_ref,
-    change_ref, state_ref, gradient_ref, direction_ref, kept_ref,
+    mine_ref, other_ref, near_ref, base_ref, mixed_ref, depth_ref, step_ref,
+    change_ref, state_ref, gradient_ref, direction_ref, kept_ref, faces_ref, plan_ref,
 ):
     loops, _, rows, cols = mine_ref.shape
     loop = lax.axis_index("loop")
+    make_plan(mine_ref, other_ref, faces_ref, plan_ref)
 
     def total(value):
         parts = [
@@ -1025,17 +1026,18 @@
     )(packed, mixed, extra, held_weight, held_observed, basis, near_start, fixed)
     mine = lax.all_to_all(fields, "loop", 0, 0)
     theirs = lax.ppermute(mine, "lat", swap)
-    faces, plan = call(
-        plan_kernel, [(6, height, 2 * cols), (pairs, cols)], vmem=large, name="plan"
-    )(mine, theirs)
     shapes = (flat, (2, rows, cols), (2, rows, cols))
     state_next, gradient, direction = call(
         functools.partial(solve_kernel, levels, scale),
         shapes,
-        scratch=[pltpu.VMEM((2, loops, rows, 2 * cols), F32)],
+        scratch=[
+            pltpu.VMEM((2, loops, rows, 2 * cols), F32),
+            pltpu.VMEM((6, height, 2 * cols), F32),
+            pltpu.VMEM((pairs, cols), F32),
+        ],
         vmem=large,
         name="solve",
-    )(mine, theirs, faces, around, base, plan, mixed, depth, step, change)
+    )(mine, theirs, around, base, mixed, depth, step, change)
     return (state_next.reshape(2, levels, rows, cols), gradient, direction)
 
 

time: 35.8 us -> 35.7 us (level)
  no operation moved by 1% of the time
where the time goes in v13:
time: 35.7 us; the launch traced here: 35.5 us
  blocking collectives  11.1 us (31%)
  Pallas kernels  10 us (28%)
  starting transfers between devices  8.62 us (24%)
  waiting for transfers between devices  5 us (14%)
  between operations  0.7 us (2%)
    all_to_all x1, blocking collectives, on_device(): mine = lax.all_to_all(fields, 'loop', 0, 0)  11.1 us
    ppermute x1, starting transfers between devices, on_device(): second_hist = lax.ppermute(second_hist, 'loop', following)  3.57 us
    ppermute x1, starting transfers between devices, on_device(): first_hist = lax.ppermute(first_hist, 'loop', partner)  3 us
    pallas_call x1, Pallas kernels, on_device(): call(functools.partial(solve_kernel, levels, scale), shapes, scratch=[plt...  2.7 us
    ppermute x1, waiting for transfers between devices, on_device(): first = lax.ppermute(first, 'loop', partner)  2.42 us
    pallas_call x1, Pallas kernels, on_device(): pl.pallas_call(functools.partial(basis_kernel, rows, pairs), out_shape=[j...  1.91 us
    ppermute x1, starting transfers between devices, on_device(): second = lax.ppermute(second, 'loop', following)  1.9 us
    pallas_call x1, Pallas kernels, on_device(): pl.pallas_call(functools.partial(pack_kernel, levels, padded), out_shape=...  1.62 us
  transfers between devices with their start and end apart: 6, of which 4 were waited for; matrix products, arithmetic and copies ran while one was open for 0% of the time, Pallas kernels for 13%

profile of v13, /device:TPU:0, one launch (start us, length us, event | category | flops | bytes accessed | tf_op | source)
XLA Modules:
  0.0 35.5 jit_solution(9853296092553403418)
XLA Ops:
  0.6 1.6 %pack.1 = (f32[8,112,128]{2,1,0:T(8,128)S(1)}, f32[8,16,128]{2,1,0:T(8,128)S(1)}, f32[176,128]{1,0:T(8,128)S(1)}, f32[176,128]{1,0:T(8,128)S(1)}, f32[128,128]{1,0:T(8,128)S(1)}, /*index=5*/f32[128,128]{1,0:T(8,128)S(1)}) custom-call(f32[2,400,128]{2,1,0:T(8,128)} %bitcast.18, f32[2,8,128]{2,1,0:T(8,128)} %refs_1_.1, s32[8,128]{1,0:T(8,128)} %refs_2_.1, ...), custom_call_target="tpu_custom_call" | custom-call | tf_op jit(solution)/shard_map/pack/pallas_call | solution.py:931
  2.3 3.0 %collective-permute-start.2 = (f32[176,128]{1,0:T(8,128)S(1)}, f32[176,128]{1,0:T(8,128)S(1)}, u32[]{:S(2)}, u32[]{:S(2)}) collective-permute-start(f32[176,128]{1,0:T(8,128)S(1)} %get-tuple-element.34), channel_id=1, source_target_pairs={{0,2},{2,0},{4,6},{6,4},{8,10},{10,8},{12,14},{14,12},{1,3},{3,1},... | collective-permute-start | bytes 270344 | tf_op jit(solution)/shard_map/ppermute | solution.py:946
  5.3 3.6 %collective-permute-start.3 = (f32[176,128]{1,0:T(8,128)S(1)}, f32[176,128]{1,0:T(8,128)S(1)}, u32[]{:S(2)}, u32[]{:S(2)}) collective-permute-start(f32[176,128]{1,0:T(8,128)S(1)} %get-tuple-element.35), channel_id=1, source_target_pairs={{0,14},{2,4},{4,2},{6,8},{8,6},{10,12},{12,10},{14,0},{1,15},{3,5}... | collective-permute-start | bytes 270344 | tf_op jit(solution)/shard_map/ppermute | solution.py:949
  8.8 0.8 %pairs.1 = (f32[296,128]{1,0:T(8,128)S(1)}, f32[296,128]{1,0:T(8,128)S(1)}, f32[112,128]{1,0:T(8,128)S(1)}, f32[8,128]{1,0:T(8,128)S(1)}, f32[4,8,128]{2,1,0:T(8...) custom-call(f32[8,112,128]{2,1,0:T(8,128)S(1)} %get-tuple-element.29.rows_ref, ...), custom_call_target="tpu_custom_call" | custom-call | tf_op jit(solution)/shard_map/pairs/pallas_call | solution.py:950
  9.6 0.1 collective-permute-start
  9.7 1.9 %collective-permute-start.1 = (f32[296,128]{1,0:T(8,128)S(1)}, f32[296,128]{1,0:T(8,128)S(1)}, u32[]{:S(2)}, u32[]{:S(2)}) collective-permute-start(f32[296,128]{1,0:T(8,128)S(1)} %get-tuple-element.33), channel_id=1, source_target_pairs={{0,14},{2,4},{4,2},{6,8},{8,6},{10,12},{12,10},{14,0},{1,15},{3,5}... | collective-permute-start | bytes 454664 | tf_op jit(solution)/shard_map/ppermute | solution.py:959
  11.6 0.0 collective-permute-done.2.first_ref.first_hist_ref
  11.6 1.0 %collective-permute-done.3.second_ref.second_hist_ref = f32[176,128]{1,0:T(8,128)S(1)} collective-permute-done((f32[176,128]{1,0:T(8,128)S(1)}, f32[176,128]{1,0:T(8,128)S(1)}, u32[]{:S(2)}, u32[]{:S(2)}) %collective-permute-start.3) | collective-permute-done | bytes 90144 | tf_op jit(solution)/shard_map/ppermute | solution.py:949
  12.6 0.2 border.1
  12.8 0.1 collective-permute-start.4
  12.9 1.1 %hold.1 = (f32[448,128]{1,0:T(8,128)S(1)}, f32[2,448,128]{2,1,0:T(8,128)S(1)}) custom-call(f32[400,128]{1,0:T(8,128)} %bitcast.17, f32[2,400,128]{2,1,0:T(8,128)} %bitcast.15), custom_call_target="tpu_custom_call" | custom-call | tf_op jit(solution)/shard_map/hold/pallas_call | solution.py:971
  14.0 0.2 collective-permute-done.4.other_ref
  14.2 1.9 %basis.1 = (f32[11,8,16,128]{3,2,1,0:T(8,128)S(1)}, f32[6,24,256]{2,1,0:T(8,128)S(1)}, f32[2,8,128]{2,1,0:T(8,128)S(1)}, f32[8,128]{1,0:T(8,128)S(1)}) custom-call(f32[544,128]{1,0:T(8,128)S(1)} %get-tuple-element.40.mine_ref, f32[240,128]{1,0:T(8,128)S(1)} %collective-permute-done.4.other_ref, f32[8,16,128]{2,1,0:T(8,128)S(1)} %bitcast.9, ...), custom_call_target="tpu_custom_call" | custom-call | tf_op jit(solution)/shard_map/basis/pallas_call | solution.py:997
  16.1 0.4 %strip.1.extra_ref = f32[112,128]{1,0:T(8,128)S(1)} custom-call(f32[240,128]{1,0:T(8,128)S(1)} %get-tuple-element.41.mine_ref, f32[240,128]{1,0:T(8,128)S(1)} %collective-permute-done.4.other_ref, f32[448,128]{1,0:T(8,128)S(1)} %get-tuple-element.43._.weight_ref), custom_call_target="tpu_custom_call" | custom-call | tf_op jit(solution)/shard_map/strip/pallas_call | solution.py:980
  16.6 2.4 %collective-permute-done.first_ref = f32[296,128]{1,0:T(8,128)S(1)} collective-permute-done((f32[296,128]{1,0:T(8,128)S(1)}, f32[296,128]{1,0:T(8,128)S(1)}, u32[]{:S(2)}, u32[]{:S(2)}) %collective-permute-start) | collective-permute-done | bytes 151584 | tf_op jit(solution)/shard_map/ppermute | solution.py:958
  19.0 0.0 collective-permute-done.1.second_ref
  19.0 0.8 %mix.1.main_ref = f32[8,112,128]{2,1,0:T(8,128)S(1)} custom-call(f32[8,112,128]{2,1,0:T(8,128)S(1)} %get-tuple-element.29.rows_ref, f32[296,128]{1,0:T(8,128)S(1)} %collective-permute-done.first_ref, f32[296,128]{1,0:T(8,128)S(1)} %collective-permute-done.1.second_ref, f32[176,128]{1,0:T(8,128)S(1)} %collective-permute-done.2.first_ref.first_hist_ref, ...), custom_call_target="tpu_custom_call" | custom-call | tf_op jit(solution)/shard_map/mix/pallas_call | solution.py:1011
  19.8 0.4 %fields.1 = (f32[2,448,128]{2,1,0:T(8,128)S(1)}, f32[8,6,8,128]{3,2,1,0:T(8,128)S(1)}) custom-call(f32[8,112,128]{2,1,0:T(8,128)S(1)} %get-tuple-element.29.rows_ref, f32[8,112,128]{2,1,0:T(8,128)S(1)} %mix.1.main_ref, f32[112,128]{1,0:T(8,128)S(1)} %strip.1.extra_ref, f32[448,128]{1,0:T(8,128)S(1)} %get-tuple-element.43._.weight_ref, ...), custom_call_target="tpu_custom_call" | custom-call | tf_op jit(solution)/shard_map/fields/pallas_call | solution.py:1021
  20.2 11.1 %all_to_all.5.mine_ref = f32[8,6,8,128]{3,2,1,0:T(8,128)S(1)} all-to-all(f32[8,6,8,128]{3,2,1,0:T(8,128)S(1)} %get-tuple-element.47), channel_id=1, replica_groups=mesh['members'=2,'loop'=8,'lat'=2] {'loop'}, dimensions={0} | all-to-all | bytes 393216 | tf_op jit(solution)/shard_map/all_to_all | solution.py:1027
  31.4 0.0 collective-permute-start.5
  31.4 1.4 %collective-permute-done.5.other_ref = f32[8,6,8,128]{3,2,1,0:T(8,128)S(1)} collective-permute-done((f32[8,6,8,128]{3,2,1,0:T(8,128)S(1)}, f32[8,6,8,128]{3,2,1,0:T(8,128)S(1)}, u32[]{:S(2)}, u32[]{:S(2)}) %collective-permute-start.5) | collective-permute-done | bytes 196640 | tf_op jit(solution)/shard_map/ppermute | solution.py:1028
  32.8 2.7 %solve.1 = (f32[2,400,128]{2,1,0:T(8,128)}, f32[2,8,128]{2,1,0:T(8,128)}, f32[2,8,128]{2,1,0:T(8,128)}) custom-call(f32[8,6,8,128]{3,2,1,0:T(8,128)S(1)} %all_to_all.5.mine_ref, f32[8,6,8,128]{3,2,1,0:T(8,128)S(1)} %collective-permute-done.5.other_ref, f32[6,24,256]{2,1,0:T(8,128)S(1)} %get-tuple-element.48.near_ref, ...), custom_call_target="tpu_custom_call" | custom-call | tf_op jit(solution)/shard_map/solve/pallas_call | solution.py:1030
Async XLA Ops:
  2.3 9.4 %collective-permute-start.2 = (f32[176,128]{1,0:T(8,128)S(1)}, f32[176,128]{1,0:T(8,128)S(1)}, u32[]{:S(2)}, u32[]{:S(2)}) collective-permute-start(f32[176,128]{1,0:T(8,128)S(1)} %get-tuple-element.34), channel_id=1, source_target_pairs={{0,2},{2,0},{4,6},{6,4},{8,10},{10,8},{12,14},{14,12},{1,3},{3,1},... | collective-permute-start | bytes 270344 | tf_op jit(solution)/shard_map/ppermute | solution.py:946
  5.3 7.3 %collective-permute-start.3 = (f32[176,128]{1,0:T(8,128)S(1)}, f32[176,128]{1,0:T(8,128)S(1)}, u32[]{:S(2)}, u32[]{:S(2)}) collective-permute-start(f32[176,128]{1,0:T(8,128)S(1)} %get-tuple-element.35), channel_id=1, source_target_pairs={{0,14},{2,4},{4,2},{6,8},{8,6},{10,12},{12,10},{14,0},{1,15},{3,5}... | collective-permute-start | bytes 270344 | tf_op jit(solution)/shard_map/ppermute | solution.py:949
  9.6 9.3 %collective-permute-start = (f32[296,128]{1,0:T(8,128)S(1)}, f32[296,128]{1,0:T(8,128)S(1)}, u32[]{:S(2)}, u32[]{:S(2)}) collective-permute-start(f32[296,128]{1,0:T(8,128)S(1)} %get-tuple-element.32), channel_id=1, source_target_pairs={{0,2},{2,0},{4,6},{6,4},{8,10},{10,8},{12,14},{14,12},{1,3},{3,1},... | collective-permute-start | bytes 454664 | tf_op jit(solution)/shard_map/ppermute | solution.py:958
  9.7 9.3 %collective-permute-start.1 = (f32[296,128]{1,0:T(8,128)S(1)}, f32[296,128]{1,0:T(8,128)S(1)}, u32[]{:S(2)}, u32[]{:S(2)}) collective-permute-start(f32[296,128]{1,0:T(8,128)S(1)} %get-tuple-element.33), channel_id=1, source_target_pairs={{0,14},{2,4},{4,2},{6,8},{8,6},{10,12},{12,10},{14,0},{1,15},{3,5}... | collective-permute-start | bytes 454664 | tf_op jit(solution)/shard_map/ppermute | solution.py:959
  12.8 1.4 %collective-permute-start.4 = (f32[240,128]{1,0:T(8,128)S(1)}, f32[240,128]{1,0:T(8,128)S(1)}, u32[]{:S(2)}, u32[]{:S(2)}) collective-permute-start(f32[240,128]{1,0:T(8,128)S(1)} %get-tuple-element.41.mine_ref), channel_id=1, source_target_pairs={{0,1},{1,0},{2,3},{3,2},{4,5},{5,4},{6,7},{7,6},{8,9},{9,8},{10,11... | collective-permute-start | bytes 368648 | tf_op jit(solution)/shard_map/ppermute | solution.py:970
  31.4 1.4 %collective-permute-start.5 = (f32[8,6,8,128]{3,2,1,0:T(8,128)S(1)}, f32[8,6,8,128]{3,2,1,0:T(8,128)S(1)}, u32[]{:S(2)}, u32[]{:S(2)}) collective-permute-start(f32[8,6,8,128]{3,2,1,0:T(8,128)S(1)} %all_to_all.5.mine_ref), channel_id=1, source_target_pairs={{0,1},{1,0},{2,3},{3,2},{4,5},{5,4},{6,7},{7,6},{8,9},{9,8},{10,11... | collective-permute-start | bytes 589832 | tf_op jit(solution)/shard_map/ppermute | solution.py:1028
